TPU v7x, 32 devices: a whole 2x2x4 slice. The times are simulated.
32 devices in a mesh: fsdp: 32 (over z, y, x, core).
Axes of the slice: x: 2, y: 2, z: 4, core: 2. Of those that a mesh axis runs over, the one named last changes fastest.
Arguments:
- tokens: bfloat16 [6144, 2048], P('fsdp'), may hold values from -6 to 6
- cotangent: bfloat16 [6144, 2048], P('fsdp'), may hold values from -6 to 6
- norm_gains: bfloat16 [4, 2048], P(None, 'fsdp'), may hold values from 0.5 to 1.5
- attention_in: bfloat16 [2048, 6144], P('fsdp'), may hold values from -0.125 to 0.125
- attention_out: bfloat16 [2048, 2048], P('fsdp'), may hold values from -0.75 to 0.75
- router_weight: bfloat16 [2048, 16], P('fsdp'), may hold values from -0.0625 to 0.0625
- expert_in: bfloat16 [32, 2048, 1024], P('fsdp'), may hold values from -0.125 to 0.125
- expert_out: bfloat16 [32, 512, 2048], P('fsdp'), may hold values from -0.75 to 0.75
- routes: int32 [6144, 8], P('fsdp'), may hold values from 0 to 15, all different within a row; in each aligned block of 192 rows (0 to 191, 192 to 383, ...) at most 128 rows name the same one
- lengths: int32 [32, 3], P('fsdp'), may hold values from 1 to 96, 192 in all within a row
Outputs:
- output: bfloat16 [6144, 2048], P('fsdp')
- input_grad: float32 [6144, 2048], P('fsdp')
- gains_grad: float32 [4, 2048], P(None, 'fsdp')
- attention_in_grad: float32 [2048, 6144], P('fsdp')
- attention_out_grad: float32 [2048, 2048], P('fsdp')
- router_grad: float32 [2048, 16], P('fsdp')
- expert_in_grad: float32 [32, 2048, 1024], P('fsdp')
- expert_out_grad: float32 [32, 512, 2048], P('fsdp')
Inputs may be any that keep to these rules, and one draw needn't show every extreme that they name: `routes`: in the rows of one device no expert is named by more than 128 rows, a bound that some block reaches. Each device's lengths add up to 192; its longest sequence has exactly 96 tokens.
All inputs are finite; a program needn't handle non-finite values.
Results may differ from a plain program's by a relative error of at most 0.015.
Values may be sent and summed in bfloat16 or wider, within the bound.
No kernel may reach another device: no remote copies, remote signals or barrier semaphores. Data moves between devices by JAX's collectives and lax.ppermute only.
A program may use at most 320 MiB of HBM per device.

v0:
```python
import jax
import jax.numpy as jnp
from jax import lax
from jax.sharding import PartitionSpec as P

D = 2048
HEADS = 16
HEAD_DIM = 128


EPSILON = 1e-05
ROPE_BASE = 10000.0
MASKED = -1000000000.0


def root_norm(vector, scaling):
    return vector * lax.rsqrt(jnp.mean(vector * vector, axis=-1, keepdims=True) + EPSILON) * scaling


def rotary(vector, cos_table, sin_table):
    half_dim = vector.shape[-1] // 2
    first = vector[..., :half_dim]
    second = vector[..., half_dim:]
    return jnp.concatenate(
        [first * cos_table - second * sin_table, second * cos_table + first * sin_table], axis=-1
    )


def layout(lengths, number):
    ends_at = jnp.cumsum(lengths)
    places = jnp.arange(number, dtype=jnp.int32)
    segment = jnp.sum((places[:, None] >= ends_at[None, :]).astype(jnp.int32), axis=1)
    starts = ends_at - lengths
    select_mask = (
        segment[:, None] == jnp.arange(lengths.shape[0], dtype=jnp.int32)[None, :]
    ).astype(jnp.int32)
    position = places - jnp.sum(select_mask * starts[None, :], axis=1)
    return (segment, position)


def tables(position):
    half_dim = HEAD_DIM // 2
    inverse = ROPE_BASE ** (-2.0 * jnp.arange(half_dim, dtype=jnp.float32) / HEAD_DIM)
    angles = position.astype(jnp.float32)[:, None] * inverse[None, :]
    return (jnp.cos(angles)[:, None, :], jnp.sin(angles)[:, None, :])


def prepare(projected, query_gain, key_gain, cos_table, sin_table):
    count_rows = projected.shape[0]
    query_heads = root_norm(projected[:, :D], query_gain).reshape(count_rows, HEADS, HEAD_DIM)
    key_heads = root_norm(projected[:, D : 2 * D], key_gain).reshape(count_rows, HEADS, HEAD_DIM)
    value_heads = projected[:, 2 * D :].reshape(count_rows, HEADS, HEAD_DIM)
    return (
        rotary(query_heads, cos_table, sin_table),
        rotary(key_heads, cos_table, sin_table),
        value_heads,
    )


def softmax_rows(logits):
    row_max = jnp.max(logits, axis=-1, keepdims=True)
    exponent = jnp.exp(logits - row_max)
    return exponent / jnp.sum(exponent, axis=-1, keepdims=True)


def dot_first(left, right):
    return lax.dot_general(
        left, right, (((0,), (0,)), ((), ())), preferred_element_type=jnp.float32
    )


def dot_last(left, right):
    return lax.dot_general(
        left, right, (((1,), (1,)), ((), ())), preferred_element_type=jnp.float32
    )


def shards(
    tokens,
    cotangent,
    norm_gains,
    attention_in,
    attention_out,
    router_weight,
    expert_in,
    expert_out,
    routes,
    lengths,
):
    row_count = tokens.shape[0]
    devices_count = lax.axis_size("fsdp")
    experts = devices_count // 2
    choose = routes.shape[1]
    half_units = expert_out.shape[1]
    capacity = 4 * row_count * choose // (3 * experts)
    scaling = HEAD_DIM ** (-0.5)
    gain_full, gathered_in, gathered_out, gathered_router = (
        lax.all_gather(norm_gains, "fsdp", axis=1, tiled=True),
        lax.all_gather(attention_in, "fsdp", axis=0, tiled=True),
        lax.all_gather(attention_out, "fsdp", axis=0, tiled=True),
        lax.all_gather(router_weight, "fsdp", axis=0, tiled=True),
    )
    gain_rows = gain_full.astype(jnp.float32)
    segment, position = layout(lengths[0], row_count)
    cos_table, sin_table = tables(position)
    places = jnp.arange(row_count, dtype=jnp.int32)
    allowed = ((segment[:, None] == segment[None, :]) & (places[:, None] >= places[None, :]))[None]
    inputs = tokens.astype(jnp.float32)
    normed_input = root_norm(inputs, gain_rows[0]).astype(jnp.bfloat16)
    projected = jnp.dot(normed_input, gathered_in, preferred_element_type=jnp.float32)

    def prepare_local(projected_value, query_gain, key_gain):
        return prepare(projected_value, query_gain, key_gain, cos_table, sin_table)

    (query_f, key_f, value_f), prepare_back = jax.vjp(
        prepare_local, projected, gain_rows[1], gain_rows[2]
    )
    query_heads = query_f.astype(jnp.bfloat16)
    key_heads = key_f.astype(jnp.bfloat16)
    value_heads = value_f.astype(jnp.bfloat16)

    def score_block():
        raw_scores = (
            jnp.einsum("qhd,khd->hqk", query_heads, key_heads, preferred_element_type=jnp.float32)
            * scaling
        )
        return jnp.where(allowed, raw_scores, MASKED)

    scores = score_block()
    row_max = jnp.max(scores, axis=-1, keepdims=True)
    exponent = jnp.exp(scores - row_max)
    row_sum = jnp.sum(exponent, axis=-1, keepdims=True)
    log_total = row_max + jnp.log(row_sum)
    attend_probs = (exponent / row_sum).astype(jnp.bfloat16)
    attended = (
        jnp.einsum("hqk,khd->qhd", attend_probs, value_heads, preferred_element_type=jnp.float32)
        .reshape(row_count, D)
        .astype(jnp.bfloat16)
    )
    branch_out = jnp.dot(attended, gathered_out, preferred_element_type=jnp.float32)
    residual = inputs + branch_out
    normed = root_norm(residual, gain_rows[3]).astype(jnp.bfloat16)
    logits = jnp.dot(normed, gathered_router, preferred_element_type=jnp.float32)
    router_probs = softmax_rows(logits)
    chosen = jnp.take_along_axis(router_probs, routes, axis=1)
    gate_total = jnp.sum(chosen, axis=1, keepdims=True)
    gate_values = chosen / gate_total
    flat_routes = routes.reshape(-1)
    route_hits = (flat_routes[:, None] == jnp.arange(experts, dtype=jnp.int32)[None, :]).astype(
        jnp.int32
    )
    slot_index = jnp.sum((jnp.cumsum(route_hits, axis=0) - route_hits) * route_hits, axis=1)
    target = flat_routes * capacity + slot_index
    owner_token = (
        jnp.zeros((experts * capacity,), jnp.int32)
        .at[target]
        .set(jnp.arange(row_count * choose, dtype=jnp.int32) // choose)
    )
    filled = (
        jnp.zeros((experts * capacity,), jnp.bfloat16)
        .at[target]
        .set(jnp.ones((row_count * choose,), jnp.bfloat16))
    )
    outgoing = jnp.repeat(
        (normed[owner_token] * filled[:, None]).reshape(experts, capacity, D), 2, axis=0
    )
    arrived = lax.all_to_all(outgoing, "fsdp", split_axis=0, concat_axis=0, tiled=True).reshape(
        devices_count * capacity, D
    )
    gate_up_out = jnp.dot(arrived, expert_in[0], preferred_element_type=jnp.float32)
    gate_part = gate_up_out[:, :half_units]
    up_part = gate_up_out[:, half_units:]
    hidden_f, swiglu_back = jax.vjp(
        lambda gate_in, up_in: jax.nn.silu(gate_in) * up_in, gate_part, up_part
    )
    hidden = hidden_f.astype(jnp.bfloat16)
    produced = (
        jnp.dot(hidden, expert_out[0], preferred_element_type=jnp.float32)
        .astype(jnp.bfloat16)
        .reshape(devices_count, capacity, D)
    )
    returned = (
        lax.all_to_all(produced, "fsdp", split_axis=0, concat_axis=0, tiled=True)
        .reshape(experts, 2, capacity, D)
        .astype(jnp.float32)
    )
    returned = jnp.sum(returned, axis=1).reshape(experts * capacity, D)
    picked = returned[target].reshape(row_count, choose, D)
    expert_sum = jnp.sum(gate_values[:, :, None] * picked, axis=1)
    output = (residual + expert_sum).astype(jnp.bfloat16)
    back_in, back_out, back_router = (
        lax.all_gather(attention_in, "fsdp", axis=0, tiled=True),
        lax.all_gather(attention_out, "fsdp", axis=0, tiled=True),
        lax.all_gather(router_weight, "fsdp", axis=0, tiled=True),
    )
    upstream = cotangent.astype(jnp.float32)
    gate_grad = jnp.sum(upstream[:, None, :] * picked, axis=2)
    send_grad = (
        (gate_values[:, :, None] * upstream[:, None, :])
        .astype(jnp.bfloat16)
        .reshape(row_count * choose, D)
    )
    grad_buffer = (
        jnp.zeros((experts * capacity, D), jnp.bfloat16)
        .at[target]
        .set(send_grad)
        .reshape(experts, capacity, D)
    )
    grad_buffer = jnp.repeat(grad_buffer, 2, axis=0)
    grad_arrived = lax.all_to_all(
        grad_buffer, "fsdp", split_axis=0, concat_axis=0, tiled=True
    ).reshape(devices_count * capacity, D)
    grad_hidden = dot_last(grad_arrived, expert_out[0])
    expert_out_grad = dot_first(hidden, grad_arrived)
    grad_gate, grad_up = swiglu_back(grad_hidden)
    grad_gate_up = jnp.concatenate([grad_gate, grad_up], axis=1).astype(jnp.bfloat16)
    expert_in_grad = dot_first(arrived, grad_gate_up)
    grad_rows = (
        dot_last(grad_gate_up, expert_in[0])
        .astype(jnp.bfloat16)
        .reshape(devices_count, capacity, D)
    )
    grad_back = (
        lax.all_to_all(grad_rows, "fsdp", split_axis=0, concat_axis=0, tiled=True)
        .reshape(experts, 2, capacity, D)
        .astype(jnp.float32)
    )
    grad_back = jnp.sum(grad_back, axis=1).reshape(experts * capacity, D)
    dispatch_grad = jnp.sum(grad_back[target].reshape(row_count, choose, D), axis=1)
    chosen_grad = (gate_grad - jnp.sum(gate_grad * gate_values, axis=1, keepdims=True)) / gate_total
    expert_match = (
        routes[:, :, None] == jnp.arange(experts, dtype=jnp.int32)[None, None, :]
    ).astype(jnp.float32)
    prob_grad = jnp.sum(expert_match * chosen_grad[:, :, None], axis=1)
    logit_grad = (
        router_probs * (prob_grad - jnp.sum(prob_grad * router_probs, axis=1, keepdims=True))
    ).astype(jnp.bfloat16)
    router_grad = dot_first(normed, logit_grad)
    normed_grad = dispatch_grad + dot_last(logit_grad, back_router)
    _, second_back = jax.vjp(root_norm, residual, gain_rows[3])
    residual_norm_grad, second_gain_grad = second_back(normed_grad)
    residual_grad = upstream + residual_norm_grad
    branch_grad = residual_grad.astype(jnp.bfloat16)
    out_grad = dot_first(attended, branch_grad)
    attended_grad = (
        dot_last(branch_grad, back_out).astype(jnp.bfloat16).reshape(row_count, HEADS, HEAD_DIM)
    )
    recomputed = jnp.exp(score_block() - log_total)
    value_grad = jnp.einsum(
        "hqk,qhd->khd", attend_probs, attended_grad, preferred_element_type=jnp.float32
    )
    attend_grad = jnp.einsum(
        "qhd,khd->hqk", attended_grad, value_heads, preferred_element_type=jnp.float32
    )
    row_delta = jnp.sum(recomputed * attend_grad, axis=-1, keepdims=True)
    score_grad = (recomputed * (attend_grad - row_delta)).astype(jnp.bfloat16)
    query_grad = (
        jnp.einsum("hqk,khd->qhd", score_grad, key_heads, preferred_element_type=jnp.float32)
        * scaling
    )
    key_grad = (
        jnp.einsum("hqk,qhd->khd", score_grad, query_heads, preferred_element_type=jnp.float32)
        * scaling
    )
    projected_grad, query_gain_grad, key_gain_grad = prepare_back(
        (query_grad, key_grad, value_grad)
    )
    projected_grad = projected_grad.astype(jnp.bfloat16)
    attention_in_grad = dot_first(normed_input, projected_grad)
    normed_input_grad = dot_last(projected_grad, back_in)
    _, first_back = jax.vjp(root_norm, inputs, gain_rows[0])
    input_norm_grad, first_gain_grad = first_back(normed_input_grad)
    input_grad = residual_grad + input_norm_grad
    gains_grad = jnp.stack([first_gain_grad, query_gain_grad, key_gain_grad, second_gain_grad])
    gains_share, in_share, out_share, router_share = (
        lax.psum_scatter(gains_grad, "fsdp", scatter_dimension=1, tiled=True),
        lax.psum_scatter(attention_in_grad, "fsdp", scatter_dimension=0, tiled=True),
        lax.psum_scatter(out_grad, "fsdp", scatter_dimension=0, tiled=True),
        lax.psum_scatter(router_grad, "fsdp", scatter_dimension=0, tiled=True),
    )
    return (
        output,
        input_grad,
        gains_share,
        in_share,
        out_share,
        router_share,
        expert_in_grad[None],
        expert_out_grad[None],
    )


def solution(mesh):
    in_specs = (
        P("fsdp", None),
        P("fsdp", None),
        P(None, "fsdp"),
        P("fsdp", None),
        P("fsdp", None),
        P("fsdp", None),
        P("fsdp", None, None),
        P("fsdp", None, None),
        P("fsdp", None),
        P("fsdp", None),
    )
    out_specs = (
        P("fsdp", None),
        P("fsdp", None),
        P(None, "fsdp"),
        P("fsdp", None),
        P("fsdp", None),
        P("fsdp", None),
        P("fsdp", None, None),
        P("fsdp", None, None),
    )
    return jax.shard_map(shards, mesh=mesh, in_specs=in_specs, out_specs=out_specs, check_vma=False)
```

profile of v0, /device:TPU:0, one launch (start us, length us, event | category | flops | bytes accessed | tf_op | source)
XLA Modules:
  0.0 2881.1 jit_solution(1922226778136018712)
XLA Ops:
  9.7 43.8 %all-gather = bf16[32,64,4]{1,2,0:T(4,128)(2,1)S(1)} all-gather(bf16[1,64,4]{1,2,0:T(4,128)(2,1)} %bitcast.232), channel_id=1, replica_groups=mesh['fsdp'=32] {'fsdp'}, dimensions={0}, use_global_device_ids=true | all-gather | bytes 16896 | tf_op jit(solution)/shard_map/all_gather | solution.py:98
  54.1 4.5 reduce-window.11
  59.4 6.2 scatter_custom_fusion
  65.6 11.1 scatter_custom_fusion.1
  77.8 90.6 %all-gather.5.cloned.1.call-done = bf16[2048,6144]{1,0:T(8,128)(2,1)} async-done(((bf16[64,6144]{1,0:T(8,128)(2,1)}), bf16[2048,6144]{1,0:T(8,128)(2,1)}) %all-gather.5.cloned.1.call-update) | async-done | bytes 25165840 | tf_op jit(solution)/shard_map/all_gather | solution.py:99
  168.4 11.1 fusion.52
  183.2 2.1 subtract_convert_fusion.1
  190.4 1.6 fusion.32
  192.1 54.8 %all-gather.7.cloned.1.call-done = bf16[2048,2048]{1,0:T(8,128)(2,1)} async-done(((bf16[64,2048]{1,0:T(8,128)(2,1)}), bf16[2048,2048]{1,0:T(8,128)(2,1)}) %all-gather.7.cloned.1.call-update) | async-done | bytes 8388624 | tf_op jit(solution)/shard_map/all_gather | solution.py:100
  246.9 5.6 multiply_reduce_fusion.5
  253.9 11.0 gather_fusion
  264.9 7.4 broadcast_multiply_fusion
  272.3 10.8 broadcast_in_dim.50
  283.1 4.0 all-to-all-start
  287.4 323.1 %all-gather.1 = bf16[32,64,16]{1,2,0:T(8,128)(2,1)S(1)} all-gather(bf16[1,64,16]{1,2,0:T(8,128)(2,1)S(1)} %bitcast.231), channel_id=1, replica_groups=mesh['fsdp'=32] {'fsdp'}, dimensions={0}, use_global_device_ids=true | all-gather | bytes 67584 | tf_op jit(solution)/shard_map/all_gather | solution.py:101
  610.7 2.5 convert_element_type.114
  614.2 12.7 gather_fusion.3
  627.4 15.2 scatter_custom_fusion.2
  642.6 17.5 all-to-all-done
  660.1 10.8 broadcast_in_dim.52
  670.8 60.2 %all-to-all-start.2 = ((bf16[32,128,2048]{2,1,0:T(8,128)(2,1)}), bf16[32,128,2048]{2,1,0:T(8,128)(2,1)}, u32[]{:S(2)}, u32[]{:S(2)}) async-start(bf16[32,128,2048]{2,1,0:T(8,128)(2,1)} %bitcast.197), calls=%async_computation.2 | async-start | bytes 33554432 | tf_op jit(solution)/shard_map/all_to_all | solution.py:210
  731.1 23.7 fusion.14
  754.8 349.1 %all-to-all-done.2 = bf16[32,128,2048]{2,1,0:T(8,128)(2,1)} async-done(((bf16[32,128,2048]{2,1,0:T(8,128)(2,1)}), bf16[32,128,2048]{2,1,0:T(8,128)(2,1)}, u32[]{:S(2)}, u32[]{:S(2)}) %all-to-all-start.2) | async-done | bytes 16777248 | tf_op jit(solution)/shard_map/all_to_all | solution.py:210
  1103.8 23.0 fusion.5
  1126.9 25.6 convolution_convert_fusion
  1152.5 3.9 all-to-all-start.3
  1156.4 14.7 convolution_convert_fusion.1
  1171.0 358.1 %all-to-all-done.3 = bf16[32,128,2048]{2,1,0:T(8,128)(2,1)} async-done(((bf16[32,128,2048]{2,1,0:T(8,128)(2,1)}), bf16[32,128,2048]{2,1,0:T(8,128)(2,1)}, u32[]{:S(2)}, u32[]{:S(2)}) %all-to-all-start.3) | async-done | bytes 16777248 | tf_op jit(solution)/shard_map/all_to_all | solution.py:224
  1529.1 4.1 all-to-all-start.1
  1533.3 14.5 convert_reduce_fusion
  1547.8 18.3 gather_fusion.2
  1566.1 8.7 bitcast_reduce_fusion
  1574.8 331.1 %all-to-all-done.1 = bf16[32,128,2048]{2,1,0:T(8,128)(2,1)} async-done(((bf16[32,128,2048]{2,1,0:T(8,128)(2,1)}), bf16[32,128,2048]{2,1,0:T(8,128)(2,1)}, u32[]{:S(2)}, u32[]{:S(2)}) %all-to-all-start.1) | async-done | bytes 16777248 | tf_op jit(solution)/shard_map/all_to_all | solution.py:183
  1905.9 14.2 convert_reduce_fusion.1
  1920.2 18.4 gather_fusion.1
  1938.7 9.1 fusion.2
  1948.1 2.2 multiply_reduce_fusion.1
  1951.8 7.0 fusion.31
  1968.7 2.5 add_add_fusion.2
  1972.4 14.9 fusion.24
  1990.5 9.6 fusion.34
  2001.5 19.5 fusion.50
  2021.1 15.1 convolution_bitcast_fusion
  2036.2 23.2 fusion.12
  2061.0 58.6 %reduce-scatter.13.cloned.1.call-done = f32[64,4]{1,0:T(8,128)} async-done(((f32[2048,4]{1,0:T(8,128)}), f32[64,4]{1,0:T(8,128)}) %reduce-scatter.13.cloned.1.call-update) | async-done | bytes 1040
  2121.0 131.5 %reduce-scatter.15.cloned.1.call-done = f32[64,16]{1,0:T(8,128)} async-done(((f32[2048,16]{1,0:T(8,128)}), f32[64,16]{1,0:T(8,128)}) %reduce-scatter.15.cloned.1.call-update) | async-done | bytes 4112
  2254.0 180.2 %reduce-scatter.11.cloned.1.call-done = f32[64,2048]{1,0:T(8,128)} async-done(((f32[2048,2048]{1,0:T(8,128)}), f32[64,2048]{1,0:T(8,128)}) %reduce-scatter.11.cloned.1.call-update) | async-done | bytes 524304 | tf_op jit(solution)/shard_map/reduce_scatter | solution.py:278
  2434.1 440.0 %reduce-scatter.9.cloned.1.call-done = f32[64,6144]{1,0:T(8,128)} async-done(((f32[2048,6144]{1,0:T(8,128)}), f32[64,6144]{1,0:T(8,128)}) %reduce-scatter.9.cloned.1.call-update) | async-done | bytes 1572880 | tf_op jit(solution)/shard_map/reduce_scatter | solution.py:277
  (264 shorter events, 38.1 us)
Async XLA Ops:
  7.2 1096.7 %copy-start = (bf16[1,512,2048]{2,1,0:T(8,128)(2,1)S(1)}, bf16[1,512,2048]{2,1,0:T(8,128)(2,1)}, u32[]{:S(2)}) copy-start(bf16[1,512,2048]{2,1,0:T(8,128)(2,1)} %param.17) | copy-start | bytes 6291460
  7.2 46.4 %copy-start.42 = (s32[192,8]{0,1:T(8,128)S(1)}, s32[192,8]{0,1:T(8,128)}, u32[]{:S(2)}) copy-start(s32[192,8]{0,1:T(8,128)} %param.18) | copy-start | bytes 18436
  7.2 46.7 %copy-start.81 = (s32[1,3]{1,0:T(1,128)S(1)}, s32[1,3]{1,0:T(1,128)}, u32[]{:S(2)}) copy-start(s32[1,3]{1,0:T(1,128)} %param.19) | copy-start | bytes 40
  7.2 69.7 %copy-start.13 = (bf16[192,2048]{1,0:T(8,128)(2,1)S(1)}, bf16[192,2048]{1,0:T(8,128)(2,1)}, u32[]{:S(2)}) copy-start(bf16[192,2048]{1,0:T(8,128)(2,1)} %param.10) | copy-start | bytes 2359300
  7.2 161.2 %all-gather.5.cloned.1.call-start = ((), (), s32[]{:S(2)}) async-start(), calls=%async_computation.8 | async-start | bytes 25952256 | tf_op jit(solution)/shard_map/all_gather | solution.py:99
  8.0 239.0 %all-gather.7.cloned.1.call-start = ((), (), s32[]{:S(2)}) async-start(), calls=%async_computation.9 | async-start | bytes 8650752 | tf_op jit(solution)/shard_map/all_gather | solution.py:100
  59.4 568.0 %copy-start.58 = (s32[1536]{0:T(1024)}, s32[1536]{0:T(1024)S(1)}, u32[]{:S(2)}) copy-start(s32[1536]{0:T(1024)S(1)} %fusion.65) | copy-start | bytes 18436
  77.2 102.3 %copy-start.56 = (f32[192]{0:T(256)}, f32[192]{0:T(256)S(1)}, u32[]{:S(2)}) copy-start(f32[192]{0:T(256)S(1)} %fusion.71) | copy-start | bytes 2308
  77.7 105.5 %copy-start.30 = (f32[192,64]{1,0:T(8,128)}, f32[192,64]{1,0:T(8,128)S(1)}, u32[]{:S(2)}) copy-start(f32[192,64]{1,0:T(8,128)S(1)} %get-tuple-element.51) | copy-start | bytes 147460
  77.8 105.5 %copy-start.32 = (f32[192,64]{1,0:T(8,128)}, f32[192,64]{1,0:T(8,128)S(1)}, u32[]{:S(2)}) copy-start(f32[192,64]{1,0:T(8,128)S(1)} %get-tuple-element.52) | copy-start | bytes 147460
  77.8 101.7 %copy-start.38 = (f32[1,2048]{1,0:T(1,128)}, f32[1,2048]{1,0:T(1,128)S(1)}, u32[]{:S(2)}) copy-start(f32[1,2048]{1,0:T(1,128)S(1)} %get-tuple-element.50) | copy-start | bytes 24580
  77.8 102.1 %copy-start.50 = (f32[1,2048]{1,0:T(1,128)}, f32[1,2048]{1,0:T(1,128)S(1)}, u32[]{:S(2)}) copy-start(f32[1,2048]{1,0:T(1,128)S(1)} %get-tuple-element.48) | copy-start | bytes 24580
  77.8 102.1 %copy-start.52 = (f32[1,2048]{1,0:T(1,128)}, f32[1,2048]{1,0:T(1,128)S(1)}, u32[]{:S(2)}) copy-start(f32[1,2048]{1,0:T(1,128)S(1)} %get-tuple-element.49) | copy-start | bytes 24580
  77.8 174.7 %copy-start.48 = (f32[1,2048]{1,0:T(1,128)}, f32[1,2048]{1,0:T(1,128)S(1)}, u32[]{:S(2)}) copy-start(f32[1,2048]{1,0:T(1,128)S(1)} %get-tuple-element.47) | copy-start | bytes 24580
  179.5 9.7 copy-start.6
  252.5 12.4 copy-start.79
  252.5 12.4 copy-start.66
  253.9 359.3 %copy-start.2 = (bf16[192,2048]{1,0:T(8,128)(2,1)}, bf16[192,2048]{1,0:T(8,128)(2,1)S(1)}, u32[]{:S(2)}) copy-start(bf16[192,2048]{1,0:T(8,128)(2,1)S(1)} %multiply_convert_fusion.3) | copy-start | bytes 2359300
  283.1 376.9 %all-to-all-start = ((bf16[32,128,2048]{2,1,0:T(8,128)(2,1)}), bf16[32,128,2048]{2,1,0:T(8,128)(2,1)}, u32[]{:S(2)}, u32[]{:S(2)}) async-start(bf16[32,128,2048]{2,1,0:T(8,128)(2,1)} %bitcast.196), calls=%async_computation | async-start | bytes 33554432 | tf_op jit(solution)/shard_map/all_to_all | solution.py:167
  613.5 13.3 copy-start.60
  614.1 12.8 copy-start.68
  627.1 15.5 copy-start.76
  627.1 15.5 copy-start.54
  627.3 15.3 copy-start.34
  670.8 433.0 %all-to-all-start.2 = ((bf16[32,128,2048]{2,1,0:T(8,128)(2,1)}), bf16[32,128,2048]{2,1,0:T(8,128)(2,1)}, u32[]{:S(2)}, u32[]{:S(2)}) async-start(bf16[32,128,2048]{2,1,0:T(8,128)(2,1)} %bitcast.197), calls=%async_computation.2 | async-start | bytes 33554432 | tf_op jit(solution)/shard_map/all_to_all | solution.py:210
  1152.5 376.6 %all-to-all-start.3 = ((bf16[32,128,2048]{2,1,0:T(8,128)(2,1)}), bf16[32,128,2048]{2,1,0:T(8,128)(2,1)}, u32[]{:S(2)}, u32[]{:S(2)}) async-start(bf16[32,128,2048]{2,1,0:T(8,128)(2,1)} %bitcast.203), calls=%async_computation.3 | async-start | bytes 33554432 | tf_op jit(solution)/shard_map/all_to_all | solution.py:224
  1529.1 376.8 %all-to-all-start.1 = ((bf16[32,128,2048]{2,1,0:T(8,128)(2,1)}), bf16[32,128,2048]{2,1,0:T(8,128)(2,1)}, u32[]{:S(2)}, u32[]{:S(2)}) async-start(bf16[32,128,2048]{2,1,0:T(8,128)(2,1)} %bitcast.202), calls=%async_computation.1 | async-start | bytes 33554432 | tf_op jit(solution)/shard_map/all_to_all | solution.py:183
  1533.2 586.4 %reduce-scatter.13.cloned.1.call-start = ((), (), s32[]{:S(2)}) async-start(), calls=%async_computation.12 | async-start | bytes 1081344
  1920.2 18.4 copy-start.35
  1938.6 9.3 copy-start.55
  1938.6 9.3 copy-start.77
  1938.6 9.3 copy-start.43
  1938.6 9.3 copy-start.41
  1938.6 9.3 copy-start.61
  1938.6 9.3 copy-start.69
  1938.6 9.4 copy-start.8
  1938.6 9.4 copy-start.37
  1938.6 9.4 copy-start.49
  1938.7 9.4 copy-start.67
  1950.4 9.1 slice-start
  1988.8 263.7 %reduce-scatter.15.cloned.1.call-start = ((), (), s32[]{:S(2)}) async-start(), calls=%async_computation.13 | async-start | bytes 1081344
  1990.4 443.7 %reduce-scatter.11.cloned.1.call-start = ((), (), s32[]{:S(2)}) async-start(), calls=%async_computation.11 | async-start | bytes 17301504 | tf_op jit(solution)/shard_map/reduce_scatter | solution.py:278
  2000.1 874.0 %reduce-scatter.9.cloned.1.call-start = ((), (), s32[]{:S(2)}) async-start(), calls=%async_computation.10 | async-start | bytes 51904512 | tf_op jit(solution)/shard_map/reduce_scatter | solution.py:277
  2021.0 15.1 copy-start.82
  2036.2 23.2 copy-start.71
  2036.2 23.2 copy-start.12
  2036.2 23.3 copy-start.29
  2059.4 814.7 %copy-start.1 = (bf16[1,512,2048]{2,1,0:T(8,128)(2,1)S(1)}, bf16[1,512,2048]{2,1,0:T(8,128)(2,1)}, u32[]{:S(2)}) copy-start(bf16[1,512,2048]{2,1,0:T(8,128)(2,1)} %param.17) | copy-start | bytes 6291460
  (47 other events, 107.0 us)
Sparse Core Ops, SparseCore 0:
  10.9 157.4 all-gather.4
  171.3 75.6 all-gather.6
  1988.9 130.6 reduce-scatter.12
  2121.8 130.7 reduce-scatter.14
  2255.2 178.8 reduce-scatter.10
  2441.0 433.0 reduce-scatter.8
where the time goes:
time: 2890 us; the launch traced here: 2880 us
  waiting for transfers between devices  2010 us (70%)
  blocking collectives  367 us (13%)
  matrix products  203 us (7%)
  local copies, waits for them, and re-layouts  119 us (4%)
  other arithmetic  90.7 us (3%)
  starting transfers between devices  72.4 us (3%)
    reduce_scatter x1, waiting for transfers between devices, shards(): lax.psum_scatter(attention_in_grad, 'fsdp', scatter_dimension=0, tiled=True)  440 us
    all_to_all x1, waiting for transfers between devices, shards(): lax.all_to_all(grad_rows, 'fsdp', split_axis=0, concat_axis=0, tiled=True)  358 us
    all_to_all x1, waiting for transfers between devices, shards(): lax.all_to_all(grad_buffer, 'fsdp', split_axis=0, concat_axis=0, tiled=True)  349 us
    all_to_all x1, waiting for transfers between devices, shards(): lax.all_to_all(produced, 'fsdp', split_axis=0, concat_axis=0, tiled=True)  331 us
    all_gather x1, blocking collectives, shards(): lax.all_gather(router_weight, 'fsdp', axis=0, tiled=True)  323 us
    unnamed x8, waiting for transfers between devices  192 us
    reduce_scatter x1, waiting for transfers between devices, shards(): lax.psum_scatter(out_grad, 'fsdp', scatter_dimension=0, tiled=True)  180 us
    all_gather x1, waiting for transfers between devices, shards(): lax.all_gather(attention_in, 'fsdp', axis=0, tiled=True)  90.6 us
  transfers between devices with their start and end apart: 10, of which 10 were waited for; matrix products, arithmetic and copies ran while one was open for 8% of the time, Pallas kernels for 0%

commit v1 on v0

--- a/solution.py
+++ b/solution.py
@@ -1,6 +1,10 @@
+import functools
+
 import jax
 import jax.numpy as jnp
 from jax import lax
+from jax.experimental import pallas as pl
+from jax.experimental.pallas import tpu as pltpu
 from jax.sharding import PartitionSpec as P
 
 D = 2048
@@ -75,7 +79,7 @@
     )
 
 
-def shards(
+def shards_routed(
     tokens,
     cotangent,
     norm_gains,
@@ -290,6 +294,433 @@
     )
 
 
+def product(left, right):
+    return jnp.dot(left, right, preferred_element_type=jnp.float32)
+
+
+PLANE = 8
+WIDE = 128
+
+
+class Moves:
+    def __init__(self, count):
+        planes = count // PLANE
+        order = list(range(0, planes, 2)) + list(range(1, planes, 2))[::-1]
+        after = {order[i]: order[(i + 1) % planes] for i in range(planes)}
+        self.planes = planes
+        self.ring = [(i, after[i // PLANE] * PLANE + i % PLANE) for i in range(count)]
+        self.first = [(i, i ^ (4 if i & 1 else 2)) for i in range(count)]
+        self.second = [(i, i ^ (2 if i & 1 else 4)) for i in range(count)]
+        self.core = [(i, i ^ 1) for i in range(count)]
+
+
+def send(value, pairs):
+    return lax.ppermute(value, "fsdp", pairs)
+
+
+def spread(moves, block):
+    groups = []
+    current = block
+    for step in range(moves.planes):
+        if step:
+            current = send(current, moves.ring)
+        near = send(current, moves.first)
+        own = [current, near, send(current, moves.second), send(near, moves.second)]
+        groups.append(own + [send(item, moves.core) for item in own])
+    return groups
+
+
+def collect_plane(moves, kept, sent):
+    kept = kept.astype(jnp.float32) + send(sent, moves.core).astype(jnp.float32)
+    kept = kept.astype(jnp.bfloat16)
+    back = send(kept[2:], moves.second)
+    near = (kept[1].astype(jnp.float32) + back[1].astype(jnp.float32)).astype(jnp.bfloat16)
+    home = kept[0].astype(jnp.float32) + back[0].astype(jnp.float32)
+    return home + send(near, moves.first).astype(jnp.float32)
+
+
+def collect_ring(moves, sums):
+    total = sums[1]
+    for step in range(2, moves.planes):
+        total = sums[step] + send(total.astype(jnp.bfloat16), moves.ring).astype(jnp.float32)
+    return sums[0] + send(total.astype(jnp.bfloat16), moves.ring).astype(jnp.float32)
+
+
+def expert_body(per_step, cap, experts, meta, *refs):
+    row_refs, grad_refs = refs[:PLANE], refs[PLANE : 2 * PLANE]
+    in_hbm, out_hbm = refs[2 * PLANE : 2 * PLANE + 2]
+    outputs = refs[2 * PLANE + 6 : 2 * PLANE + 14]
+    x_save, dy_save, m_save, du_save, out_keep, out_send, row_keep, row_send = outputs
+    rows_v, grads_v, in_v, out_v, row_sem, grad_sem, weight_sem = refs[2 * PLANE + 14 :]
+    step = pl.program_id(0)
+    count, width, half = rows_v.shape[1], grads_v.shape[2], out_v.shape[0]
+    expert, device = meta[0], meta[1]
+    bf, f32 = jnp.bfloat16, jnp.float32
+
+    def fetch_rows(j):
+        return pltpu.make_async_copy(row_refs[j], rows_v.at[j], row_sem.at[j])
+
+    def fetch_grads(j):
+        return pltpu.make_async_copy(grad_refs[j], grads_v.at[j], grad_sem.at[j])
+
+    fetch_in = pltpu.make_async_copy(in_hbm, in_v, weight_sem.at[0])
+    fetch_out = pltpu.make_async_copy(out_hbm, out_v, weight_sem.at[1])
+
+    @pl.when(step == 0)
+    def _():
+        for j in range(per_step):
+            fetch_rows(j).start()
+        fetch_in.start()
+        for j in range(per_step):
+            fetch_grads(j).start()
+        fetch_out.start()
+        for j in range(per_step, PLANE):
+            fetch_rows(j).start()
+            fetch_grads(j).start()
+
+    members = [step * per_step + j for j in range(per_step)]
+    for j in members:
+        pltpu.make_async_copy(row_refs[0], rows_v.at[j], row_sem.at[j]).wait()
+    lane8 = lax.broadcasted_iota(jnp.int32, (8, WIDE), 1)
+    row8 = lax.broadcasted_iota(jnp.int32, (8, WIDE), 0)
+    pick = (
+        jnp.where((row8 == 0) & (lane8 == expert), 1.0, 0.0)
+        + jnp.where((row8 == 1) & (lane8 == experts + expert), 1.0, 0.0)
+        + jnp.where((row8 == 1) & (lane8 == 2 * experts + expert), 1.0, 0.0)
+    ).astype(bf)
+    lanes = lax.broadcasted_iota(jnp.int32, (count, WIDE), 1)
+    slots_down = lax.broadcasted_iota(jnp.int32, (cap, count), 0)
+    slots_along = lax.broadcasted_iota(jnp.int32, (count, cap), 1)
+    gather, scatter, taken, gates = [], [], [], []
+    for j in members:
+        extra = rows_v[j, :, width:]
+        info = dot_last(pick, extra)
+        chosen = slots_down == info[0:1].astype(jnp.int32)
+        gates.append(jnp.sum(jnp.where(chosen, info[1:2], 0.0), axis=1, keepdims=True))
+        gather.append(jnp.where(chosen, 1.0, 0.0).astype(bf))
+        slot = jnp.sum(
+            jnp.where(lanes == expert, extra.astype(f32), 0.0), axis=1, keepdims=True
+        ).astype(jnp.int32)
+        scatter.append(jnp.where(slots_along == slot, 1.0, 0.0).astype(bf))
+        taken.append(product(gather[-1], rows_v[j, :, :width]).astype(bf))
+    x = jnp.concatenate(taken, axis=0)
+    gate = jnp.concatenate(gates, axis=0)
+    x_save[...] = x
+
+    @pl.when(step == 0)
+    def _():
+        fetch_in.wait()
+
+    u = product(x, in_v[...])
+    gate_part, up_part = u[:, :half], u[:, half:]
+    sigmoid = 1.0 / (1.0 + jnp.exp(-gate_part))
+    silu = gate_part * sigmoid
+    m = (silu * up_part).astype(bf)
+    m_save[...] = m
+
+    @pl.when(step == 0)
+    def _():
+        fetch_out.wait()
+
+    y = product(m, out_v[...])
+    for j in members:
+        pltpu.make_async_copy(grad_refs[0], grads_v.at[j], grad_sem.at[j]).wait()
+    g = jnp.concatenate([product(gather[i], grads_v[j]) for i, j in enumerate(members)], axis=0)
+    dgate = jnp.sum(g * y, axis=1, keepdims=True)
+    z = (gate * y).astype(bf)
+    dy = (gate * g).astype(bf)
+    dy_save[...] = dy
+    dm = dot_last(dy, out_v[...])
+    slope = sigmoid * (1.0 + gate_part * (1.0 - sigmoid))
+    du = jnp.concatenate([dm * up_part * slope, dm * silu], axis=1).astype(bf)
+    du_save[...] = du
+    drows = dot_last(du, in_v[...]).astype(bf)
+    upper = dgate.astype(bf).astype(f32)
+    lane_m = lax.broadcasted_iota(jnp.int32, (per_step * cap, WIDE), 1)
+    pair = jnp.where(
+        lane_m == 2 * device,
+        upper,
+        jnp.where(lane_m == 2 * device + 1, dgate - upper, 0.0),
+    ).astype(bf)
+
+    def put(out_ref, row_ref):
+        for i in range(per_step):
+            own = slice(i * cap, (i + 1) * cap)
+            out_ref[i] = product(scatter[i], z[own]).astype(bf)
+            row_ref[i, :, :width] = product(scatter[i], drows[own]).astype(bf)
+            row_ref[i, :, width:] = product(scatter[i], pair[own]).astype(bf)
+
+    half_way = PLANE // per_step // 2
+
+    @pl.when(step < half_way)
+    def _():
+        put(out_keep, row_keep)
+
+    @pl.when(step >= half_way)
+    def _():
+        put(out_send, row_send)
+
+
+def expert_group(meta, rows, grads, weight_in, weight_out, saved, index, groups, cap, experts):
+    per_step = 2
+    count, wide = rows[0].shape
+    width, half = grads[0].shape[1], weight_out.shape[0]
+    steps = PLANE // per_step
+    half_way = steps // 2
+    bf = jnp.bfloat16
+
+    def shape(*dims):
+        return jax.ShapeDtypeStruct(dims, bf)
+
+    def saves(columns):
+        return pl.BlockSpec((per_step * cap, columns), lambda i: (index * steps + i, 0))
+
+    def keeps(columns):
+        return pl.BlockSpec((per_step, count, columns), lambda i: (jnp.minimum(i, half_way - 1), 0, 0))
+
+    def sends(columns):
+        return pl.BlockSpec((per_step, count, columns), lambda i: (jnp.maximum(i - half_way, 0), 0, 0))
+
+    anywhere = pl.BlockSpec(memory_space=pl.ANY)
+    aliases = {2 * PLANE + 3 + t: t for t in range(4)}
+    if saved is None:
+        saved, aliases = [jnp.zeros((16, WIDE), bf)] * 4, {}
+    slots = groups * PLANE * cap
+    return pl.pallas_call(
+        functools.partial(expert_body, per_step, cap, experts),
+        grid=(steps,),
+        out_shape=[
+            shape(slots, width),
+            shape(slots, width),
+            shape(slots, half),
+            shape(slots, 2 * half),
+            shape(PLANE // 2, count, width),
+            shape(PLANE // 2, count, width),
+            shape(PLANE // 2, count, wide),
+            shape(PLANE // 2, count, wide),
+        ],
+        in_specs=[pl.BlockSpec(memory_space=pltpu.SMEM)] + [anywhere] * (2 * PLANE + 6),
+        out_specs=[
+            saves(width),
+            saves(width),
+            saves(half),
+            saves(2 * half),
+            keeps(width),
+            sends(width),
+            keeps(wide),
+            sends(wide),
+        ],
+        scratch_shapes=[
+            pltpu.VMEM((PLANE, count, wide), bf),
+            pltpu.VMEM((PLANE, count, width), bf),
+            pltpu.VMEM(weight_in.shape, bf),
+            pltpu.VMEM(weight_out.shape, bf),
+            pltpu.SemaphoreType.DMA((PLANE,)),
+            pltpu.SemaphoreType.DMA((PLANE,)),
+            pltpu.SemaphoreType.DMA((2,)),
+        ],
+        input_output_aliases=aliases,
+        compiler_params=pltpu.CompilerParams(
+            vmem_limit_bytes=58 << 20, dimension_semantics=("arbitrary",)
+        ),
+        cost_estimate=pl.CostEstimate(
+            flops=16 * 10**9, bytes_accessed=60 << 20, transcendentals=PLANE * cap * half
+        ),
+        name="expert_group",
+    )(meta, *rows, *grads, weight_in, weight_out, *saved)
+
+
+def shards_dense(
+    tokens,
+    cotangent,
+    norm_gains,
+    attention_in,
+    attention_out,
+    router_weight,
+    expert_in,
+    expert_out,
+    routes,
+    lengths,
+):
+    row_count = tokens.shape[0]
+    devices_count = lax.axis_size("fsdp")
+    moves = Moves(devices_count)
+    device = lax.axis_index("fsdp")
+    experts = devices_count // 2
+    choose = routes.shape[1]
+    capacity = 4 * row_count * choose // (3 * experts)
+    scaling = HEAD_DIM ** (-0.5)
+    bf = jnp.bfloat16
+    gain_full, gathered_in, gathered_out, gathered_router = (
+        lax.all_gather(norm_gains, "fsdp", axis=1, tiled=True),
+        lax.all_gather(attention_in, "fsdp", axis=0, tiled=True),
+        lax.all_gather(attention_out, "fsdp", axis=0, tiled=True),
+        lax.all_gather(router_weight, "fsdp", axis=0, tiled=True),
+    )
+    gain_rows = gain_full.astype(jnp.float32)
+    grad_groups = spread(moves, cotangent)
+
+    expert_ids = jnp.arange(experts, dtype=jnp.int32)
+    match = jnp.sum((routes[:, :, None] == expert_ids[None, None, :]).astype(jnp.float32), axis=1)
+    places = jnp.arange(row_count, dtype=jnp.int32)
+    before = (places[:, None] > places[None, :]).astype(bf)
+    rank = jnp.where(match > 0, product(before, match.astype(bf)), -1.0).astype(bf)
+
+    segment, position = layout(lengths[0], row_count)
+    cos_table, sin_table = tables(position)
+    allowed = ((segment[:, None] == segment[None, :]) & (places[:, None] >= places[None, :]))[None]
+    inputs = tokens.astype(jnp.float32)
+    normed_input = root_norm(inputs, gain_rows[0]).astype(bf)
+    projected = product(normed_input, gathered_in)
+
+    def prepare_local(projected_value, query_gain, key_gain):
+        return prepare(projected_value, query_gain, key_gain, cos_table, sin_table)
+
+    (query_f, key_f, value_f), prepare_back = jax.vjp(
+        prepare_local, projected, gain_rows[1], gain_rows[2]
+    )
+    query_heads = query_f.astype(bf)
+    key_heads = key_f.astype(bf)
+    value_heads = value_f.astype(bf)
+
+    def score_block():
+        raw_scores = (
+            jnp.einsum("qhd,khd->hqk", query_heads, key_heads, preferred_element_type=jnp.float32)
+            * scaling
+        )
+        return jnp.where(allowed, raw_scores, MASKED)
+
+    scores = score_block()
+    row_max = jnp.max(scores, axis=-1, keepdims=True)
+    exponent = jnp.exp(scores - row_max)
+    row_sum = jnp.sum(exponent, axis=-1, keepdims=True)
+    log_total = row_max + jnp.log(row_sum)
+    attend_probs = (exponent / row_sum).astype(bf)
+    attended = (
+        jnp.einsum("hqk,khd->qhd", attend_probs, value_heads, preferred_element_type=jnp.float32)
+        .reshape(row_count, D)
+        .astype(bf)
+    )
+    branch_out = product(attended, gathered_out)
+    residual = inputs + branch_out
+    normed = root_norm(residual, gain_rows[3]).astype(bf)
+    logits = product(normed, gathered_router)
+    router_probs = softmax_rows(logits)
+    gate_total = jnp.sum(router_probs * match, axis=1, keepdims=True)
+    gate_values = router_probs * match / gate_total
+    upper = lax.reduce_precision(gate_values, 8, 7)
+    extra = jnp.concatenate(
+        [
+            rank,
+            upper.astype(bf),
+            (gate_values - upper).astype(bf),
+            jnp.zeros((row_count, WIDE - 3 * experts), bf),
+        ],
+        axis=1,
+    )
+    row_groups = spread(moves, jnp.concatenate([normed, extra], axis=1))
+
+    meta = jnp.stack([device // 2, device]).astype(jnp.int32)
+    saved, out_parts, row_parts = None, [], []
+    for index in range(moves.planes):
+        *saved, out_keep, out_send, row_keep, row_send = expert_group(
+            meta,
+            row_groups[index],
+            grad_groups[index],
+            expert_in[0],
+            expert_out[0],
+            saved,
+            index,
+            moves.planes,
+            capacity,
+            experts,
+        )
+        out_parts.append((out_keep, out_send))
+        row_parts.append((row_keep, row_send))
+    row_total = collect_ring(moves, [collect_plane(moves, *part) for part in row_parts])
+    x_rows, dy_rows, m_rows, du_rows = saved
+    expert_in_grad = dot_first(x_rows, du_rows)
+    expert_out_grad = dot_first(m_rows, dy_rows)
+
+    upstream = cotangent.astype(jnp.float32)
+    dispatch_grad = row_total[:, :D]
+    gate_grad = jnp.sum(
+        row_total[:, D : D + 4 * experts].reshape(row_count, experts, 4), axis=2
+    )
+    chosen_grad = (
+        match * (gate_grad - jnp.sum(gate_grad * gate_values, axis=1, keepdims=True)) / gate_total
+    )
+    logit_grad = (
+        router_probs * (chosen_grad - jnp.sum(chosen_grad * router_probs, axis=1, keepdims=True))
+    ).astype(bf)
+    router_grad = dot_first(normed, logit_grad)
+    normed_grad = dispatch_grad + dot_last(logit_grad, gathered_router)
+    _, second_back = jax.vjp(root_norm, residual, gain_rows[3])
+    residual_norm_grad, second_gain_grad = second_back(normed_grad)
+    residual_grad = upstream + residual_norm_grad
+    branch_grad = residual_grad.astype(bf)
+
+    out_parts, branch_grad = lax.optimization_barrier((out_parts, branch_grad))
+    out_total = collect_ring(moves, [collect_plane(moves, *part) for part in out_parts])
+    output = (residual + out_total).astype(bf)
+
+    out_grad = dot_first(attended, branch_grad)
+    attended_grad = (
+        dot_last(branch_grad, gathered_out).astype(bf).reshape(row_count, HEADS, HEAD_DIM)
+    )
+    recomputed = jnp.exp(score_block() - log_total)
+    value_grad = jnp.einsum(
+        "hqk,qhd->khd", attend_probs, attended_grad, preferred_element_type=jnp.float32
+    )
+    attend_grad = jnp.einsum(
+        "qhd,khd->hqk", attended_grad, value_heads, preferred_element_type=jnp.float32
+    )
+    row_delta = jnp.sum(recomputed * attend_grad, axis=-1, keepdims=True)
+    score_grad = (recomputed * (attend_grad - row_delta)).astype(bf)
+    query_grad = (
+        jnp.einsum("hqk,khd->qhd", score_grad, key_heads, preferred_element_type=jnp.float32)
+        * scaling
+    )
+    key_grad = (
+        jnp.einsum("hqk,qhd->khd", score_grad, query_heads, preferred_element_type=jnp.float32)
+        * scaling
+    )
+    projected_grad, query_gain_grad, key_gain_grad = prepare_back(
+        (query_grad, key_grad, value_grad)
+    )
+    projected_grad = projected_grad.astype(bf)
+    attention_in_grad = dot_first(normed_input, projected_grad)
+    normed_input_grad = dot_last(projected_grad, gathered_in)
+    _, first_back = jax.vjp(root_norm, inputs, gain_rows[0])
+    input_norm_grad, first_gain_grad = first_back(normed_input_grad)
+    input_grad = residual_grad + input_norm_grad
+    gains_grad = jnp.stack([first_gain_grad, query_gain_grad, key_gain_grad, second_gain_grad])
+    small = jnp.concatenate([gains_grad.T, router_grad], axis=1)
+    small_share, in_share, out_share = (
+        lax.psum_scatter(small, "fsdp", scatter_dimension=0, tiled=True),
+        lax.psum_scatter(attention_in_grad.astype(bf), "fsdp", scatter_dimension=0, tiled=True),
+        lax.psum_scatter(out_grad.astype(bf), "fsdp", scatter_dimension=0, tiled=True),
+    )
+    return (
+        output,
+        input_grad,
+        small_share[:, :4].T,
+        in_share.astype(jnp.float32),
+        out_share.astype(jnp.float32),
+        small_share[:, 4:],
+        expert_in_grad[None],
+        expert_out_grad[None],
+    )
+
+
+def shards(*arguments):
+    routes = arguments[8]
+    experts = lax.axis_size("fsdp") // 2
+    if 2 * routes.shape[1] >= experts:
+        return shards_dense(*arguments)
+    return shards_routed(*arguments)
+
+
 def solution(mesh):
     in_specs = (
         P("fsdp", None),

time: 2890 us -> 1300 us (0.45)
  waiting for transfers between devices: 2010 us -> 751 us
  blocking collectives: 367 us -> 99.6 us
  Pallas kernels: 0 us -> 136 us
  matrix products: 203 us -> 102 us
  local copies, waits for them, and re-layouts: 119 us -> 31.1 us
    all_to_all x4 -> x0, waiting for transfers between devices: 1060 us -> none  [the longest x1 358 us: shards(): lax.all_to_all(grad_rows, 'fsdp', split_axis=0, concat_axis=0, tiled=True)]
    ppermute x0 -> x92, waiting for transfers between devices: none -> 269 us  [send(): return lax.ppermute(value, 'fsdp', pairs)]
    all_gather x2, blocking collectives: 367 us -> 99.6 us  [the longest x1 61.7 us: shards_dense(): lax.all_gather(norm_gains, 'fsdp', axis=1, tiled=True)]
    reduce_scatter x2, waiting for transfers between devices: 620 us -> 367 us  [the longest x1 248 us: shards_dense(): lax.psum_scatter(attention_in_grad.astype(bf), 'fsdp', scatter_dimension=...]
    unnamed x8 -> x6, waiting for transfers between devices: 192 us -> 1.43 us
    pallas_call x0 -> x4, Pallas kernels: none -> 136 us  [expert_group(): pl.pallas_call(functools.partial(expert_body, per_step, cap, experts), gr...]
    ppermute x0 -> x92, starting transfers between devices: none -> 92.8 us  [send(): return lax.ppermute(value, 'fsdp', pairs)]
    all_to_all x4 -> x0, starting transfers between devices: 72.2 us -> none  [the longest x1 60.2 us: shards(): lax.all_to_all(grad_buffer, 'fsdp', split_axis=0, concat_axis=0, tiled=True)]
  transfers between devices with their start and end apart: 10 -> 97, of which waited for: 10 -> 38; matrix products, arithmetic and copies ran while one was open for 8% -> 10% of each run, Pallas kernels for 0% -> 10%
where the time goes in v1:
time: 1300 us; the launch traced here: 1290 us
  waiting for transfers between devices  751 us (58%)
  Pallas kernels  136 us (10%)
  matrix products  102 us (8%)
  blocking collectives  99.6 us (8%)
  starting transfers between devices  93 us (7%)
  other arithmetic  67.1 us (5%)
  local copies, waits for them, and re-layouts  31.1 us (2%)
  between operations  15.4 us (1%)
    ppermute x92, waiting for transfers between devices, send(): return lax.ppermute(value, 'fsdp', pairs)  269 us
    reduce_scatter x1, waiting for transfers between devices, shards_dense(): lax.psum_scatter(attention_in_grad.astype(bf), 'fsdp', scatter_dimension=...  248 us
    pallas_call x4, Pallas kernels, expert_group(): pl.pallas_call(functools.partial(expert_body, per_step, cap, experts), gr...  136 us
    reduce_scatter x1, waiting for transfers between devices, shards_dense(): lax.psum_scatter(out_grad.astype(bf), 'fsdp', scatter_dimension=0, tiled=...  118 us
    ppermute x92, starting transfers between devices, send(): return lax.ppermute(value, 'fsdp', pairs)  92.8 us
    all_gather x1, waiting for transfers between devices, shards_dense(): lax.all_gather(attention_in, 'fsdp', axis=0, tiled=True)  69.1 us
    all_gather x1, blocking collectives, shards_dense(): lax.all_gather(norm_gains, 'fsdp', axis=1, tiled=True)  61.7 us
    dot_general x5, matrix products, dot_first(): lax.dot_general(left, right, (((0,), (0,)), ((), ())), preferred_element_...  52.4 us
  transfers between devices with their start and end apart: 97, of which 38 were waited for; matrix products, arithmetic and copies ran while one was open for 10% of the time, Pallas kernels for 10%

profile of v1, /device:TPU:0, one launch (start us, length us, event | category | flops | bytes accessed | tf_op | source)
XLA Modules:
  0.0 1294.9 jit_solution(17002659936014753483)
XLA Ops:
  16.9 61.7 %all-gather = bf16[32,64,4]{1,2,0:T(4,128)(2,1)S(1)} all-gather(bf16[1,64,4]{1,2,0:T(4,128)(2,1)} %bitcast.231), channel_id=1, replica_groups=mesh['fsdp'=32] {'fsdp'}, dimensions={0}, use_global_device_ids=true | all-gather | bytes 16896 | tf_op jit(solution)/shard_map/all_gather | solution.py:555
  78.7 37.8 %all-gather.1 = bf16[32,64,16]{1,2,0:T(8,128)(2,1)S(1)} all-gather(bf16[1,64,16]{1,2,0:T(8,128)(2,1)} %bitcast.229), channel_id=1, replica_groups=mesh['fsdp'=32] {'fsdp'}, dimensions={0}, use_global_device_ids=true | all-gather | bytes 67584 | tf_op jit(solution)/shard_map/all_gather | solution.py:558
  121.6 69.1 %all-gather.5.cloned.1.call-done = bf16[2048,6144]{1,0:T(8,128)(2,1)} async-done(((bf16[64,6144]{1,0:T(8,128)(2,1)}), bf16[2048,6144]{1,0:T(8,128)(2,1)}) %all-gather.5.cloned.1.call-update) | async-done | bytes 25165840 | tf_op jit(solution)/shard_map/all_gather | solution.py:556
  190.7 10.9 fusion.51
  213.6 10.9 collective-permute-done.24.refs_10_
  234.4 14.2 %collective-permute-done.40.refs_10_ = bf16[192,2048]{1,0:T(8,128)(2,1)} collective-permute-done((bf16[192,2048]{1,0:T(8,128)(2,1)}, bf16[192,2048]{1,0:T(8,128)(2,1)}, u32[]{:S(2)}, u32[]{:S(2)}) %collective-permute-start.40) | collective-permute-done | bytes 786464 | tf_op jit(solution)/shard_map/ppermute | solution.py:318
  248.7 5.4 collective-permute-done.39.refs_9_
  257.1 44.5 %all-gather.7.cloned.1.call-done = bf16[2048,2048]{1,0:T(8,128)(2,1)} async-done(((bf16[64,2048]{1,0:T(8,128)(2,1)}), bf16[2048,2048]{1,0:T(8,128)(2,1)}) %all-gather.7.cloned.1.call-update) | async-done | bytes 8388624 | tf_op jit(solution)/shard_map/all_gather | solution.py:557
  301.6 5.7 multiply_reduce_fusion.5
  322.4 6.6 collective-permute-done.57.refs_11_
  333.1 8.4 collective-permute-done.14.refs_0_
  344.8 4.4 collective-permute-done.1.refs_2_
  349.2 3.4 collective-permute-start.15
  352.9 8.7 collective-permute-done.30.refs_0_
  361.9 4.2 collective-permute-done.16.refs_2_
  380.1 5.7 collective-permute-done.46.refs_0_
  387.0 8.6 collective-permute-done.32.refs_2_
  398.0 11.8 collective-permute-done.17.refs_3_
  412.7 33.7 %expert_group.4 = (bf16[4096,2048]{1,0:T(8,128)(2,1)}, bf16[4096,2048]{1,0:T(8,128)(2,1)}, bf16[4096,512]{1,0:T(8,128)(2,1)}, bf16[4096,1024]{1,0:T(8,128)(2,1)}...) custom-call(s32[2]{0:T(128)} %pad_add_fusion.meta, ...), custom_call_target="tpu_custom_call" | custom-call | flops 16000000000 | bytes 62914560 | tf_op jit(solution)/shard_map/expert_group/pallas_call | solution.py:489
  449.0 33.9 %expert_group.5 = (bf16[4096,2048]{1,0:T(8,128)(2,1)}, bf16[4096,2048]{1,0:T(8,128)(2,1)}, bf16[4096,512]{1,0:T(8,128)(2,1)}, bf16[4096,1024]{1,0:T(8,128)(2,1)}...) custom-call(s32[2]{0:T(128)} %pad_add_fusion.meta, ...), custom_call_target="tpu_custom_call", output_to_operand_aliasing={{0}: (19, {}), {1}: (20, {}), {2}: (21, {}), {3}: (22, {})} | custom-call | flops 16000000000 | bytes 62914560 | tf_op jit(solution)/shard_map/expert_group/pallas_call | solution.py:489
  484.6 34.3 %expert_group.6 = (bf16[4096,2048]{1,0:T(8,128)(2,1)}, bf16[4096,2048]{1,0:T(8,128)(2,1)}, bf16[4096,512]{1,0:T(8,128)(2,1)}, bf16[4096,1024]{1,0:T(8,128)(2,1)}...) custom-call(s32[2]{0:T(128)} %pad_add_fusion.meta, ...), custom_call_target="tpu_custom_call", output_to_operand_aliasing={{0}: (19, {}), {1}: (20, {}), {2}: (21, {}), {3}: (22, {})} | custom-call | flops 16000000000 | bytes 62914560 | tf_op jit(solution)/shard_map/expert_group/pallas_call | solution.py:489
  519.9 33.8 %expert_group.7 = (bf16[4096,2048]{1,0:T(8,128)(2,1)}, bf16[4096,2048]{1,0:T(8,128)(2,1)}, bf16[4096,512]{1,0:T(8,128)(2,1)}, bf16[4096,1024]{1,0:T(8,128)(2,1)}...) custom-call(s32[2]{0:T(128)} %pad_add_fusion.meta, ...), custom_call_target="tpu_custom_call", output_to_operand_aliasing={{0}: (19, {}), {1}: (20, {}), {2}: (21, {}), {3}: (22, {})} | custom-call | flops 16000000000 | bytes 62914560 | tf_op jit(solution)/shard_map/expert_group/pallas_call | solution.py:489
  554.2 3.7 add_convert_fusion
  564.2 15.4 %collective-permute-done.72 = bf16[2,192,2176]{2,1,0:T(8,128)(2,1)S(1)} collective-permute-done((bf16[2,192,2176]{2,1,0:T(8,128)(2,1)S(1)}, bf16[2,192,2176]{2,1,0:T(8,128)(2,1)S(1)}, u32[]{:S(2)}, u32[]{:S(2)}) %collective-permute-start.72) | collective-permute-done | bytes 1671200 | tf_op jit(solution)/shard_map/ppermute | solution.py:318
  582.8 18.7 %collective-permute-done.73 = bf16[192,2176]{1,0:T(8,128)(2,1)S(1)} collective-permute-done((bf16[192,2176]{1,0:T(8,128)(2,1)S(1)}, bf16[192,2176]{1,0:T(8,128)(2,1)S(1)}, u32[]{:S(2)}, u32[]{:S(2)}) %collective-permute-start.73) | collective-permute-done | bytes 835616 | tf_op jit(solution)/shard_map/ppermute | solution.py:318
  609.6 11.1 collective-permute-done.74
  620.7 7.6 collective-permute-done.70
  635.2 25.0 %collective-permute-done.63 = bf16[2,192,2176]{2,1,0:T(8,128)(2,1)S(1)} collective-permute-done((bf16[2,192,2176]{2,1,0:T(8,128)(2,1)S(1)}, bf16[2,192,2176]{2,1,0:T(8,128)(2,1)S(1)}, u32[]{:S(2)}, u32[]{:S(2)}) %collective-permute-start.63) | collective-permute-done | bytes 1671200 | tf_op jit(solution)/shard_map/ppermute | solution.py:318
  665.3 7.8 collective-permute-done.64
  673.1 9.2 collective-permute-done.76
  701.5 6.7 fusion.25
  717.5 3.3 add_add_fusion.2
  720.8 16.0 %fusion.10 = (f32[2048]{0:T(1024)S(1)}, f32[192]{0:T(256)S(1)}, f32[192,2048]{1,0:T(8,128)}) fusion(bf16[192,2048]{1,0:T(8,128)(2,1)S(1)} %copy-done.12, f32[192]{0:T(256)S(1)} %copy-done.64, f32[2048]{0:T(1024)S(1)} %bitcast.211, bf16[2048,6144]{1,0:T(8,128)(2,1)} %all-gather.5.cloned.1.call-done, f32[192,2048]{1,0:T(8,128)} %get-tuple-element.107, ...), kind=kOutput, calls=%fused_computation.47 | convolution fusion | flops 4838127616 | bytes 32261632 | tf_op jit(solution)/shard_map/dot_general | solution.py:77
  738.4 5.6 convolution_convert_fusion.1
  745.6 13.1 %convolution_convert_fusion = bf16[2048,6144]{1,0:T(8,128)(2,1)} fusion(bf16[192,2048]{1,0:T(8,128)(2,1)S(1)} %copy-done.13, f32[2048]{0:T(1024)S(1)} %bitcast.212, f32[192]{0:T(256)S(1)} %copy-done.64, f32[192,2048]{1,0:T(8,128)} %get-tuple-element.107, f32[192,2048]{1,0:T(8,128)} %get-tuple-element.106, f32[192,2048]{1,0:T(8,128)S(1)} %bitcast.209), kind=kOutput, calls=%fused_computation | convolution fusion | flops 4849532928 | bytes 30679808 | tf_op jit(solution)/shard_map/dot_general | solution.py:71
  761.6 9.1 collective-permute-done.83
  770.8 3.4 add_convert_fusion.5
  778.4 21.7 %convolution_bitcast_fusion = f32[1,2048,1024]{2,1,0:T(8,128)} fusion(bf16[4096,2048]{1,0:T(8,128)(2,1)} %get-tuple-element.86, bf16[4096,1024]{1,0:T(8,128)(2,1)S(1)} %bitcast.195), kind=kOutput, calls=%fused_computation.11 | convolution fusion | flops 17179869184 | bytes 33554432 | tf_op jit(solution)/shard_map/dot_general | solution.py:71
  800.2 13.0 %collective-permute-done.87 = bf16[2,192,2048]{2,1,0:T(8,128)(2,1)S(1)} collective-permute-done((bf16[2,192,2048]{2,1,0:T(8,128)(2,1)S(1)}, bf16[2,192,2048]{2,1,0:T(8,128)(2,1)S(1)}, u32[]{:S(2)}, u32[]{:S(2)}) %collective-permute-start.87) | collective-permute-done | bytes 1572896 | tf_op jit(solution)/shard_map/ppermute | solution.py:318
  822.2 12.6 collective-permute-done.88
  843.3 9.6 collective-permute-done.81
  863.7 10.4 convolution_bitcast_fusion.1
  874.1 5.1 collective-permute-done.78
  893.3 4.3 collective-permute-done.79
  897.6 16.3 %collective-permute-done.91 = bf16[192,2048]{1,0:T(8,128)(2,1)} collective-permute-done((bf16[192,2048]{1,0:T(8,128)(2,1)}, bf16[192,2048]{1,0:T(8,128)(2,1)}, u32[]{:S(2)}, u32[]{:S(2)}) %collective-permute-start.91) | collective-permute-done | bytes 786464 | tf_op jit(solution)/shard_map/ppermute | solution.py:318
  913.9 3.3 fusion.24
  917.2 118.3 %reduce-scatter.8.cloned.1.call-done = bf16[64,2048]{1,0:T(8,128)(2,1)} async-done(((bf16[2048,2048]{1,0:T(8,128)(2,1)}), bf16[64,2048]{1,0:T(8,128)(2,1)}) %reduce-scatter.8.cloned.1.call-update) | async-done | bytes 262160 | tf_op jit(solution)/shard_map/reduce_scatter | solution.py:702
  1037.3 248.4 %reduce-scatter.6.cloned.1.call-done = bf16[64,6144]{1,0:T(8,128)(2,1)} async-done(((bf16[2048,6144]{1,0:T(8,128)(2,1)}), bf16[64,6144]{1,0:T(8,128)(2,1)}) %reduce-scatter.6.cloned.1.call-update) | async-done | bytes 786448 | tf_op jit(solution)/shard_map/reduce_scatter | solution.py:701
  (474 shorter events, 203.1 us)
Async XLA Ops:
  7.2 183.5 %all-gather.5.cloned.1.call-start = ((), (), s32[]{:S(2)}) async-start(), calls=%async_computation.3 | async-start | bytes 25952256 | tf_op jit(solution)/shard_map/all_gather | solution.py:556
  7.9 293.7 %all-gather.7.cloned.1.call-start = ((), (), s32[]{:S(2)}) async-start(), calls=%async_computation.4 | async-start | bytes 8650752 | tf_op jit(solution)/shard_map/all_gather | solution.py:557
  8.7 881.7 %reduce-scatter.10.cloned.1.call-start = ((), (), s32[]{:S(2)}) async-start(), calls=%async_computation.7 | async-start | bytes 1081344
  8.7 195.2 %collective-permute-start.10 = (bf16[192,2048]{1,0:T(8,128)(2,1)}, bf16[192,2048]{1,0:T(8,128)(2,1)}, u32[]{:S(2)}, u32[]{:S(2)}) collective-permute-start(bf16[192,2048]{1,0:T(8,128)(2,1)} %refs_8_.1), channel_id=1, source_target_pairs={{0,1},{1,0},{2,3},{3,2},{4,5},{5,4},{6,7},{7,6},{8,9},{9,8},{10,11... | collective-permute-start | bytes 2359304 | tf_op jit(solution)/shard_map/ppermute | solution.py:318
  9.2 110.6 %collective-permute-start.8 = (bf16[192,2048]{1,0:T(8,128)(2,1)}, bf16[192,2048]{1,0:T(8,128)(2,1)}, u32[]{:S(2)}, u32[]{:S(2)}) collective-permute-start(bf16[192,2048]{1,0:T(8,128)(2,1)} %refs_8_.1), channel_id=1, source_target_pairs={{0,4},{1,3},{2,6},{3,1},{4,0},{5,7},{6,2},{7,5},{8,12},{9,11},{10,... | collective-permute-start | bytes 2359304 | tf_op jit(solution)/shard_map/ppermute | solution.py:318
  11.8 107.6 %collective-permute-start.7 = (bf16[192,2048]{1,0:T(8,128)(2,1)}, bf16[192,2048]{1,0:T(8,128)(2,1)}, u32[]{:S(2)}, u32[]{:S(2)}) collective-permute-start(bf16[192,2048]{1,0:T(8,128)(2,1)} %refs_8_.1), channel_id=1, source_target_pairs={{0,2},{1,5},{2,0},{3,7},{4,6},{5,1},{6,4},{7,3},{8,10},{9,13},{10,... | collective-permute-start | bytes 2359304 | tf_op jit(solution)/shard_map/ppermute | solution.py:318
  13.3 108.3 %collective-permute-start.22 = (bf16[192,2048]{1,0:T(8,128)(2,1)}, bf16[192,2048]{1,0:T(8,128)(2,1)}, u32[]{:S(2)}, u32[]{:S(2)}) collective-permute-start(bf16[192,2048]{1,0:T(8,128)(2,1)} %refs_8_.1), channel_id=1, source_target_pairs={{0,16},{1,17},{2,18},{3,19},{4,20},{5,21},{6,22},{7,23},{8,0},{9,1... | collective-permute-start | bytes 2359304 | tf_op jit(solution)/shard_map/ppermute | solution.py:318
  119.4 86.3 %collective-permute-start.11 = (bf16[192,2048]{1,0:T(8,128)(2,1)}, bf16[192,2048]{1,0:T(8,128)(2,1)}, u32[]{:S(2)}, u32[]{:S(2)}) collective-permute-start(bf16[192,2048]{1,0:T(8,128)(2,1)} %collective-permute-done.7.refs_9_), channel_id=1, source_target_pairs={{0,1},{1,0},{2,3},{3,2},{4,5},{5,4},{6,7},{7,6},{8,9},{9,8},{10,11... | collective-permute-start | bytes 2359304 | tf_op jit(solution)/shard_map/ppermute | solution.py:318
  119.8 87.6 %collective-permute-start.9 = (bf16[192,2048]{1,0:T(8,128)(2,1)}, bf16[192,2048]{1,0:T(8,128)(2,1)}, u32[]{:S(2)}, u32[]{:S(2)}) collective-permute-start(bf16[192,2048]{1,0:T(8,128)(2,1)} %collective-permute-done.7.refs_9_), channel_id=1, source_target_pairs={{0,4},{1,3},{2,6},{3,1},{4,0},{5,7},{6,2},{7,5},{8,12},{9,11},{10,... | collective-permute-start | bytes 2359304 | tf_op jit(solution)/shard_map/ppermute | solution.py:318
  119.8 84.5 %collective-permute-start.12 = (bf16[192,2048]{1,0:T(8,128)(2,1)}, bf16[192,2048]{1,0:T(8,128)(2,1)}, u32[]{:S(2)}, u32[]{:S(2)}) collective-permute-start(bf16[192,2048]{1,0:T(8,128)(2,1)} %collective-permute-done.8.refs_10_), channel_id=1, source_target_pairs={{0,1},{1,0},{2,3},{3,2},{4,5},{5,4},{6,7},{7,6},{8,9},{9,8},{10,11... | collective-permute-start | bytes 2359304 | tf_op jit(solution)/shard_map/ppermute | solution.py:318
  121.6 85.8 %collective-permute-start.38 = (bf16[192,2048]{1,0:T(8,128)(2,1)}, bf16[192,2048]{1,0:T(8,128)(2,1)}, u32[]{:S(2)}, u32[]{:S(2)}) collective-permute-start(bf16[192,2048]{1,0:T(8,128)(2,1)} %collective-permute-done.22.refs_8_), channel_id=1, source_target_pairs={{0,16},{1,17},{2,18},{3,19},{4,20},{5,21},{6,22},{7,23},{8,0},{9,1... | collective-permute-start | bytes 2359304 | tf_op jit(solution)/shard_map/ppermute | solution.py:318
  233.3 74.3 %collective-permute-start.25 = (bf16[192,2048]{1,0:T(8,128)(2,1)}, bf16[192,2048]{1,0:T(8,128)(2,1)}, u32[]{:S(2)}, u32[]{:S(2)}) collective-permute-start(bf16[192,2048]{1,0:T(8,128)(2,1)} %collective-permute-done.23.refs_9_), channel_id=1, source_target_pairs={{0,4},{1,3},{2,6},{3,1},{4,0},{5,7},{6,2},{7,5},{8,12},{9,11},{10,... | collective-permute-start | bytes 2359304 | tf_op jit(solution)/shard_map/ppermute | solution.py:318
  248.7 59.2 %collective-permute-start.58 = (bf16[192,2048]{1,0:T(8,128)(2,1)}, bf16[192,2048]{1,0:T(8,128)(2,1)}, u32[]{:S(2)}, u32[]{:S(2)}) collective-permute-start(bf16[192,2048]{1,0:T(8,128)(2,1)} %collective-permute-done.54.refs_8_), channel_id=1, source_target_pairs={{0,1},{1,0},{2,3},{3,2},{4,5},{5,4},{6,7},{7,6},{8,9},{9,8},{10,11... | collective-permute-start | bytes 2359304 | tf_op jit(solution)/shard_map/ppermute | solution.py:318
  254.0 56.3 %collective-permute-start.56 = (bf16[192,2048]{1,0:T(8,128)(2,1)}, bf16[192,2048]{1,0:T(8,128)(2,1)}, u32[]{:S(2)}, u32[]{:S(2)}) collective-permute-start(bf16[192,2048]{1,0:T(8,128)(2,1)} %collective-permute-done.54.refs_8_), channel_id=1, source_target_pairs={{0,4},{1,3},{2,6},{3,1},{4,0},{5,7},{6,2},{7,5},{8,12},{9,11},{10,... | collective-permute-start | bytes 2359304 | tf_op jit(solution)/shard_map/ppermute | solution.py:318
  255.7 54.6 %collective-permute-start.55 = (bf16[192,2048]{1,0:T(8,128)(2,1)}, bf16[192,2048]{1,0:T(8,128)(2,1)}, u32[]{:S(2)}, u32[]{:S(2)}) collective-permute-start(bf16[192,2048]{1,0:T(8,128)(2,1)} %collective-permute-done.54.refs_8_), channel_id=1, source_target_pairs={{0,2},{1,5},{2,0},{3,7},{4,6},{5,1},{6,4},{7,3},{8,10},{9,13},{10,... | collective-permute-start | bytes 2359304 | tf_op jit(solution)/shard_map/ppermute | solution.py:318
  257.1 53.7 %collective-permute-start.44 = (bf16[192,2048]{1,0:T(8,128)(2,1)}, bf16[192,2048]{1,0:T(8,128)(2,1)}, u32[]{:S(2)}, u32[]{:S(2)}) collective-permute-start(bf16[192,2048]{1,0:T(8,128)(2,1)} %collective-permute-done.40.refs_10_), channel_id=1, source_target_pairs={{0,1},{1,0},{2,3},{3,2},{4,5},{5,4},{6,7},{7,6},{8,9},{9,8},{10,11... | collective-permute-start | bytes 2359304 | tf_op jit(solution)/shard_map/ppermute | solution.py:318
  377.8 31.9 %collective-permute-start.17 = (bf16[192,2176]{1,0:T(8,128)(2,1)}, bf16[192,2176]{1,0:T(8,128)(2,1)}, u32[]{:S(2)}, u32[]{:S(2)}) collective-permute-start(bf16[192,2176]{1,0:T(8,128)(2,1)} %collective-permute-done.15.refs_1_), channel_id=1, source_target_pairs={{0,4},{1,3},{2,6},{3,1},{4,0},{5,7},{6,2},{7,5},{8,12},{9,11},{10,... | collective-permute-start | bytes 2506760 | tf_op jit(solution)/shard_map/ppermute | solution.py:318
  386.5 60.7 %collective-permute-start.19 = (bf16[192,2176]{1,0:T(8,128)(2,1)}, bf16[192,2176]{1,0:T(8,128)(2,1)}, u32[]{:S(2)}, u32[]{:S(2)}) collective-permute-start(bf16[192,2176]{1,0:T(8,128)(2,1)} %collective-permute-done.15.refs_1_), channel_id=1, source_target_pairs={{0,1},{1,0},{2,3},{3,2},{4,5},{5,4},{6,7},{7,6},{8,9},{9,8},{10,11... | collective-permute-start | bytes 2506760 | tf_op jit(solution)/shard_map/ppermute | solution.py:318
  395.6 50.7 %collective-permute-start.20 = (bf16[192,2176]{1,0:T(8,128)(2,1)}, bf16[192,2176]{1,0:T(8,128)(2,1)}, u32[]{:S(2)}, u32[]{:S(2)}) collective-permute-start(bf16[192,2176]{1,0:T(8,128)(2,1)} %copy-done.40), channel_id=1, source_target_pairs={{0,1},{1,0},{2,3},{3,2},{4,5},{5,4},{6,7},{7,6},{8,9},{9,8},{10,11... | collective-permute-start | bytes 2506760 | tf_op jit(solution)/shard_map/ppermute | solution.py:318
  396.0 52.2 %collective-permute-start.47 = (bf16[192,2176]{1,0:T(8,128)(2,1)}, bf16[192,2176]{1,0:T(8,128)(2,1)S(1)}, u32[]{:S(2)}, u32[]{:S(2)}) collective-permute-start(bf16[192,2176]{1,0:T(8,128)(2,1)} %collective-permute-done.46.refs_0_), channel_id=1, source_target_pairs={{0,2},{1,5},{2,0},{3,7},{4,6},{5,1},{6,4},{7,3},{8,10},{9,13},{10,... | collective-permute-start | bytes 2506760 | tf_op jit(solution)/shard_map/ppermute | solution.py:318
  409.8 38.5 %collective-permute-start.33 = (bf16[192,2176]{1,0:T(8,128)(2,1)}, bf16[192,2176]{1,0:T(8,128)(2,1)S(1)}, u32[]{:S(2)}, u32[]{:S(2)}) collective-permute-start(bf16[192,2176]{1,0:T(8,128)(2,1)} %collective-permute-done.31.refs_1_), channel_id=1, source_target_pairs={{0,4},{1,3},{2,6},{3,1},{4,0},{5,7},{6,2},{7,5},{8,12},{9,11},{10,... | collective-permute-start | bytes 2506760 | tf_op jit(solution)/shard_map/ppermute | solution.py:318
  412.1 36.9 %collective-permute-start.21 = (bf16[192,2176]{1,0:T(8,128)(2,1)}, bf16[192,2176]{1,0:T(8,128)(2,1)}, u32[]{:S(2)}, u32[]{:S(2)}) collective-permute-start(bf16[192,2176]{1,0:T(8,128)(2,1)} %collective-permute-done.17.refs_3_), channel_id=1, source_target_pairs={{0,1},{1,0},{2,3},{3,2},{4,5},{5,4},{6,7},{7,6},{8,9},{9,8},{10,11... | collective-permute-start | bytes 2506760 | tf_op jit(solution)/shard_map/ppermute | solution.py:318
  446.4 36.6 %collective-permute-start.48 = (bf16[192,2176]{1,0:T(8,128)(2,1)}, bf16[192,2176]{1,0:T(8,128)(2,1)S(1)}, u32[]{:S(2)}, u32[]{:S(2)}) collective-permute-start(bf16[192,2176]{1,0:T(8,128)(2,1)} %collective-permute-done.46.refs_0_), channel_id=1, source_target_pairs={{0,4},{1,3},{2,6},{3,1},{4,0},{5,7},{6,2},{7,5},{8,12},{9,11},{10,... | collective-permute-start | bytes 2506760 | tf_op jit(solution)/shard_map/ppermute | solution.py:318
  447.2 36.4 %collective-permute-start.35 = (bf16[192,2176]{1,0:T(8,128)(2,1)}, bf16[192,2176]{1,0:T(8,128)(2,1)}, u32[]{:S(2)}, u32[]{:S(2)}) collective-permute-start(bf16[192,2176]{1,0:T(8,128)(2,1)} %collective-permute-done.31.refs_1_), channel_id=1, source_target_pairs={{0,1},{1,0},{2,3},{3,2},{4,5},{5,4},{6,7},{7,6},{8,9},{9,8},{10,11... | collective-permute-start | bytes 2506760 | tf_op jit(solution)/shard_map/ppermute | solution.py:318
  448.2 35.3 %collective-permute-start.36 = (bf16[192,2176]{1,0:T(8,128)(2,1)}, bf16[192,2176]{1,0:T(8,128)(2,1)}, u32[]{:S(2)}, u32[]{:S(2)}) collective-permute-start(bf16[192,2176]{1,0:T(8,128)(2,1)} %collective-permute-done.32.refs_2_), channel_id=1, source_target_pairs={{0,1},{1,0},{2,3},{3,2},{4,5},{5,4},{6,7},{7,6},{8,9},{9,8},{10,11... | collective-permute-start | bytes 2506760 | tf_op jit(solution)/shard_map/ppermute | solution.py:318
  448.3 35.7 %collective-permute-start.49 = (bf16[192,2176]{1,0:T(8,128)(2,1)S(1)}, bf16[192,2176]{1,0:T(8,128)(2,1)}, u32[]{:S(2)}, u32[]{:S(2)}) collective-permute-start(bf16[192,2176]{1,0:T(8,128)(2,1)S(1)} %collective-permute-done.47.refs_1_), channel_id=1, source_target_pairs={{0,4},{1,3},{2,6},{3,1},{4,0},{5,7},{6,2},{7,5},{8,12},{9,11},{10,... | collective-permute-start | bytes 2506760 | tf_op jit(solution)/shard_map/ppermute | solution.py:318
  449.0 35.1 %collective-permute-start.37 = (bf16[192,2176]{1,0:T(8,128)(2,1)S(1)}, bf16[192,2176]{1,0:T(8,128)(2,1)}, u32[]{:S(2)}, u32[]{:S(2)}) collective-permute-start(bf16[192,2176]{1,0:T(8,128)(2,1)S(1)} %collective-permute-done.33.refs_3_), channel_id=1, source_target_pairs={{0,1},{1,0},{2,3},{3,2},{4,5},{5,4},{6,7},{7,6},{8,9},{9,8},{10,11... | collective-permute-start | bytes 2506760 | tf_op jit(solution)/shard_map/ppermute | solution.py:318
  483.0 71.3 %collective-permute-start.71 = (bf16[4,192,2176]{2,1,0:T(8,128)(2,1)}, bf16[4,192,2176]{2,1,0:T(8,128)(2,1)}, u32[]{:S(2)}, u32[]{:S(2)}) collective-permute-start(bf16[4,192,2176]{2,1,0:T(8,128)(2,1)} %get-tuple-element.76), channel_id=1, source_target_pairs={{0,1},{1,0},{2,3},{3,2},{4,5},{5,4},{6,7},{7,6},{8,9},{9,8},{10,11... | collective-permute-start | bytes 10027016 | tf_op jit(solution)/shard_map/ppermute | solution.py:318
  483.5 35.3 %collective-permute-start.50 = (bf16[192,2176]{1,0:T(8,128)(2,1)}, bf16[192,2176]{1,0:T(8,128)(2,1)}, u32[]{:S(2)}, u32[]{:S(2)}) collective-permute-start(bf16[192,2176]{1,0:T(8,128)(2,1)} %collective-permute-done.46.refs_0_), channel_id=1, source_target_pairs={{0,1},{1,0},{2,3},{3,2},{4,5},{5,4},{6,7},{7,6},{8,9},{9,8},{10,11... | collective-permute-start | bytes 2506760 | tf_op jit(solution)/shard_map/ppermute | solution.py:318
  483.6 35.4 %collective-permute-start.51 = (bf16[192,2176]{1,0:T(8,128)(2,1)S(1)}, bf16[192,2176]{1,0:T(8,128)(2,1)}, u32[]{:S(2)}, u32[]{:S(2)}) collective-permute-start(bf16[192,2176]{1,0:T(8,128)(2,1)S(1)} %collective-permute-done.47.refs_1_), channel_id=1, source_target_pairs={{0,1},{1,0},{2,3},{3,2},{4,5},{5,4},{6,7},{7,6},{8,9},{9,8},{10,11... | collective-permute-start | bytes 2506760 | tf_op jit(solution)/shard_map/ppermute | solution.py:318
  484.0 35.0 %collective-permute-start.52 = (bf16[192,2176]{1,0:T(8,128)(2,1)S(1)}, bf16[192,2176]{1,0:T(8,128)(2,1)}, u32[]{:S(2)}, u32[]{:S(2)}) collective-permute-start(bf16[192,2176]{1,0:T(8,128)(2,1)S(1)} %collective-permute-done.48.refs_2_), channel_id=1, source_target_pairs={{0,1},{1,0},{2,3},{3,2},{4,5},{5,4},{6,7},{7,6},{8,9},{9,8},{10,11... | collective-permute-start | bytes 2506760 | tf_op jit(solution)/shard_map/ppermute | solution.py:318
  484.1 34.9 %collective-permute-start.53 = (bf16[192,2176]{1,0:T(8,128)(2,1)}, bf16[192,2176]{1,0:T(8,128)(2,1)S(1)}, u32[]{:S(2)}, u32[]{:S(2)}) collective-permute-start(bf16[192,2176]{1,0:T(8,128)(2,1)} %collective-permute-done.49.refs_3_), channel_id=1, source_target_pairs={{0,1},{1,0},{2,3},{3,2},{4,5},{5,4},{6,7},{7,6},{8,9},{9,8},{10,11... | collective-permute-start | bytes 2506760 | tf_op jit(solution)/shard_map/ppermute | solution.py:318
  518.8 40.7 %collective-permute-start.68 = (bf16[4,192,2176]{2,1,0:T(8,128)(2,1)}, bf16[4,192,2176]{2,1,0:T(8,128)(2,1)}, u32[]{:S(2)}, u32[]{:S(2)}) collective-permute-start(bf16[4,192,2176]{2,1,0:T(8,128)(2,1)} %get-tuple-element.74), channel_id=1, source_target_pairs={{0,1},{1,0},{2,3},{3,2},{4,5},{5,4},{6,7},{7,6},{8,9},{9,8},{10,11... | collective-permute-start | bytes 10027016 | tf_op jit(solution)/shard_map/ppermute | solution.py:318
  559.5 48.8 %collective-permute-start.62 = (bf16[4,192,2176]{2,1,0:T(8,128)(2,1)}, bf16[4,192,2176]{2,1,0:T(8,128)(2,1)S(1)}, u32[]{:S(2)}, u32[]{:S(2)}) collective-permute-start(bf16[4,192,2176]{2,1,0:T(8,128)(2,1)} %get-tuple-element.70), channel_id=1, source_target_pairs={{0,1},{1,0},{2,3},{3,2},{4,5},{5,4},{6,7},{7,6},{8,9},{9,8},{10,11... | collective-permute-start | bytes 10027016 | tf_op jit(solution)/shard_map/ppermute | solution.py:318
  562.8 43.7 %collective-permute-start.69 = (bf16[2,192,2176]{2,1,0:T(8,128)(2,1)S(1)}, bf16[2,192,2176]{2,1,0:T(8,128)(2,1)S(1)}, u32[]{:S(2)}, u32[]{:S(2)}) collective-permute-start(bf16[2,192,2176]{2,1,0:T(8,128)(2,1)S(1)} %slice.245), channel_id=1, source_target_pairs={{0,4},{1,3},{2,6},{3,1},{4,0},{5,7},{6,2},{7,5},{8,12},{9,11},{10,... | collective-permute-start | bytes 5013512 | tf_op jit(solution)/shard_map/ppermute | solution.py:318
  582.4 50.9 %collective-permute-start.66 = (bf16[2,192,2176]{2,1,0:T(8,128)(2,1)S(1)}, bf16[2,192,2176]{2,1,0:T(8,128)(2,1)S(1)}, u32[]{:S(2)}, u32[]{:S(2)}) collective-permute-start(bf16[2,192,2176]{2,1,0:T(8,128)(2,1)S(1)} %slice.240), channel_id=1, source_target_pairs={{0,4},{1,3},{2,6},{3,1},{4,0},{5,7},{6,2},{7,5},{8,12},{9,11},{10,... | collective-permute-start | bytes 5013512 | tf_op jit(solution)/shard_map/ppermute | solution.py:318
  609.3 50.9 %collective-permute-start.63 = (bf16[2,192,2176]{2,1,0:T(8,128)(2,1)S(1)}, bf16[2,192,2176]{2,1,0:T(8,128)(2,1)S(1)}, u32[]{:S(2)}, u32[]{:S(2)}) collective-permute-start(bf16[2,192,2176]{2,1,0:T(8,128)(2,1)S(1)} %slice.235), channel_id=1, source_target_pairs={{0,4},{1,3},{2,6},{3,1},{4,0},{5,7},{6,2},{7,5},{8,12},{9,11},{10,... | collective-permute-start | bytes 5013512 | tf_op jit(solution)/shard_map/ppermute | solution.py:318
  628.7 33.4 %collective-permute-start.75 = (bf16[192,2176]{1,0:T(8,128)(2,1)S(1)}, bf16[192,2176]{1,0:T(8,128)(2,1)S(1)}, u32[]{:S(2)}, u32[]{:S(2)}) collective-permute-start(bf16[192,2176]{1,0:T(8,128)(2,1)S(1)} %fusion.5), channel_id=1, source_target_pairs={{0,16},{1,17},{2,18},{3,19},{4,20},{5,21},{6,22},{7,23},{8,0},{9,1... | collective-permute-start | bytes 2506760 | tf_op jit(solution)/shard_map/ppermute | solution.py:318
  633.6 28.5 %collective-permute-start.67 = (bf16[192,2176]{1,0:T(8,128)(2,1)S(1)}, bf16[192,2176]{1,0:T(8,128)(2,1)S(1)}, u32[]{:S(2)}, u32[]{:S(2)}) collective-permute-start(bf16[192,2176]{1,0:T(8,128)(2,1)S(1)} %fusion.29), channel_id=1, source_target_pairs={{0,2},{1,5},{2,0},{3,7},{4,6},{5,1},{6,4},{7,3},{8,10},{9,13},{10,... | collective-permute-start | bytes 2506760 | tf_op jit(solution)/shard_map/ppermute | solution.py:318
  738.3 297.2 %reduce-scatter.8.cloned.1.call-start = ((), (), s32[]{:S(2)}) async-start(), calls=%async_computation.6 | async-start | bytes 8650752 | tf_op jit(solution)/shard_map/reduce_scatter | solution.py:702
  744.0 541.7 %reduce-scatter.6.cloned.1.call-start = ((), (), s32[]{:S(2)}) async-start(), calls=%async_computation.5 | async-start | bytes 25952256 | tf_op jit(solution)/shard_map/reduce_scatter | solution.py:701
  761.1 78.6 %collective-permute-start.77 = (bf16[4,192,2048]{2,1,0:T(8,128)(2,1)}, bf16[4,192,2048]{2,1,0:T(8,128)(2,1)S(1)}, u32[]{:S(2)}, u32[]{:S(2)}) collective-permute-start(bf16[4,192,2048]{2,1,0:T(8,128)(2,1)} %get-tuple-element.78), channel_id=1, source_target_pairs={{0,1},{1,0},{2,3},{3,2},{4,5},{5,4},{6,7},{7,6},{8,9},{9,8},{10,11... | collective-permute-start | bytes 9437192 | tf_op jit(solution)/shard_map/ppermute | solution.py:318
  761.1 53.6 %collective-permute-start.80 = (bf16[4,192,2048]{2,1,0:T(8,128)(2,1)}, bf16[4,192,2048]{2,1,0:T(8,128)(2,1)S(1)}, u32[]{:S(2)}, u32[]{:S(2)}) collective-permute-start(bf16[4,192,2048]{2,1,0:T(8,128)(2,1)} %get-tuple-element.80), channel_id=1, source_target_pairs={{0,1},{1,0},{2,3},{3,2},{4,5},{5,4},{6,7},{7,6},{8,9},{9,8},{10,11... | collective-permute-start | bytes 9437192 | tf_op jit(solution)/shard_map/ppermute | solution.py:318
  774.3 44.3 %collective-permute-start.84 = (bf16[2,192,2048]{2,1,0:T(8,128)(2,1)S(1)}, bf16[2,192,2048]{2,1,0:T(8,128)(2,1)}, u32[]{:S(2)}, u32[]{:S(2)}) collective-permute-start(bf16[2,192,2048]{2,1,0:T(8,128)(2,1)S(1)} %slice.267), channel_id=1, source_target_pairs={{0,4},{1,3},{2,6},{3,1},{4,0},{5,7},{6,2},{7,5},{8,12},{9,11},{10,... | collective-permute-start | bytes 4718600 | tf_op jit(solution)/shard_map/ppermute | solution.py:318
  777.6 35.5 %collective-permute-start.87 = (bf16[2,192,2048]{2,1,0:T(8,128)(2,1)S(1)}, bf16[2,192,2048]{2,1,0:T(8,128)(2,1)S(1)}, u32[]{:S(2)}, u32[]{:S(2)}) collective-permute-start(bf16[2,192,2048]{2,1,0:T(8,128)(2,1)S(1)} %slice.272), channel_id=1, source_target_pairs={{0,4},{1,3},{2,6},{3,1},{4,0},{5,7},{6,2},{7,5},{8,12},{9,11},{10,... | collective-permute-start | bytes 4718600 | tf_op jit(solution)/shard_map/ppermute | solution.py:318
  816.4 36.5 %collective-permute-start.81 = (bf16[2,192,2048]{2,1,0:T(8,128)(2,1)S(1)}, bf16[2,192,2048]{2,1,0:T(8,128)(2,1)}, u32[]{:S(2)}, u32[]{:S(2)}) collective-permute-start(bf16[2,192,2048]{2,1,0:T(8,128)(2,1)S(1)} %slice.262), channel_id=1, source_target_pairs={{0,4},{1,3},{2,6},{3,1},{4,0},{5,7},{6,2},{7,5},{8,12},{9,11},{10,... | collective-permute-start | bytes 4718600 | tf_op jit(solution)/shard_map/ppermute | solution.py:318
  820.9 35.5 %collective-permute-start.85 = (bf16[192,2048]{1,0:T(8,128)(2,1)}, bf16[192,2048]{1,0:T(8,128)(2,1)}, u32[]{:S(2)}, u32[]{:S(2)}) collective-permute-start(bf16[192,2048]{1,0:T(8,128)(2,1)} %fusion.34), channel_id=1, source_target_pairs={{0,2},{1,5},{2,0},{3,7},{4,6},{5,1},{6,4},{7,3},{8,10},{9,13},{10,... | collective-permute-start | bytes 2359304 | tf_op jit(solution)/shard_map/ppermute | solution.py:318
  841.6 37.6 %collective-permute-start.78 = (bf16[2,192,2048]{2,1,0:T(8,128)(2,1)S(1)}, bf16[2,192,2048]{2,1,0:T(8,128)(2,1)}, u32[]{:S(2)}, u32[]{:S(2)}) collective-permute-start(bf16[2,192,2048]{2,1,0:T(8,128)(2,1)S(1)} %slice.257), channel_id=1, source_target_pairs={{0,4},{1,3},{2,6},{3,1},{4,0},{5,7},{6,2},{7,5},{8,12},{9,11},{10,... | collective-permute-start | bytes 4718600 | tf_op jit(solution)/shard_map/ppermute | solution.py:318
  (147 other events, 2495.0 us)
Sparse Core Ops, SparseCore 0:
  10.9 179.7 all-gather.4
  193.6 107.9 all-gather.6
  738.4 142.8 reduce-scatter.9
  883.6 151.8 reduce-scatter.7
  1042.9 242.7 reduce-scatter.5

commit v2 on v1

--- a/solution.py
+++ b/solution.py
@@ -312,22 +312,71 @@
         self.first = [(i, i ^ (4 if i & 1 else 2)) for i in range(count)]
         self.second = [(i, i ^ (2 if i & 1 else 4)) for i in range(count)]
         self.core = [(i, i ^ 1) for i in range(count)]
+        self.flip = [[(i, i ^ mask) for i in range(count)] for mask in range(PLANE)]
+        self.masks = ((0, 2, 4, 6, 1, 5, 3, 7), (0, 4, 2, 6, 1, 3, 5, 7))
+        device = lax.axis_index("fsdp")
+        self.device = device
+        self.place, self.plane, self.core_id = device % PLANE, device // PLANE, device % 2
+        spots = jnp.asarray([order.index(i) for i in range(planes)], jnp.int32)
+        self.planes_back = jnp.asarray(order, jnp.int32)[
+            (spots[self.plane] - jnp.arange(planes, dtype=jnp.int32)) % planes
+        ]
+        self.steps_from = (spots[self.plane] - spots) % planes
 
 
 def send(value, pairs):
     return lax.ppermute(value, "fsdp", pairs)
 
 
+def pick(value, index):
+    return lax.dynamic_index_in_dim(value, index, 0, keepdims=False)
+
+
+def spread_plane(moves, block):
+    near = send(block, moves.first)
+    own = [block, near, send(block, moves.second), send(near, moves.second)]
+    return own + [send(item, moves.core) for item in own]
+
+
 def spread(moves, block):
     groups = []
-    current = block
     for step in range(moves.planes):
         if step:
-            current = send(current, moves.ring)
-        near = send(current, moves.first)
-        own = [current, near, send(current, moves.second), send(near, moves.second)]
-        groups.append(own + [send(item, moves.core) for item in own])
+            block = send(block, moves.ring)
+        groups.append(spread_plane(moves, block))
     return groups
+
+
+def round_ring(moves, block):
+    blocks = [block]
+    for _ in range(1, moves.planes):
+        blocks.append(send(blocks[-1], moves.ring))
+    return blocks
+
+
+def trade(moves, pieces):
+    got = [pick(pieces, moves.place)]
+    for mask in range(1, PLANE):
+        got.append(send(pick(pieces, moves.place ^ mask), moves.flip[mask]))
+    return jnp.take(jnp.stack(got), moves.place ^ jnp.arange(PLANE, dtype=jnp.int32), axis=0)
+
+
+def plane_total(moves, parts):
+    even, odd = moves.masks
+    swap = moves.core_id == 0
+    parts = jnp.where(
+        swap,
+        jnp.stack([parts[:, even.index(m)] for m in range(PLANE)], axis=1),
+        jnp.stack([parts[:, odd.index(m)] for m in range(PLANE)], axis=1),
+    )
+    for bit in (1, 2, 4):
+        other = send(parts, moves.flip[bit])
+        parts = parts + jnp.stack([other[:, m ^ bit] for m in range(PLANE)], axis=1)
+    return jnp.where(
+        swap,
+        jnp.stack([parts[:, m] for m in even], axis=1),
+        jnp.stack([parts[:, m] for m in odd], axis=1),
+    )
 
 
 def collect_plane(moves, kept, sent):
@@ -339,11 +388,11 @@
     return home + send(near, moves.first).astype(jnp.float32)
 
 
-def collect_ring(moves, sums):
+def collect_ring(moves, sums, kind=jnp.bfloat16):
     total = sums[1]
     for step in range(2, moves.planes):
-        total = sums[step] + send(total.astype(jnp.bfloat16), moves.ring).astype(jnp.float32)
-    return sums[0] + send(total.astype(jnp.bfloat16), moves.ring).astype(jnp.float32)
+        total = sums[step] + send(total.astype(kind), moves.ring).astype(jnp.float32)
+    return sums[0] + send(total.astype(kind), moves.ring).astype(jnp.float32)
 
 
 def expert_body(per_step, cap, experts, meta, *refs):
@@ -530,6 +579,18 @@
     )(meta, *rows, *grads, weight_in, weight_out, *saved)
 
 
+def turn(pairs, cos_table, sin_table, way):
+    half_dim = HEAD_DIM // 2
+    first, second = pairs[..., :half_dim], pairs[..., half_dim:]
+    sin_table = way * sin_table
+    return jnp.concatenate(
+        [first * cos_table - second * sin_table, second * cos_table + first * sin_table], axis=-1
+    )
+
+
+SMALL = 20
+
+
 def shards_dense(
     tokens,
     cotangent,
@@ -545,47 +606,104 @@
     row_count = tokens.shape[0]
     devices_count = lax.axis_size("fsdp")
     moves = Moves(devices_count)
-    device = lax.axis_index("fsdp")
     experts = devices_count // 2
     choose = routes.shape[1]
     capacity = 4 * row_count * choose // (3 * experts)
     scaling = HEAD_DIM ** (-0.5)
-    bf = jnp.bfloat16
-    gain_full, gathered_in, gathered_out, gathered_router = (
-        lax.all_gather(norm_gains, "fsdp", axis=1, tiled=True),
-        lax.all_gather(attention_in, "fsdp", axis=0, tiled=True),
-        lax.all_gather(attention_out, "fsdp", axis=0, tiled=True),
-        lax.all_gather(router_weight, "fsdp", axis=0, tiled=True),
-    )
-    gain_rows = gain_full.astype(jnp.float32)
+    bf, f32 = jnp.bfloat16, jnp.float32
+    own_rows = attention_in.shape[0]
+    heads = HEADS // PLANE
+    mine = heads * HEAD_DIM
+    columns = HEADS // 4
+    core, column = moves.core_id, moves.place // 2
+
+    small = jnp.concatenate([router_weight, norm_gains.T], axis=1).reshape(-1)
+    riders = jnp.concatenate([small, lengths[0].astype(bf)])
+    riders = jnp.pad(riders, (0, 2 * 3 * mine - riders.shape[0])).reshape(2, 3 * mine)
+    pieces = (
+        attention_in.reshape(own_rows, 3, 2, heads, columns, HEAD_DIM)
+        .transpose(4, 2, 0, 1, 3, 5)
+        .reshape(PLANE, own_rows, 3 * mine)
+    )
+    pieces = jnp.concatenate(
+        [pieces, jnp.broadcast_to(jnp.pad(riders, ((0, 6), (0, 0))), (PLANE, 8, 3 * mine))], axis=1
+    )
+    arrived = trade(moves, pieces)
+    token_blocks = spread_plane(moves, tokens)
+    rider_ring = round_ring(moves, arrived[:, own_rows : own_rows + 2].reshape(2 * PLANE, 3 * mine))
+    in_ring = round_ring(moves, arrived[:, :own_rows].reshape(PLANE * own_rows, 3 * mine))
+    out_ring = round_ring(moves, attention_out)
     grad_groups = spread(moves, cotangent)
 
+    riders_all = jnp.stack(rider_ring).reshape(moves.planes, PLANE, 6 * mine)
+    lengths_plane = riders_all[0, :, small.shape[0] : small.shape[0] + lengths.shape[1]]
+    masks = jnp.where(core == 0, *(jnp.asarray(m, jnp.int32) for m in moves.masks))
+    lengths_all = jnp.take(lengths_plane, moves.place ^ masks, axis=0).astype(jnp.int32)
+    small_all = jnp.take(riders_all[:, :, : small.shape[0]], moves.steps_from, axis=0)
+    small_all = small_all.reshape(D, SMALL).astype(f32)
+    router_full, gain_rows = small_all[:, : SMALL - 4].astype(bf), small_all[:, SMALL - 4 :].T
+
+    def own_heads(full):
+        return full.reshape(2, heads, columns, HEAD_DIM)[core, :, column].reshape(1, mine)
+
+    query_gain, key_gain = own_heads(gain_rows[1]), own_heads(gain_rows[2])
+    in_full = jnp.take(jnp.stack(in_ring), moves.steps_from, axis=0).reshape(D, 3 * mine)
+    out_line = jnp.take(jnp.stack(out_ring), moves.steps_from, axis=0)
+    out_mine = lax.dynamic_slice_in_dim(out_line, heads * core, heads, 0)
+    out_other = send(lax.dynamic_slice_in_dim(out_line, heads * (1 - core), heads, 0), moves.core)
+    out_full = jnp.stack(
+        [jnp.where(core == 0, out_mine, out_other), jnp.where(core == 0, out_other, out_mine)],
+        axis=1,
+    ).reshape(mine, D)
+
     expert_ids = jnp.arange(experts, dtype=jnp.int32)
-    match = jnp.sum((routes[:, :, None] == expert_ids[None, None, :]).astype(jnp.float32), axis=1)
+    match = jnp.sum((routes[:, :, None] == expert_ids[None, None, :]).astype(f32), axis=1)
     places = jnp.arange(row_count, dtype=jnp.int32)
     before = (places[:, None] > places[None, :]).astype(bf)
     rank = jnp.where(match > 0, product(before, match.astype(bf)), -1.0).astype(bf)
 
-    segment, position = layout(lengths[0], row_count)
-    cos_table, sin_table = tables(position)
-    allowed = ((segment[:, None] == segment[None, :]) & (places[:, None] >= places[None, :]))[None]
-    inputs = tokens.astype(jnp.float32)
-    normed_input = root_norm(inputs, gain_rows[0]).astype(bf)
-    projected = product(normed_input, gathered_in)
-
-    def prepare_local(projected_value, query_gain, key_gain):
-        return prepare(projected_value, query_gain, key_gain, cos_table, sin_table)
-
-    (query_f, key_f, value_f), prepare_back = jax.vjp(
-        prepare_local, projected, gain_rows[1], gain_rows[2]
-    )
-    query_heads = query_f.astype(bf)
-    key_heads = key_f.astype(bf)
-    value_heads = value_f.astype(bf)
+    segment, position = jax.vmap(lambda item: layout(item, row_count))(lengths_all)
+    cos_table, sin_table = tables(position.reshape(-1))
+    allowed = (segment[:, :, None] == segment[:, None, :]) & (
+        places[:, None] >= places[None, :]
+    )[None]
+    allowed = allowed[:, None]
+    token_all = jnp.concatenate(token_blocks, axis=0).astype(f32)
+    normed_all = root_norm(token_all, gain_rows[0][None]).astype(bf)
+    projected = sum(
+        product(
+            lax.dynamic_slice_in_dim(
+                normed_all, moves.planes_back[step] * PLANE * own_rows, PLANE * own_rows, 1
+            ),
+            in_ring[step],
+        )
+        for step in range(moves.planes)
+    )
+    query_raw, key_raw, value_raw = (projected[:, i * mine : (i + 1) * mine] for i in range(3))
+
+    def by_block(value):
+        return value.reshape(PLANE, row_count, heads, HEAD_DIM)
+
+    def row_totals(first, second):
+        sums = jnp.stack([jnp.sum(first, axis=1), jnp.sum(second, axis=1)])
+        sums = plane_total(moves, sums.reshape(2, PLANE, row_count)).reshape(2, -1, 1)
+        return sums[0], sums[1]
+
+    query_sum, key_sum = row_totals(query_raw * query_raw, key_raw * key_raw)
+    query_root = lax.rsqrt(query_sum / D + EPSILON)
+    key_root = lax.rsqrt(key_sum / D + EPSILON)
+
+    def turned(raw, root, gain, way=1.0):
+        value = (raw * root * gain).reshape(-1, heads, HEAD_DIM)
+        return turn(value, cos_table, sin_table, way)
+
+    query_heads = by_block(turned(query_raw, query_root, query_gain).astype(bf))
+    key_heads = by_block(turned(key_raw, key_root, key_gain).astype(bf))
+    value_heads = by_block(value_raw.astype(bf))
 
     def score_block():
         raw_scores = (
-            jnp.einsum("qhd,khd->hqk", query_heads, key_heads, preferred_element_type=jnp.float32)
+            jnp.einsum("bqhd,bkhd->bhqk", query_heads, key_heads, preferred_element_type=f32)
             * scaling
         )
         return jnp.where(allowed, raw_scores, MASKED)
@@ -597,14 +715,19 @@
     log_total = row_max + jnp.log(row_sum)
     attend_probs = (exponent / row_sum).astype(bf)
     attended = (
-        jnp.einsum("hqk,khd->qhd", attend_probs, value_heads, preferred_element_type=jnp.float32)
-        .reshape(row_count, D)
+        jnp.einsum("bhqk,bkhd->bqhd", attend_probs, value_heads, preferred_element_type=f32)
+        .reshape(-1, mine)
         .astype(bf)
     )
-    branch_out = product(attended, gathered_out)
-    residual = inputs + branch_out
-    normed = root_norm(residual, gain_rows[3]).astype(bf)
-    logits = product(normed, gathered_router)
+
+    def home(partial):
+        partial = partial.astype(bf).reshape(PLANE, row_count, D)
+        return collect_plane(moves, partial[: PLANE // 2], partial[PLANE // 2 :])
+
+    inputs = tokens.astype(f32)
+    residual = inputs + home(product(attended, out_full))
+    normed = root_norm(residual, gain_rows[3][None]).astype(bf)
+    logits = product(normed, router_full)
     router_probs = softmax_rows(logits)
     gate_total = jnp.sum(router_probs * match, axis=1, keepdims=True)
     gate_values = router_probs * match / gate_total
@@ -620,7 +743,7 @@
     )
     row_groups = spread(moves, jnp.concatenate([normed, extra], axis=1))
 
-    meta = jnp.stack([device // 2, device]).astype(jnp.int32)
+    meta = jnp.stack([moves.device // 2, moves.device]).astype(jnp.int32)
     saved, out_parts, row_parts = None, [], []
     for index in range(moves.planes):
         *saved, out_keep, out_send, row_keep, row_send = expert_group(
@@ -642,11 +765,9 @@
     expert_in_grad = dot_first(x_rows, du_rows)
     expert_out_grad = dot_first(m_rows, dy_rows)
 
-    upstream = cotangent.astype(jnp.float32)
+    upstream = cotangent.astype(f32)
     dispatch_grad = row_total[:, :D]
-    gate_grad = jnp.sum(
-        row_total[:, D : D + 4 * experts].reshape(row_count, experts, 4), axis=2
-    )
+    gate_grad = jnp.sum(row_total[:, D : D + 4 * experts].reshape(row_count, experts, 4), axis=2)
     chosen_grad = (
         match * (gate_grad - jnp.sum(gate_grad * gate_values, axis=1, keepdims=True)) / gate_total
     )
@@ -654,60 +775,119 @@
         router_probs * (chosen_grad - jnp.sum(chosen_grad * router_probs, axis=1, keepdims=True))
     ).astype(bf)
     router_grad = dot_first(normed, logit_grad)
-    normed_grad = dispatch_grad + dot_last(logit_grad, gathered_router)
+    normed_grad = dispatch_grad + dot_last(logit_grad, router_full)
     _, second_back = jax.vjp(root_norm, residual, gain_rows[3])
     residual_norm_grad, second_gain_grad = second_back(normed_grad)
     residual_grad = upstream + residual_norm_grad
-    branch_grad = residual_grad.astype(bf)
-
-    out_parts, branch_grad = lax.optimization_barrier((out_parts, branch_grad))
+    branch_all = jnp.concatenate(spread_plane(moves, residual_grad.astype(bf)), axis=0)
+
+    out_parts, branch_all = lax.optimization_barrier((out_parts, branch_all))
     out_total = collect_ring(moves, [collect_plane(moves, *part) for part in out_parts])
     output = (residual + out_total).astype(bf)
 
-    out_grad = dot_first(attended, branch_grad)
-    attended_grad = (
-        dot_last(branch_grad, gathered_out).astype(bf).reshape(row_count, HEADS, HEAD_DIM)
-    )
+    out_grad = dot_first(attended, branch_all).astype(bf).reshape(heads, 2, own_rows, D)
+    out_grad_mine = jnp.where(core == 0, out_grad[:, 0], out_grad[:, 1])
+    out_grad_other = send(jnp.where(core == 0, out_grad[:, 1], out_grad[:, 0]), moves.core)
+    out_grad_line = jnp.where(
+        core == 0,
+        jnp.concatenate([out_grad_mine, out_grad_other]),
+        jnp.concatenate([out_grad_other, out_grad_mine]),
+    )
+    out_share = collect_ring(
+        moves,
+        [pick(out_grad_line, moves.planes_back[k]).astype(f32) for k in range(moves.planes)],
+    )
+
+    attended_grad = by_block(dot_last(branch_all, out_full).astype(bf))
     recomputed = jnp.exp(score_block() - log_total)
     value_grad = jnp.einsum(
-        "hqk,qhd->khd", attend_probs, attended_grad, preferred_element_type=jnp.float32
+        "bhqk,bqhd->bkhd", attend_probs, attended_grad, preferred_element_type=f32
     )
     attend_grad = jnp.einsum(
-        "qhd,khd->hqk", attended_grad, value_heads, preferred_element_type=jnp.float32
+        "bqhd,bkhd->bhqk", attended_grad, value_heads, preferred_element_type=f32
     )
     row_delta = jnp.sum(recomputed * attend_grad, axis=-1, keepdims=True)
     score_grad = (recomputed * (attend_grad - row_delta)).astype(bf)
     query_grad = (
-        jnp.einsum("hqk,khd->qhd", score_grad, key_heads, preferred_element_type=jnp.float32)
+        jnp.einsum("bhqk,bkhd->bqhd", score_grad, key_heads, preferred_element_type=f32) * scaling
+    )
+    key_grad = (
+        jnp.einsum("bhqk,bqhd->bkhd", score_grad, query_heads, preferred_element_type=f32)
         * scaling
     )
-    key_grad = (
-        jnp.einsum("hqk,qhd->khd", score_grad, query_heads, preferred_element_type=jnp.float32)
-        * scaling
-    )
-    projected_grad, query_gain_grad, key_gain_grad = prepare_back(
-        (query_grad, key_grad, value_grad)
-    )
-    projected_grad = projected_grad.astype(bf)
-    attention_in_grad = dot_first(normed_input, projected_grad)
-    normed_input_grad = dot_last(projected_grad, gathered_in)
+
+    def back_turned(value):
+        value = value.reshape(-1, heads, HEAD_DIM)
+        return turn(value, cos_table, sin_table, -1.0).reshape(-1, mine)
+
+    query_grad, key_grad = back_turned(query_grad), back_turned(key_grad)
+    query_dot, key_dot = row_totals(
+        query_grad * query_gain * query_raw, key_grad * key_gain * key_raw
+    )
+
+    def norm_back(grad, raw, root, gain, dots):
+        return root * gain * grad - raw * (root * root * root * dots / D)
+
+    projected_grad = jnp.concatenate(
+        [
+            norm_back(query_grad, query_raw, query_root, query_gain, query_dot),
+            norm_back(key_grad, key_raw, key_root, key_gain, key_dot),
+            value_grad.reshape(-1, mine),
+        ],
+        axis=1,
+    ).astype(bf)
+    in_grad = dot_first(normed_all, projected_grad).astype(bf)
+    in_sum = collect_ring(
+        moves,
+        [
+            lax.dynamic_slice_in_dim(
+                in_grad, moves.planes_back[k] * PLANE * own_rows, PLANE * own_rows, 0
+            ).astype(f32)
+            for k in range(moves.planes)
+        ],
+    )
+    in_share = (
+        trade(moves, in_sum.astype(bf).reshape(PLANE, own_rows, 3 * mine))
+        .reshape(columns, 2, own_rows, 3, heads, HEAD_DIM)
+        .transpose(2, 3, 1, 4, 0, 5)
+        .reshape(own_rows, 3 * D)
+        .astype(f32)
+    )
+    normed_input_grad = home(dot_last(projected_grad, in_full))
     _, first_back = jax.vjp(root_norm, inputs, gain_rows[0])
     input_norm_grad, first_gain_grad = first_back(normed_input_grad)
     input_grad = residual_grad + input_norm_grad
-    gains_grad = jnp.stack([first_gain_grad, query_gain_grad, key_gain_grad, second_gain_grad])
-    small = jnp.concatenate([gains_grad.T, router_grad], axis=1)
-    small_share, in_share, out_share = (
-        lax.psum_scatter(small, "fsdp", scatter_dimension=0, tiled=True),
-        lax.psum_scatter(attention_in_grad.astype(bf), "fsdp", scatter_dimension=0, tiled=True),
-        lax.psum_scatter(out_grad.astype(bf), "fsdp", scatter_dimension=0, tiled=True),
-    )
+
+    def own_gain(grad, raw, root):
+        own = jnp.sum(grad * raw * root, axis=0).reshape(1, heads, 1, HEAD_DIM)
+        here = (jnp.arange(2) == core)[:, None, None, None] & (jnp.arange(columns) == column)[
+            None, None, :, None
+        ]
+        return jnp.where(here, own, 0.0).reshape(D)
+
+    gains_grad = jnp.stack(
+        [
+            first_gain_grad,
+            own_gain(query_grad, query_raw, query_root),
+            own_gain(key_grad, key_raw, key_root),
+            second_gain_grad,
+        ],
+        axis=1,
+    )
+    small_grad = jnp.concatenate([router_grad, gains_grad], axis=1)
+    small_grad = small_grad.reshape(moves.planes, PLANE, own_rows * SMALL)
+    small_sum = collect_ring(
+        moves, [pick(small_grad, moves.planes_back[k]) for k in range(moves.planes)], f32
+    )
+    small_share = jnp.sum(trade(moves, small_sum.reshape(PLANE, -1, WIDE)), axis=0)
+    small_share = small_share.reshape(own_rows, SMALL)
     return (
         output,
         input_grad,
-        small_share[:, :4].T,
-        in_share.astype(jnp.float32),
-        out_share.astype(jnp.float32),
-        small_share[:, 4:],
+        small_share[:, SMALL - 4 :].T,
+        in_share,
+        out_share,
+        small_share[:, : SMALL - 4],
         expert_in_grad[None],
         expert_out_grad[None],
     )
@@ -716,7 +896,7 @@
 def shards(*arguments):
     routes = arguments[8]
     experts = lax.axis_size("fsdp") // 2
-    if 2 * routes.shape[1] >= experts:
+    if 2 * routes.shape[1] >= experts and HEADS == experts:
         return shards_dense(*arguments)
     return shards_routed(*arguments)
 

time: 1300 us -> 1150 us (0.88)
  waiting for transfers between devices: 751 us -> 502 us
  blocking collectives: 99.6 us -> 0 us
  local copies, waits for them, and re-layouts: 31.1 us -> 120 us
  starting transfers between devices: 93 us -> 161 us
  other arithmetic: 67.1 us -> 124 us
  matrix products: 102 us -> 83.4 us
    reduce_scatter x2 -> x0, waiting for transfers between devices: 367 us -> none  [the longest x1 248 us: shards_dense(): lax.psum_scatter(attention_in_grad.astype(bf), 'fsdp', scatter_dimension=...]
    ppermute x92 -> x159, waiting for transfers between devices: 269 us -> 502 us  [send(): return lax.ppermute(value, 'fsdp', pairs)]
    all_gather x2 -> x0, waiting for transfers between devices: 114 us -> none  [the longest x1 69.1 us: shards_dense(): lax.all_gather(attention_in, 'fsdp', axis=0, tiled=True)]
    all_gather x2 -> x0, blocking collectives: 99.6 us -> none  [the longest x1 61.7 us: shards_dense(): lax.all_gather(norm_gains, 'fsdp', axis=1, tiled=True)]
    ppermute x92 -> x159, starting transfers between devices: 92.8 us -> 161 us  [send(): return lax.ppermute(value, 'fsdp', pairs)]
    unnamed x202 -> x325, local copies, waits for them, and re-layouts: 15.7 us -> 50.3 us
    reshape x1 -> x13, local copies, waits for them, and re-layouts: 1.36 us -> 18.1 us  [the longest x3 6.84 us: by_block(): return value.reshape(PLANE, row_count, heads, HEAD_DIM)]
    gather x0 -> x9, local copies, waits for them, and re-layouts: none -> 16 us  [the longest x4 6.72 us: trade(): jnp.take(jnp.stack(got), moves.place ^ jnp.arange(PLANE, dtype=jnp.int32)...]
  transfers between devices with their start and end apart: 97 -> 159, of which waited for: 38 -> 65; matrix products, arithmetic and copies ran while one was open for 10% -> 21% of each run, Pallas kernels for 10% -> 12%
where the time goes in v2:
time: 1150 us; the launch traced here: 1140 us
  waiting for transfers between devices  502 us (44%)
  starting transfers between devices  161 us (14%)
  Pallas kernels  135 us (12%)
  other arithmetic  124 us (11%)
  local copies, waits for them, and re-layouts  120 us (10%)
  matrix products  83.4 us (7%)
  between operations  13.6 us (1%)
    ppermute x159, waiting for transfers between devices, send(): return lax.ppermute(value, 'fsdp', pairs)  502 us
    ppermute x159, starting transfers between devices, send(): return lax.ppermute(value, 'fsdp', pairs)  161 us
    pallas_call x4, Pallas kernels, expert_group(): pl.pallas_call(functools.partial(expert_body, per_step, cap, experts), gr...  135 us
    dot_general x5, matrix products, dot_first(): lax.dot_general(left, right, (((0,), (0,)), ((), ())), preferred_element_...  51.6 us
    unnamed x325, local copies, waits for them, and re-layouts  50.3 us
    convert_element_type x10, other arithmetic, collect_plane(): kept = kept.astype(jnp.bfloat16)  29.6 us
  transfers between devices with their start and end apart: 159, of which 65 were waited for; matrix products, arithmetic and copies ran while one was open for 21% of the time, Pallas kernels for 12%

profile of v2, /device:TPU:0, one launch (start us, length us, event | category | flops | bytes accessed | tf_op | source)
XLA Modules:
  0.0 1139.6 jit_solution(15414937500377904460)
XLA Ops:
  22.5 4.9 collective-permute-done.8
  27.4 5.2 collective-permute-done.9
  48.8 5.0 collective-permute-done.13
  75.6 18.0 %collective-permute-done.24 = bf16[64,2048]{1,0:T(8,128)(2,1)S(1)} collective-permute-done((bf16[64,2048]{1,0:T(8,128)(2,1)S(1)}, bf16[64,2048]{1,0:T(8,128)(2,1)S(1)}, u32[]{:S(2)}, u32[]{:S(2)}) %collective-permute-start.24) | collective-permute-done | bytes 262176 | tf_op jit(solution)/shard_map/ppermute | solution.py:328
  121.6 10.1 collective-permute-done.18
  203.0 14.2 %collective-permute-done.38.refs_10_ = bf16[192,2048]{1,0:T(8,128)(2,1)S(1)} collective-permute-done((bf16[192,2048]{1,0:T(8,128)(2,1)S(1)}, bf16[192,2048]{1,0:T(8,128)(2,1)S(1)}, u32[]{:S(2)}, u32[]{:S(2)}) %collective-permute-start.38) | collective-permute-done | bytes 786464 | tf_op jit(solution)/shard_map/ppermute | solution.py:328
  225.9 21.8 %collective-permute-done.39.refs_11_ = bf16[192,2048]{1,0:T(8,128)(2,1)S(1)} collective-permute-done((bf16[192,2048]{1,0:T(8,128)(2,1)S(1)}, bf16[192,2048]{1,0:T(8,128)(2,1)S(1)}, u32[]{:S(2)}, u32[]{:S(2)}) %collective-permute-start.39) | collective-permute-done | bytes 786464 | tf_op jit(solution)/shard_map/ppermute | solution.py:328
  253.7 8.7 collective-permute-done.54.refs_10_
  271.8 9.6 collective-permute-done.70.refs_10_
  285.7 14.1 %collective-permute-done.29 = bf16[192,2048]{1,0:T(8,128)(2,1)} collective-permute-done((bf16[192,2048]{1,0:T(8,128)(2,1)}, bf16[192,2048]{1,0:T(8,128)(2,1)}, u32[]{:S(2)}, u32[]{:S(2)}) %collective-permute-start.29) | collective-permute-done | bytes 786464 | tf_op jit(solution)/shard_map/ppermute | solution.py:328
  304.2 12.4 %collective-permute-done.86.refs_10_ = bf16[192,2048]{1,0:T(8,128)(2,1)} collective-permute-done((bf16[192,2048]{1,0:T(8,128)(2,1)}, bf16[192,2048]{1,0:T(8,128)(2,1)}, u32[]{:S(2)}, u32[]{:S(2)}) %collective-permute-start.86) | collective-permute-done | bytes 786464 | tf_op jit(solution)/shard_map/ppermute | solution.py:328
  325.6 7.8 collective-permute-done.87.refs_11_
  336.2 5.3 collective-permute-done.44.refs_0_
  346.8 8.2 collective-permute-done.31.refs_2_
  356.6 5.1 collective-permute-done.60.refs_0_
  364.6 7.8 collective-permute-done.46.refs_2_
  384.2 6.3 collective-permute-done.76.refs_0_
  391.7 8.4 collective-permute-done.62.refs_2_
  401.4 13.0 %collective-permute-done.47.refs_3_ = bf16[192,2176]{1,0:T(8,128)(2,1)} collective-permute-done((bf16[192,2176]{1,0:T(8,128)(2,1)}, bf16[192,2176]{1,0:T(8,128)(2,1)}, u32[]{:S(2)}, u32[]{:S(2)}) %collective-permute-start.47) | collective-permute-done | bytes 835616 | tf_op jit(solution)/shard_map/ppermute | solution.py:328
  416.4 33.6 %expert_group.4 = (bf16[4096,2048]{1,0:T(8,128)(2,1)}, bf16[4096,2048]{1,0:T(8,128)(2,1)}, bf16[4096,512]{1,0:T(8,128)(2,1)}, bf16[4096,1024]{1,0:T(8,128)(2,1)}...) custom-call(s32[2]{0:T(128)} %pad_add_fusion.meta, ...), custom_call_target="tpu_custom_call" | custom-call | flops 16000000000 | bytes 62914560 | tf_op jit(solution)/shard_map/expert_group/pallas_call | solution.py:538
  452.6 33.9 %expert_group.5 = (bf16[4096,2048]{1,0:T(8,128)(2,1)}, bf16[4096,2048]{1,0:T(8,128)(2,1)}, bf16[4096,512]{1,0:T(8,128)(2,1)}, bf16[4096,1024]{1,0:T(8,128)(2,1)}...) custom-call(s32[2]{0:T(128)} %pad_add_fusion.meta, ...), custom_call_target="tpu_custom_call", output_to_operand_aliasing={{0}: (19, {}), {1}: (20, {}), {2}: (21, {}), {3}: (22, {})} | custom-call | flops 16000000000 | bytes 62914560 | tf_op jit(solution)/shard_map/expert_group/pallas_call | solution.py:538
  488.1 33.9 %expert_group.6 = (bf16[4096,2048]{1,0:T(8,128)(2,1)}, bf16[4096,2048]{1,0:T(8,128)(2,1)}, bf16[4096,512]{1,0:T(8,128)(2,1)}, bf16[4096,1024]{1,0:T(8,128)(2,1)}...) custom-call(s32[2]{0:T(128)} %pad_add_fusion.meta, ...), custom_call_target="tpu_custom_call", output_to_operand_aliasing={{0}: (19, {}), {1}: (20, {}), {2}: (21, {}), {3}: (22, {})} | custom-call | flops 16000000000 | bytes 62914560 | tf_op jit(solution)/shard_map/expert_group/pallas_call | solution.py:538
  523.2 34.1 %expert_group.7 = (bf16[4096,2048]{1,0:T(8,128)(2,1)}, bf16[4096,2048]{1,0:T(8,128)(2,1)}, bf16[4096,512]{1,0:T(8,128)(2,1)}, bf16[4096,1024]{1,0:T(8,128)(2,1)}...) custom-call(s32[2]{0:T(128)} %pad_add_fusion.meta, ...), custom_call_target="tpu_custom_call", output_to_operand_aliasing={{0}: (19, {}), {1}: (20, {}), {2}: (21, {}), {3}: (22, {})} | custom-call | flops 16000000000 | bytes 62914560 | tf_op jit(solution)/shard_map/expert_group/pallas_call | solution.py:538
  579.4 6.9 collective-permute-done.102
  592.6 16.7 %collective-permute-done.103 = bf16[192,2176]{1,0:T(8,128)(2,1)S(1)} collective-permute-done((bf16[192,2176]{1,0:T(8,128)(2,1)S(1)}, bf16[192,2176]{1,0:T(8,128)(2,1)S(1)}, u32[]{:S(2)}, u32[]{:S(2)}) %collective-permute-start.103) | collective-permute-done | bytes 835616 | tf_op jit(solution)/shard_map/ppermute | solution.py:328
  618.9 12.0 %collective-permute-done.104 = bf16[192,2176]{1,0:T(8,128)(2,1)S(1)} collective-permute-done((bf16[192,2176]{1,0:T(8,128)(2,1)S(1)}, bf16[192,2176]{1,0:T(8,128)(2,1)S(1)}, u32[]{:S(2)}, u32[]{:S(2)}) %collective-permute-start.104) | collective-permute-done | bytes 835616 | tf_op jit(solution)/shard_map/ppermute | solution.py:328
  630.9 5.4 collective-permute-done.100
  650.0 16.9 %collective-permute-done.93 = bf16[2,192,2176]{2,1,0:T(8,128)(2,1)} collective-permute-done((bf16[2,192,2176]{2,1,0:T(8,128)(2,1)}, bf16[2,192,2176]{2,1,0:T(8,128)(2,1)}, u32[]{:S(2)}, u32[]{:S(2)}) %collective-permute-start.93) | collective-permute-done | bytes 1671200 | tf_op jit(solution)/shard_map/ppermute | solution.py:328
  681.1 11.4 collective-permute-done.106
  700.9 24.2 %convolution_bitcast_fusion = f32[1,2048,1024]{2,1,0:T(8,128)} fusion(bf16[4096,2048]{1,0:T(8,128)(2,1)} %get-tuple-element.86, bf16[4096,1024]{1,0:T(8,128)(2,1)} %get-tuple-element.87), kind=kOutput, calls=%fused_computation.28 | convolution fusion | flops 17179869184 | bytes 33554432 | tf_op jit(solution)/shard_map/dot_general | solution.py:71
  727.2 10.4 convolution_bitcast_fusion.1
  740.5 5.2 collective-permute-done.109
  750.9 5.7 convolution_convert_fusion.4
  782.2 5.8 convolution_convert_fusion.3
  806.0 10.1 convolution_convert_fusion.2
  823.5 14.1 %collective-permute-done.145 = bf16[512,768]{1,0:T(8,128)(2,1)S(1)} collective-permute-done((bf16[512,768]{1,0:T(8,128)(2,1)S(1)}, bf16[512,768]{1,0:T(8,128)(2,1)S(1)}, u32[]{:S(2)}, u32[]{:S(2)}) %collective-permute-start.145) | collective-permute-done | bytes 786464 | tf_op jit(solution)/shard_map/ppermute | solution.py:328
  841.2 5.4 convolution_convert_fusion
  846.8 13.2 %collective-permute-done.146 = bf16[512,768]{1,0:T(8,128)(2,1)S(1)} collective-permute-done((bf16[512,768]{1,0:T(8,128)(2,1)S(1)}, bf16[512,768]{1,0:T(8,128)(2,1)S(1)}, u32[]{:S(2)}, u32[]{:S(2)}) %collective-permute-start.146) | collective-permute-done | bytes 786464 | tf_op jit(solution)/shard_map/ppermute | solution.py:328
  866.3 15.8 %collective-permute-done.147 = bf16[512,768]{1,0:T(8,128)(2,1)S(1)} collective-permute-done((bf16[512,768]{1,0:T(8,128)(2,1)S(1)}, bf16[512,768]{1,0:T(8,128)(2,1)S(1)}, u32[]{:S(2)}, u32[]{:S(2)}) %collective-permute-start.147) | collective-permute-done | bytes 786464 | tf_op jit(solution)/shard_map/ppermute | solution.py:328
  886.4 4.5 collective-permute-done.158
  917.0 4.6 collective-permute-done.154
  965.7 34.9 %collective-permute-done.133 = bf16[2,192,2048]{2,1,0:T(8,128)(2,1)S(1)} collective-permute-done((bf16[2,192,2048]{2,1,0:T(8,128)(2,1)S(1)}, bf16[2,192,2048]{2,1,0:T(8,128)(2,1)S(1)}, u32[]{:S(2)}, u32[]{:S(2)}) %collective-permute-start.133) | collective-permute-done | bytes 1572896 | tf_op jit(solution)/shard_map/ppermute | solution.py:328
  1004.4 27.2 %collective-permute-done.124 = bf16[2,192,2048]{2,1,0:T(8,128)(2,1)S(1)} collective-permute-done((bf16[2,192,2048]{2,1,0:T(8,128)(2,1)S(1)}, bf16[2,192,2048]{2,1,0:T(8,128)(2,1)S(1)}, u32[]{:S(2)}, u32[]{:S(2)}) %collective-permute-start.124) | collective-permute-done | bytes 1572896 | tf_op jit(solution)/shard_map/ppermute | solution.py:328
  1042.0 17.7 %collective-permute-done.121 = bf16[2,192,2048]{2,1,0:T(8,128)(2,1)} collective-permute-done((bf16[2,192,2048]{2,1,0:T(8,128)(2,1)}, bf16[2,192,2048]{2,1,0:T(8,128)(2,1)}, u32[]{:S(2)}, u32[]{:S(2)}) %collective-permute-start.121) | collective-permute-done | bytes 1572896 | tf_op jit(solution)/shard_map/ppermute | solution.py:328
  1070.7 16.2 %collective-permute-done.137 = f32[8,1280]{1,0:T(8,128)S(1)} collective-permute-done((f32[8,1280]{1,0:T(8,128)S(1)}, f32[8,1280]{1,0:T(8,128)S(1)}, u32[]{:S(2)}, u32[]{:S(2)}) %collective-permute-start.137) | collective-permute-done | bytes 40992 | tf_op jit(solution)/shard_map/ppermute | solution.py:328
  1098.4 14.1 %collective-permute-done.127 = bf16[192,2048]{1,0:T(8,128)(2,1)S(1)} collective-permute-done((bf16[192,2048]{1,0:T(8,128)(2,1)S(1)}, bf16[192,2048]{1,0:T(8,128)(2,1)S(1)}, u32[]{:S(2)}, u32[]{:S(2)}) %collective-permute-start.127) | collective-permute-done | bytes 786464 | tf_op jit(solution)/shard_map/ppermute | solution.py:328
  1119.6 14.9 %collective-permute-done.128 = bf16[192,2048]{1,0:T(8,128)(2,1)} collective-permute-done((bf16[192,2048]{1,0:T(8,128)(2,1)}, bf16[192,2048]{1,0:T(8,128)(2,1)}, u32[]{:S(2)}, u32[]{:S(2)}) %collective-permute-start.128) | collective-permute-done | bytes 786464 | tf_op jit(solution)/shard_map/ppermute | solution.py:328
  1134.5 4.9 fusion.13
  (864 shorter events, 486.7 us)
Async XLA Ops:
  0.6 106.6 %collective-permute-start.1 = (bf16[192,2048]{1,0:T(8,128)(2,1)}, bf16[192,2048]{1,0:T(8,128)(2,1)}, u32[]{:S(2)}, u32[]{:S(2)}) collective-permute-start(bf16[192,2048]{1,0:T(8,128)(2,1)} %param.14), channel_id=1, source_target_pairs={{0,4},{1,3},{2,6},{3,1},{4,0},{5,7},{6,2},{7,5},{8,12},{9,11},{10,... | collective-permute-start | bytes 2359304 | tf_op jit(solution)/shard_map/ppermute | solution.py:328
  3.7 100.3 %collective-permute-start = (bf16[192,2048]{1,0:T(8,128)(2,1)}, bf16[192,2048]{1,0:T(8,128)(2,1)}, u32[]{:S(2)}, u32[]{:S(2)}) collective-permute-start(bf16[192,2048]{1,0:T(8,128)(2,1)} %param.14), channel_id=1, source_target_pairs={{0,2},{1,5},{2,0},{3,7},{4,6},{5,1},{6,4},{7,3},{8,10},{9,13},{10,... | collective-permute-start | bytes 2359304 | tf_op jit(solution)/shard_map/ppermute | solution.py:328
  5.2 111.9 %collective-permute-start.3 = (bf16[192,2048]{1,0:T(8,128)(2,1)}, bf16[192,2048]{1,0:T(8,128)(2,1)}, u32[]{:S(2)}, u32[]{:S(2)}) collective-permute-start(bf16[192,2048]{1,0:T(8,128)(2,1)} %param.14), channel_id=1, source_target_pairs={{0,1},{1,0},{2,3},{3,2},{4,5},{5,4},{6,7},{7,6},{8,9},{9,8},{10,11... | collective-permute-start | bytes 2359304 | tf_op jit(solution)/shard_map/ppermute | solution.py:328
  5.2 68.3 %collective-permute-start.23 = (bf16[64,2048]{1,0:T(8,128)(2,1)}, bf16[64,2048]{1,0:T(8,128)(2,1)S(1)}, u32[]{:S(2)}, u32[]{:S(2)}) collective-permute-start(bf16[64,2048]{1,0:T(8,128)(2,1)} %param.18), channel_id=1, source_target_pairs={{0,16},{1,17},{2,18},{3,19},{4,20},{5,21},{6,22},{7,23},{8,0},{9,1... | collective-permute-start | bytes 786440 | tf_op jit(solution)/shard_map/ppermute | solution.py:328
  70.6 41.3 %collective-permute-start.17 = (bf16[512,768]{1,0:T(8,128)(2,1)S(1)}, bf16[512,768]{1,0:T(8,128)(2,1)}, u32[]{:S(2)}, u32[]{:S(2)}) collective-permute-start(bf16[512,768]{1,0:T(8,128)(2,1)S(1)} %bitcast.388), channel_id=1, source_target_pairs={{0,16},{1,17},{2,18},{3,19},{4,20},{5,21},{6,22},{7,23},{8,0},{9,1... | collective-permute-start | bytes 2359304 | tf_op jit(solution)/shard_map/ppermute | solution.py:328
  117.1 41.1 %collective-permute-start.26 = (bf16[2,64,2048]{2,1,0:T(8,128)(2,1)S(1)}, bf16[2,64,2048]{2,1,0:T(8,128)(2,1)}, u32[]{:S(2)}, u32[]{:S(2)}) collective-permute-start(bf16[2,64,2048]{2,1,0:T(8,128)(2,1)S(1)} %constant_dynamic-slice_fusion.9), channel_id=1, source_target_pairs={{0,1},{1,0},{2,3},{3,2},{4,5},{5,4},{6,7},{7,6},{8,9},{9,8},{10,11... | collective-permute-start | bytes 1572872 | tf_op jit(solution)/shard_map/ppermute | solution.py:328
  218.8 33.5 %collective-permute-start.28 = (bf16[2,192,2048]{2,1,0:T(8,128)(2,1)S(1)}, bf16[2,192,2048]{2,1,0:T(8,128)(2,1)S(1)}, u32[]{:S(2)}, u32[]{:S(2)}) collective-permute-start(bf16[2,192,2048]{2,1,0:T(8,128)(2,1)S(1)} %slice.759), channel_id=1, source_target_pairs={{0,4},{1,3},{2,6},{3,1},{4,0},{5,7},{6,2},{7,5},{8,12},{9,11},{10,... | collective-permute-start | bytes 4718600 | tf_op jit(solution)/shard_map/ppermute | solution.py:328
  225.2 37.1 %collective-permute-start.54 = (bf16[192,2048]{1,0:T(8,128)(2,1)S(1)}, bf16[192,2048]{1,0:T(8,128)(2,1)}, u32[]{:S(2)}, u32[]{:S(2)}) collective-permute-start(bf16[192,2048]{1,0:T(8,128)(2,1)S(1)} %collective-permute-done.52.refs_8_), channel_id=1, source_target_pairs={{0,4},{1,3},{2,6},{3,1},{4,0},{5,7},{6,2},{7,5},{8,12},{9,11},{10,... | collective-permute-start | bytes 2359304 | tf_op jit(solution)/shard_map/ppermute | solution.py:328
  269.7 30.1 %collective-permute-start.29 = (bf16[192,2048]{1,0:T(8,128)(2,1)}, bf16[192,2048]{1,0:T(8,128)(2,1)}, u32[]{:S(2)}, u32[]{:S(2)}) collective-permute-start(bf16[192,2048]{1,0:T(8,128)(2,1)} %fusion.52), channel_id=1, source_target_pairs={{0,2},{1,5},{2,0},{3,7},{4,6},{5,1},{6,4},{7,3},{8,10},{9,13},{10,... | collective-permute-start | bytes 2359304 | tf_op jit(solution)/shard_map/ppermute | solution.py:328
  283.0 33.6 %collective-permute-start.86 = (bf16[192,2048]{1,0:T(8,128)(2,1)}, bf16[192,2048]{1,0:T(8,128)(2,1)}, u32[]{:S(2)}, u32[]{:S(2)}) collective-permute-start(bf16[192,2048]{1,0:T(8,128)(2,1)} %collective-permute-done.84.refs_8_), channel_id=1, source_target_pairs={{0,4},{1,3},{2,6},{3,1},{4,0},{5,7},{6,2},{7,5},{8,12},{9,11},{10,... | collective-permute-start | bytes 2359304 | tf_op jit(solution)/shard_map/ppermute | solution.py:328
  284.3 32.3 %collective-permute-start.85 = (bf16[192,2048]{1,0:T(8,128)(2,1)}, bf16[192,2048]{1,0:T(8,128)(2,1)}, u32[]{:S(2)}, u32[]{:S(2)}) collective-permute-start(bf16[192,2048]{1,0:T(8,128)(2,1)} %collective-permute-done.84.refs_8_), channel_id=1, source_target_pairs={{0,2},{1,5},{2,0},{3,7},{4,6},{5,1},{6,4},{7,3},{8,10},{9,13},{10,... | collective-permute-start | bytes 2359304 | tf_op jit(solution)/shard_map/ppermute | solution.py:328
  383.3 31.2 %collective-permute-start.47 = (bf16[192,2176]{1,0:T(8,128)(2,1)}, bf16[192,2176]{1,0:T(8,128)(2,1)}, u32[]{:S(2)}, u32[]{:S(2)}) collective-permute-start(bf16[192,2176]{1,0:T(8,128)(2,1)} %collective-permute-done.45.refs_1_), channel_id=1, source_target_pairs={{0,4},{1,3},{2,6},{3,1},{4,0},{5,7},{6,2},{7,5},{8,12},{9,11},{10,... | collective-permute-start | bytes 2506760 | tf_op jit(solution)/shard_map/ppermute | solution.py:328
  391.2 59.6 %collective-permute-start.49 = (bf16[192,2176]{1,0:T(8,128)(2,1)}, bf16[192,2176]{1,0:T(8,128)(2,1)}, u32[]{:S(2)}, u32[]{:S(2)}) collective-permute-start(bf16[192,2176]{1,0:T(8,128)(2,1)} %collective-permute-done.45.refs_1_), channel_id=1, source_target_pairs={{0,1},{1,0},{2,3},{3,2},{4,5},{5,4},{6,7},{7,6},{8,9},{9,8},{10,11... | collective-permute-start | bytes 2506760 | tf_op jit(solution)/shard_map/ppermute | solution.py:328
  400.1 50.0 %collective-permute-start.50 = (bf16[192,2176]{1,0:T(8,128)(2,1)}, bf16[192,2176]{1,0:T(8,128)(2,1)}, u32[]{:S(2)}, u32[]{:S(2)}) collective-permute-start(bf16[192,2176]{1,0:T(8,128)(2,1)} %copy-done.74), channel_id=1, source_target_pairs={{0,1},{1,0},{2,3},{3,2},{4,5},{5,4},{6,7},{7,6},{8,9},{9,8},{10,11... | collective-permute-start | bytes 2506760 | tf_op jit(solution)/shard_map/ppermute | solution.py:328
  400.1 51.5 %collective-permute-start.77 = (bf16[192,2176]{1,0:T(8,128)(2,1)}, bf16[192,2176]{1,0:T(8,128)(2,1)S(1)}, u32[]{:S(2)}, u32[]{:S(2)}) collective-permute-start(bf16[192,2176]{1,0:T(8,128)(2,1)} %collective-permute-done.76.refs_0_), channel_id=1, source_target_pairs={{0,2},{1,5},{2,0},{3,7},{4,6},{5,1},{6,4},{7,3},{8,10},{9,13},{10,... | collective-permute-start | bytes 2506760 | tf_op jit(solution)/shard_map/ppermute | solution.py:328
  414.5 37.2 %collective-permute-start.63 = (bf16[192,2176]{1,0:T(8,128)(2,1)}, bf16[192,2176]{1,0:T(8,128)(2,1)S(1)}, u32[]{:S(2)}, u32[]{:S(2)}) collective-permute-start(bf16[192,2176]{1,0:T(8,128)(2,1)} %collective-permute-done.61.refs_1_), channel_id=1, source_target_pairs={{0,4},{1,3},{2,6},{3,1},{4,0},{5,7},{6,2},{7,5},{8,12},{9,11},{10,... | collective-permute-start | bytes 2506760 | tf_op jit(solution)/shard_map/ppermute | solution.py:328
  415.8 36.8 %collective-permute-start.51 = (bf16[192,2176]{1,0:T(8,128)(2,1)}, bf16[192,2176]{1,0:T(8,128)(2,1)}, u32[]{:S(2)}, u32[]{:S(2)}) collective-permute-start(bf16[192,2176]{1,0:T(8,128)(2,1)} %collective-permute-done.47.refs_3_), channel_id=1, source_target_pairs={{0,1},{1,0},{2,3},{3,2},{4,5},{5,4},{6,7},{7,6},{8,9},{9,8},{10,11... | collective-permute-start | bytes 2506760 | tf_op jit(solution)/shard_map/ppermute | solution.py:328
  450.0 36.5 %collective-permute-start.78 = (bf16[192,2176]{1,0:T(8,128)(2,1)}, bf16[192,2176]{1,0:T(8,128)(2,1)S(1)}, u32[]{:S(2)}, u32[]{:S(2)}) collective-permute-start(bf16[192,2176]{1,0:T(8,128)(2,1)} %collective-permute-done.76.refs_0_), channel_id=1, source_target_pairs={{0,4},{1,3},{2,6},{3,1},{4,0},{5,7},{6,2},{7,5},{8,12},{9,11},{10,... | collective-permute-start | bytes 2506760 | tf_op jit(solution)/shard_map/ppermute | solution.py:328
  450.8 36.4 %collective-permute-start.65 = (bf16[192,2176]{1,0:T(8,128)(2,1)}, bf16[192,2176]{1,0:T(8,128)(2,1)}, u32[]{:S(2)}, u32[]{:S(2)}) collective-permute-start(bf16[192,2176]{1,0:T(8,128)(2,1)} %collective-permute-done.61.refs_1_), channel_id=1, source_target_pairs={{0,1},{1,0},{2,3},{3,2},{4,5},{5,4},{6,7},{7,6},{8,9},{9,8},{10,11... | collective-permute-start | bytes 2506760 | tf_op jit(solution)/shard_map/ppermute | solution.py:328
  451.5 35.6 %collective-permute-start.66 = (bf16[192,2176]{1,0:T(8,128)(2,1)}, bf16[192,2176]{1,0:T(8,128)(2,1)}, u32[]{:S(2)}, u32[]{:S(2)}) collective-permute-start(bf16[192,2176]{1,0:T(8,128)(2,1)} %collective-permute-done.62.refs_2_), channel_id=1, source_target_pairs={{0,1},{1,0},{2,3},{3,2},{4,5},{5,4},{6,7},{7,6},{8,9},{9,8},{10,11... | collective-permute-start | bytes 2506760 | tf_op jit(solution)/shard_map/ppermute | solution.py:328
  451.6 36.0 %collective-permute-start.79 = (bf16[192,2176]{1,0:T(8,128)(2,1)S(1)}, bf16[192,2176]{1,0:T(8,128)(2,1)}, u32[]{:S(2)}, u32[]{:S(2)}) collective-permute-start(bf16[192,2176]{1,0:T(8,128)(2,1)S(1)} %collective-permute-done.77.refs_1_), channel_id=1, source_target_pairs={{0,4},{1,3},{2,6},{3,1},{4,0},{5,7},{6,2},{7,5},{8,12},{9,11},{10,... | collective-permute-start | bytes 2506760 | tf_op jit(solution)/shard_map/ppermute | solution.py:328
  452.6 35.1 %collective-permute-start.67 = (bf16[192,2176]{1,0:T(8,128)(2,1)S(1)}, bf16[192,2176]{1,0:T(8,128)(2,1)}, u32[]{:S(2)}, u32[]{:S(2)}) collective-permute-start(bf16[192,2176]{1,0:T(8,128)(2,1)S(1)} %collective-permute-done.63.refs_3_), channel_id=1, source_target_pairs={{0,1},{1,0},{2,3},{3,2},{4,5},{5,4},{6,7},{7,6},{8,9},{9,8},{10,11... | collective-permute-start | bytes 2506760 | tf_op jit(solution)/shard_map/ppermute | solution.py:328
  486.6 71.2 %collective-permute-start.101 = (bf16[4,192,2176]{2,1,0:T(8,128)(2,1)}, bf16[4,192,2176]{2,1,0:T(8,128)(2,1)}, u32[]{:S(2)}, u32[]{:S(2)}) collective-permute-start(bf16[4,192,2176]{2,1,0:T(8,128)(2,1)} %get-tuple-element.76), channel_id=1, source_target_pairs={{0,1},{1,0},{2,3},{3,2},{4,5},{5,4},{6,7},{7,6},{8,9},{9,8},{10,11... | collective-permute-start | bytes 10027016 | tf_op jit(solution)/shard_map/ppermute | solution.py:328
  487.1 35.0 %collective-permute-start.80 = (bf16[192,2176]{1,0:T(8,128)(2,1)}, bf16[192,2176]{1,0:T(8,128)(2,1)}, u32[]{:S(2)}, u32[]{:S(2)}) collective-permute-start(bf16[192,2176]{1,0:T(8,128)(2,1)} %collective-permute-done.76.refs_0_), channel_id=1, source_target_pairs={{0,1},{1,0},{2,3},{3,2},{4,5},{5,4},{6,7},{7,6},{8,9},{9,8},{10,11... | collective-permute-start | bytes 2506760 | tf_op jit(solution)/shard_map/ppermute | solution.py:328
  487.2 35.1 %collective-permute-start.81 = (bf16[192,2176]{1,0:T(8,128)(2,1)S(1)}, bf16[192,2176]{1,0:T(8,128)(2,1)}, u32[]{:S(2)}, u32[]{:S(2)}) collective-permute-start(bf16[192,2176]{1,0:T(8,128)(2,1)S(1)} %collective-permute-done.77.refs_1_), channel_id=1, source_target_pairs={{0,1},{1,0},{2,3},{3,2},{4,5},{5,4},{6,7},{7,6},{8,9},{9,8},{10,11... | collective-permute-start | bytes 2506760 | tf_op jit(solution)/shard_map/ppermute | solution.py:328
  487.6 34.6 %collective-permute-start.82 = (bf16[192,2176]{1,0:T(8,128)(2,1)S(1)}, bf16[192,2176]{1,0:T(8,128)(2,1)}, u32[]{:S(2)}, u32[]{:S(2)}) collective-permute-start(bf16[192,2176]{1,0:T(8,128)(2,1)S(1)} %collective-permute-done.78.refs_2_), channel_id=1, source_target_pairs={{0,1},{1,0},{2,3},{3,2},{4,5},{5,4},{6,7},{7,6},{8,9},{9,8},{10,11... | collective-permute-start | bytes 2506760 | tf_op jit(solution)/shard_map/ppermute | solution.py:328
  487.7 34.6 %collective-permute-start.83 = (bf16[192,2176]{1,0:T(8,128)(2,1)}, bf16[192,2176]{1,0:T(8,128)(2,1)S(1)}, u32[]{:S(2)}, u32[]{:S(2)}) collective-permute-start(bf16[192,2176]{1,0:T(8,128)(2,1)} %collective-permute-done.79.refs_3_), channel_id=1, source_target_pairs={{0,1},{1,0},{2,3},{3,2},{4,5},{5,4},{6,7},{7,6},{8,9},{9,8},{10,11... | collective-permute-start | bytes 2506760 | tf_op jit(solution)/shard_map/ppermute | solution.py:328
  522.1 52.2 %collective-permute-start.98 = (bf16[4,192,2176]{2,1,0:T(8,128)(2,1)}, bf16[4,192,2176]{2,1,0:T(8,128)(2,1)}, u32[]{:S(2)}, u32[]{:S(2)}) collective-permute-start(bf16[4,192,2176]{2,1,0:T(8,128)(2,1)} %get-tuple-element.74), channel_id=1, source_target_pairs={{0,1},{1,0},{2,3},{3,2},{4,5},{5,4},{6,7},{7,6},{8,9},{9,8},{10,11... | collective-permute-start | bytes 10027016 | tf_op jit(solution)/shard_map/ppermute | solution.py:328
  557.3 31.7 %collective-permute-start.95 = (bf16[4,192,2176]{2,1,0:T(8,128)(2,1)}, bf16[4,192,2176]{2,1,0:T(8,128)(2,1)}, u32[]{:S(2)}, u32[]{:S(2)}) collective-permute-start(bf16[4,192,2176]{2,1,0:T(8,128)(2,1)} %get-tuple-element.72), channel_id=1, source_target_pairs={{0,1},{1,0},{2,3},{3,2},{4,5},{5,4},{6,7},{7,6},{8,9},{9,8},{10,11... | collective-permute-start | bytes 10027016 | tf_op jit(solution)/shard_map/ppermute | solution.py:328
  574.3 41.6 %collective-permute-start.92 = (bf16[4,192,2176]{2,1,0:T(8,128)(2,1)}, bf16[4,192,2176]{2,1,0:T(8,128)(2,1)S(1)}, u32[]{:S(2)}, u32[]{:S(2)}) collective-permute-start(bf16[4,192,2176]{2,1,0:T(8,128)(2,1)} %get-tuple-element.70), channel_id=1, source_target_pairs={{0,1},{1,0},{2,3},{3,2},{4,5},{5,4},{6,7},{7,6},{8,9},{9,8},{10,11... | collective-permute-start | bytes 10027016 | tf_op jit(solution)/shard_map/ppermute | solution.py:328
  578.4 36.1 %collective-permute-start.99 = (bf16[2,192,2176]{2,1,0:T(8,128)(2,1)S(1)}, bf16[2,192,2176]{2,1,0:T(8,128)(2,1)S(1)}, u32[]{:S(2)}, u32[]{:S(2)}) collective-permute-start(bf16[2,192,2176]{2,1,0:T(8,128)(2,1)S(1)} %slice.776), channel_id=1, source_target_pairs={{0,4},{1,3},{2,6},{3,1},{4,0},{5,7},{6,2},{7,5},{8,12},{9,11},{10,... | collective-permute-start | bytes 5013512 | tf_op jit(solution)/shard_map/ppermute | solution.py:328
  591.9 48.0 %collective-permute-start.96 = (bf16[2,192,2176]{2,1,0:T(8,128)(2,1)S(1)}, bf16[2,192,2176]{2,1,0:T(8,128)(2,1)S(1)}, u32[]{:S(2)}, u32[]{:S(2)}) collective-permute-start(bf16[2,192,2176]{2,1,0:T(8,128)(2,1)S(1)} %slice.771), channel_id=1, source_target_pairs={{0,4},{1,3},{2,6},{3,1},{4,0},{5,7},{6,2},{7,5},{8,12},{9,11},{10,... | collective-permute-start | bytes 5013512 | tf_op jit(solution)/shard_map/ppermute | solution.py:328
  618.3 48.6 %collective-permute-start.93 = (bf16[2,192,2176]{2,1,0:T(8,128)(2,1)}, bf16[2,192,2176]{2,1,0:T(8,128)(2,1)}, u32[]{:S(2)}, u32[]{:S(2)}) collective-permute-start(bf16[2,192,2176]{2,1,0:T(8,128)(2,1)} %slice.766), channel_id=1, source_target_pairs={{0,4},{1,3},{2,6},{3,1},{4,0},{5,7},{6,2},{7,5},{8,12},{9,11},{10,... | collective-permute-start | bytes 5013512 | tf_op jit(solution)/shard_map/ppermute | solution.py:328
  637.6 32.2 %collective-permute-start.105 = (bf16[192,2176]{1,0:T(8,128)(2,1)}, bf16[192,2176]{1,0:T(8,128)(2,1)}, u32[]{:S(2)}, u32[]{:S(2)}) collective-permute-start(bf16[192,2176]{1,0:T(8,128)(2,1)} %fusion.8), channel_id=1, source_target_pairs={{0,16},{1,17},{2,18},{3,19},{4,20},{5,21},{6,22},{7,23},{8,0},{9,1... | collective-permute-start | bytes 2506760 | tf_op jit(solution)/shard_map/ppermute | solution.py:328
  641.4 28.4 %collective-permute-start.97 = (bf16[192,2176]{1,0:T(8,128)(2,1)}, bf16[192,2176]{1,0:T(8,128)(2,1)}, u32[]{:S(2)}, u32[]{:S(2)}) collective-permute-start(bf16[192,2176]{1,0:T(8,128)(2,1)} %fusion.49), channel_id=1, source_target_pairs={{0,2},{1,5},{2,0},{3,7},{4,6},{5,1},{6,4},{7,3},{8,10},{9,13},{10,... | collective-permute-start | bytes 2506760 | tf_op jit(solution)/shard_map/ppermute | solution.py:328
  820.7 112.9 %collective-permute-start.114 = (bf16[4,192,2048]{2,1,0:T(8,128)(2,1)}, bf16[4,192,2048]{2,1,0:T(8,128)(2,1)}, u32[]{:S(2)}, u32[]{:S(2)}) collective-permute-start(bf16[4,192,2048]{2,1,0:T(8,128)(2,1)} %get-tuple-element.78), channel_id=1, source_target_pairs={{0,1},{1,0},{2,3},{3,2},{4,5},{5,4},{6,7},{7,6},{8,9},{9,8},{10,11... | collective-permute-start | bytes 9437192 | tf_op jit(solution)/shard_map/ppermute | solution.py:328
  820.9 118.0 %collective-permute-start.117 = (bf16[4,192,2048]{2,1,0:T(8,128)(2,1)}, bf16[4,192,2048]{2,1,0:T(8,128)(2,1)}, u32[]{:S(2)}, u32[]{:S(2)}) collective-permute-start(bf16[4,192,2048]{2,1,0:T(8,128)(2,1)} %get-tuple-element.80), channel_id=1, source_target_pairs={{0,1},{1,0},{2,3},{3,2},{4,5},{5,4},{6,7},{7,6},{8,9},{9,8},{10,11... | collective-permute-start | bytes 9437192 | tf_op jit(solution)/shard_map/ppermute | solution.py:328
  821.2 128.6 %collective-permute-start.123 = (bf16[4,192,2048]{2,1,0:T(8,128)(2,1)}, bf16[4,192,2048]{2,1,0:T(8,128)(2,1)}, u32[]{:S(2)}, u32[]{:S(2)}) collective-permute-start(bf16[4,192,2048]{2,1,0:T(8,128)(2,1)} %get-tuple-element.84), channel_id=1, source_target_pairs={{0,1},{1,0},{2,3},{3,2},{4,5},{5,4},{6,7},{7,6},{8,9},{9,8},{10,11... | collective-permute-start | bytes 9437192 | tf_op jit(solution)/shard_map/ppermute | solution.py:328
  866.2 79.0 %collective-permute-start.132 = (bf16[4,192,2048]{2,1,0:T(8,128)(2,1)}, bf16[4,192,2048]{2,1,0:T(8,128)(2,1)}, u32[]{:S(2)}, u32[]{:S(2)}) collective-permute-start(bf16[4,192,2048]{2,1,0:T(8,128)(2,1)} %bitcast.81), channel_id=1, source_target_pairs={{0,1},{1,0},{2,3},{3,2},{4,5},{5,4},{6,7},{7,6},{8,9},{9,8},{10,11... | collective-permute-start | bytes 9437192 | tf_op jit(solution)/shard_map/ppermute | solution.py:328
  921.6 34.5 %collective-permute-start.120 = (bf16[4,192,2048]{2,1,0:T(8,128)(2,1)}, bf16[4,192,2048]{2,1,0:T(8,128)(2,1)}, u32[]{:S(2)}, u32[]{:S(2)}) collective-permute-start(bf16[4,192,2048]{2,1,0:T(8,128)(2,1)} %get-tuple-element.82), channel_id=1, source_target_pairs={{0,1},{1,0},{2,3},{3,2},{4,5},{5,4},{6,7},{7,6},{8,9},{9,8},{10,11... | collective-permute-start | bytes 9437192 | tf_op jit(solution)/shard_map/ppermute | solution.py:328
  944.3 57.7 %collective-permute-start.118 = (bf16[2,192,2048]{2,1,0:T(8,128)(2,1)S(1)}, bf16[2,192,2048]{2,1,0:T(8,128)(2,1)S(1)}, u32[]{:S(2)}, u32[]{:S(2)}) collective-permute-start(bf16[2,192,2048]{2,1,0:T(8,128)(2,1)S(1)} %slice.793), channel_id=1, source_target_pairs={{0,4},{1,3},{2,6},{3,1},{4,0},{5,7},{6,2},{7,5},{8,12},{9,11},{10,... | collective-permute-start | bytes 4718600 | tf_op jit(solution)/shard_map/ppermute | solution.py:328
  948.6 52.0 %collective-permute-start.133 = (bf16[2,192,2048]{2,1,0:T(8,128)(2,1)S(1)}, bf16[2,192,2048]{2,1,0:T(8,128)(2,1)S(1)}, u32[]{:S(2)}, u32[]{:S(2)}) collective-permute-start(bf16[2,192,2048]{2,1,0:T(8,128)(2,1)S(1)} %slice.846), channel_id=1, source_target_pairs={{0,4},{1,3},{2,6},{3,1},{4,0},{5,7},{6,2},{7,5},{8,12},{9,11},{10,... | collective-permute-start | bytes 4718600 | tf_op jit(solution)/shard_map/ppermute | solution.py:328
  954.9 76.8 %collective-permute-start.124 = (bf16[2,192,2048]{2,1,0:T(8,128)(2,1)S(1)}, bf16[2,192,2048]{2,1,0:T(8,128)(2,1)S(1)}, u32[]{:S(2)}, u32[]{:S(2)}) collective-permute-start(bf16[2,192,2048]{2,1,0:T(8,128)(2,1)S(1)} %slice.803), channel_id=1, source_target_pairs={{0,4},{1,3},{2,6},{3,1},{4,0},{5,7},{6,2},{7,5},{8,12},{9,11},{10,... | collective-permute-start | bytes 4718600 | tf_op jit(solution)/shard_map/ppermute | solution.py:328
  962.2 97.5 %collective-permute-start.121 = (bf16[2,192,2048]{2,1,0:T(8,128)(2,1)}, bf16[2,192,2048]{2,1,0:T(8,128)(2,1)}, u32[]{:S(2)}, u32[]{:S(2)}) collective-permute-start(bf16[2,192,2048]{2,1,0:T(8,128)(2,1)} %slice.798), channel_id=1, source_target_pairs={{0,4},{1,3},{2,6},{3,1},{4,0},{5,7},{6,2},{7,5},{8,12},{9,11},{10,... | collective-permute-start | bytes 4718600 | tf_op jit(solution)/shard_map/ppermute | solution.py:328
  964.7 154.9 %collective-permute-start.116 = (bf16[192,2048]{1,0:T(8,128)(2,1)}, bf16[192,2048]{1,0:T(8,128)(2,1)}, u32[]{:S(2)}, u32[]{:S(2)}) collective-permute-start(bf16[192,2048]{1,0:T(8,128)(2,1)} %fusion.53), channel_id=1, source_target_pairs={{0,2},{1,5},{2,0},{3,7},{4,6},{5,1},{6,4},{7,3},{8,10},{9,13},{10,... | collective-permute-start | bytes 2359304 | tf_op jit(solution)/shard_map/ppermute | solution.py:328
  1000.9 33.2 %collective-permute-start.134 = (bf16[192,2048]{1,0:T(8,128)(2,1)S(1)}, bf16[192,2048]{1,0:T(8,128)(2,1)S(1)}, u32[]{:S(2)}, u32[]{:S(2)}) collective-permute-start(bf16[192,2048]{1,0:T(8,128)(2,1)S(1)} %fusion.57), channel_id=1, source_target_pairs={{0,2},{1,5},{2,0},{3,7},{4,6},{5,1},{6,4},{7,3},{8,10},{9,13},{10,... | collective-permute-start | bytes 2359304 | tf_op jit(solution)/shard_map/ppermute | solution.py:328
  1003.3 95.0 %collective-permute-start.119 = (bf16[192,2048]{1,0:T(8,128)(2,1)}, bf16[192,2048]{1,0:T(8,128)(2,1)}, u32[]{:S(2)}, u32[]{:S(2)}) collective-permute-start(bf16[192,2048]{1,0:T(8,128)(2,1)} %fusion.54), channel_id=1, source_target_pairs={{0,2},{1,5},{2,0},{3,7},{4,6},{5,1},{6,4},{7,3},{8,10},{9,13},{10,... | collective-permute-start | bytes 2359304 | tf_op jit(solution)/shard_map/ppermute | solution.py:328
  1033.2 32.4 %collective-permute-start.125 = (bf16[192,2048]{1,0:T(8,128)(2,1)}, bf16[192,2048]{1,0:T(8,128)(2,1)}, u32[]{:S(2)}, u32[]{:S(2)}) collective-permute-start(bf16[192,2048]{1,0:T(8,128)(2,1)} %fusion.56), channel_id=1, source_target_pairs={{0,2},{1,5},{2,0},{3,7},{4,6},{5,1},{6,4},{7,3},{8,10},{9,13},{10,... | collective-permute-start | bytes 2359304 | tf_op jit(solution)/shard_map/ppermute | solution.py:328
  (249 other events, 4744.2 us)

commit v3 on v0

--- a/solution.py
+++ b/solution.py
@@ -1,6 +1,10 @@
+import functools
+
 import jax
 import jax.numpy as jnp
 from jax import lax
+from jax.experimental import pallas as pl
+from jax.experimental.pallas import tpu as pltpu
 from jax.sharding import PartitionSpec as P
 
 D = 2048
@@ -75,7 +79,7 @@
     )
 
 
-def shards(
+def shards_routed(
     tokens,
     cotangent,
     norm_gains,
@@ -290,6 +294,1088 @@
     )
 
 
+def product(left, right):
+    return jnp.dot(left, right, preferred_element_type=jnp.float32)
+
+
+def widen(value):
+    return value.astype(jnp.float32)
+
+
+PLANE = 8
+SPOTS = 4
+WIDE = 128
+
+
+class Moves:
+    def __init__(self, count):
+        planes = count // PLANE
+        order = list(range(0, planes, 2)) + list(range(1, planes, 2))[::-1]
+        after = {order[i]: order[(i + 1) % planes] for i in range(planes)}
+        self.planes = planes
+        self.ring = [(i, after[i // PLANE] * PLANE + i % PLANE) for i in range(count)]
+        self.first = [(i, i ^ (4 if i & 1 else 2)) for i in range(count)]
+        self.second = [(i, i ^ (2 if i & 1 else 4)) for i in range(count)]
+        self.core = [(i, i ^ 1) for i in range(count)]
+        self.spots = [[(i, i ^ (2 * mask)) for i in range(count)] for mask in range(SPOTS)]
+        device = lax.axis_index("fsdp")
+        self.device = device
+        self.plane, self.spot, self.core_id = device // PLANE, device % PLANE // 2, device % 2
+        rank = jnp.asarray([order.index(i) for i in range(planes)], jnp.int32)
+        self.planes_back = jnp.asarray(order, jnp.int32)[
+            (rank[self.plane] - jnp.arange(planes, dtype=jnp.int32)) % planes
+        ]
+        self.steps_from = (rank[self.plane] - rank) % planes
+        self.group_spots = self.spot ^ jnp.where(
+            self.core_id == 0, jnp.asarray([0, 1, 2, 3]), jnp.asarray([0, 2, 1, 3])
+        )
+
+
+def send(value, pairs):
+    return lax.ppermute(value, "fsdp", pairs)
+
+
+def tie(*values):
+    return lax.optimization_barrier(values)
+
+
+def plane_total(moves, parts):
+    def swapped(value):
+        return jnp.where(moves.core_id == 0, value, value[:, jnp.asarray([0, 2, 1, 3])])
+
+    parts = swapped(parts)
+    for bit in (1, 2):
+        other = send(parts, moves.spots[bit])
+        parts = parts + jnp.stack([other[:, m ^ bit] for m in range(SPOTS)], axis=1)
+    return swapped(parts)
+
+
+def full_spec(*dims):
+    return pl.BlockSpec(dims, lambda *_: (0,) * len(dims))
+
+
+SCALARS = pl.BlockSpec(memory_space=pltpu.SMEM)
+ANYWHERE = pl.BlockSpec(memory_space=pl.ANY)
+
+
+def params(mebibytes):
+    return pltpu.CompilerParams(vmem_limit_bytes=mebibytes << 20)
+
+
+def cost(flops, moved, special=0):
+    return pl.CostEstimate(flops=flops, bytes_accessed=moved, transcendentals=special)
+
+
+def column_places(spot, mask, lines):
+    for part in range(3):
+        for line in range(lines):
+            piece = (part * lines + line) * HEAD_DIM
+            whole = ((part * lines + line) * SPOTS + (spot ^ mask)) * HEAD_DIM
+            yield pl.ds(pl.multiple_of(whole, HEAD_DIM), HEAD_DIM), pl.ds(piece, HEAD_DIM)
+
+
+def split_body(lines, meta, whole_ref, *pieces):
+    for mask, piece in enumerate(pieces):
+        for whole_at, piece_at in column_places(meta[0], mask, lines):
+            piece[:, piece_at] = whole_ref[:, whole_at]
+
+
+def split_columns(spot, whole):
+    rows, columns = whole.shape
+    return pl.pallas_call(
+        functools.partial(split_body, HEADS // SPOTS),
+        out_shape=[jax.ShapeDtypeStruct((rows, columns // SPOTS), whole.dtype)] * SPOTS,
+        in_specs=[SCALARS, full_spec(rows, columns)],
+        out_specs=[full_spec(rows, columns // SPOTS)] * SPOTS,
+        compiler_params=params(16),
+        name="split_columns",
+    )(spot.reshape(1), whole)
+
+
+def join_body(lines, meta, *refs):
+    *pieces, whole_ref = refs
+    for mask, piece in enumerate(pieces):
+        for whole_at, piece_at in column_places(meta[0], mask, lines):
+            whole_ref[:, whole_at] = widen(piece[:, piece_at])
+
+
+def join_columns(spot, pieces):
+    rows, columns = pieces[0].shape
+    return pl.pallas_call(
+        functools.partial(join_body, HEADS // SPOTS),
+        out_shape=jax.ShapeDtypeStruct((rows, columns * SPOTS), jnp.float32),
+        in_specs=[SCALARS] + [full_spec(rows, columns)] * SPOTS,
+        out_specs=full_spec(rows, columns * SPOTS),
+        compiler_params=params(16),
+        name="join_columns",
+    )(spot.reshape(1), *pieces)
+
+
+def expert_body(index, cap, experts, blocks, meta, *refs):
+    row_refs, grad_refs, weights = refs[:blocks], refs[blocks : 2 * blocks], refs[2 * blocks :][:4]
+    refs = refs[2 * blocks + 4 + 6 :]
+    saves, out_parts, row_parts = refs[:6], refs[6 : 6 + blocks], refs[6 + blocks :][:blocks]
+    rows_v, grads_v, in_v, out_v, x_v, dy_v, m_v, du_v, part_v, back_v, sem, done = refs[
+        6 + 2 * blocks :
+    ]
+    bf, f32 = jnp.bfloat16, jnp.float32
+    count, width, half = rows_v.shape[1], grads_v.shape[2], out_v.shape[1]
+    expert = meta[0]
+
+    def fetch(ref, place, n):
+        copy = pltpu.make_async_copy(ref, place, sem.at[n])
+        copy.start()
+        return copy
+
+    fetch_rows = [fetch(ref, rows_v.at[j], j) for j, ref in enumerate(row_refs)]
+    fetch_in = [fetch(weights[h], in_v.at[h], blocks + h) for h in range(2)]
+    fetch_out = [fetch(weights[2 + h], out_v.at[h], blocks + 2 + h) for h in range(2)]
+    fetch_grads = [fetch(ref, grads_v.at[j], blocks + 4 + j) for j, ref in enumerate(grad_refs)]
+    leaving = []
+
+    def leave(place, ref):
+        leaving.append(pltpu.make_async_copy(place, ref, done.at[len(leaving)]))
+        leaving[-1].start()
+
+    def save(place, n):
+        leave(place, saves[n].at[pl.ds(index * cap, blocks * cap)])
+
+    lane8 = lax.broadcasted_iota(jnp.int32, (8, WIDE), 1)
+    row8 = lax.broadcasted_iota(jnp.int32, (8, WIDE), 0)
+    picker = (
+        jnp.where((row8 == 0) & (lane8 == expert), 1.0, 0.0)
+        + jnp.where((row8 == 1) & (lane8 == experts + expert), 1.0, 0.0)
+        + jnp.where((row8 == 1) & (lane8 == 2 * experts + expert), 1.0, 0.0)
+    ).astype(bf)
+    lanes = lax.broadcasted_iota(jnp.int32, (count, WIDE), 1)
+    slots_down = lax.broadcasted_iota(jnp.int32, (cap, count), 0)
+    slots_along = lax.broadcasted_iota(jnp.int32, (count, cap), 1)
+    gather, scatter, gates = [], [], []
+    slots = [slice(j * cap, (j + 1) * cap) for j in range(blocks)]
+    for j in range(blocks):
+        fetch_rows[j].wait()
+        extra = rows_v[j, :, width:]
+        info = dot_last(picker, extra)
+        chosen = slots_down == info[0:1].astype(jnp.int32)
+        gates.append(jnp.sum(jnp.where(chosen, info[1:2], 0.0), axis=1, keepdims=True))
+        gather.append(jnp.where(chosen, 1.0, 0.0).astype(bf))
+        slot = jnp.sum(
+            jnp.where(lanes == expert, widen(extra), 0.0), axis=1, keepdims=True
+        ).astype(jnp.int32)
+        scatter.append(jnp.where(slots_along == slot, 1.0, 0.0).astype(bf))
+        x_v[slots[j], :] = product(gather[j], rows_v[j, :, :width]).astype(bf)
+    gate = jnp.concatenate(gates, axis=0)
+    save(x_v, 0)
+    x = x_v[...]
+    inner = []
+    for h in range(2):
+        fetch_in[h].wait()
+        u = product(x, in_v[h])
+        gate_part, up_part = u[:, :half], u[:, half:]
+        sigmoid = 1.0 / (1.0 + jnp.exp(-gate_part))
+        silu = gate_part * sigmoid
+        inner.append((gate_part, up_part, sigmoid, silu))
+        m_v[h] = (silu * up_part).astype(bf)
+        save(m_v.at[h], 2 + h)
+    for copy in fetch_out:
+        copy.wait()
+    y = product(m_v[0], out_v[0]) + product(m_v[1], out_v[1])
+    for copy in fetch_grads:
+        copy.wait()
+    g = jnp.concatenate([product(gather[j], grads_v[j]) for j in range(blocks)], axis=0)
+    dgate = jnp.sum(g * y, axis=1, keepdims=True)
+    z = (gate * y).astype(bf)
+    dy_v[...] = (gate * g).astype(bf)
+    save(dy_v, 1)
+    for j in range(blocks):
+        part_v[j] = product(scatter[j], z[slots[j]]).astype(bf)
+        leave(part_v.at[j], out_parts[j])
+    dy = dy_v[...]
+    for h in range(2):
+        gate_part, up_part, sigmoid, silu = inner[h]
+        dm = dot_last(dy, out_v[h])
+        slope = sigmoid * (1.0 + gate_part * (1.0 - sigmoid))
+        du_v[h, :, :half] = (dm * up_part * slope).astype(bf)
+        du_v[h, :, half:] = (dm * silu).astype(bf)
+        save(du_v.at[h], 4 + h)
+    drows = (dot_last(du_v[0], in_v[0]) + dot_last(du_v[1], in_v[1])).astype(bf)
+    upper = widen(dgate.astype(bf))
+    lane_m = lax.broadcasted_iota(jnp.int32, (blocks * cap, WIDE), 1)
+    pair = jnp.where(
+        lane_m == 2 * expert, upper, jnp.where(lane_m == 2 * expert + 1, dgate - upper, 0.0)
+    ).astype(bf)
+    for j in range(blocks):
+        back_v[j, :, :width] = product(scatter[j], drows[slots[j]]).astype(bf)
+        back_v[j, :, width:] = product(scatter[j], pair[slots[j]]).astype(bf)
+        leave(back_v.at[j], row_parts[j])
+    for copy in leaving:
+        copy.wait()
+
+
+def expert_blocks(meta, rows, grads, weights, saved, index, total, cap, experts):
+    blocks = len(rows)
+    count, wide = rows[0].shape
+    width, half = grads[0].shape[1], weights[2].shape[0]
+    bf = jnp.bfloat16
+    used = blocks * cap
+
+    def shape(*dims):
+        return jax.ShapeDtypeStruct(dims, bf)
+
+    aliases = {2 * blocks + 5 + t: t for t in range(6)}
+    if saved is None:
+        saved, aliases = [jnp.zeros((16, WIDE), bf)] * 6, {}
+    save_columns = (width, width, half, half, 2 * half, 2 * half)
+    results = pl.pallas_call(
+        functools.partial(expert_body, index, cap, experts, blocks),
+        out_shape=[shape(total * cap, columns) for columns in save_columns]
+        + [shape(count, width)] * blocks
+        + [shape(count, wide)] * blocks,
+        in_specs=[SCALARS] + [ANYWHERE] * (2 * blocks + 10),
+        out_specs=[ANYWHERE] * (6 + 2 * blocks),
+        scratch_shapes=[
+            pltpu.VMEM((blocks, count, wide), bf),
+            pltpu.VMEM((blocks, count, width), bf),
+            pltpu.VMEM((2, width, 2 * half), bf),
+            pltpu.VMEM((2, half, width), bf),
+            pltpu.VMEM((used, width), bf),
+            pltpu.VMEM((used, width), bf),
+            pltpu.VMEM((2, used, half), bf),
+            pltpu.VMEM((2, used, 2 * half), bf),
+            pltpu.VMEM((blocks, count, width), bf),
+            pltpu.VMEM((blocks, count, wide), bf),
+            pltpu.SemaphoreType.DMA((2 * blocks + 4,)),
+            pltpu.SemaphoreType.DMA((6 + 2 * blocks,)),
+        ],
+        input_output_aliases=aliases,
+        compiler_params=params(58),
+        cost_estimate=cost(blocks * 38 * 10**8, 30 << 20, 2 * used * half),
+        name="expert_blocks",
+    )(meta, *rows, *grads, *weights, *saved)
+    return results[:6], results[6 : 6 + blocks], results[6 + blocks :]
+
+
+def eye(count):
+    return lax.broadcasted_iota(jnp.int32, (count, count), 0) == lax.broadcasted_iota(
+        jnp.int32, (count, count), 1
+    )
+
+
+def as_column(row):
+    return jnp.sum(jnp.where(eye(row.shape[1]), row, 0.0), axis=1, keepdims=True)
+
+
+def as_row(column):
+    return jnp.sum(jnp.where(eye(column.shape[0]), column, 0.0), axis=0, keepdims=True)
+
+
+def rolled(value):
+    return pltpu.roll(value, HEAD_DIM // 2, 1)
+
+
+def root_of(total):
+    return lax.rsqrt(total / D + EPSILON)
+
+
+def weights_of(query, key, start):
+    count = query.shape[0]
+    rows = lax.broadcasted_iota(jnp.int32, (count, count), 0)
+    columns = lax.broadcasted_iota(jnp.int32, (count, count), 1)
+    allowed = (columns <= rows) & (columns >= start.astype(jnp.int32))
+    scores = jnp.where(allowed, dot_last(query, key) * HEAD_DIM ** (-0.5), MASKED)
+    exponent = jnp.exp(scores - jnp.max(scores, axis=1, keepdims=True))
+    return exponent / jnp.sum(exponent, axis=1, keepdims=True)
+
+
+def spans(mine):
+    return [slice(h, h + HEAD_DIM) for h in range(0, mine, HEAD_DIM)]
+
+
+def project_body(planes, own_rows, meta, gain, *refs):
+    blocks, own, other = refs[:SPOTS], refs[SPOTS : SPOTS + planes], refs[SPOTS + planes :][:planes]
+    proj_ref, a_ref, in_ref, sums_ref = refs[SPOTS + 2 * planes :][:4]
+    x_v, a_v, in_v, proj_v, sem, in_sem, done = refs[SPOTS + 2 * planes + 4 :]
+    spot, core = meta[0], meta[1]
+    count = x_v.shape[1]
+    mine = proj_v.shape[1] // 3
+    fetch_x = [pltpu.make_async_copy(ref, x_v.at[j], sem.at[j]) for j, ref in enumerate(blocks)]
+    for copy in fetch_x:
+        copy.start()
+    fetch_in = []
+    for k in range(planes):
+        for mask in range(SPOTS):
+            chunk = meta[2 + k] * PLANE + (spot ^ mask) * 2
+            for n, (refs_k, c) in enumerate(((own, core), (other, 1 - core))):
+                at = pl.multiple_of((chunk + c) * own_rows, own_rows)
+                fetch_in.append(
+                    pltpu.make_async_copy(
+                        refs_k[k].at[mask],
+                        in_v.at[pl.ds(at, own_rows)],
+                        in_sem.at[(k * SPOTS + mask) * 2 + n],
+                    )
+                )
+                fetch_in[-1].start()
+    for j in range(SPOTS):
+        fetch_x[j].wait()
+        x = widen(x_v[j])
+        root = lax.rsqrt(jnp.mean(x * x, axis=1, keepdims=True) + EPSILON)
+        a_v[j * count : (j + 1) * count, :] = (x * root * gain[...]).astype(jnp.bfloat16)
+    leaving = [pltpu.make_async_copy(a_v, a_ref, done.at[0])]
+    leaving[0].start()
+    for copy in fetch_in:
+        copy.wait()
+    leaving.append(pltpu.make_async_copy(in_v, in_ref, done.at[1]))
+    leaving[1].start()
+    for n in range(3):
+        part = slice(n * mine, (n + 1) * mine)
+        value = product(a_v[...], in_v[:, part])
+        proj_v[:, part] = value
+        leaving.append(
+            pltpu.make_async_copy(proj_v.at[:, part], proj_ref.at[:, part], done.at[2 + n])
+        )
+        leaving[-1].start()
+        if n < 2:
+            squares = jnp.sum(value * value, axis=1, keepdims=True)
+            for j in range(SPOTS):
+                sums_ref[n, j : j + 1, :] = as_row(squares[j * count : (j + 1) * count])
+    for copy in leaving:
+        copy.wait()
+
+
+def project(moves, gain, blocks, own, other):
+    planes, own_rows, width = len(own), own[0].shape[1], own[0].shape[2]
+    count, depth = blocks[0].shape
+    bf, f32 = jnp.bfloat16, jnp.float32
+    rows = SPOTS * count
+    meta = jnp.concatenate([jnp.stack([moves.spot, moves.core_id]), moves.planes_back])
+    shape = jax.ShapeDtypeStruct
+    return pl.pallas_call(
+        functools.partial(project_body, planes, own_rows),
+        out_shape=[
+            shape((rows, width), f32),
+            shape((rows, depth), bf),
+            shape((depth, width), bf),
+            shape((2, SPOTS, count), f32),
+        ],
+        in_specs=[SCALARS, full_spec(1, depth)] + [ANYWHERE] * (SPOTS + 2 * planes),
+        out_specs=[ANYWHERE] * 3 + [full_spec(2, SPOTS, count)],
+        scratch_shapes=[
+            pltpu.VMEM((SPOTS, count, depth), bf),
+            pltpu.VMEM((rows, depth), bf),
+            pltpu.VMEM((depth, width), bf),
+            pltpu.VMEM((rows, width), f32),
+            pltpu.SemaphoreType.DMA((SPOTS,)),
+            pltpu.SemaphoreType.DMA((2 * SPOTS * planes,)),
+            pltpu.SemaphoreType.DMA((5,)),
+        ],
+        compiler_params=params(40),
+        cost_estimate=cost(5 * 10**9, 20 << 20),
+        name="project",
+    )(meta.astype(jnp.int32), gain, *blocks, *own, *other)
+
+
+def by_block(count, width):
+    return [pl.BlockSpec((count, width), lambda i: (0, 0))] * SPOTS
+
+
+def put_by_block(step, refs, value):
+    for n, ref in enumerate(refs):
+
+        @pl.when(step == n)
+        def _(ref=ref):
+            ref[...] = value
+
+
+def forward_body(planes, own_rows, meta, totals, starts, gains, proj_ref, cos_ref, sin_ref, *refs):
+    own, other = refs[:planes], refs[planes : 2 * planes]
+    q_ref, k_ref, v_ref, o_ref, out_w, *parts = refs[2 * planes :][: 5 + SPOTS]
+    sem = refs[-1]
+    step = pl.program_id(0)
+    bf = jnp.bfloat16
+    mine = q_ref.shape[1]
+    fetches = []
+    for k in range(planes):
+        for n, (refs_k, c) in enumerate(((own, meta[1]), (other, 1 - meta[1]))):
+            at = pl.multiple_of((meta[2 + k] * 2 + c) * own_rows, own_rows)
+            fetches.append(
+                pltpu.make_async_copy(
+                    refs_k[k], out_w.at[pl.ds(at, own_rows)], sem.at[2 * k + n]
+                )
+            )
+
+    @pl.when(step == 0)
+    def _():
+        for copy in fetches:
+            copy.start()
+
+    query_root = root_of(as_column(totals[0, pl.ds(step, 1), :]))
+    key_root = root_of(as_column(totals[1, pl.ds(step, 1), :]))
+    start = as_column(starts[pl.ds(step, 1), :])
+    cos, sin = cos_ref[...], sin_ref[...]
+    for own_span in spans(mine):
+        at = own_span.start
+        query = proj_ref[:, at : at + HEAD_DIM] * query_root * gains[0:1, own_span]
+        key = proj_ref[:, mine + at : mine + at + HEAD_DIM] * key_root * gains[1:2, own_span]
+        value = proj_ref[:, 2 * mine + at : 2 * mine + at + HEAD_DIM].astype(bf)
+        query = (query * cos + rolled(query) * sin).astype(bf)
+        key = (key * cos + rolled(key) * sin).astype(bf)
+        weights = weights_of(query, key, start).astype(bf)
+        q_ref[:, own_span] = query
+        k_ref[:, own_span] = key
+        v_ref[:, own_span] = value
+        o_ref[:, own_span] = product(weights, value).astype(bf)
+
+    @pl.when(step == 0)
+    def _():
+        for copy in fetches:
+            copy.wait()
+
+    put_by_block(step, parts, product(o_ref[...], out_w[...]).astype(bf))
+
+
+def block_spec(count, columns):
+    return pl.BlockSpec((count, columns), lambda i: (i, 0))
+
+
+def attend_forward(moves, totals, starts, gains, projected, cos_all, sin_all, own, other):
+    planes, own_rows = len(own), own[0].shape[0]
+    rows, mine = projected.shape[0], gains.shape[1]
+    count = rows // SPOTS
+    bf = jnp.bfloat16
+    meta = jnp.concatenate([jnp.stack([moves.spot, moves.core_id]), moves.planes_back])
+    return pl.pallas_call(
+        functools.partial(forward_body, planes, own_rows),
+        grid=(SPOTS,),
+        out_shape=[jax.ShapeDtypeStruct((rows, mine), bf)] * 4
+        + [jax.ShapeDtypeStruct((mine, D), bf)]
+        + [jax.ShapeDtypeStruct((count, D), bf)] * SPOTS,
+        in_specs=[
+            SCALARS,
+            full_spec(*totals.shape),
+            full_spec(*starts.shape),
+            full_spec(*gains.shape),
+            block_spec(count, 3 * mine),
+            block_spec(count, HEAD_DIM),
+            block_spec(count, HEAD_DIM),
+        ]
+        + [ANYWHERE] * (2 * planes),
+        out_specs=[block_spec(count, mine)] * 4 + [full_spec(mine, D)] + by_block(count, D),
+        scratch_shapes=[pltpu.SemaphoreType.DMA((2 * planes,))],
+        compiler_params=params(40),
+        cost_estimate=cost(5 * 10**9, 20 << 20),
+        name="attend_forward",
+    )(meta.astype(jnp.int32), totals, starts, gains, projected, cos_all, sin_all, *own, *other)
+
+
+def backward_body(
+    meta, totals, starts, gains, proj_ref, cos_ref, sin_ref, q_ref, k_ref, v_ref, o_ref, out_w, *refs
+):
+    blocks = refs[:SPOTS]
+    dq_ref, dk_ref, dv_ref, sums_ref, own_grad, other_grad, gain_grad = refs[SPOTS : SPOTS + 7]
+    grads_v, total_v, sem = refs[SPOTS + 7 :]
+    step = pl.program_id(0)
+    bf = jnp.bfloat16
+    mine = q_ref.shape[1]
+
+    @pl.when(step == 0)
+    def _():
+        for n in range(SPOTS):
+            pltpu.make_async_copy(blocks[n], grads_v.at[n], sem.at[n]).start()
+        total_v[...] = jnp.zeros_like(total_v)
+        gain_grad[...] = jnp.zeros_like(gain_grad)
+
+    pltpu.make_async_copy(blocks[0], grads_v.at[step], sem.at[step]).wait()
+    grads = grads_v[step]
+    total_v[...] += dot_first(o_ref[...], grads)
+    do = dot_last(grads, out_w[...]).astype(bf)
+    roots = [root_of(as_column(totals[n, pl.ds(step, 1), :])) for n in range(2)]
+    start = as_column(starts[pl.ds(step, 1), :])
+    cos, sin = cos_ref[...], sin_ref[...]
+    sums = [0.0, 0.0]
+    for own in spans(mine):
+        query, key, value = q_ref[:, own], k_ref[:, own], v_ref[:, own]
+        weights = weights_of(query, key, start)
+        dv_ref[:, own] = dot_first(weights.astype(bf), do[:, own]).astype(bf)
+        dweights = dot_last(do[:, own], value)
+        inner = jnp.sum(weights * dweights, axis=1, keepdims=True)
+        dscores = (weights * (dweights - inner)).astype(bf)
+        for n, (grad, ref) in enumerate(
+            ((product(dscores, key), dq_ref), (dot_first(dscores, query), dk_ref))
+        ):
+            grad = grad * HEAD_DIM ** (-0.5)
+            grad = grad * cos - rolled(grad) * sin
+            ref[:, own] = grad
+            at = n * mine + own.start
+            raw = grad * proj_ref[:, at : at + HEAD_DIM]
+            sums[n] += jnp.sum(raw * gains[n : n + 1, own], axis=1, keepdims=True)
+            gain_grad[n : n + 1, own] += jnp.sum(raw * roots[n], axis=0, keepdims=True)
+    for n in range(2):
+        sums_ref[n, pl.ds(step, 1), :] = as_row(sums[n])
+
+    @pl.when(step == SPOTS - 1)
+    def _():
+        planes, own_rows = own_grad.shape[:2]
+        for k in range(planes):
+            for ref, c in ((own_grad, meta[1]), (other_grad, 1 - meta[1])):
+                at = pl.multiple_of((meta[2 + k] * 2 + c) * own_rows, own_rows)
+                ref[k] = total_v[pl.ds(at, own_rows), :].astype(bf)
+
+
+def attend_backward(
+    moves, totals, starts, gains, projected, cos_all, sin_all, heads, out_full, blocks
+):
+    rows, mine = projected.shape[0], gains.shape[1]
+    count = rows // SPOTS
+    planes = moves.planes
+    own_rows = mine // (2 * planes)
+    bf, f32 = jnp.bfloat16, jnp.float32
+    meta = jnp.concatenate([jnp.stack([moves.spot, moves.core_id]), moves.planes_back])
+    shape = jax.ShapeDtypeStruct
+    return pl.pallas_call(
+        backward_body,
+        grid=(SPOTS,),
+        out_shape=[
+            shape((rows, mine), f32),
+            shape((rows, mine), f32),
+            shape((rows, mine), bf),
+            shape((2, SPOTS, count), f32),
+            shape((planes, own_rows, D), bf),
+            shape((planes, own_rows, D), bf),
+            shape((8, mine), f32),
+        ],
+        in_specs=[
+            SCALARS,
+            full_spec(*totals.shape),
+            full_spec(*starts.shape),
+            full_spec(*gains.shape),
+            block_spec(count, 3 * mine),
+            block_spec(count, HEAD_DIM),
+            block_spec(count, HEAD_DIM),
+        ]
+        + [block_spec(count, mine)] * 4
+        + [full_spec(*out_full.shape)]
+        + [ANYWHERE] * SPOTS,
+        out_specs=[block_spec(count, mine)] * 3
+        + [full_spec(2, SPOTS, count)]
+        + [full_spec(planes, own_rows, D)] * 2
+        + [full_spec(8, mine)],
+        scratch_shapes=[
+            pltpu.VMEM((SPOTS, count, D), bf),
+            pltpu.VMEM((mine, D), f32),
+            pltpu.SemaphoreType.DMA((SPOTS,)),
+        ],
+        compiler_params=params(48),
+        cost_estimate=cost(7 * 10**9, 25 << 20),
+        name="attend_backward",
+    )(
+        meta.astype(jnp.int32),
+        totals,
+        starts,
+        gains,
+        projected,
+        cos_all,
+        sin_all,
+        *heads,
+        out_full,
+        *blocks,
+    )
+
+
+def project_back_body(
+    planes, own_rows, meta, totals, dots, gains, proj_ref, dq_ref, dk_ref, dv_ref, a_ref, *refs
+):
+    dp_ref, own, other, total_v = refs[0], refs[1 : 1 + planes], refs[1 + planes : -1], refs[-1]
+    step = pl.program_id(0)
+    bf = jnp.bfloat16
+    mine = dv_ref.shape[1]
+    count = dv_ref.shape[0] // 2
+    for n, ref in enumerate((dq_ref, dk_ref)):
+        columns = slice(n * mine, (n + 1) * mine)
+        for j in range(2):
+            rows = slice(j * count, (j + 1) * count)
+            root = root_of(as_column(totals[n, pl.ds(2 * step + j, 1), :]))
+            inner = as_column(dots[n, pl.ds(2 * step + j, 1), :])
+            grad = root * gains[n : n + 1, :] * ref[rows, :]
+            grad = grad - proj_ref[rows, columns] * (root * root * root * inner / D)
+            dp_ref[rows, columns] = grad.astype(bf)
+    dp_ref[:, 2 * mine :] = dv_ref[...]
+
+    @pl.when(step == 0)
+    def _():
+        total_v[...] = dot_first(a_ref[...], dp_ref[...])
+
+    @pl.when(step == 1)
+    def _():
+        total_v[...] += dot_first(a_ref[...], dp_ref[...])
+        for k in range(planes):
+            for mask in range(SPOTS):
+                chunk = meta[2 + k] * PLANE + (meta[0] ^ mask) * 2
+                for refs_k, c in ((own, meta[1]), (other, 1 - meta[1])):
+                    at = pl.multiple_of((chunk + c) * own_rows, own_rows)
+                    refs_k[k][mask] = total_v[pl.ds(at, own_rows), :].astype(bf)
+
+
+def project_back(moves, totals, dots, gains, projected, dq, dk, dv, normed_all):
+    rows, mine = dv.shape
+    planes = moves.planes
+    own_rows = D // (planes * PLANE)
+    bf = jnp.bfloat16
+    meta = jnp.concatenate([jnp.stack([moves.spot, moves.core_id]), moves.planes_back])
+    half = rows // 2
+    pieces = (SPOTS, own_rows, 3 * mine)
+    return pl.pallas_call(
+        functools.partial(project_back_body, planes, own_rows),
+        grid=(2,),
+        out_shape=[jax.ShapeDtypeStruct((rows, 3 * mine), bf)]
+        + [jax.ShapeDtypeStruct(pieces, bf)] * (2 * planes),
+        in_specs=[
+            SCALARS,
+            full_spec(*totals.shape),
+            full_spec(*dots.shape),
+            full_spec(*gains.shape),
+            block_spec(half, 3 * mine),
+            block_spec(half, mine),
+            block_spec(half, mine),
+            block_spec(half, mine),
+            block_spec(half, D),
+        ],
+        out_specs=[block_spec(half, 3 * mine)] + [full_spec(*pieces)] * (2 * planes),
+        scratch_shapes=[pltpu.VMEM((D, 3 * mine), jnp.float32)],
+        compiler_params=params(60),
+        cost_estimate=cost(5 * 10**9, 30 << 20),
+        name="project_back",
+    )(meta.astype(jnp.int32), totals, dots, gains, projected, dq, dk, dv, normed_all)
+
+
+def rows_back_body(dp_ref, in_w, *refs):
+    blocks, parts, gain_grad, (x_v, sem) = (
+        refs[:SPOTS],
+        refs[SPOTS : 2 * SPOTS],
+        refs[2 * SPOTS],
+        refs[2 * SPOTS + 1 :],
+    )
+    step = pl.program_id(0)
+
+    @pl.when(step == 0)
+    def _():
+        for n in range(SPOTS):
+            pltpu.make_async_copy(blocks[n], x_v.at[n], sem.at[n]).start()
+        gain_grad[...] = jnp.zeros_like(gain_grad)
+
+    value = dot_last(dp_ref[...], in_w[...])
+    put_by_block(step, parts, value.astype(jnp.bfloat16))
+    pltpu.make_async_copy(blocks[0], x_v.at[step], sem.at[step]).wait()
+    x = widen(x_v[step])
+    root = lax.rsqrt(jnp.mean(x * x, axis=1, keepdims=True) + EPSILON)
+    gain_grad[...] += jnp.sum(value * (x * root), axis=0, keepdims=True)
+
+
+def rows_back(projected_grad, in_full, blocks):
+    rows, columns = projected_grad.shape
+    count = rows // SPOTS
+    bf = jnp.bfloat16
+    return pl.pallas_call(
+        rows_back_body,
+        grid=(SPOTS,),
+        out_shape=[jax.ShapeDtypeStruct((count, D), bf)] * SPOTS
+        + [jax.ShapeDtypeStruct((1, D), jnp.float32)],
+        in_specs=[block_spec(count, columns), full_spec(*in_full.shape)] + [ANYWHERE] * SPOTS,
+        out_specs=by_block(count, D) + [full_spec(1, D)],
+        scratch_shapes=[
+            pltpu.VMEM((SPOTS, count, D), bf),
+            pltpu.SemaphoreType.DMA((SPOTS,)),
+        ],
+        compiler_params=params(48),
+        cost_estimate=cost(5 * 10**9, 12 << 20),
+        name="rows_back",
+    )(projected_grad, in_full, *blocks)
+
+
+SMALL = 20
+
+
+def shards_dense(
+    tokens,
+    cotangent,
+    norm_gains,
+    attention_in,
+    attention_out,
+    router_weight,
+    expert_in,
+    expert_out,
+    routes,
+    lengths,
+):
+    row_count = tokens.shape[0]
+    devices_count = lax.axis_size("fsdp")
+    moves = Moves(devices_count)
+    planes, core, spot = moves.planes, moves.core_id, moves.spot
+    ring, first, second, cores = moves.ring, moves.first, moves.second, moves.core
+    experts = devices_count // 2
+    choose = routes.shape[1]
+    capacity = 4 * row_count * choose // (3 * experts)
+    bf, f32 = jnp.bfloat16, jnp.float32
+    own_rows = attention_in.shape[0]
+    lines = HEADS // SPOTS
+    mine = lines * HEAD_DIM
+
+    def low(value):
+        return value.astype(bf)
+
+    flat = jnp.concatenate(
+        [router_weight.T.reshape(-1), norm_gains.reshape(-1), lengths[0].astype(bf)]
+    )
+    riders = [jnp.pad(flat, (0, -flat.shape[0] % WIDE)).reshape(-1, WIDE)]
+    pieces = split_columns(spot, attention_in)
+    near_x = send(tokens, first)
+    riders.append(send(riders[0], ring))
+    out_own = [attention_out, send(attention_out, ring)]
+    weights = [expert_in[0], send(expert_in[0], cores), expert_out[0], send(expert_out[0], cores)]
+    riders, out_own, pieces = tie(riders, out_own, pieces)
+
+    riders.append(send(riders[1], ring))
+    out_own.append(send(out_own[1], ring))
+    traded = [pieces[0]] + [send(pieces[m], moves.spots[m]) for m in range(1, SPOTS)]
+    riders, out_own, traded, near_x = tie(riders, out_own, traded, near_x)
+
+    in_own = [jnp.stack(traded)]
+    riders.append(send(riders[2], ring))
+    out_own.append(send(out_own[2], ring))
+    in_own.append(send(in_own[0], ring))
+    blocks_x = [tokens, near_x, send(tokens, second), send(near_x, second)]
+    riders_all = jnp.stack(riders)
+    for pairs in (moves.spots[1], moves.spots[2], cores):
+        riders_all = jnp.concatenate([riders_all, send(riders_all, pairs)])
+    in_own, blocks_x, riders_all, out_own = tie(in_own, blocks_x, riders_all, out_own)
+
+    in_own.append(send(in_own[1], ring))
+    in_other = [send(item, cores) for item in in_own[:2]]
+    out_other = [send(item, cores) for item in out_own]
+    grads = {(0, 0): [cotangent, send(cotangent, first)]}
+    in_own, in_other, grads = tie(in_own, in_other, grads)
+
+    in_own.append(send(in_own[2], ring))
+    in_other.append(send(in_own[2], cores))
+    grads[0, 1] = [send(item, second) for item in grads[0, 0]]
+
+    ids = jnp.arange(devices_count, dtype=jnp.int32)
+    source = (
+        ((ids % 2) ^ core) * (SPOTS * planes)
+        + ((ids % PLANE // 2) ^ spot) * planes
+        + moves.steps_from[ids // PLANE]
+    )
+    arrived = jnp.take(riders_all, source, axis=0).reshape(devices_count, -1)
+    small_all = arrived[:, : SMALL * own_rows].reshape(devices_count, SMALL, own_rows)
+    small_all = small_all.transpose(1, 0, 2).reshape(SMALL, D)
+    router_full, gain_rows = small_all[: SMALL - 4], widen(small_all[SMALL - 4 :])
+    lengths_all = arrived[:, SMALL * own_rows : SMALL * own_rows + lengths.shape[1]]
+    lengths_all = jnp.take(
+        lengths_all, moves.plane * PLANE + moves.group_spots * 2 + core, axis=0
+    ).astype(jnp.int32)
+    gains = jnp.stack(
+        [
+            lax.dynamic_index_in_dim(
+                gain_rows[n].reshape(lines, SPOTS, HEAD_DIM), spot, 1, keepdims=False
+            ).reshape(mine)
+            for n in (1, 2)
+        ]
+    )
+    places = jnp.arange(row_count, dtype=jnp.int32)
+    _, position = jax.vmap(lambda item: layout(item, row_count))(lengths_all)
+    starts = (places[None] - position).astype(f32)
+    cos_half, sin_half = (table[:, 0] for table in tables(position.reshape(-1)))
+    cos_all = jnp.concatenate([cos_half, cos_half], axis=1)
+    sin_all = jnp.concatenate([-sin_half, sin_half], axis=1)
+
+    expert_ids = jnp.arange(experts, dtype=jnp.int32)
+    match = jnp.sum((routes[:, :, None] == expert_ids[None, None, :]).astype(f32), axis=1)
+    before = (places[:, None] > places[None, :]).astype(bf)
+    rank = jnp.where(match > 0, product(before, match.astype(bf)), -1.0).astype(bf)
+
+    in_own, in_other, grads, starts, cos_all, sin_all, gains, rank = tie(
+        in_own, in_other, grads, starts, cos_all, sin_all, gains, rank
+    )
+    in_other.append(send(in_own[3], cores))
+    own_1 = send(cotangent, ring)
+    projected, normed_all, in_full, sums = project(
+        moves, gain_rows[0:1], blocks_x, in_own, in_other
+    )
+    totals = plane_total(moves, sums)
+    totals, own_1 = tie(totals, own_1)
+
+    near_1 = send(grads[0, 0][1], ring)
+    across_1 = send(own_1, second)
+    attention = (moves, totals, starts, gains, projected, cos_all, sin_all)
+    results = attend_forward(*attention, out_own, out_other)
+    heads, out_full, parts = results[:4], results[4], results[5:]
+    parts, near_1, across_1 = tie(parts, near_1, across_1)
+
+    def cross(parts):
+        return [send(parts[2], second), send(parts[3], second)]
+
+    def gather_near(parts, backs):
+        near = low(widen(parts[1]) + widen(backs[1]))
+        return widen(parts[0]) + widen(backs[0]), send(near, first)
+
+    own_2 = send(own_1, ring)
+    backs = cross(parts)
+    backs, own_2 = tie(backs, own_2)
+    near_2 = send(near_1, ring)
+    home, near = gather_near(parts, backs)
+    home, near, near_2 = tie(home, near, near_2)
+
+    grads[1, 0] = [own_1, near_1]
+    grads[1, 1] = [across_1, send(near_1, second)]
+    grads[2, 0] = [own_2, near_2]
+    inputs = widen(tokens)
+    residual = inputs + (home + widen(near))
+    normed = low(root_norm(residual, gain_rows[3][None]))
+    logits = dot_last(normed, router_full)
+    router_probs = softmax_rows(logits)
+    gate_total = jnp.sum(router_probs * match, axis=1, keepdims=True)
+    gate_values = router_probs * match / gate_total
+    upper = lax.reduce_precision(gate_values, 8, 7)
+    extra = jnp.concatenate(
+        [
+            rank,
+            upper.astype(bf),
+            (gate_values - upper).astype(bf),
+            jnp.zeros((row_count, WIDE - 3 * experts), bf),
+        ],
+        axis=1,
+    )
+    rows = jnp.concatenate([normed, extra], axis=1)
+    rows, grads = tie(rows, grads)
+
+    meta = (moves.device // 2).reshape(1).astype(jnp.int32)
+    saved, done = None, 0
+    row_parts, out_parts = {}, {}
+
+    def run_expert(group, which, blocks):
+        nonlocal saved, done
+        saved, outs, backs = expert_blocks(
+            meta,
+            blocks,
+            grads[group, which],
+            weights,
+            saved,
+            done,
+            planes * SPOTS,
+            capacity,
+            experts,
+        )
+        done += len(blocks)
+        out_parts.setdefault(group, []).extend(outs)
+        row_parts.setdefault(group, []).extend(backs)
+
+    row_near = send(rows, first)
+    row_1 = send(rows, ring)
+    (row_near,) = tie(row_near)
+
+    near_row_1 = send(row_near, ring)
+    across = [send(rows, second), send(row_near, second)]
+    run_expert(0, 0, [rows, row_near])
+    saved, across, row_1 = tie(saved, across, row_1)
+
+    row_2 = send(row_1, ring)
+    across_row_1 = send(row_1, second)
+    grads[2, 1] = [send(item, second) for item in grads[2, 0]]
+    run_expert(0, 1, across)
+    saved, near_row_1, across_row_1, grads[2, 1] = tie(
+        saved, near_row_1, across_row_1, grads[2, 1]
+    )
+
+    near_row_2 = send(near_row_1, ring)
+    own_3 = send(own_2, ring)
+    across = [across_row_1, send(near_row_1, second)]
+    run_expert(1, 0, [row_1, near_row_1])
+    saved, across, row_2 = tie(saved, across, row_2)
+
+    row_3 = send(row_2, ring)
+    across_row_2 = send(row_2, second)
+    run_expert(1, 1, across)
+    saved, near_row_2, own_3, across_row_2 = tie(saved, near_row_2, own_3, across_row_2)
+
+    near_row_3 = send(near_row_2, ring)
+    across = [across_row_2, send(near_row_2, second)]
+    grads[3, 0] = [own_3, send(own_3, first)]
+    across_3 = send(own_3, second)
+    backs_1 = cross(row_parts[1])
+    run_expert(2, 0, [row_2, near_row_2])
+    saved, across, row_3, grads[3, 0], across_3 = tie(
+        saved, across, row_3, grads[3, 0], across_3
+    )
+
+    across_row_3 = send(row_3, second)
+    grads[3, 1] = [across_3, send(grads[3, 0][1], second)]
+    run_expert(2, 1, across)
+    saved, near_row_3, across_row_3, backs_1 = tie(saved, near_row_3, across_row_3, backs_1)
+
+    across = [across_row_3, send(near_row_3, second)]
+    home_1, near_1 = gather_near(row_parts[1], backs_1)
+    backs_2 = cross(row_parts[2])
+    run_expert(3, 0, [row_3, near_row_3])
+    saved, across, grads[3, 1], home_1, near_1, backs_2 = tie(
+        saved, across, grads[3, 1], home_1, near_1, backs_2
+    )
+
+    total = send(low(home_1 + widen(near_1)), ring)
+    home_2, near_2 = gather_near(row_parts[2], backs_2)
+    backs_0 = cross(row_parts[0])
+    run_expert(3, 1, across)
+    saved, total, home_2, near_2 = tie(saved, total, home_2, near_2)
+
+    total = send(low(widen(total) + (home_2 + widen(near_2))), ring)
+    backs_3 = cross(row_parts[3])
+    x_rows, dy_rows, m_own, m_other, du_own, du_other = saved
+    in_theirs = dot_first(x_rows, du_other)
+    total, backs_3, backs_0, in_theirs = tie(total, backs_3, backs_0, in_theirs)
+
+    home_3, near_3 = gather_near(row_parts[3], backs_3)
+    home_0, near_0 = gather_near(row_parts[0], backs_0)
+    in_theirs = send(in_theirs, cores)
+    out_theirs = dot_first(m_other, dy_rows)
+    home_3, near_3, home_0, near_0, out_theirs = tie(home_3, near_3, home_0, near_0, out_theirs)
+
+    total = send(low(widen(total) + (home_3 + widen(near_3))), ring)
+    out_theirs = send(out_theirs, cores)
+    out_backs = {1: cross(out_parts[1])}
+    (total,) = tie(total)
+    row_total = widen(total) + (home_0 + widen(near_0))
+
+    upstream = widen(cotangent)
+    dispatch_grad = row_total[:, :D]
+    gate_grad = jnp.sum(row_total[:, D : D + 2 * experts].reshape(row_count, experts, 2), axis=2)
+    chosen_grad = (
+        match * (gate_grad - jnp.sum(gate_grad * gate_values, axis=1, keepdims=True)) / gate_total
+    )
+    logit_grad = low(
+        router_probs * (chosen_grad - jnp.sum(chosen_grad * router_probs, axis=1, keepdims=True))
+    )
+    normed_grad = dispatch_grad + product(logit_grad, router_full)
+    _, second_back = jax.vjp(root_norm, residual, gain_rows[3])
+    residual_norm_grad, second_gain_grad = second_back(normed_grad)
+    residual_grad = upstream + residual_norm_grad
+    branch_grad = low(residual_grad)
+    branch_near = send(branch_grad, first)
+    branch_near, out_backs = tie(branch_near, out_backs)
+
+    branch_blocks = [
+        branch_grad,
+        branch_near,
+        send(branch_grad, second),
+        send(branch_near, second),
+    ]
+    expert_in_grad = dot_first(x_rows, du_own) + in_theirs
+    expert_out_grad = dot_first(m_own, dy_rows) + out_theirs
+    router_grad = dot_first(logit_grad, normed)
+    branch_blocks, expert_in_grad, expert_out_grad, router_grad = tie(
+        branch_blocks, expert_in_grad, expert_out_grad, router_grad
+    )
+
+    out_homes = {1: gather_near(out_parts[1], out_backs[1])}
+    out_backs[2] = cross(out_parts[2])
+    dq, dk, dv, dots, own_grad, other_grad, gain_grads = attend_backward(
+        *attention, heads, out_full, branch_blocks
+    )
+    dots, out_homes, out_backs = tie(dots, out_homes, out_backs)
+
+    out_total = send(low(out_homes[1][0] + widen(out_homes[1][1])), ring)
+    other_grad = send(other_grad, cores)
+    out_homes[2] = gather_near(out_parts[2], out_backs[2])
+    out_backs[3] = cross(out_parts[3])
+    dots = plane_total(moves, dots)
+    projected_grad, *in_grads = project_back(
+        moves, totals, dots, gains, projected, dq, dk, dv, normed_all
+    )
+    in_grads, out_total, out_homes, out_backs, other_grad = tie(
+        in_grads, out_total, out_homes, out_backs, other_grad
+    )
+
+    others = [send(in_grads[planes + k], cores) for k in range(planes)]
+    in_sums = [widen(in_grads[k]) + widen(others[k]) for k in range(planes)]
+    out_sums = [widen(own_grad[k]) + widen(other_grad[k]) for k in range(planes)]
+    in_total = send(low(in_sums[1]), ring)
+    out_share = send(low(out_sums[1]), ring)
+    *parts, first_gain_grad = rows_back(projected_grad, in_full, blocks_x)
+    in_total, out_share, parts = tie(in_total, out_share, parts)
+
+    backs = cross(parts)
+    in_total = send(low(widen(in_total) + in_sums[2]), ring)
+    out_share = send(low(widen(out_share) + out_sums[2]), ring)
+    out_total = send(low(widen(out_total) + out_homes[2][0] + widen(out_homes[2][1])), ring)
+    in_total, out_share, backs = tie(in_total, out_share, backs)
+
+    home, near = gather_near(parts, backs)
+    in_total = send(low(widen(in_total) + in_sums[3]), ring)
+    out_share = widen(send(low(widen(out_share) + out_sums[3]), ring)) + out_sums[0]
+    out_homes[3] = gather_near(out_parts[3], out_backs[3])
+    out_backs[0] = cross(out_parts[0])
+    in_total, home, near, out_total, out_homes, out_backs = tie(
+        in_total, home, near, out_total, out_homes, out_backs
+    )
+
+    out_total = send(low(widen(out_total) + out_homes[3][0] + widen(out_homes[3][1])), ring)
+    in_total = low(widen(in_total) + in_sums[0])
+    traded = [in_total[0]] + [send(in_total[m], moves.spots[m]) for m in range(1, SPOTS)]
+    in_share = join_columns(spot, traded)
+    out_homes[0] = gather_near(out_parts[0], out_backs[0])
+    output = low(residual + (widen(out_total) + (out_homes[0][0] + widen(out_homes[0][1]))))
+    _, first_back = jax.vjp(lambda value: root_norm(value, gain_rows[0]), inputs)
+    (input_norm_grad,) = first_back(home + widen(near))
+    input_grad = residual_grad + input_norm_grad
+
+    here = (jnp.arange(SPOTS, dtype=jnp.int32) == spot)[None, :, None]
+
+    def own_gain(row):
+        return jnp.where(here, row.reshape(lines, 1, HEAD_DIM), 0.0).reshape(1, D)
+
+    small_grad = jnp.concatenate(
+        [
+            router_grad,
+            first_gain_grad,
+            own_gain(gain_grads[0]),
+            own_gain(gain_grads[1]),
+            second_gain_grad[None],
+        ]
+    )
+    span = PLANE * own_rows
+
+    def plane_part(step):
+        return lax.dynamic_slice_in_dim(small_grad, moves.planes_back[step] * span, span, 1)
+
+    small_total = plane_part(1)
+    for step in (*range(2, planes), 0):
+        small_total = plane_part(step) + send(small_total, ring)
+    for bit, pairs in ((spot // 2, moves.spots[2]), (spot % 2, moves.spots[1])):
+        span //= 2
+        kept = lax.dynamic_slice_in_dim(small_total, bit * span, span, 1)
+        given = lax.dynamic_slice_in_dim(small_total, (1 - bit) * span, span, 1)
+        small_total = kept + send(given, pairs)
+    left, right = small_total[:, :own_rows], small_total[:, own_rows:]
+    small_share = jnp.where(core == 0, left, right) + send(
+        jnp.where(core == 0, right, left), cores
+    )
+    return (
+        output,
+        input_grad,
+        small_share[SMALL - 4 :],
+        in_share,
+        out_share,
+        small_share[: SMALL - 4].T,
+        expert_in_grad[None],
+        expert_out_grad[None],
+    )
+
+
+def shards(*arguments):
+    routes = arguments[8]
+    experts = lax.axis_size("fsdp") // 2
+    if 2 * routes.shape[1] >= experts and HEADS == experts:
+        return shards_dense(*arguments)
+    return shards_routed(*arguments)
+
+
 def solution(mesh):
     in_specs = (
         P("fsdp", None),

time: 2890 us -> 819 us (0.28)
  waiting for transfers between devices: 2010 us -> 349 us
  blocking collectives: 367 us -> 0 us
  Pallas kernels: 0 us -> 177 us
  matrix products: 203 us -> 47.2 us
  local copies, waits for them, and re-layouts: 119 us -> 51.4 us
  starting transfers between devices: 72.4 us -> 129 us
  other arithmetic: 90.7 us -> 52.3 us
    all_to_all x4 -> x0, waiting for transfers between devices: 1060 us -> none  [the longest x1 358 us: shards(): lax.all_to_all(grad_rows, 'fsdp', split_axis=0, concat_axis=0, tiled=True)]
    reduce_scatter x2 -> x0, waiting for transfers between devices: 620 us -> none  [the longest x1 440 us: shards(): lax.psum_scatter(attention_in_grad, 'fsdp', scatter_dimension=0, tiled=True)]
    all_gather x2 -> x0, blocking collectives: 367 us -> none  [the longest x1 323 us: shards(): lax.all_gather(router_weight, 'fsdp', axis=0, tiled=True)]
    ppermute x0 -> x123, waiting for transfers between devices: none -> 349 us  [send(): return lax.ppermute(value, 'fsdp', pairs)]
    unnamed x8 -> x0, waiting for transfers between devices: 192 us -> none
    pallas_call x0 -> x15, Pallas kernels: none -> 177 us  [the longest x8 103 us: expert_blocks(): pl.pallas_call(functools.partial(expert_body, index, cap, experts, blocks...]
    all_gather x2 -> x0, waiting for transfers between devices: 145 us -> none  [the longest x1 90.6 us: shards(): lax.all_gather(attention_in, 'fsdp', axis=0, tiled=True)]
    ppermute x0 -> x123, starting transfers between devices: none -> 129 us  [send(): return lax.ppermute(value, 'fsdp', pairs)]
  transfers between devices with their start and end apart: 10 -> 123, of which waited for: 10 -> 50; matrix products, arithmetic and copies ran while one was open for 8% -> 15% of each run, Pallas kernels for 0% -> 17%
where the time goes in v3:
time: 819 us; the launch traced here: 810 us
  waiting for transfers between devices  349 us (43%)
  Pallas kernels  177 us (22%)
  starting transfers between devices  129 us (16%)
  other arithmetic  52.3 us (6%)
  local copies, waits for them, and re-layouts  51.4 us (6%)
  matrix products  47.2 us (6%)
    ppermute x123, waiting for transfers between devices, send(): return lax.ppermute(value, 'fsdp', pairs)  349 us
    ppermute x123, starting transfers between devices, send(): return lax.ppermute(value, 'fsdp', pairs)  129 us
    pallas_call x8, Pallas kernels, expert_blocks(): pl.pallas_call(functools.partial(expert_body, index, cap, experts, blocks...  103 us
    dot_general x5, matrix products, dot_first(): lax.dot_general(left, right, (((0,), (0,)), ((), ())), preferred_element_...  43.7 us
    unnamed x229, local copies, waits for them, and re-layouts  28.2 us
    convert_element_type x26, other arithmetic, low(): return value.astype(bf)  24 us
    pallas_call x1, Pallas kernels, attend_backward(): pl.pallas_call(backward_body, grid=(SPOTS,), out_shape=[shape((rows, mine...  21.2 us
  transfers between devices with their start and end apart: 123, of which 50 were waited for; matrix products, arithmetic and copies ran while one was open for 15% of the time, Pallas kernels for 17%

profile of v3, /device:TPU:0, one launch (start us, length us, event | category | flops | bytes accessed | tf_op | source)
XLA Modules:
  0.0 809.6 jit_solution(14319782337070137654)
XLA Ops:
  2.8 4.1 collective-permute-start
  46.6 4.2 collective-permute-done.13
  67.5 12.0 %collective-permute-done.16.refs_6_ = bf16[4,64,1536]{2,1,0:T(8,128)(2,1)} collective-permute-done((bf16[4,64,1536]{2,1,0:T(8,128)(2,1)}, bf16[4,64,1536]{2,1,0:T(8,128)(2,1)}, u32[]{:S(2)}, u32[]{:S(2)}) %collective-permute-start.16) | collective-permute-done | bytes 786464 | tf_op jit(solution)/shard_map/ppermute | solution.py:335
  86.2 13.0 %collective-permute-done.20.refs_7_ = bf16[4,64,1536]{2,1,0:T(8,128)(2,1)} collective-permute-done((bf16[4,64,1536]{2,1,0:T(8,128)(2,1)}, bf16[4,64,1536]{2,1,0:T(8,128)(2,1)}, u32[]{:S(2)}, u32[]{:S(2)}) %collective-permute-start.20) | collective-permute-done | bytes 786464 | tf_op jit(solution)/shard_map/ppermute | solution.py:335
  109.0 11.1 %project.1 = (f32[768,1536]{1,0:T(8,128)}, bf16[768,2048]{1,0:T(8,128)(2,1)S(1)}, bf16[2048,1536]{1,0:T(8,128)(2,1)}, f32[2,4,192]{2,1,0:T(4,128)S(1)}) custom-call(s32[6]{0:T(128)S(1)} %pad_add_fusion.meta, f32[1,2048]{1,0:T(1,128)S(1)} %slice.155.gain, bf16[192,2048]{1,0:T(8,128)(2,1)S(1)} %copy-done, ...), custom_call_target="tpu_custom_call" | custom-call | flops 5000000000 | bytes 20971520 | tf_op jit(solution)/shard_map/project/pallas_call | solution.py:652
  130.5 14.7 %collective-permute-done.27.refs_2_ = bf16[192,2048]{1,0:T(8,128)(2,1)} collective-permute-done((bf16[192,2048]{1,0:T(8,128)(2,1)}, bf16[192,2048]{1,0:T(8,128)(2,1)}, u32[]{:S(2)}, u32[]{:S(2)}) %collective-permute-start.27) | collective-permute-done | bytes 786464 | tf_op jit(solution)/shard_map/ppermute | solution.py:335
  153.4 11.0 %attend_forward.1 = (bf16[768,512]{1,0:T(8,128)(2,1)S(1)}, bf16[768,512]{1,0:T(8,128)(2,1)S(1)}, bf16[768,512]{1,0:T(8,128)(2,1)S(1)}, bf16[768,512]{1,0:T(8,128...) custom-call(s32[6]{0:T(128)S(1)} %pad_add_fusion.meta, ...), custom_call_target="tpu_custom_call" | custom-call | flops 5000000000 | bytes 20971520 | tf_op jit(solution)/shard_map/attend_forward/pallas_call | solution.py:746
  170.9 8.1 %collective-permute-done.36.refs_2_ = bf16[192,2048]{1,0:T(8,128)(2,1)} collective-permute-done((bf16[192,2048]{1,0:T(8,128)(2,1)}, bf16[192,2048]{1,0:T(8,128)(2,1)}, u32[]{:S(2)}, u32[]{:S(2)}) %collective-permute-start.36) | collective-permute-done | bytes 786464 | tf_op jit(solution)/shard_map/ppermute | solution.py:335
  180.0 8.4 %collective-permute-done.35 = bf16[192,2048]{1,0:T(8,128)(2,1)S(1)} collective-permute-done((bf16[192,2048]{1,0:T(8,128)(2,1)S(1)}, bf16[192,2048]{1,0:T(8,128)(2,1)S(1)}, u32[]{:S(2)}, u32[]{:S(2)}) %collective-permute-start.35) | collective-permute-done | bytes 786464 | tf_op jit(solution)/shard_map/ppermute | solution.py:335
  194.7 15.3 %collective-permute-done.37 = bf16[192,2048]{1,0:T(8,128)(2,1)} collective-permute-done((bf16[192,2048]{1,0:T(8,128)(2,1)}, bf16[192,2048]{1,0:T(8,128)(2,1)}, u32[]{:S(2)}, u32[]{:S(2)}) %collective-permute-start.37) | collective-permute-done | bytes 786464 | tf_op jit(solution)/shard_map/ppermute | solution.py:335
  218.5 18.1 %collective-permute-done.40.refs_1_ = bf16[192,2176]{1,0:T(8,128)(2,1)} collective-permute-done((bf16[192,2176]{1,0:T(8,128)(2,1)}, bf16[192,2176]{1,0:T(8,128)(2,1)}, u32[]{:S(2)}, u32[]{:S(2)}) %collective-permute-start.40) | collective-permute-done | bytes 835616 | tf_op jit(solution)/shard_map/ppermute | solution.py:335
  240.7 12.8 %expert_blocks.8 = (bf16[2048,2048]{1,0:T(8,128)(2,1)}, bf16[2048,2048]{1,0:T(8,128)(2,1)}, bf16[2048,512]{1,0:T(8,128)(2,1)}, bf16[2048,512]{1,0:T(8,128)(2,1)}...) custom-call(s32[1]{0:T(128)} %bitcast.26.meta, ...), custom_call_target="tpu_custom_call" | custom-call | flops 7600000000 | bytes 31457280 | tf_op jit(solution)/shard_map/expert_blocks/pallas_call | solution.py:529
  257.2 12.8 %expert_blocks.9 = (bf16[2048,2048]{1,0:T(8,128)(2,1)}, bf16[2048,2048]{1,0:T(8,128)(2,1)}, bf16[2048,512]{1,0:T(8,128)(2,1)}, bf16[2048,512]{1,0:T(8,128)(2,1)}...) custom-call(s32[1]{0:T(128)} %bitcast.26.meta, ...), custom_call_target="tpu_custom_call", output_to_operand_aliasing={{0}: (9, {}), {1}: (10, {}), {2}: (11, {}), {3}: (12, {}), ... | custom-call | flops 7600000000 | bytes 31457280 | tf_op jit(solution)/shard_map/expert_blocks/pallas_call | solution.py:529
  270.0 4.9 collective-permute-done.48.refs_2_
  274.9 8.4 %collective-permute-done.49.refs_3_ = bf16[192,2048]{1,0:T(8,128)(2,1)} collective-permute-done((bf16[192,2048]{1,0:T(8,128)(2,1)}, bf16[192,2048]{1,0:T(8,128)(2,1)}, u32[]{:S(2)}, u32[]{:S(2)}) %collective-permute-start.49) | collective-permute-done | bytes 786464 | tf_op jit(solution)/shard_map/ppermute | solution.py:335
  286.1 12.9 %expert_blocks.10 = (bf16[2048,2048]{1,0:T(8,128)(2,1)}, bf16[2048,2048]{1,0:T(8,128)(2,1)}, bf16[2048,512]{1,0:T(8,128)(2,1)}, bf16[2048,512]{1,0:T(8,128)(2,1)...) custom-call(s32[1]{0:T(128)} %bitcast.26.meta, ...), custom_call_target="tpu_custom_call", output_to_operand_aliasing={{0}: (9, {}), {1}: (10, {}), {2}: (11, {}), {3}: (12, {}), ... | custom-call | flops 7600000000 | bytes 31457280 | tf_op jit(solution)/shard_map/expert_blocks/pallas_call | solution.py:529
  304.4 12.8 %expert_blocks.11 = (bf16[2048,2048]{1,0:T(8,128)(2,1)}, bf16[2048,2048]{1,0:T(8,128)(2,1)}, bf16[2048,512]{1,0:T(8,128)(2,1)}, bf16[2048,512]{1,0:T(8,128)(2,1)...) custom-call(s32[1]{0:T(128)} %bitcast.26.meta, ...), custom_call_target="tpu_custom_call", output_to_operand_aliasing={{0}: (9, {}), {1}: (10, {}), {2}: (11, {}), {3}: (12, {}), ... | custom-call | flops 7600000000 | bytes 31457280 | tf_op jit(solution)/shard_map/expert_blocks/pallas_call | solution.py:529
  317.2 4.0 collective-permute-done.53.refs_2_
  324.3 13.0 %expert_blocks.12 = (bf16[2048,2048]{1,0:T(8,128)(2,1)}, bf16[2048,2048]{1,0:T(8,128)(2,1)}, bf16[2048,512]{1,0:T(8,128)(2,1)}, bf16[2048,512]{1,0:T(8,128)(2,1)...) custom-call(s32[1]{0:T(128)} %bitcast.26.meta, ...), custom_call_target="tpu_custom_call", output_to_operand_aliasing={{0}: (9, {}), {1}: (10, {}), {2}: (11, {}), {3}: (12, {}), ... | custom-call | flops 7600000000 | bytes 31457280 | tf_op jit(solution)/shard_map/expert_blocks/pallas_call | solution.py:529
  338.5 4.2 collective-permute-done.57.refs_3_
  347.6 12.8 %expert_blocks.13 = (bf16[2048,2048]{1,0:T(8,128)(2,1)}, bf16[2048,2048]{1,0:T(8,128)(2,1)}, bf16[2048,512]{1,0:T(8,128)(2,1)}, bf16[2048,512]{1,0:T(8,128)(2,1)...) custom-call(s32[1]{0:T(128)} %bitcast.26.meta, ...), custom_call_target="tpu_custom_call", output_to_operand_aliasing={{0}: (9, {}), {1}: (10, {}), {2}: (11, {}), {3}: (12, {}), ... | custom-call | flops 7600000000 | bytes 31457280 | tf_op jit(solution)/shard_map/expert_blocks/pallas_call | solution.py:529
  362.6 6.6 collective-permute-done.60.refs_0_
  372.5 13.3 %expert_blocks.14 = (bf16[2048,2048]{1,0:T(8,128)(2,1)}, bf16[2048,2048]{1,0:T(8,128)(2,1)}, bf16[2048,512]{1,0:T(8,128)(2,1)}, bf16[2048,512]{1,0:T(8,128)(2,1)...) custom-call(s32[1]{0:T(128)} %bitcast.26.meta, ...), custom_call_target="tpu_custom_call", output_to_operand_aliasing={{0}: (9, {}), {1}: (10, {}), {2}: (11, {}), {3}: (12, {}), ... | custom-call | flops 7600000000 | bytes 31457280 | tf_op jit(solution)/shard_map/expert_blocks/pallas_call | solution.py:529
  385.9 18.6 %collective-permute-done.64.refs_3_ = bf16[192,2048]{1,0:T(8,128)(2,1)} collective-permute-done((bf16[192,2048]{1,0:T(8,128)(2,1)}, bf16[192,2048]{1,0:T(8,128)(2,1)}, u32[]{:S(2)}, u32[]{:S(2)}) %collective-permute-start.64) | collective-permute-done | bytes 786464 | tf_op jit(solution)/shard_map/ppermute | solution.py:335
  406.5 6.9 collective-permute-done.63.refs_1_
  418.1 5.7 collective-permute-start.68
  423.8 12.8 %expert_blocks.15 = (bf16[2048,2048]{1,0:T(8,128)(2,1)}, bf16[2048,2048]{1,0:T(8,128)(2,1)}, bf16[2048,512]{1,0:T(8,128)(2,1)}, bf16[2048,512]{1,0:T(8,128)(2,1)...) custom-call(s32[1]{0:T(128)} %bitcast.26.meta, ...), custom_call_target="tpu_custom_call", output_to_operand_aliasing={{0}: (9, {}), {1}: (10, {}), {2}: (11, {}), {3}: (12, {}), ... | custom-call | flops 7600000000 | bytes 31457280 | tf_op jit(solution)/shard_map/expert_blocks/pallas_call | solution.py:529
  443.8 13.6 %fusion.52 = f32[2048,1024]{1,0:T(8,128)} fusion(bf16[2048,2048]{1,0:T(8,128)(2,1)} %get-tuple-element.573, bf16[2048,1024]{1,0:T(8,128)(2,1)S(1)} %copy-done.40), kind=kOutput, calls=%fused_computation.230 | convolution fusion | flops 8589934592 | bytes 20971520 | tf_op jit(solution)/shard_map/dot_general | solution.py:71
  457.4 6.0 fusion.53
  468.6 8.9 %collective-permute-done.76 = bf16[192,2176]{1,0:T(8,128)(2,1)S(1)} collective-permute-done((bf16[192,2176]{1,0:T(8,128)(2,1)S(1)}, bf16[192,2176]{1,0:T(8,128)(2,1)S(1)}, u32[]{:S(2)}, u32[]{:S(2)}) %collective-permute-start.76) | collective-permute-done | bytes 835616 | tf_op jit(solution)/shard_map/ppermute | solution.py:335
  477.5 12.7 %collective-permute-done.75 = bf16[192,2176]{1,0:T(8,128)(2,1)S(1)} collective-permute-done((bf16[192,2176]{1,0:T(8,128)(2,1)S(1)}, bf16[192,2176]{1,0:T(8,128)(2,1)S(1)}, u32[]{:S(2)}, u32[]{:S(2)}) %collective-permute-start.75) | collective-permute-done | bytes 835616 | tf_op jit(solution)/shard_map/ppermute | solution.py:335
  492.9 10.4 %collective-permute-done.77 = bf16[192,2176]{1,0:T(8,128)(2,1)S(1)} collective-permute-done((bf16[192,2176]{1,0:T(8,128)(2,1)S(1)}, bf16[192,2176]{1,0:T(8,128)(2,1)S(1)}, u32[]{:S(2)}, u32[]{:S(2)}) %collective-permute-start.77) | collective-permute-done | bytes 835616 | tf_op jit(solution)/shard_map/ppermute | solution.py:335
  523.0 15.2 %collective-permute-done.78.refs_1_ = bf16[192,2048]{1,0:T(8,128)(2,1)} collective-permute-done((bf16[192,2048]{1,0:T(8,128)(2,1)S(1)}, bf16[192,2048]{1,0:T(8,128)(2,1)}, u32[]{:S(2)}, u32[]{:S(2)}) %collective-permute-start.78) | collective-permute-done | bytes 786464 | tf_op jit(solution)/shard_map/ppermute | solution.py:335
  543.3 10.5 %convolution_add_fusion.1 = f32[512,2048]{1,0:T(8,128)} fusion(f32[512,2048]{1,0:T(8,128)} %collective-permute-done.84, bf16[2048,512]{1,0:T(8,128)(2,1)S(1)} %copy-done.41, bf16[2048,2048]{1,0:T(8,128)(2,1)} %get-tuple-element.585), kind=kOutput, calls=%fused_computation.8 | convolution fusion | flops 4296015872 | bytes 18874368 | tf_op jit(solution)/shard_map/dot_general | solution.py:71
  556.0 12.6 %convolution_add_fusion = f32[2048,1024]{1,0:T(8,128)} fusion(f32[2048,1024]{1,0:T(8,128)} %collective-permute-done.83, bf16[2048,2048]{1,0:T(8,128)(2,1)S(1)} %bitcast.111, bf16[2048,1024]{1,0:T(8,128)(2,1)S(1)} %copy-done.39), kind=kOutput, calls=%fused_computation.7 | convolution fusion | flops 8592031744 | bytes 29360128 | tf_op jit(solution)/shard_map/dot_general | solution.py:71
  569.7 21.2 %attend_backward.1 = (f32[768,512]{1,0:T(8,128)}, f32[768,512]{1,0:T(8,128)}, bf16[768,512]{1,0:T(8,128)(2,1)S(1)}, f32[2,4,192]{2,1,0:T(4,128)S(1)}, bf16[4,64,...) custom-call(s32[6]{0:T(128)S(1)} %copy-done.6, f32[2,4,192]{2,1,0:T(4,128)S(1)} %copy-done.3, ...), custom_call_target="tpu_custom_call" | custom-call | flops 7000000000 | bytes 26214400 | tf_op jit(solution)/shard_map/attend_backward/pallas_call | solution.py:834
  601.4 15.0 %project_back.1 = (bf16[768,1536]{1,0:T(8,128)(2,1)}, bf16[4,64,1536]{2,1,0:T(8,128)(2,1)}, bf16[4,64,1536]{2,1,0:T(8,128)(2,1)}, bf16[4,64,1536]{2,1,0:T(8,128)...) custom-call(s32[6]{0:T(128)} %copy-done.5, ...), custom_call_target="tpu_custom_call" | custom-call | flops 5000000000 | bytes 31457280 | tf_op jit(solution)/shard_map/project_back/pallas_call | solution.py:926
  617.5 13.7 %rows_back.1 = (bf16[192,2048]{1,0:T(8,128)(2,1)S(1)}, bf16[192,2048]{1,0:T(8,128)(2,1)S(1)}, bf16[192,2048]{1,0:T(8,128)(2,1)S(1)}, bf16[192,2048]{1,0:T(8,128)(2,1)S(1)}, f32[1,2048]{1,0:T(1,128)S(1)}) custom-call(bf16[768,1536]{1,0:T(8,128)(2,1)} %get-tuple-element.634.dp_ref, bf16[2048,1536]{1,0:T(8,128)(2,1)} %get-tuple-element.635.in_w, ...), custom_call_target="tpu_custom_call" | custom-call | flops 5000000000 | bytes 12582912 | tf_op jit(solution)/shard_map/rows_back/pallas_call | solution.py:977
  650.2 18.6 %collective-permute-done.115 = f32[20,256]{1,0:T(8,128)S(1)} collective-permute-done((f32[20,256]{1,0:T(8,128)S(1)}, f32[20,256]{1,0:T(8,128)S(1)}, u32[]{:S(2)}, u32[]{:S(2)}) %collective-permute-start.115) | collective-permute-done | bytes 20512 | tf_op jit(solution)/shard_map/ppermute | solution.py:335
  676.1 8.5 %collective-permute-done.90 = bf16[192,2048]{1,0:T(8,128)(2,1)S(1)} collective-permute-done((bf16[192,2048]{1,0:T(8,128)(2,1)S(1)}, bf16[192,2048]{1,0:T(8,128)(2,1)S(1)}, u32[]{:S(2)}, u32[]{:S(2)}) %collective-permute-start.90) | collective-permute-done | bytes 786464 | tf_op jit(solution)/shard_map/ppermute | solution.py:335
  690.8 5.1 collective-permute-done.97
  695.9 16.7 %collective-permute-done.96 = bf16[4,64,1536]{2,1,0:T(8,128)(2,1)S(1)} collective-permute-done((bf16[4,64,1536]{2,1,0:T(8,128)(2,1)S(1)}, bf16[4,64,1536]{2,1,0:T(8,128)(2,1)S(1)}, u32[]{:S(2)}, u32[]{:S(2)}) %collective-permute-start.96) | collective-permute-done | bytes 786464 | tf_op jit(solution)/shard_map/ppermute | solution.py:335
  718.1 20.5 %collective-permute-done.100 = bf16[64,2048]{1,0:T(8,128)(2,1)S(1)} collective-permute-done((bf16[64,2048]{1,0:T(8,128)(2,1)S(1)}, bf16[64,2048]{1,0:T(8,128)(2,1)S(1)}, u32[]{:S(2)}, u32[]{:S(2)}) %collective-permute-start.100) | collective-permute-done | bytes 262176 | tf_op jit(solution)/shard_map/ppermute | solution.py:335
  744.6 14.2 %collective-permute-done.108 = bf16[192,2048]{1,0:T(8,128)(2,1)S(1)} collective-permute-done((bf16[192,2048]{1,0:T(8,128)(2,1)S(1)}, bf16[192,2048]{1,0:T(8,128)(2,1)S(1)}, u32[]{:S(2)}, u32[]{:S(2)}) %collective-permute-start.108) | collective-permute-done | bytes 786464 | tf_op jit(solution)/shard_map/ppermute | solution.py:335
  758.7 8.4 %collective-permute-done.109 = bf16[192,2048]{1,0:T(8,128)(2,1)S(1)} collective-permute-done((bf16[192,2048]{1,0:T(8,128)(2,1)S(1)}, bf16[192,2048]{1,0:T(8,128)(2,1)S(1)}, u32[]{:S(2)}, u32[]{:S(2)}) %collective-permute-start.109) | collective-permute-done | bytes 786464 | tf_op jit(solution)/shard_map/ppermute | solution.py:335
  770.9 8.3 %collective-permute-done.105 = bf16[192,2048]{1,0:T(8,128)(2,1)S(1)} collective-permute-done((bf16[192,2048]{1,0:T(8,128)(2,1)S(1)}, bf16[192,2048]{1,0:T(8,128)(2,1)S(1)}, u32[]{:S(2)}, u32[]{:S(2)}) %collective-permute-start.105) | collective-permute-done | bytes 786464 | tf_op jit(solution)/shard_map/ppermute | solution.py:335
  779.1 7.2 collective-permute-done.104
  799.3 8.7 %collective-permute-done.110 = bf16[192,2048]{1,0:T(8,128)(2,1)S(1)} collective-permute-done((bf16[192,2048]{1,0:T(8,128)(2,1)S(1)}, bf16[192,2048]{1,0:T(8,128)(2,1)S(1)}, u32[]{:S(2)}, u32[]{:S(2)}) %collective-permute-start.110) | collective-permute-done | bytes 786464 | tf_op jit(solution)/shard_map/ppermute | solution.py:335
  (605 shorter events, 266.3 us)
Async XLA Ops:
  8.5 25.0 %collective-permute-start.7 = (bf16[192,2048]{1,0:T(8,128)(2,1)}, bf16[192,2048]{1,0:T(8,128)(2,1)S(1)}, u32[]{:S(2)}, u32[]{:S(2)}) collective-permute-start(bf16[192,2048]{1,0:T(8,128)(2,1)} %refs_0_.2), channel_id=1, source_target_pairs={{0,2},{1,5},{2,0},{3,7},{4,6},{5,1},{6,4},{7,3},{8,10},{9,13},{10,... | collective-permute-start | bytes 2359304 | tf_op jit(solution)/shard_map/ppermute | solution.py:335
  26.6 29.9 %collective-permute-start.9 = (bf16[192,2048]{1,0:T(8,128)(2,1)}, bf16[192,2048]{1,0:T(8,128)(2,1)S(1)}, u32[]{:S(2)}, u32[]{:S(2)}) collective-permute-start(bf16[192,2048]{1,0:T(8,128)(2,1)} %refs_0_.2), channel_id=1, source_target_pairs={{0,4},{1,3},{2,6},{3,1},{4,0},{5,7},{6,2},{7,5},{8,12},{9,11},{10,... | collective-permute-start | bytes 2359304 | tf_op jit(solution)/shard_map/ppermute | solution.py:335
  128.3 39.7 %collective-permute-start.32 = (bf16[192,2048]{1,0:T(8,128)(2,1)}, bf16[192,2048]{1,0:T(8,128)(2,1)}, u32[]{:S(2)}, u32[]{:S(2)}) collective-permute-start(bf16[192,2048]{1,0:T(8,128)(2,1)} %collective-permute-done.19.refs_3_), channel_id=1, source_target_pairs={{0,16},{1,17},{2,18},{3,19},{4,20},{5,21},{6,22},{7,23},{8,0},{9,1... | collective-permute-start | bytes 2359304 | tf_op jit(solution)/shard_map/ppermute | solution.py:335
  149.0 29.9 %collective-permute-start.36 = (bf16[192,2048]{1,0:T(8,128)(2,1)}, bf16[192,2048]{1,0:T(8,128)(2,1)}, u32[]{:S(2)}, u32[]{:S(2)}) collective-permute-start(bf16[192,2048]{1,0:T(8,128)(2,1)} %collective-permute-done.27.refs_2_), channel_id=1, source_target_pairs={{0,16},{1,17},{2,18},{3,19},{4,20},{5,21},{6,22},{7,23},{8,0},{9,1... | collective-permute-start | bytes 2359304 | tf_op jit(solution)/shard_map/ppermute | solution.py:335
  170.1 70.0 %collective-permute-start.41 = (bf16[2048,1024]{1,0:T(8,128)(2,1)}, bf16[2048,1024]{1,0:T(8,128)(2,1)}, u32[]{:S(2)}, u32[]{:S(2)}) collective-permute-start(bf16[2048,1024]{1,0:T(8,128)(2,1)} %bitcast.27.refs_4_), channel_id=1, source_target_pairs={{0,1},{1,0},{2,3},{3,2},{4,5},{5,4},{6,7},{7,6},{8,9},{9,8},{10,11... | collective-permute-start | bytes 12582920 | tf_op jit(solution)/shard_map/ppermute | solution.py:335
  170.1 24.6 %collective-permute-start.38 = (bf16[192,2048]{1,0:T(8,128)(2,1)}, bf16[192,2048]{1,0:T(8,128)(2,1)}, u32[]{:S(2)}, u32[]{:S(2)}) collective-permute-start(bf16[192,2048]{1,0:T(8,128)(2,1)} %collective-permute-done.32.refs_3_), channel_id=1, source_target_pairs={{0,16},{1,17},{2,18},{3,19},{4,20},{5,21},{6,22},{7,23},{8,0},{9,1... | collective-permute-start | bytes 2359304 | tf_op jit(solution)/shard_map/ppermute | solution.py:335
  189.7 49.8 %collective-permute-start.42 = (bf16[512,2048]{1,0:T(8,128)(2,1)}, bf16[512,2048]{1,0:T(8,128)(2,1)}, u32[]{:S(2)}, u32[]{:S(2)}) collective-permute-start(bf16[512,2048]{1,0:T(8,128)(2,1)} %bitcast.28.refs_6_), channel_id=1, source_target_pairs={{0,1},{1,0},{2,3},{3,2},{4,5},{5,4},{6,7},{7,6},{8,9},{9,8},{10,11... | collective-permute-start | bytes 6291464 | tf_op jit(solution)/shard_map/ppermute | solution.py:335
  190.2 27.5 %collective-permute-start.39 = (bf16[192,2048]{1,0:T(8,128)(2,1)}, bf16[192,2048]{1,0:T(8,128)(2,1)}, u32[]{:S(2)}, u32[]{:S(2)}) collective-permute-start(bf16[192,2048]{1,0:T(8,128)(2,1)} %collective-permute-done.32.refs_3_), channel_id=1, source_target_pairs={{0,4},{1,3},{2,6},{3,1},{4,0},{5,7},{6,2},{7,5},{8,12},{9,11},{10,... | collective-permute-start | bytes 2359304 | tf_op jit(solution)/shard_map/ppermute | solution.py:335
  217.6 35.9 %collective-permute-start.43 = (bf16[192,2176]{1,0:T(8,128)(2,1)}, bf16[192,2176]{1,0:T(8,128)(2,1)}, u32[]{:S(2)}, u32[]{:S(2)}) collective-permute-start(bf16[192,2176]{1,0:T(8,128)(2,1)} %concatenate.40.refs_0_), channel_id=1, source_target_pairs={{0,4},{1,3},{2,6},{3,1},{4,0},{5,7},{6,2},{7,5},{8,12},{9,11},{10,... | collective-permute-start | bytes 2506760 | tf_op jit(solution)/shard_map/ppermute | solution.py:335
  217.8 35.8 %collective-permute-start.45 = (bf16[192,2176]{1,0:T(8,128)(2,1)}, bf16[192,2176]{1,0:T(8,128)(2,1)}, u32[]{:S(2)}, u32[]{:S(2)}) collective-permute-start(bf16[192,2176]{1,0:T(8,128)(2,1)} %concatenate.40.refs_0_), channel_id=1, source_target_pairs={{0,16},{1,17},{2,18},{3,19},{4,20},{5,21},{6,22},{7,23},{8,0},{9,1... | collective-permute-start | bytes 2506760 | tf_op jit(solution)/shard_map/ppermute | solution.py:335
  239.5 43.8 %collective-permute-start.46 = (bf16[192,2176]{1,0:T(8,128)(2,1)}, bf16[192,2176]{1,0:T(8,128)(2,1)S(1)}, u32[]{:S(2)}, u32[]{:S(2)}) collective-permute-start(bf16[192,2176]{1,0:T(8,128)(2,1)} %collective-permute-done.40.refs_1_), channel_id=1, source_target_pairs={{0,16},{1,17},{2,18},{3,19},{4,20},{5,21},{6,22},{7,23},{8,0},{9,1... | collective-permute-start | bytes 2506760 | tf_op jit(solution)/shard_map/ppermute | solution.py:335
  253.6 29.8 %collective-permute-start.47 = (bf16[192,2176]{1,0:T(8,128)(2,1)}, bf16[192,2176]{1,0:T(8,128)(2,1)S(1)}, u32[]{:S(2)}, u32[]{:S(2)}) collective-permute-start(bf16[192,2176]{1,0:T(8,128)(2,1)} %collective-permute-done.45.refs_0_), channel_id=1, source_target_pairs={{0,4},{1,3},{2,6},{3,1},{4,0},{5,7},{6,2},{7,5},{8,12},{9,11},{10,... | collective-permute-start | bytes 2506760 | tf_op jit(solution)/shard_map/ppermute | solution.py:335
  255.7 27.7 %collective-permute-start.49 = (bf16[192,2048]{1,0:T(8,128)(2,1)}, bf16[192,2048]{1,0:T(8,128)(2,1)}, u32[]{:S(2)}, u32[]{:S(2)}) collective-permute-start(bf16[192,2048]{1,0:T(8,128)(2,1)} %collective-permute-done.38.refs_3_), channel_id=1, source_target_pairs={{0,4},{1,3},{2,6},{3,1},{4,0},{5,7},{6,2},{7,5},{8,12},{9,11},{10,... | collective-permute-start | bytes 2359304 | tf_op jit(solution)/shard_map/ppermute | solution.py:335
  255.7 43.2 %collective-permute-start.51 = (bf16[192,2176]{1,0:T(8,128)(2,1)}, bf16[192,2176]{1,0:T(8,128)(2,1)S(1)}, u32[]{:S(2)}, u32[]{:S(2)}) collective-permute-start(bf16[192,2176]{1,0:T(8,128)(2,1)} %collective-permute-done.45.refs_0_), channel_id=1, source_target_pairs={{0,16},{1,17},{2,18},{3,19},{4,20},{5,21},{6,22},{7,23},{8,0},{9,1... | collective-permute-start | bytes 2506760 | tf_op jit(solution)/shard_map/ppermute | solution.py:335
  284.5 36.7 %collective-permute-start.52 = (bf16[192,2176]{1,0:T(8,128)(2,1)S(1)}, bf16[192,2176]{1,0:T(8,128)(2,1)S(1)}, u32[]{:S(2)}, u32[]{:S(2)}) collective-permute-start(bf16[192,2176]{1,0:T(8,128)(2,1)S(1)} %collective-permute-done.46.refs_1_), channel_id=1, source_target_pairs={{0,16},{1,17},{2,18},{3,19},{4,20},{5,21},{6,22},{7,23},{8,0},{9,1... | collective-permute-start | bytes 2506760 | tf_op jit(solution)/shard_map/ppermute | solution.py:335
  302.9 34.4 %collective-permute-start.56 = (bf16[192,2176]{1,0:T(8,128)(2,1)S(1)}, bf16[192,2176]{1,0:T(8,128)(2,1)}, u32[]{:S(2)}, u32[]{:S(2)}) collective-permute-start(bf16[192,2176]{1,0:T(8,128)(2,1)S(1)} %collective-permute-done.51.refs_0_), channel_id=1, source_target_pairs={{0,16},{1,17},{2,18},{3,19},{4,20},{5,21},{6,22},{7,23},{8,0},{9,1... | collective-permute-start | bytes 2506760 | tf_op jit(solution)/shard_map/ppermute | solution.py:335
  323.4 37.2 %collective-permute-start.61 = (bf16[192,2176]{1,0:T(8,128)(2,1)}, bf16[192,2176]{1,0:T(8,128)(2,1)S(1)}, u32[]{:S(2)}, u32[]{:S(2)}) collective-permute-start(bf16[192,2176]{1,0:T(8,128)(2,1)} %get-tuple-element.519), channel_id=1, source_target_pairs={{0,4},{1,3},{2,6},{3,1},{4,0},{5,7},{6,2},{7,5},{8,12},{9,11},{10,... | collective-permute-start | bytes 2506760 | tf_op jit(solution)/shard_map/ppermute | solution.py:335
  337.3 25.2 %collective-permute-start.62 = (bf16[192,2176]{1,0:T(8,128)(2,1)}, bf16[192,2176]{1,0:T(8,128)(2,1)}, u32[]{:S(2)}, u32[]{:S(2)}) collective-permute-start(bf16[192,2176]{1,0:T(8,128)(2,1)} %get-tuple-element.520), channel_id=1, source_target_pairs={{0,4},{1,3},{2,6},{3,1},{4,0},{5,7},{6,2},{7,5},{8,12},{9,11},{10,... | collective-permute-start | bytes 2506760 | tf_op jit(solution)/shard_map/ppermute | solution.py:335
  360.4 44.8 %collective-permute-start.66 = (bf16[192,2176]{1,0:T(8,128)(2,1)}, bf16[192,2176]{1,0:T(8,128)(2,1)S(1)}, u32[]{:S(2)}, u32[]{:S(2)}) collective-permute-start(bf16[192,2176]{1,0:T(8,128)(2,1)} %get-tuple-element.542), channel_id=1, source_target_pairs={{0,4},{1,3},{2,6},{3,1},{4,0},{5,7},{6,2},{7,5},{8,12},{9,11},{10,... | collective-permute-start | bytes 2506760 | tf_op jit(solution)/shard_map/ppermute | solution.py:335
  360.6 45.9 %collective-permute-start.67 = (bf16[192,2176]{1,0:T(8,128)(2,1)}, bf16[192,2176]{1,0:T(8,128)(2,1)}, u32[]{:S(2)}, u32[]{:S(2)}) collective-permute-start(bf16[192,2176]{1,0:T(8,128)(2,1)} %get-tuple-element.543), channel_id=1, source_target_pairs={{0,4},{1,3},{2,6},{3,1},{4,0},{5,7},{6,2},{7,5},{8,12},{9,11},{10,... | collective-permute-start | bytes 2506760 | tf_op jit(solution)/shard_map/ppermute | solution.py:335
  362.5 42.0 %collective-permute-start.64 = (bf16[192,2048]{1,0:T(8,128)(2,1)}, bf16[192,2048]{1,0:T(8,128)(2,1)}, u32[]{:S(2)}, u32[]{:S(2)}) collective-permute-start(bf16[192,2048]{1,0:T(8,128)(2,1)} %collective-permute-done.57.refs_3_), channel_id=1, source_target_pairs={{0,4},{1,3},{2,6},{3,1},{4,0},{5,7},{6,2},{7,5},{8,12},{9,11},{10,... | collective-permute-start | bytes 2359304 | tf_op jit(solution)/shard_map/ppermute | solution.py:335
  371.5 35.1 %collective-permute-start.65 = (bf16[192,2176]{1,0:T(8,128)(2,1)}, bf16[192,2176]{1,0:T(8,128)(2,1)}, u32[]{:S(2)}, u32[]{:S(2)}) collective-permute-start(bf16[192,2176]{1,0:T(8,128)(2,1)} %add_convert_fusion.6), channel_id=1, source_target_pairs={{0,2},{1,5},{2,0},{3,7},{4,6},{5,1},{6,4},{7,3},{8,10},{9,13},{10,... | collective-permute-start | bytes 2506760 | tf_op jit(solution)/shard_map/ppermute | solution.py:335
  371.5 41.9 %collective-permute-start.63 = (bf16[192,2176]{1,0:T(8,128)(2,1)}, bf16[192,2176]{1,0:T(8,128)(2,1)}, u32[]{:S(2)}, u32[]{:S(2)}) collective-permute-start(bf16[192,2176]{1,0:T(8,128)(2,1)} %collective-permute-done.59.refs_1_), channel_id=1, source_target_pairs={{0,4},{1,3},{2,6},{3,1},{4,0},{5,7},{6,2},{7,5},{8,12},{9,11},{10,... | collective-permute-start | bytes 2506760 | tf_op jit(solution)/shard_map/ppermute | solution.py:335
  404.5 58.9 %collective-permute-start.73 = (bf16[192,2176]{1,0:T(8,128)(2,1)}, bf16[192,2176]{1,0:T(8,128)(2,1)S(1)}, u32[]{:S(2)}, u32[]{:S(2)}) collective-permute-start(bf16[192,2176]{1,0:T(8,128)(2,1)} %get-tuple-element.571), channel_id=1, source_target_pairs={{0,4},{1,3},{2,6},{3,1},{4,0},{5,7},{6,2},{7,5},{8,12},{9,11},{10,... | collective-permute-start | bytes 2506760 | tf_op jit(solution)/shard_map/ppermute | solution.py:335
  405.1 58.3 %collective-permute-start.74 = (bf16[192,2176]{1,0:T(8,128)(2,1)}, bf16[192,2176]{1,0:T(8,128)(2,1)}, u32[]{:S(2)}, u32[]{:S(2)}) collective-permute-start(bf16[192,2176]{1,0:T(8,128)(2,1)} %get-tuple-element.572), channel_id=1, source_target_pairs={{0,4},{1,3},{2,6},{3,1},{4,0},{5,7},{6,2},{7,5},{8,12},{9,11},{10,... | collective-permute-start | bytes 2506760 | tf_op jit(solution)/shard_map/ppermute | solution.py:335
  436.6 26.8 %collective-permute-start.71 = (bf16[192,2176]{1,0:T(8,128)(2,1)}, bf16[192,2176]{1,0:T(8,128)(2,1)S(1)}, u32[]{:S(2)}, u32[]{:S(2)}) collective-permute-start(bf16[192,2176]{1,0:T(8,128)(2,1)} %get-tuple-element.569), channel_id=1, source_target_pairs={{0,4},{1,3},{2,6},{3,1},{4,0},{5,7},{6,2},{7,5},{8,12},{9,11},{10,... | collective-permute-start | bytes 2506760 | tf_op jit(solution)/shard_map/ppermute | solution.py:335
  437.6 25.8 %collective-permute-start.72 = (bf16[192,2176]{1,0:T(8,128)(2,1)}, bf16[192,2176]{1,0:T(8,128)(2,1)S(1)}, u32[]{:S(2)}, u32[]{:S(2)}) collective-permute-start(bf16[192,2176]{1,0:T(8,128)(2,1)} %get-tuple-element.570), channel_id=1, source_target_pairs={{0,4},{1,3},{2,6},{3,1},{4,0},{5,7},{6,2},{7,5},{8,12},{9,11},{10,... | collective-permute-start | bytes 2506760 | tf_op jit(solution)/shard_map/ppermute | solution.py:335
  467.3 86.6 %collective-permute-start.83 = (f32[2048,1024]{1,0:T(8,128)}, f32[2048,1024]{1,0:T(8,128)}, u32[]{:S(2)}, u32[]{:S(2)}) collective-permute-start(f32[2048,1024]{1,0:T(8,128)} %fusion.52), channel_id=1, source_target_pairs={{0,1},{1,0},{2,3},{3,2},{4,5},{5,4},{6,7},{7,6},{8,9},{9,8},{10,11... | collective-permute-start | bytes 25165832 | tf_op jit(solution)/shard_map/ppermute | solution.py:335
  490.8 30.2 %collective-permute-start.79 = (bf16[192,2048]{1,0:T(8,128)(2,1)}, bf16[192,2048]{1,0:T(8,128)(2,1)}, u32[]{:S(2)}, u32[]{:S(2)}) collective-permute-start(bf16[192,2048]{1,0:T(8,128)(2,1)} %get-tuple-element.590), channel_id=1, source_target_pairs={{0,4},{1,3},{2,6},{3,1},{4,0},{5,7},{6,2},{7,5},{8,12},{9,11},{10,... | collective-permute-start | bytes 2359304 | tf_op jit(solution)/shard_map/ppermute | solution.py:335
  490.9 30.1 %collective-permute-start.80 = (bf16[192,2048]{1,0:T(8,128)(2,1)}, bf16[192,2048]{1,0:T(8,128)(2,1)}, u32[]{:S(2)}, u32[]{:S(2)}) collective-permute-start(bf16[192,2048]{1,0:T(8,128)(2,1)} %get-tuple-element.591), channel_id=1, source_target_pairs={{0,4},{1,3},{2,6},{3,1},{4,0},{5,7},{6,2},{7,5},{8,12},{9,11},{10,... | collective-permute-start | bytes 2359304 | tf_op jit(solution)/shard_map/ppermute | solution.py:335
  492.9 49.5 %collective-permute-start.84 = (f32[512,2048]{1,0:T(8,128)}, f32[512,2048]{1,0:T(8,128)}, u32[]{:S(2)}, u32[]{:S(2)}) collective-permute-start(f32[512,2048]{1,0:T(8,128)} %fusion.53), channel_id=1, source_target_pairs={{0,1},{1,0},{2,3},{3,2},{4,5},{5,4},{6,7},{7,6},{8,9},{9,8},{10,11... | collective-permute-start | bytes 12582920 | tf_op jit(solution)/shard_map/ppermute | solution.py:335
  521.0 70.8 %collective-permute-start.86 = (bf16[192,2048]{1,0:T(8,128)(2,1)}, bf16[192,2048]{1,0:T(8,128)(2,1)}, u32[]{:S(2)}, u32[]{:S(2)}) collective-permute-start(bf16[192,2048]{1,0:T(8,128)(2,1)} %get-tuple-element.606), channel_id=1, source_target_pairs={{0,4},{1,3},{2,6},{3,1},{4,0},{5,7},{6,2},{7,5},{8,12},{9,11},{10,... | collective-permute-start | bytes 2359304 | tf_op jit(solution)/shard_map/ppermute | solution.py:335
  521.0 70.8 %collective-permute-start.87 = (bf16[192,2048]{1,0:T(8,128)(2,1)}, bf16[192,2048]{1,0:T(8,128)(2,1)}, u32[]{:S(2)}, u32[]{:S(2)}) collective-permute-start(bf16[192,2048]{1,0:T(8,128)(2,1)} %get-tuple-element.607), channel_id=1, source_target_pairs={{0,4},{1,3},{2,6},{3,1},{4,0},{5,7},{6,2},{7,5},{8,12},{9,11},{10,... | collective-permute-start | bytes 2359304 | tf_op jit(solution)/shard_map/ppermute | solution.py:335
  538.3 30.3 %collective-permute-start.81 = (bf16[192,2048]{1,0:T(8,128)(2,1)S(1)}, bf16[192,2048]{1,0:T(8,128)(2,1)S(1)}, u32[]{:S(2)}, u32[]{:S(2)}) collective-permute-start(bf16[192,2048]{1,0:T(8,128)(2,1)S(1)} %get-tuple-element.597.refs_0_), channel_id=1, source_target_pairs={{0,4},{1,3},{2,6},{3,1},{4,0},{5,7},{6,2},{7,5},{8,12},{9,11},{10,... | collective-permute-start | bytes 2359304 | tf_op jit(solution)/shard_map/ppermute | solution.py:335
  542.4 49.5 %collective-permute-start.85 = (bf16[192,2048]{1,0:T(8,128)(2,1)S(1)}, bf16[192,2048]{1,0:T(8,128)(2,1)}, u32[]{:S(2)}, u32[]{:S(2)}) collective-permute-start(bf16[192,2048]{1,0:T(8,128)(2,1)S(1)} %add_convert_fusion.19), channel_id=1, source_target_pairs={{0,2},{1,5},{2,0},{3,7},{4,6},{5,1},{6,4},{7,3},{8,10},{9,13},{10,... | collective-permute-start | bytes 2359304 | tf_op jit(solution)/shard_map/ppermute | solution.py:335
  645.2 29.3 %collective-permute-start.92 = (bf16[192,2048]{1,0:T(8,128)(2,1)}, bf16[192,2048]{1,0:T(8,128)(2,1)S(1)}, u32[]{:S(2)}, u32[]{:S(2)}) collective-permute-start(bf16[192,2048]{1,0:T(8,128)(2,1)} %get-tuple-element.627), channel_id=1, source_target_pairs={{0,4},{1,3},{2,6},{3,1},{4,0},{5,7},{6,2},{7,5},{8,12},{9,11},{10,... | collective-permute-start | bytes 2359304 | tf_op jit(solution)/shard_map/ppermute | solution.py:335
  645.2 30.8 %collective-permute-start.93 = (bf16[192,2048]{1,0:T(8,128)(2,1)}, bf16[192,2048]{1,0:T(8,128)(2,1)S(1)}, u32[]{:S(2)}, u32[]{:S(2)}) collective-permute-start(bf16[192,2048]{1,0:T(8,128)(2,1)} %get-tuple-element.628), channel_id=1, source_target_pairs={{0,4},{1,3},{2,6},{3,1},{4,0},{5,7},{6,2},{7,5},{8,12},{9,11},{10,... | collective-permute-start | bytes 2359304 | tf_op jit(solution)/shard_map/ppermute | solution.py:335
  649.1 27.0 %collective-permute-start.91 = (bf16[192,2048]{1,0:T(8,128)(2,1)S(1)}, bf16[192,2048]{1,0:T(8,128)(2,1)S(1)}, u32[]{:S(2)}, u32[]{:S(2)}) collective-permute-start(bf16[192,2048]{1,0:T(8,128)(2,1)S(1)} %add_convert_fusion.17), channel_id=1, source_target_pairs={{0,2},{1,5},{2,0},{3,7},{4,6},{5,1},{6,4},{7,3},{8,10},{9,13},{10,... | collective-permute-start | bytes 2359304 | tf_op jit(solution)/shard_map/ppermute | solution.py:335
  650.2 34.4 %collective-permute-start.94 = (bf16[4,64,2048]{2,1,0:T(8,128)(2,1)}, bf16[4,64,2048]{2,1,0:T(8,128)(2,1)S(1)}, u32[]{:S(2)}, u32[]{:S(2)}) collective-permute-start(bf16[4,64,2048]{2,1,0:T(8,128)(2,1)} %get-tuple-element.629), channel_id=1, source_target_pairs={{0,1},{1,0},{2,3},{3,2},{4,5},{5,4},{6,7},{7,6},{8,9},{9,8},{10,11... | collective-permute-start | bytes 3145736 | tf_op jit(solution)/shard_map/ppermute | solution.py:335
  688.9 54.8 %collective-permute-start.103 = (bf16[4,64,1536]{2,1,0:T(8,128)(2,1)S(1)}, bf16[4,64,1536]{2,1,0:T(8,128)(2,1)S(1)}, u32[]{:S(2)}, u32[]{:S(2)}) collective-permute-start(bf16[4,64,1536]{2,1,0:T(8,128)(2,1)S(1)} %copy-done.103), channel_id=1, source_target_pairs={{0,1},{1,0},{2,3},{3,2},{4,5},{5,4},{6,7},{7,6},{8,9},{9,8},{10,11... | collective-permute-start | bytes 2359304 | tf_op jit(solution)/shard_map/ppermute | solution.py:335
  712.9 26.5 %collective-permute-start.99 = (bf16[4,64,1536]{2,1,0:T(8,128)(2,1)S(1)}, bf16[4,64,1536]{2,1,0:T(8,128)(2,1)S(1)}, u32[]{:S(2)}, u32[]{:S(2)}) collective-permute-start(bf16[4,64,1536]{2,1,0:T(8,128)(2,1)S(1)} %add_convert_fusion.15), channel_id=1, source_target_pairs={{0,16},{1,17},{2,18},{3,19},{4,20},{5,21},{6,22},{7,23},{8,0},{9,1... | collective-permute-start | bytes 2359304 | tf_op jit(solution)/shard_map/ppermute | solution.py:335
  715.6 25.1 %collective-permute-start.101 = (bf16[192,2048]{1,0:T(8,128)(2,1)S(1)}, bf16[192,2048]{1,0:T(8,128)(2,1)S(1)}, u32[]{:S(2)}, u32[]{:S(2)}) collective-permute-start(bf16[192,2048]{1,0:T(8,128)(2,1)S(1)} %copy-done.17), channel_id=1, source_target_pairs={{0,4},{1,3},{2,6},{3,1},{4,0},{5,7},{6,2},{7,5},{8,12},{9,11},{10,... | collective-permute-start | bytes 2359304 | tf_op jit(solution)/shard_map/ppermute | solution.py:335
  716.0 25.6 %collective-permute-start.102 = (bf16[192,2048]{1,0:T(8,128)(2,1)S(1)}, bf16[192,2048]{1,0:T(8,128)(2,1)S(1)}, u32[]{:S(2)}, u32[]{:S(2)}) collective-permute-start(bf16[192,2048]{1,0:T(8,128)(2,1)S(1)} %copy-done.15), channel_id=1, source_target_pairs={{0,4},{1,3},{2,6},{3,1},{4,0},{5,7},{6,2},{7,5},{8,12},{9,11},{10,... | collective-permute-start | bytes 2359304 | tf_op jit(solution)/shard_map/ppermute | solution.py:335
  739.5 27.7 %collective-permute-start.109 = (bf16[192,2048]{1,0:T(8,128)(2,1)S(1)}, bf16[192,2048]{1,0:T(8,128)(2,1)S(1)}, u32[]{:S(2)}, u32[]{:S(2)}) collective-permute-start(bf16[192,2048]{1,0:T(8,128)(2,1)S(1)} %copy-done.100), channel_id=1, source_target_pairs={{0,4},{1,3},{2,6},{3,1},{4,0},{5,7},{6,2},{7,5},{8,12},{9,11},{10,... | collective-permute-start | bytes 2359304 | tf_op jit(solution)/shard_map/ppermute | solution.py:335
  740.7 30.2 %collective-permute-start.107 = (bf16[192,2048]{1,0:T(8,128)(2,1)S(1)}, bf16[192,2048]{1,0:T(8,128)(2,1)S(1)}, u32[]{:S(2)}, u32[]{:S(2)}) collective-permute-start(bf16[192,2048]{1,0:T(8,128)(2,1)S(1)} %add_convert_fusion.11), channel_id=1, source_target_pairs={{0,2},{1,5},{2,0},{3,7},{4,6},{5,1},{6,4},{7,3},{8,10},{9,13},{10,... | collective-permute-start | bytes 2359304 | tf_op jit(solution)/shard_map/ppermute | solution.py:335
  741.6 29.3 %collective-permute-start.106 = (bf16[192,2048]{1,0:T(8,128)(2,1)S(1)}, bf16[192,2048]{1,0:T(8,128)(2,1)S(1)}, u32[]{:S(2)}, u32[]{:S(2)}) collective-permute-start(bf16[192,2048]{1,0:T(8,128)(2,1)S(1)} %add_convert_fusion.12), channel_id=1, source_target_pairs={{0,16},{1,17},{2,18},{3,19},{4,20},{5,21},{6,22},{7,23},{8,0},{9,1... | collective-permute-start | bytes 2359304 | tf_op jit(solution)/shard_map/ppermute | solution.py:335
  743.7 24.4 %collective-permute-start.122 = (bf16[64,2048]{1,0:T(8,128)(2,1)S(1)}, bf16[64,2048]{1,0:T(8,128)(2,1)S(1)}, u32[]{:S(2)}, u32[]{:S(2)}) collective-permute-start(bf16[64,2048]{1,0:T(8,128)(2,1)S(1)} %fusion.5), channel_id=1, source_target_pairs={{0,16},{1,17},{2,18},{3,19},{4,20},{5,21},{6,22},{7,23},{8,0},{9,1... | collective-permute-start | bytes 786440 | tf_op jit(solution)/shard_map/ppermute | solution.py:335
  758.7 27.6 %collective-permute-start.118 = (bf16[4,64,1536]{2,1,0:T(8,128)(2,1)S(1)}, bf16[4,64,1536]{2,1,0:T(8,128)(2,1)S(1)}, u32[]{:S(2)}, u32[]{:S(2)}) collective-permute-start(bf16[4,64,1536]{2,1,0:T(8,128)(2,1)S(1)} %copy-done.102), channel_id=1, source_target_pairs={{0,1},{1,0},{2,3},{3,2},{4,5},{5,4},{6,7},{7,6},{8,9},{9,8},{10,11... | collective-permute-start | bytes 2359304 | tf_op jit(solution)/shard_map/ppermute | solution.py:335
  (187 other events, 3593.1 us)

commit v4 on v3

--- a/solution.py
+++ b/solution.py
@@ -305,6 +305,8 @@
 PLANE = 8
 SPOTS = 4
 WIDE = 128
+SMALL = 20
+FIRST_GAIN = SMALL - 4
 
 
 class Moves:
@@ -339,15 +341,13 @@
     return lax.optimization_barrier(values)
 
 
-def plane_total(moves, parts):
-    def swapped(value):
-        return jnp.where(moves.core_id == 0, value, value[:, jnp.asarray([0, 2, 1, 3])])
-
-    parts = swapped(parts)
-    for bit in (1, 2):
-        other = send(parts, moves.spots[bit])
-        parts = parts + jnp.stack([other[:, m ^ bit] for m in range(SPOTS)], axis=1)
-    return swapped(parts)
+def by_spot(moves, parts):
+    return jnp.where(moves.core_id == 0, parts, parts[:, jnp.asarray([0, 2, 1, 3])])
+
+
+def plane_step(moves, parts, bit):
+    other = send(parts, moves.spots[bit])
+    return parts + jnp.stack([other[:, m ^ bit] for m in range(SPOTS)], axis=1)
 
 
 def full_spec(*dims):
@@ -374,39 +374,65 @@
             yield pl.ds(pl.multiple_of(whole, HEAD_DIM), HEAD_DIM), pl.ds(piece, HEAD_DIM)
 
 
-def split_body(lines, meta, whole_ref, *pieces):
+def split_body(lines, spot, lengths, whole_ref, router_ref, gains_ref, *pieces):
+    rows, columns = pieces[0].shape[0], pieces[0].shape[1] - WIDE
+    routers = router_ref.shape[1]
+    lane = lax.broadcasted_iota(jnp.int32, (rows, WIDE), 1)
+    row = lax.broadcasted_iota(jnp.int32, (rows, WIDE), 0)
+    spread = lax.broadcasted_iota(jnp.int32, (routers, WIDE), 0) == lax.broadcasted_iota(
+        jnp.int32, (routers, WIDE), 1
+    )
+    riding = product(router_ref[...], jnp.where(spread, 1.0, 0.0).astype(jnp.bfloat16))
+    for n in range(gains_ref.shape[0]):
+        column = as_column(widen(gains_ref[...])[n : n + 1, :])
+        riding = jnp.where(lane == FIRST_GAIN + n, column, riding)
+    for n in range(lengths.shape[1]):
+        riding = jnp.where((lane == SMALL) & (row == n), lengths[0, n].astype(jnp.float32), riding)
     for mask, piece in enumerate(pieces):
-        for whole_at, piece_at in column_places(meta[0], mask, lines):
+        for whole_at, piece_at in column_places(spot[0], mask, lines):
             piece[:, piece_at] = whole_ref[:, whole_at]
-
-
-def split_columns(spot, whole):
+        piece[:, columns:] = riding.astype(jnp.bfloat16)
+
+
+def split_columns(spot, whole, router, gains, lengths):
     rows, columns = whole.shape
+    columns = columns // SPOTS + WIDE
     return pl.pallas_call(
         functools.partial(split_body, HEADS // SPOTS),
-        out_shape=[jax.ShapeDtypeStruct((rows, columns // SPOTS), whole.dtype)] * SPOTS,
-        in_specs=[SCALARS, full_spec(rows, columns)],
-        out_specs=[full_spec(rows, columns // SPOTS)] * SPOTS,
-        compiler_params=params(16),
+        out_shape=[jax.ShapeDtypeStruct((rows, columns), whole.dtype)] * SPOTS,
+        in_specs=[
+            SCALARS,
+            SCALARS,
+            full_spec(*whole.shape),
+            full_spec(*router.shape),
+            full_spec(*gains.shape),
+        ],
+        out_specs=[full_spec(rows, columns)] * SPOTS,
+        compiler_params=params(60),
         name="split_columns",
-    )(spot.reshape(1), whole)
+    )(spot.reshape(1), lengths, whole, router, gains)
 
 
 def join_body(lines, meta, *refs):
-    *pieces, whole_ref = refs
+    *pieces, whole_ref, small_ref = refs
     for mask, piece in enumerate(pieces):
         for whole_at, piece_at in column_places(meta[0], mask, lines):
             whole_ref[:, whole_at] = widen(piece[:, piece_at])
+    small_ref[...] = sum(widen(piece[:, piece.shape[1] - WIDE :]) for piece in pieces)
 
 
 def join_columns(spot, pieces):
-    rows, columns = pieces[0].shape
+    rows, wide = pieces[0].shape
+    columns = wide - WIDE
     return pl.pallas_call(
         functools.partial(join_body, HEADS // SPOTS),
-        out_shape=jax.ShapeDtypeStruct((rows, columns * SPOTS), jnp.float32),
-        in_specs=[SCALARS] + [full_spec(rows, columns)] * SPOTS,
-        out_specs=full_spec(rows, columns * SPOTS),
-        compiler_params=params(16),
+        out_shape=[
+            jax.ShapeDtypeStruct((rows, columns * SPOTS), jnp.float32),
+            jax.ShapeDtypeStruct((rows, WIDE), jnp.float32),
+        ],
+        in_specs=[SCALARS] + [full_spec(rows, wide)] * SPOTS,
+        out_specs=[full_spec(rows, columns * SPOTS), full_spec(rows, WIDE)],
+        compiler_params=params(60),
         name="join_columns",
     )(spot.reshape(1), *pieces)
 
@@ -548,7 +574,7 @@
             pltpu.SemaphoreType.DMA((6 + 2 * blocks,)),
         ],
         input_output_aliases=aliases,
-        compiler_params=params(58),
+        compiler_params=params(60),
         cost_estimate=cost(blocks * 38 * 10**8, 30 << 20, 2 * used * half),
         name="expert_blocks",
     )(meta, *rows, *grads, *weights, *saved)
@@ -591,10 +617,10 @@
     return [slice(h, h + HEAD_DIM) for h in range(0, mine, HEAD_DIM)]
 
 
-def project_body(planes, own_rows, meta, gain, *refs):
+def project_body(planes, own_rows, meta, *refs):
     blocks, own, other = refs[:SPOTS], refs[SPOTS : SPOTS + planes], refs[SPOTS + planes :][:planes]
-    proj_ref, a_ref, in_ref, sums_ref = refs[SPOTS + 2 * planes :][:4]
-    x_v, a_v, in_v, proj_v, sem, in_sem, done = refs[SPOTS + 2 * planes + 4 :]
+    proj_ref, a_ref, in_ref, sums_ref, small_ref, gains_ref = refs[SPOTS + 2 * planes :][:6]
+    x_v, a_v, in_v, proj_v, sem, in_sem, done = refs[SPOTS + 2 * planes + 6 :]
     spot, core = meta[0], meta[1]
     count = x_v.shape[1]
     mine = proj_v.shape[1] // 3
@@ -615,16 +641,30 @@
                     )
                 )
                 fetch_in[-1].start()
+    roots = []
     for j in range(SPOTS):
         fetch_x[j].wait()
         x = widen(x_v[j])
-        root = lax.rsqrt(jnp.mean(x * x, axis=1, keepdims=True) + EPSILON)
-        a_v[j * count : (j + 1) * count, :] = (x * root * gain[...]).astype(jnp.bfloat16)
-    leaving = [pltpu.make_async_copy(a_v, a_ref, done.at[0])]
-    leaving[0].start()
+        roots.append(lax.rsqrt(jnp.mean(x * x, axis=1, keepdims=True) + EPSILON))
     for copy in fetch_in:
         copy.wait()
-    leaving.append(pltpu.make_async_copy(in_v, in_ref, done.at[1]))
+    leaving = [pltpu.make_async_copy(in_v, in_ref, done.at[0])]
+    leaving[0].start()
+    turn_by = lax.broadcasted_iota(jnp.int32, (small_ref.shape[0], WIDE), 0) == (
+        lax.broadcasted_iota(jnp.int32, (small_ref.shape[0], WIDE), 1)
+    )
+    small = dot_last(jnp.where(turn_by, 1.0, 0.0).astype(jnp.bfloat16), in_v[:, 3 * mine :])
+    small_ref[...] = small
+    for line in range(mine // HEAD_DIM):
+        at = pl.multiple_of((line * SPOTS + spot) * HEAD_DIM, HEAD_DIM)
+        for n in range(2):
+            gains_ref[n : n + 1, line * HEAD_DIM : (line + 1) * HEAD_DIM] = small_ref[
+                FIRST_GAIN + 1 + n : FIRST_GAIN + 2 + n, pl.ds(at, HEAD_DIM)
+            ]
+    gain = small[FIRST_GAIN : FIRST_GAIN + 1, :]
+    for j in range(SPOTS):
+        a_v[j * count : (j + 1) * count, :] = (widen(x_v[j]) * roots[j] * gain).astype(jnp.bfloat16)
+    leaving.append(pltpu.make_async_copy(a_v, a_ref, done.at[1]))
     leaving[1].start()
     for n in range(3):
         part = slice(n * mine, (n + 1) * mine)
@@ -642,8 +682,9 @@
         copy.wait()
 
 
-def project(moves, gain, blocks, own, other):
-    planes, own_rows, width = len(own), own[0].shape[1], own[0].shape[2]
+def project(moves, blocks, own, other):
+    planes, own_rows, wide = len(own), own[0].shape[1], own[0].shape[2]
+    width = wide - WIDE
     count, depth = blocks[0].shape
     bf, f32 = jnp.bfloat16, jnp.float32
     rows = SPOTS * count
@@ -654,24 +695,27 @@
         out_shape=[
             shape((rows, width), f32),
             shape((rows, depth), bf),
-            shape((depth, width), bf),
+            shape((depth, wide), bf),
             shape((2, SPOTS, count), f32),
+            shape((32, depth), f32),
+            shape((2, width // 3), f32),
         ],
-        in_specs=[SCALARS, full_spec(1, depth)] + [ANYWHERE] * (SPOTS + 2 * planes),
-        out_specs=[ANYWHERE] * 3 + [full_spec(2, SPOTS, count)],
+        in_specs=[SCALARS] + [ANYWHERE] * (SPOTS + 2 * planes),
+        out_specs=[ANYWHERE] * 3
+        + [full_spec(2, SPOTS, count), full_spec(32, depth), full_spec(2, width // 3)],
         scratch_shapes=[
             pltpu.VMEM((SPOTS, count, depth), bf),
             pltpu.VMEM((rows, depth), bf),
-            pltpu.VMEM((depth, width), bf),
+            pltpu.VMEM((depth, wide), bf),
             pltpu.VMEM((rows, width), f32),
             pltpu.SemaphoreType.DMA((SPOTS,)),
             pltpu.SemaphoreType.DMA((2 * SPOTS * planes,)),
             pltpu.SemaphoreType.DMA((5,)),
         ],
-        compiler_params=params(40),
+        compiler_params=params(60),
         cost_estimate=cost(5 * 10**9, 20 << 20),
         name="project",
-    )(meta.astype(jnp.int32), gain, *blocks, *own, *other)
+    )(meta.astype(jnp.int32), *blocks, *own, *other)
 
 
 def by_block(count, width):
@@ -761,7 +805,7 @@
         + [ANYWHERE] * (2 * planes),
         out_specs=[block_spec(count, mine)] * 4 + [full_spec(mine, D)] + by_block(count, D),
         scratch_shapes=[pltpu.SemaphoreType.DMA((2 * planes,))],
-        compiler_params=params(40),
+        compiler_params=params(60),
         cost_estimate=cost(5 * 10**9, 20 << 20),
         name="attend_forward",
     )(meta.astype(jnp.int32), totals, starts, gains, projected, cos_all, sin_all, *own, *other)
@@ -772,7 +816,7 @@
 ):
     blocks = refs[:SPOTS]
     dq_ref, dk_ref, dv_ref, sums_ref, own_grad, other_grad, gain_grad = refs[SPOTS : SPOTS + 7]
-    grads_v, total_v, sem = refs[SPOTS + 7 :]
+    grads_v, o_v, total_v, sem = refs[SPOTS + 7 :]
     step = pl.program_id(0)
     bf = jnp.bfloat16
     mine = q_ref.shape[1]
@@ -781,12 +825,12 @@
     def _():
         for n in range(SPOTS):
             pltpu.make_async_copy(blocks[n], grads_v.at[n], sem.at[n]).start()
-        total_v[...] = jnp.zeros_like(total_v)
         gain_grad[...] = jnp.zeros_like(gain_grad)
 
     pltpu.make_async_copy(blocks[0], grads_v.at[step], sem.at[step]).wait()
     grads = grads_v[step]
-    total_v[...] += dot_first(o_ref[...], grads)
+    count = grads.shape[0]
+    o_v[pl.ds(pl.multiple_of(step * count, 64), count), :] = o_ref[...]
     do = dot_last(grads, out_w[...]).astype(bf)
     roots = [root_of(as_column(totals[n, pl.ds(step, 1), :])) for n in range(2)]
     start = as_column(starts[pl.ds(step, 1), :])
@@ -808,17 +852,24 @@
             at = n * mine + own.start
             raw = grad * proj_ref[:, at : at + HEAD_DIM]
             sums[n] += jnp.sum(raw * gains[n : n + 1, own], axis=1, keepdims=True)
-            gain_grad[n : n + 1, own] += jnp.sum(raw * roots[n], axis=0, keepdims=True)
+            line = pl.multiple_of((own.start // HEAD_DIM * SPOTS + meta[0]) * HEAD_DIM, HEAD_DIM)
+            gain_grad[n : n + 1, pl.ds(line, HEAD_DIM)] += jnp.sum(
+                raw * roots[n], axis=0, keepdims=True
+            )
     for n in range(2):
         sums_ref[n, pl.ds(step, 1), :] = as_row(sums[n])
 
     @pl.when(step == SPOTS - 1)
     def _():
         planes, own_rows = own_grad.shape[:2]
+        total = sum(
+            dot_first(o_v[j * count : (j + 1) * count, :], grads_v[j]) for j in range(SPOTS)
+        )
+        total_v[...] = total.astype(bf)
         for k in range(planes):
             for ref, c in ((own_grad, meta[1]), (other_grad, 1 - meta[1])):
                 at = pl.multiple_of((meta[2 + k] * 2 + c) * own_rows, own_rows)
-                ref[k] = total_v[pl.ds(at, own_rows), :].astype(bf)
+                ref[k] = total_v[pl.ds(at, own_rows), :]
 
 
 def attend_backward(
@@ -841,7 +892,7 @@
             shape((2, SPOTS, count), f32),
             shape((planes, own_rows, D), bf),
             shape((planes, own_rows, D), bf),
-            shape((8, mine), f32),
+            shape((2, D), f32),
         ],
         in_specs=[
             SCALARS,
@@ -858,13 +909,14 @@
         out_specs=[block_spec(count, mine)] * 3
         + [full_spec(2, SPOTS, count)]
         + [full_spec(planes, own_rows, D)] * 2
-        + [full_spec(8, mine)],
+        + [full_spec(2, D)],
         scratch_shapes=[
             pltpu.VMEM((SPOTS, count, D), bf),
-            pltpu.VMEM((mine, D), f32),
+            pltpu.VMEM((rows, mine), bf),
+            pltpu.VMEM((mine, D), bf),
             pltpu.SemaphoreType.DMA((SPOTS,)),
         ],
-        compiler_params=params(48),
+        compiler_params=params(60),
         cost_estimate=cost(7 * 10**9, 25 << 20),
         name="attend_backward",
     )(
@@ -882,116 +934,246 @@
 
 
 def project_back_body(
-    planes, own_rows, meta, totals, dots, gains, proj_ref, dq_ref, dk_ref, dv_ref, a_ref, *refs
+    planes,
+    own_rows,
+    meta,
+    totals,
+    dots,
+    gains,
+    router_grad,
+    small_rows,
+    gain_grads,
+    second_grad,
+    proj_ref,
+    dq_ref,
+    dk_ref,
+    dv_ref,
+    a_ref,
+    in_w,
+    *refs,
 ):
-    dp_ref, own, other, total_v = refs[0], refs[1 : 1 + planes], refs[1 + planes : -1], refs[-1]
-    step = pl.program_id(0)
+    dp_ref, own, other, rest = refs[0], refs[1 : 1 + planes], refs[1 + planes], refs[2 + planes]
+    a_v, in_v, own_v, other_v, riding_v, small, sem, done = refs[3 + planes :]
     bf = jnp.bfloat16
-    mine = dv_ref.shape[1]
-    count = dv_ref.shape[0] // 2
+    rows, mine = dv_ref.shape
+    count = rows // SPOTS
+    fetches = [
+        pltpu.make_async_copy(a_ref, a_v, sem.at[0]),
+        pltpu.make_async_copy(in_w, in_v, sem.at[1]),
+    ]
+    for copy in fetches:
+        copy.start()
     for n, ref in enumerate((dq_ref, dk_ref)):
         columns = slice(n * mine, (n + 1) * mine)
-        for j in range(2):
-            rows = slice(j * count, (j + 1) * count)
-            root = root_of(as_column(totals[n, pl.ds(2 * step + j, 1), :]))
-            inner = as_column(dots[n, pl.ds(2 * step + j, 1), :])
-            grad = root * gains[n : n + 1, :] * ref[rows, :]
-            grad = grad - proj_ref[rows, columns] * (root * root * root * inner / D)
-            dp_ref[rows, columns] = grad.astype(bf)
+        for j in range(SPOTS):
+            block = slice(j * count, (j + 1) * count)
+            root = root_of(as_column(totals[n, j : j + 1, :]))
+            inner = as_column(dots[n, j : j + 1, :])
+            grad = root * gains[n : n + 1, :] * ref[block, :]
+            grad = grad - proj_ref[block, columns] * (root * root * root * inner / D)
+            dp_ref[block, columns] = grad.astype(bf)
     dp_ref[:, 2 * mine :] = dv_ref[...]
-
-    @pl.when(step == 0)
-    def _():
-        total_v[...] = dot_first(a_ref[...], dp_ref[...])
-
-    @pl.when(step == 1)
-    def _():
-        total_v[...] += dot_first(a_ref[...], dp_ref[...])
-        for k in range(planes):
-            for mask in range(SPOTS):
-                chunk = meta[2 + k] * PLANE + (meta[0] ^ mask) * 2
-                for refs_k, c in ((own, meta[1]), (other, 1 - meta[1])):
-                    at = pl.multiple_of((chunk + c) * own_rows, own_rows)
-                    refs_k[k][mask] = total_v[pl.ds(at, own_rows), :].astype(bf)
-
-
-def project_back(moves, totals, dots, gains, projected, dq, dk, dv, normed_all):
+    small[...] = jnp.zeros_like(small)
+    small[:FIRST_GAIN, :] = router_grad[...]
+    small[FIRST_GAIN : FIRST_GAIN + 1, :] = small_rows[FIRST_GAIN : FIRST_GAIN + 1, :]
+    small[FIRST_GAIN + 1 : FIRST_GAIN + 3, :] = gain_grads[...]
+    small[FIRST_GAIN + 3 : SMALL, :] = second_grad[...]
+    turn_by = lax.broadcasted_iota(jnp.int32, (small.shape[0], WIDE), 0) == (
+        lax.broadcasted_iota(jnp.int32, (small.shape[0], WIDE), 1)
+    )
+    riding_v[...] = dot_first(small[...].astype(bf), jnp.where(turn_by, 1.0, 0.0).astype(bf))
+    lane = lax.broadcasted_iota(jnp.int32, (own_rows, WIDE), 1)
+    for copy in fetches:
+        copy.wait()
+    leaving = []
+    span = PLANE * own_rows
+    for k in [*range(1, planes), 0]:
+        plane = meta[2 + k]
+        first_row = pl.multiple_of(plane * span, span)
+        grads = dot_first(a_v[:, pl.ds(first_row, span)], dp_ref[...])
+        for spot in range(SPOTS):
+            for c in range(2):
+                at = (spot * 2 + c) * own_rows
+                grad = grads[at : at + own_rows, :]
+                rows_at = pl.ds(pl.multiple_of(first_row + at, own_rows), own_rows)
+                gain_grad = jnp.sum(grad * widen(in_v[rows_at, : 3 * mine]), axis=1, keepdims=True)
+                riding = riding_v[rows_at, :]
+                riding = jnp.where(lane == FIRST_GAIN, gain_grad / riding, riding).astype(bf)
+
+                def put(place, grad=grad, riding=riding):
+                    place[:, : 3 * mine] = grad.astype(bf)
+                    place[:, 3 * mine :] = riding
+
+                @pl.when(meta[1] == c)
+                def _():
+                    put(own_v.at[k, spot ^ meta[0]])
+
+                @pl.when(meta[1] != c)
+                def _():
+                    put(other_v.at[k, spot ^ meta[0]])
+
+        target = other if k == 1 else rest.at[(k - 2) % planes]
+        for place, ref in ((own_v, own[k]), (other_v, target)):
+            leaving.append(pltpu.make_async_copy(place.at[k], ref, done.at[len(leaving)]))
+            leaving[-1].start()
+    for copy in leaving:
+        copy.wait()
+
+
+def project_back(moves, totals, dots, gains, small, in_full, projected, dq, dk, dv, normed_all):
     rows, mine = dv.shape
     planes = moves.planes
     own_rows = D // (planes * PLANE)
     bf = jnp.bfloat16
     meta = jnp.concatenate([jnp.stack([moves.spot, moves.core_id]), moves.planes_back])
-    half = rows // 2
-    pieces = (SPOTS, own_rows, 3 * mine)
+    pieces = (SPOTS, own_rows, 3 * mine + WIDE)
+    inputs = (totals, dots, gains, *small, projected, dq, dk, dv)
     return pl.pallas_call(
         functools.partial(project_back_body, planes, own_rows),
-        grid=(2,),
         out_shape=[jax.ShapeDtypeStruct((rows, 3 * mine), bf)]
-        + [jax.ShapeDtypeStruct(pieces, bf)] * (2 * planes),
-        in_specs=[
-            SCALARS,
-            full_spec(*totals.shape),
-            full_spec(*dots.shape),
-            full_spec(*gains.shape),
-            block_spec(half, 3 * mine),
-            block_spec(half, mine),
-            block_spec(half, mine),
-            block_spec(half, mine),
-            block_spec(half, D),
+        + [jax.ShapeDtypeStruct(pieces, bf)] * (planes + 1)
+        + [jax.ShapeDtypeStruct((planes - 1, *pieces), bf)],
+        in_specs=[SCALARS] + [full_spec(*item.shape) for item in inputs] + [ANYWHERE] * 2,
+        out_specs=[full_spec(rows, 3 * mine)] + [ANYWHERE] * (planes + 2),
+        scratch_shapes=[
+            pltpu.VMEM((rows, D), bf),
+            pltpu.VMEM(in_full.shape, bf),
+            pltpu.VMEM((planes, *pieces), bf),
+            pltpu.VMEM((planes, *pieces), bf),
+            pltpu.VMEM((D, WIDE), jnp.float32),
+            pltpu.VMEM((32, D), jnp.float32),
+            pltpu.SemaphoreType.DMA((2,)),
+            pltpu.SemaphoreType.DMA((2 * planes,)),
         ],
-        out_specs=[block_spec(half, 3 * mine)] + [full_spec(*pieces)] * (2 * planes),
-        scratch_shapes=[pltpu.VMEM((D, 3 * mine), jnp.float32)],
         compiler_params=params(60),
         cost_estimate=cost(5 * 10**9, 30 << 20),
         name="project_back",
-    )(meta.astype(jnp.int32), totals, dots, gains, projected, dq, dk, dv, normed_all)
-
-
-def rows_back_body(dp_ref, in_w, *refs):
-    blocks, parts, gain_grad, (x_v, sem) = (
-        refs[:SPOTS],
-        refs[SPOTS : 2 * SPOTS],
-        refs[2 * SPOTS],
-        refs[2 * SPOTS + 1 :],
-    )
-    step = pl.program_id(0)
-
-    @pl.when(step == 0)
-    def _():
-        for n in range(SPOTS):
-            pltpu.make_async_copy(blocks[n], x_v.at[n], sem.at[n]).start()
-        gain_grad[...] = jnp.zeros_like(gain_grad)
-
-    value = dot_last(dp_ref[...], in_w[...])
-    put_by_block(step, parts, value.astype(jnp.bfloat16))
-    pltpu.make_async_copy(blocks[0], x_v.at[step], sem.at[step]).wait()
-    x = widen(x_v[step])
-    root = lax.rsqrt(jnp.mean(x * x, axis=1, keepdims=True) + EPSILON)
-    gain_grad[...] += jnp.sum(value * (x * root), axis=0, keepdims=True)
-
-
-def rows_back(projected_grad, in_full, blocks):
+    )(meta.astype(jnp.int32), *inputs, normed_all, in_full)
+
+
+def rows_back_body(dp_ref, in_w, *parts):
+    value = dot_last(dp_ref[...], in_w[:, : dp_ref.shape[1]]).astype(jnp.bfloat16)
+    put_by_block(pl.program_id(0), parts, value)
+
+
+def rows_back(projected_grad, in_full):
     rows, columns = projected_grad.shape
     count = rows // SPOTS
-    bf = jnp.bfloat16
     return pl.pallas_call(
         rows_back_body,
         grid=(SPOTS,),
-        out_shape=[jax.ShapeDtypeStruct((count, D), bf)] * SPOTS
-        + [jax.ShapeDtypeStruct((1, D), jnp.float32)],
-        in_specs=[block_spec(count, columns), full_spec(*in_full.shape)] + [ANYWHERE] * SPOTS,
-        out_specs=by_block(count, D) + [full_spec(1, D)],
-        scratch_shapes=[
-            pltpu.VMEM((SPOTS, count, D), bf),
-            pltpu.SemaphoreType.DMA((SPOTS,)),
-        ],
-        compiler_params=params(48),
+        out_shape=[jax.ShapeDtypeStruct((count, D), jnp.bfloat16)] * SPOTS,
+        in_specs=[block_spec(count, columns), full_spec(*in_full.shape)],
+        out_specs=by_block(count, D),
+        compiler_params=params(60),
         cost_estimate=cost(5 * 10**9, 12 << 20),
         name="rows_back",
-    )(projected_grad, in_full, *blocks)
-
-
-SMALL = 20
+    )(projected_grad, in_full)
+
+
+def route_body(tokens, home, back, near, match, rank, small, residual_ref, rows_ref, probs_ref):
+    bf = jnp.bfloat16
+    residual = widen(tokens[...]) + (widen(home[...]) + widen(back[...]) + widen(near[...]))
+    residual_ref[...] = residual
+    root = lax.rsqrt(jnp.mean(residual * residual, axis=1, keepdims=True) + EPSILON)
+    normed = (residual * root * small[FIRST_GAIN + 3 : FIRST_GAIN + 4, :]).astype(bf)
+    rows_ref[:, :D] = normed
+    experts = match.shape[1]
+    logits = dot_last(normed, small[:experts, :].astype(bf))
+    exponent = jnp.exp(logits - jnp.max(logits, axis=1, keepdims=True))
+    probs = exponent / jnp.sum(exponent, axis=1, keepdims=True)
+    chosen = probs * match[...]
+    total = jnp.sum(chosen, axis=1, keepdims=True)
+    gates = chosen / total
+    upper = widen(gates.astype(bf))
+    behind = 0.0
+    for n, part in enumerate((rank[...], upper.astype(bf), (gates - upper).astype(bf))):
+        places = lax.broadcasted_iota(jnp.int32, (experts, WIDE), 0) + n * experts == (
+            lax.broadcasted_iota(jnp.int32, (experts, WIDE), 1)
+        )
+        behind += product(part, jnp.where(places, 1.0, 0.0).astype(bf))
+    rows_ref[:, D:] = behind.astype(bf)
+    probs_ref[0] = probs
+    probs_ref[1] = gates
+    probs_ref[2] = jnp.broadcast_to(total, probs.shape)
+
+
+def route(tokens, home, back, near, match, rank, small):
+    count, width = tokens.shape
+    experts = match.shape[1]
+    inputs = (tokens, home, back, near, match, rank, small)
+    shape = jax.ShapeDtypeStruct
+    return pl.pallas_call(
+        route_body,
+        out_shape=[
+            shape((count, width), jnp.float32),
+            shape((count, width + WIDE), jnp.bfloat16),
+            shape((3, count, experts), jnp.float32),
+        ],
+        in_specs=[full_spec(*item.shape) for item in inputs],
+        out_specs=[
+            full_spec(count, width),
+            full_spec(count, width + WIDE),
+            full_spec(3, count, experts),
+        ],
+        compiler_params=params(60),
+        cost_estimate=cost(10**8, 8 << 20),
+        name="route",
+    )(*inputs)
+
+
+def route_back_body(total, home, back, near, match, probs_ref, small, residual, upstream, *results):
+    grad_ref, branch_ref, router_ref, gain_ref = results
+    bf = jnp.bfloat16
+    rows = widen(total[...]) + (widen(home[...]) + widen(back[...]) + widen(near[...]))
+    experts = match.shape[1]
+    probs, gates, gate_total = probs_ref[0], probs_ref[1], probs_ref[2]
+    pairs = lax.broadcasted_iota(jnp.int32, (WIDE, experts), 0) // 2 == (
+        lax.broadcasted_iota(jnp.int32, (WIDE, experts), 1)
+    )
+    gate_grad = product(rows[:, D:].astype(bf), jnp.where(pairs, 1.0, 0.0).astype(bf))
+    inner = jnp.sum(gate_grad * gates, axis=1, keepdims=True)
+    chosen_grad = match[...] * (gate_grad - inner) / gate_total
+    inner = jnp.sum(chosen_grad * probs, axis=1, keepdims=True)
+    logit_grad = (probs * (chosen_grad - inner)).astype(bf)
+    normed_grad = rows[:, :D] + product(logit_grad, small[:experts, :].astype(bf))
+    gain = small[FIRST_GAIN + 3 : FIRST_GAIN + 4, :]
+    value = residual[...]
+    root = lax.rsqrt(jnp.mean(value * value, axis=1, keepdims=True) + EPSILON)
+    normed = (value * root * gain).astype(bf)
+    router_ref[...] = dot_first(logit_grad, normed)
+    scaled = normed_grad * value
+    gain_ref[...] = jnp.sum(scaled * root, axis=0, keepdims=True)
+    inner = jnp.mean(scaled * gain, axis=1, keepdims=True)
+    grad = widen(upstream[...]) + root * gain * normed_grad - value * (root * root * root * inner)
+    grad_ref[...] = grad
+    branch_ref[...] = grad.astype(bf)
+
+
+def route_back(total, home, back, near, match, probs, small, residual, upstream):
+    count, width = residual.shape
+    experts = match.shape[1]
+    inputs = (total, home, back, near, match, probs, small, residual, upstream)
+    shape = jax.ShapeDtypeStruct
+    return pl.pallas_call(
+        route_back_body,
+        out_shape=[
+            shape((count, width), jnp.float32),
+            shape((count, width), jnp.bfloat16),
+            shape((experts, width), jnp.float32),
+            shape((1, width), jnp.float32),
+        ],
+        in_specs=[full_spec(*item.shape) for item in inputs],
+        out_specs=[
+            full_spec(count, width),
+            full_spec(count, width),
+            full_spec(experts, width),
+            full_spec(1, width),
+        ],
+        compiler_params=params(60),
+        cost_estimate=cost(10**8, 10 << 20),
+        name="route_back",
+    )(*inputs)
 
 
 def shards_dense(
@@ -1022,66 +1204,34 @@
     def low(value):
         return value.astype(bf)
 
-    flat = jnp.concatenate(
-        [router_weight.T.reshape(-1), norm_gains.reshape(-1), lengths[0].astype(bf)]
-    )
-    riders = [jnp.pad(flat, (0, -flat.shape[0] % WIDE)).reshape(-1, WIDE)]
-    pieces = split_columns(spot, attention_in)
-    near_x = send(tokens, first)
-    riders.append(send(riders[0], ring))
-    out_own = [attention_out, send(attention_out, ring)]
-    weights = [expert_in[0], send(expert_in[0], cores), expert_out[0], send(expert_out[0], cores)]
-    riders, out_own, pieces = tie(riders, out_own, pieces)
-
-    riders.append(send(riders[1], ring))
-    out_own.append(send(out_own[1], ring))
+    pieces = split_columns(spot, attention_in, router_weight, norm_gains, lengths)
     traded = [pieces[0]] + [send(pieces[m], moves.spots[m]) for m in range(1, SPOTS)]
-    riders, out_own, traded, near_x = tie(riders, out_own, traded, near_x)
+    own_1 = send(cotangent, ring)
+    tokens_then, traded, own_1 = tie(tokens, traded, own_1)
 
     in_own = [jnp.stack(traded)]
-    riders.append(send(riders[2], ring))
-    out_own.append(send(out_own[2], ring))
     in_own.append(send(in_own[0], ring))
+    in_other = [send(in_own[0], cores)]
+    near_x = send(tokens_then, first)
+    near_0 = send(cotangent, first)
+    in_own, in_other, near_x = tie(in_own, in_other, near_x)
+
+    in_own.append(send(in_own[1], ring))
+    in_other.append(send(in_own[1], cores))
     blocks_x = [tokens, near_x, send(tokens, second), send(near_x, second)]
-    riders_all = jnp.stack(riders)
-    for pairs in (moves.spots[1], moves.spots[2], cores):
-        riders_all = jnp.concatenate([riders_all, send(riders_all, pairs)])
-    in_own, blocks_x, riders_all, out_own = tie(in_own, blocks_x, riders_all, out_own)
-
-    in_own.append(send(in_own[1], ring))
-    in_other = [send(item, cores) for item in in_own[:2]]
-    out_other = [send(item, cores) for item in out_own]
-    grads = {(0, 0): [cotangent, send(cotangent, first)]}
-    in_own, in_other, grads = tie(in_own, in_other, grads)
+    in_own, in_other, blocks_x, near_0 = tie(in_own, in_other, blocks_x, near_0)
 
     in_own.append(send(in_own[2], ring))
     in_other.append(send(in_own[2], cores))
+    out_own = [attention_out, send(attention_out, ring)]
+    out_other = [send(attention_out, cores)]
+    grads = {(0, 0): [cotangent, near_0], (1, 0): [own_1, send(own_1, first)]}
     grads[0, 1] = [send(item, second) for item in grads[0, 0]]
-
-    ids = jnp.arange(devices_count, dtype=jnp.int32)
-    source = (
-        ((ids % 2) ^ core) * (SPOTS * planes)
-        + ((ids % PLANE // 2) ^ spot) * planes
-        + moves.steps_from[ids // PLANE]
-    )
-    arrived = jnp.take(riders_all, source, axis=0).reshape(devices_count, -1)
-    small_all = arrived[:, : SMALL * own_rows].reshape(devices_count, SMALL, own_rows)
-    small_all = small_all.transpose(1, 0, 2).reshape(SMALL, D)
-    router_full, gain_rows = small_all[: SMALL - 4], widen(small_all[SMALL - 4 :])
-    lengths_all = arrived[:, SMALL * own_rows : SMALL * own_rows + lengths.shape[1]]
-    lengths_all = jnp.take(
-        lengths_all, moves.plane * PLANE + moves.group_spots * 2 + core, axis=0
-    ).astype(jnp.int32)
-    gains = jnp.stack(
-        [
-            lax.dynamic_index_in_dim(
-                gain_rows[n].reshape(lines, SPOTS, HEAD_DIM), spot, 1, keepdims=False
-            ).reshape(mine)
-            for n in (1, 2)
-        ]
-    )
+    columns = 3 * mine
+    lengths_all = jnp.stack([piece[: lengths.shape[1], columns + SMALL] for piece in traded])
+    lengths_all = jnp.where(core == 0, lengths_all, lengths_all[jnp.asarray([0, 2, 1, 3])])
     places = jnp.arange(row_count, dtype=jnp.int32)
-    _, position = jax.vmap(lambda item: layout(item, row_count))(lengths_all)
+    _, position = jax.vmap(lambda item: layout(item, row_count))(lengths_all.astype(jnp.int32))
     starts = (places[None] - position).astype(f32)
     cos_half, sin_half = (table[:, 0] for table in tables(position.reshape(-1)))
     cos_all = jnp.concatenate([cos_half, cos_half], axis=1)
@@ -1091,24 +1241,36 @@
     match = jnp.sum((routes[:, :, None] == expert_ids[None, None, :]).astype(f32), axis=1)
     before = (places[:, None] > places[None, :]).astype(bf)
     rank = jnp.where(match > 0, product(before, match.astype(bf)), -1.0).astype(bf)
-
-    in_own, in_other, grads, starts, cos_all, sin_all, gains, rank = tie(
-        in_own, in_other, grads, starts, cos_all, sin_all, gains, rank
-    )
+    in_own, in_other, out_other, grads[1, 0], starts, cos_all, sin_all, rank = tie(
+        in_own, in_other, out_other, grads[1, 0], starts, cos_all, sin_all, rank
+    )
+
     in_other.append(send(in_own[3], cores))
-    own_1 = send(cotangent, ring)
-    projected, normed_all, in_full, sums = project(
-        moves, gain_rows[0:1], blocks_x, in_own, in_other
-    )
-    totals = plane_total(moves, sums)
-    totals, own_1 = tie(totals, own_1)
-
-    near_1 = send(grads[0, 0][1], ring)
-    across_1 = send(own_1, second)
+    in_other, out_own, grads = tie(in_other, out_own, grads)
+    out_own.append(send(out_own[1], ring))
+    out_other.append(send(out_own[1], cores))
+    own_2 = send(own_1, ring)
+    grads[1, 1] = [send(item, second) for item in grads[1, 0]]
+    projected, normed_all, in_full, sums, small_rows, gains = project(
+        moves, blocks_x, in_own, in_other
+    )
+    sums, out_own, out_other, own_2, grads = tie(sums, out_own, out_other, own_2, grads)
+    out_own.append(send(out_own[2], ring))
+    out_other.append(send(out_own[2], cores))
+    sums = plane_step(moves, by_spot(moves, sums), 1)
+    sums, own_2 = tie(sums, own_2)
+    own_3 = send(own_2, ring)
+    totals = by_spot(moves, plane_step(moves, sums, 2))
+    totals, out_own, out_other = tie(totals, out_own, out_other)
+    out_other.append(send(out_own[3], cores))
+    totals, out_other, own_2 = tie(totals, out_other, own_2)
+
+    across_2 = send(own_2, second)
+    weights = [expert_in[0], send(expert_in[0], cores), expert_out[0], send(expert_out[0], cores)]
     attention = (moves, totals, starts, gains, projected, cos_all, sin_all)
     results = attend_forward(*attention, out_own, out_other)
     heads, out_full, parts = results[:4], results[4], results[5:]
-    parts, near_1, across_1 = tie(parts, near_1, across_1)
+    parts, weights, own_3, across_2 = tie(parts, weights, own_3, across_2)
 
     def cross(parts):
         return [send(parts[2], second), send(parts[3], second)]
@@ -1117,35 +1279,15 @@
         near = low(widen(parts[1]) + widen(backs[1]))
         return widen(parts[0]) + widen(backs[0]), send(near, first)
 
-    own_2 = send(own_1, ring)
     backs = cross(parts)
-    backs, own_2 = tie(backs, own_2)
-    near_2 = send(near_1, ring)
-    home, near = gather_near(parts, backs)
-    home, near, near_2 = tie(home, near, near_2)
-
-    grads[1, 0] = [own_1, near_1]
-    grads[1, 1] = [across_1, send(near_1, second)]
+    near_2 = send(grads[1, 0][1], ring)
+    backs, parts, near_2 = tie(backs, parts, near_2)
+    near = send(low(widen(parts[1]) + widen(backs[1])), first)
+    near_3 = send(near_2, ring)
+    (near,) = tie(near)
     grads[2, 0] = [own_2, near_2]
-    inputs = widen(tokens)
-    residual = inputs + (home + widen(near))
-    normed = low(root_norm(residual, gain_rows[3][None]))
-    logits = dot_last(normed, router_full)
-    router_probs = softmax_rows(logits)
-    gate_total = jnp.sum(router_probs * match, axis=1, keepdims=True)
-    gate_values = router_probs * match / gate_total
-    upper = lax.reduce_precision(gate_values, 8, 7)
-    extra = jnp.concatenate(
-        [
-            rank,
-            upper.astype(bf),
-            (gate_values - upper).astype(bf),
-            jnp.zeros((row_count, WIDE - 3 * experts), bf),
-        ],
-        axis=1,
-    )
-    rows = jnp.concatenate([normed, extra], axis=1)
-    rows, grads = tie(rows, grads)
+    residual, rows, probs = route(tokens, parts[0], backs[0], near, match, rank, small_rows)
+    rows, near_3 = tie(rows, near_3)
 
     meta = (moves.device // 2).reshape(1).astype(jnp.int32)
     saved, done = None, 0
@@ -1170,7 +1312,7 @@
 
     row_near = send(rows, first)
     row_1 = send(rows, ring)
-    (row_near,) = tie(row_near)
+    rows, row_near = tie(rows, row_near)
 
     near_row_1 = send(row_near, ring)
     across = [send(rows, second), send(row_near, second)]
@@ -1179,86 +1321,72 @@
 
     row_2 = send(row_1, ring)
     across_row_1 = send(row_1, second)
-    grads[2, 1] = [send(item, second) for item in grads[2, 0]]
+    grads[2, 1] = [across_2, send(near_2, second)]
+    grads[3, 0] = [own_3, near_3]
     run_expert(0, 1, across)
-    saved, near_row_1, across_row_1, grads[2, 1] = tie(
-        saved, near_row_1, across_row_1, grads[2, 1]
-    )
+    saved, near_row_1, across_row_1 = tie(saved, near_row_1, across_row_1)
 
     near_row_2 = send(near_row_1, ring)
-    own_3 = send(own_2, ring)
     across = [across_row_1, send(near_row_1, second)]
+    across_3 = send(own_3, second)
     run_expert(1, 0, [row_1, near_row_1])
-    saved, across, row_2 = tie(saved, across, row_2)
+    saved, across, row_2, row_parts[0], grads[2, 1], near_3 = tie(
+        saved, across, row_2, row_parts[0], grads[2, 1], near_3
+    )
 
     row_3 = send(row_2, ring)
     across_row_2 = send(row_2, second)
+    grads[3, 1] = [across_3, send(near_3, second)]
     run_expert(1, 1, across)
-    saved, near_row_2, own_3, across_row_2 = tie(saved, near_row_2, own_3, across_row_2)
+    saved, near_row_2, across_row_2, row_parts[0], grads[3, 1] = tie(
+        saved, near_row_2, across_row_2, row_parts[0], grads[3, 1]
+    )
 
     near_row_3 = send(near_row_2, ring)
     across = [across_row_2, send(near_row_2, second)]
-    grads[3, 0] = [own_3, send(own_3, first)]
-    across_3 = send(own_3, second)
+    backs_0 = cross(row_parts[0])
+    run_expert(2, 0, [row_2, near_row_2])
+    saved, across, row_3, row_parts[1] = tie(saved, across, row_3, row_parts[1])
+
+    across_row_3 = send(row_3, second)
     backs_1 = cross(row_parts[1])
-    run_expert(2, 0, [row_2, near_row_2])
-    saved, across, row_3, grads[3, 0], across_3 = tie(
-        saved, across, row_3, grads[3, 0], across_3
-    )
-
-    across_row_3 = send(row_3, second)
-    grads[3, 1] = [across_3, send(grads[3, 0][1], second)]
     run_expert(2, 1, across)
-    saved, near_row_3, across_row_3, backs_1 = tie(saved, near_row_3, across_row_3, backs_1)
+    saved, near_row_3, across_row_3, backs_0 = tie(saved, near_row_3, across_row_3, backs_0)
 
     across = [across_row_3, send(near_row_3, second)]
-    home_1, near_1 = gather_near(row_parts[1], backs_1)
+    run_expert(3, 0, [row_3, near_row_3])
+    saved, across, backs_1, row_parts[2] = tie(saved, across, backs_1, row_parts[2])
+
+    pair = [send(low(widen(row_parts[1][n]) + widen(backs_1[n])), ring) for n in range(2)]
     backs_2 = cross(row_parts[2])
-    run_expert(3, 0, [row_3, near_row_3])
-    saved, across, grads[3, 1], home_1, near_1, backs_2 = tie(
-        saved, across, grads[3, 1], home_1, near_1, backs_2
-    )
-
-    total = send(low(home_1 + widen(near_1)), ring)
-    home_2, near_2 = gather_near(row_parts[2], backs_2)
-    backs_0 = cross(row_parts[0])
     run_expert(3, 1, across)
-    saved, total, home_2, near_2 = tie(saved, total, home_2, near_2)
-
-    total = send(low(widen(total) + (home_2 + widen(near_2))), ring)
+    saved, pair, backs_2 = tie(saved, pair, backs_2)
+
+    near = send(low(widen(pair[1]) + widen(row_parts[2][1]) + widen(backs_2[1])), first)
+    home = widen(pair[0]) + (widen(row_parts[2][0]) + widen(backs_2[0]))
     backs_3 = cross(row_parts[3])
     x_rows, dy_rows, m_own, m_other, du_own, du_other = saved
     in_theirs = dot_first(x_rows, du_other)
-    total, backs_3, backs_0, in_theirs = tie(total, backs_3, backs_0, in_theirs)
-
-    home_3, near_3 = gather_near(row_parts[3], backs_3)
-    home_0, near_0 = gather_near(row_parts[0], backs_0)
+    home, near, backs_3, in_theirs = tie(home, near, backs_3, in_theirs)
+
+    total = send(low(home + widen(near)), ring)
+    home, near = gather_near(row_parts[3], backs_3)
     in_theirs = send(in_theirs, cores)
     out_theirs = dot_first(m_other, dy_rows)
-    home_3, near_3, home_0, near_0, out_theirs = tie(home_3, near_3, home_0, near_0, out_theirs)
-
-    total = send(low(widen(total) + (home_3 + widen(near_3))), ring)
+    total, home, near, out_theirs = tie(total, home, near, out_theirs)
+
+    total = send(low(widen(total) + (home + widen(near))), ring)
+    _, near_0 = gather_near(row_parts[0], backs_0)
     out_theirs = send(out_theirs, cores)
     out_backs = {1: cross(out_parts[1])}
-    (total,) = tie(total)
-    row_total = widen(total) + (home_0 + widen(near_0))
-
-    upstream = widen(cotangent)
-    dispatch_grad = row_total[:, :D]
-    gate_grad = jnp.sum(row_total[:, D : D + 2 * experts].reshape(row_count, experts, 2), axis=2)
-    chosen_grad = (
-        match * (gate_grad - jnp.sum(gate_grad * gate_values, axis=1, keepdims=True)) / gate_total
-    )
-    logit_grad = low(
-        router_probs * (chosen_grad - jnp.sum(chosen_grad * router_probs, axis=1, keepdims=True))
-    )
-    normed_grad = dispatch_grad + product(logit_grad, router_full)
-    _, second_back = jax.vjp(root_norm, residual, gain_rows[3])
-    residual_norm_grad, second_gain_grad = second_back(normed_grad)
-    residual_grad = upstream + residual_norm_grad
-    branch_grad = low(residual_grad)
+    total, near_0 = tie(total, near_0)
+    residual_grad, branch_grad, router_grad, second_gain_grad = route_back(
+        total, row_parts[0][0], backs_0[0], near_0, match, probs, small_rows, residual, cotangent
+    )
     branch_near = send(branch_grad, first)
-    branch_near, out_backs = tie(branch_near, out_backs)
+    branch_grad, branch_near, out_backs, out_parts = tie(
+        branch_grad, branch_near, out_backs, out_parts
+    )
 
     branch_blocks = [
         branch_grad,
@@ -1266,103 +1394,94 @@
         send(branch_grad, second),
         send(branch_near, second),
     ]
-    expert_in_grad = dot_first(x_rows, du_own) + in_theirs
+    out_pair = [
+        send(low(widen(out_parts[1][n]) + widen(out_backs[1][n])), ring) for n in range(2)
+    ]
     expert_out_grad = dot_first(m_own, dy_rows) + out_theirs
-    router_grad = dot_first(logit_grad, normed)
-    branch_blocks, expert_in_grad, expert_out_grad, router_grad = tie(
-        branch_blocks, expert_in_grad, expert_out_grad, router_grad
-    )
-
-    out_homes = {1: gather_near(out_parts[1], out_backs[1])}
+    branch_blocks, expert_out_grad, out_parts = tie(branch_blocks, expert_out_grad, out_parts)
+
     out_backs[2] = cross(out_parts[2])
     dq, dk, dv, dots, own_grad, other_grad, gain_grads = attend_backward(
         *attention, heads, out_full, branch_blocks
     )
-    dots, out_homes, out_backs = tie(dots, out_homes, out_backs)
-
-    out_total = send(low(out_homes[1][0] + widen(out_homes[1][1])), ring)
+    dots, out_backs, out_parts, out_pair, other_grad = tie(
+        dots, out_backs, out_parts, out_pair, other_grad
+    )
+
     other_grad = send(other_grad, cores)
-    out_homes[2] = gather_near(out_parts[2], out_backs[2])
+    out_pair = [
+        send(low(widen(out_pair[n]) + widen(out_parts[2][n]) + widen(out_backs[2][n])), ring)
+        for n in range(2)
+    ]
+    dots = plane_step(moves, by_spot(moves, dots), 1)
+    dots = by_spot(moves, plane_step(moves, dots, 2))
+    dots, other_grad, out_parts = tie(dots, other_grad, out_parts)
+    out_sums = [widen(own_grad[k]) + widen(other_grad[k]) for k in range(planes)]
     out_backs[3] = cross(out_parts[3])
-    dots = plane_total(moves, dots)
+    small = (router_grad, small_rows, gain_grads, second_gain_grad)
     projected_grad, *in_grads = project_back(
-        moves, totals, dots, gains, projected, dq, dk, dv, normed_all
-    )
-    in_grads, out_total, out_homes, out_backs, other_grad = tie(
-        in_grads, out_total, out_homes, out_backs, other_grad
-    )
-
-    others = [send(in_grads[planes + k], cores) for k in range(planes)]
-    in_sums = [widen(in_grads[k]) + widen(others[k]) for k in range(planes)]
-    out_sums = [widen(own_grad[k]) + widen(other_grad[k]) for k in range(planes)]
-    in_total = send(low(in_sums[1]), ring)
+        moves, totals, dots, gains, small, in_full, projected, dq, dk, dv, normed_all
+    )
+    in_grads, projected_grad, out_pair, out_backs, out_parts, out_sums = tie(
+        in_grads, projected_grad, out_pair, out_backs, out_parts, out_sums
+    )
+
+    *in_grads, others, others_rest = in_grads
+    others = send(others, cores)
+    projected_grad, in_full, others, out_backs = tie(projected_grad, in_full, others, out_backs)
+    in_total = send(low(widen(in_grads[1]) + widen(others)), ring)
+    others_rest = send(others_rest, cores)
+    out_near = send(
+        low(widen(out_pair[1]) + widen(out_parts[3][1]) + widen(out_backs[3][1])), first
+    )
     out_share = send(low(out_sums[1]), ring)
-    *parts, first_gain_grad = rows_back(projected_grad, in_full, blocks_x)
-    in_total, out_share, parts = tie(in_total, out_share, parts)
-
+    parts = rows_back(projected_grad, in_full)
+    in_total, others_rest, parts, out_near, x_rows, out_parts = tie(
+        in_total, others_rest, parts, out_near, x_rows, out_parts
+    )
+
+    in_total = send(low(widen(in_total) + (widen(in_grads[2]) + widen(others_rest[0]))), ring)
     backs = cross(parts)
-    in_total = send(low(widen(in_total) + in_sums[2]), ring)
+    out_total = low(
+        widen(out_pair[0])
+        + (widen(out_parts[3][0]) + widen(out_backs[3][0]))
+        + widen(out_near)
+    )
+    expert_in_grad = dot_first(x_rows, du_own) + in_theirs
+    in_total, backs, expert_in_grad, out_parts, out_total, out_share = tie(
+        in_total, backs, expert_in_grad, out_parts, out_total, out_share
+    )
+
+    home, near = gather_near(parts, backs)
+    in_total = send(low(widen(in_total) + (widen(in_grads[3]) + widen(others_rest[1]))), ring)
+    out_backs[0] = cross(out_parts[0])
     out_share = send(low(widen(out_share) + out_sums[2]), ring)
-    out_total = send(low(widen(out_total) + out_homes[2][0] + widen(out_homes[2][1])), ring)
-    in_total, out_share, backs = tie(in_total, out_share, backs)
-
-    home, near = gather_near(parts, backs)
-    in_total = send(low(widen(in_total) + in_sums[3]), ring)
-    out_share = widen(send(low(widen(out_share) + out_sums[3]), ring)) + out_sums[0]
-    out_homes[3] = gather_near(out_parts[3], out_backs[3])
-    out_backs[0] = cross(out_parts[0])
-    in_total, home, near, out_total, out_homes, out_backs = tie(
-        in_total, home, near, out_total, out_homes, out_backs
-    )
-
-    out_total = send(low(widen(out_total) + out_homes[3][0] + widen(out_homes[3][1])), ring)
-    in_total = low(widen(in_total) + in_sums[0])
+    out_total = send(out_total, ring)
+    in_total, home, near = tie(in_total, home, near)
+
+    in_total = low(widen(in_total) + (widen(in_grads[0]) + widen(others_rest[2])))
     traded = [in_total[0]] + [send(in_total[m], moves.spots[m]) for m in range(1, SPOTS)]
-    in_share = join_columns(spot, traded)
-    out_homes[0] = gather_near(out_parts[0], out_backs[0])
-    output = low(residual + (widen(out_total) + (out_homes[0][0] + widen(out_homes[0][1]))))
-    _, first_back = jax.vjp(lambda value: root_norm(value, gain_rows[0]), inputs)
+    _, first_back = jax.vjp(
+        lambda value: root_norm(value, small_rows[FIRST_GAIN]), widen(tokens)
+    )
     (input_norm_grad,) = first_back(home + widen(near))
     input_grad = residual_grad + input_norm_grad
-
-    here = (jnp.arange(SPOTS, dtype=jnp.int32) == spot)[None, :, None]
-
-    def own_gain(row):
-        return jnp.where(here, row.reshape(lines, 1, HEAD_DIM), 0.0).reshape(1, D)
-
-    small_grad = jnp.concatenate(
-        [
-            router_grad,
-            first_gain_grad,
-            own_gain(gain_grads[0]),
-            own_gain(gain_grads[1]),
-            second_gain_grad[None],
-        ]
-    )
-    span = PLANE * own_rows
-
-    def plane_part(step):
-        return lax.dynamic_slice_in_dim(small_grad, moves.planes_back[step] * span, span, 1)
-
-    small_total = plane_part(1)
-    for step in (*range(2, planes), 0):
-        small_total = plane_part(step) + send(small_total, ring)
-    for bit, pairs in ((spot // 2, moves.spots[2]), (spot % 2, moves.spots[1])):
-        span //= 2
-        kept = lax.dynamic_slice_in_dim(small_total, bit * span, span, 1)
-        given = lax.dynamic_slice_in_dim(small_total, (1 - bit) * span, span, 1)
-        small_total = kept + send(given, pairs)
-    left, right = small_total[:, :own_rows], small_total[:, own_rows:]
-    small_share = jnp.where(core == 0, left, right) + send(
-        jnp.where(core == 0, right, left), cores
-    )
+    traded, input_grad, out_backs, out_share, out_total = tie(
+        traded, input_grad, out_backs, out_share, out_total
+    )
+    out_share = send(low(widen(out_share) + out_sums[3]), ring)
+
+    out_home, out_near = gather_near(out_parts[0], out_backs[0])
+    in_share, small_share = join_columns(spot, traded)
+    out_share = widen(out_share) + out_sums[0]
+    output = low(residual + (widen(out_total) + (out_home + widen(out_near))))
     return (
         output,
         input_grad,
-        small_share[SMALL - 4 :],
+        small_share[:, FIRST_GAIN:SMALL].T,
         in_share,
         out_share,
-        small_share[: SMALL - 4].T,
+        small_share[:, :FIRST_GAIN],
         expert_in_grad[None],
         expert_out_grad[None],
     )

time: 819 us -> 708 us (0.86)
  waiting for transfers between devices: 349 us -> 252 us
  local copies, waits for them, and re-layouts: 51.4 us -> 25 us
  Pallas kernels: 177 us -> 202 us
  other arithmetic: 52.3 us -> 43 us
    ppermute x123 -> x109, waiting for transfers between devices: 349 us -> 252 us  [send(): return lax.ppermute(value, 'fsdp', pairs)]
    pallas_call x2 -> x4, Pallas kernels: 16.4 us -> 32.9 us  [the longest x1 20.2 us: project_back(): pl.pallas_call(functools.partial(project_back_body, planes, own_rows), ou...]
    unnamed x229 -> x173, local copies, waits for them, and re-layouts: 28.2 us -> 12.5 us
    dot_general x5 -> x4, matrix products: 43.7 us -> 47.8 us  [dot_first(): lax.dot_general(left, right, (((0,), (0,)), ((), ())), preferred_element_...]
    convert_element_type x26 -> x23, other arithmetic: 24 us -> 27.4 us  [low(): return value.astype(bf)]
    ppermute x123 -> x109, starting transfers between devices: 129 us -> 126 us  [send(): return lax.ppermute(value, 'fsdp', pairs)]
  transfers between devices with their start and end apart: 123 -> 109, of which waited for: 50 -> 44; matrix products, arithmetic and copies ran while one was open for 15% -> 14% of each run, Pallas kernels for 17% -> 29%
where the time goes in v4:
time: 708 us; the launch traced here: 699 us
  waiting for transfers between devices  252 us (36%)
  Pallas kernels  202 us (29%)
  starting transfers between devices  126 us (18%)
  matrix products  48.6 us (7%)
  other arithmetic  43 us (6%)
  local copies, waits for them, and re-layouts  25 us (4%)
    ppermute x109, waiting for transfers between devices, send(): return lax.ppermute(value, 'fsdp', pairs)  252 us
    ppermute x109, starting transfers between devices, send(): return lax.ppermute(value, 'fsdp', pairs)  126 us
    pallas_call x8, Pallas kernels, expert_blocks(): pl.pallas_call(functools.partial(expert_body, index, cap, experts, blocks...  103 us
    dot_general x4, matrix products, dot_first(): lax.dot_general(left, right, (((0,), (0,)), ((), ())), preferred_element_...  47.8 us
    convert_element_type x23, other arithmetic, low(): return value.astype(bf)  27.4 us
    pallas_call x1, Pallas kernels, attend_backward(): pl.pallas_call(backward_body, grid=(SPOTS,), out_shape=[shape((rows, mine...  22.5 us
    pallas_call x1, Pallas kernels, project_back(): pl.pallas_call(functools.partial(project_back_body, planes, own_rows), ou...  20.2 us
    pallas_call x1, Pallas kernels, attend_forward(): pl.pallas_call(functools.partial(forward_body, planes, own_rows), grid=(S...  14.7 us
  transfers between devices with their start and end apart: 109, of which 44 were waited for; matrix products, arithmetic and copies ran while one was open for 14% of the time, Pallas kernels for 29%

profile of v4, /device:TPU:0, one launch (start us, length us, event | category | flops | bytes accessed | tf_op | source)
XLA Modules:
  0.0 699.0 jit_solution(10847351164710814769)
XLA Ops:
  0.7 4.1 collective-permute-start.3
  11.8 4.9 collective-permute-done
  16.7 4.3 collective-permute-done.1
  31.7 15.0 %collective-permute-done.6.refs_1_ = bf16[192,2048]{1,0:T(8,128)(2,1)} collective-permute-done((bf16[192,2048]{1,0:T(8,128)(2,1)S(1)}, bf16[192,2048]{1,0:T(8,128)(2,1)}, u32[]{:S(2)}, u32[]{:S(2)}) %collective-permute-start.6) | collective-permute-done | bytes 786464 | tf_op jit(solution)/shard_map/ppermute | solution.py:337
  51.5 9.2 %collective-permute-done.11.refs_3_ = bf16[192,2048]{1,0:T(8,128)(2,1)} collective-permute-done((bf16[192,2048]{1,0:T(8,128)(2,1)S(1)}, bf16[192,2048]{1,0:T(8,128)(2,1)}, u32[]{:S(2)}, u32[]{:S(2)}) %collective-permute-start.11) | collective-permute-done | bytes 786464 | tf_op jit(solution)/shard_map/ppermute | solution.py:337
  73.9 6.7 collective-permute-done.15.refs_3_
  80.6 5.3 collective-permute-done.12.refs_7_
  90.4 5.8 collective-permute-done.17.refs_1_
  99.8 7.3 %collective-permute-done.19.refs_3_ = bf16[192,2048]{1,0:T(8,128)(2,1)S(1)} collective-permute-done((bf16[192,2048]{1,0:T(8,128)(2,1)}, bf16[192,2048]{1,0:T(8,128)(2,1)S(1)}, u32[]{:S(2)}, u32[]{:S(2)}) %collective-permute-start.19) | collective-permute-done | bytes 786464 | tf_op jit(solution)/shard_map/ppermute | solution.py:337
  112.7 4.2 collective-permute-done.22.refs_2_
  116.9 12.5 %project.1 = (f32[768,1536]{1,0:T(8,128)}, bf16[768,2048]{1,0:T(8,128)(2,1)}, bf16[2048,1664]{1,0:T(8,128)(2,1)}, f32[2,4,192]{2,1,0:T(4,128)}, f32[32,2048]{1,0:T(8,128)}, /*index=5*/f32[2,512]{1,0:T(2,128)}) custom-call(s32[6]{0:T(128)} %pad_add_fusion.meta, bf16[192,2048]{1,0:T(8,128)(2,1)} %tokens.1, bf16[192,2048]{1,0:T(8,128)(2,1)} %collective-permute-done.6.refs_1_, ...), custom_call_target="tpu_custom_call" | custom-call | flops 5000000000 | bytes 20971520 | tf_op jit(solution)/shard_map/project/pallas_call | solution.py:693
  150.6 14.7 %attend_forward.1 = (bf16[768,512]{1,0:T(8,128)(2,1)}, bf16[768,512]{1,0:T(8,128)(2,1)}, bf16[768,512]{1,0:T(8,128)(2,1)}, bf16[768,512]{1,0:T(8,128)(2,1)}, bf1...) custom-call(s32[6]{0:T(128)} %pad_add_fusion.meta, ...), custom_call_target="tpu_custom_call" | custom-call | flops 5000000000 | bytes 20971520 | tf_op jit(solution)/shard_map/attend_forward/pallas_call | solution.py:790
  168.3 14.5 %collective-permute-done.36.refs_3_ = bf16[192,2048]{1,0:T(8,128)(2,1)} collective-permute-done((bf16[192,2048]{1,0:T(8,128)(2,1)}, bf16[192,2048]{1,0:T(8,128)(2,1)}, u32[]{:S(2)}, u32[]{:S(2)}) %collective-permute-start.36) | collective-permute-done | bytes 786464 | tf_op jit(solution)/shard_map/ppermute | solution.py:337
  182.8 4.1 collective-permute-done.35
  194.1 6.3 collective-permute-done.37.near
  201.3 4.2 route.1
  212.5 8.3 %collective-permute-done.39.refs_1_ = bf16[192,2176]{1,0:T(8,128)(2,1)} collective-permute-done((bf16[192,2176]{1,0:T(8,128)(2,1)}, bf16[192,2176]{1,0:T(8,128)(2,1)}, u32[]{:S(2)}, u32[]{:S(2)}) %collective-permute-start.39) | collective-permute-done | bytes 835616 | tf_op jit(solution)/shard_map/ppermute | solution.py:337
  226.7 12.8 %expert_blocks.8 = (bf16[2048,2048]{1,0:T(8,128)(2,1)}, bf16[2048,2048]{1,0:T(8,128)(2,1)}, bf16[2048,512]{1,0:T(8,128)(2,1)}, bf16[2048,512]{1,0:T(8,128)(2,1)}...) custom-call(s32[1]{0:T(128)} %bitcast.12.meta, ...), custom_call_target="tpu_custom_call" | custom-call | flops 7600000000 | bytes 31457280 | tf_op jit(solution)/shard_map/expert_blocks/pallas_call | solution.py:555
  248.3 12.8 %expert_blocks.9 = (bf16[2048,2048]{1,0:T(8,128)(2,1)}, bf16[2048,2048]{1,0:T(8,128)(2,1)}, bf16[2048,512]{1,0:T(8,128)(2,1)}, bf16[2048,512]{1,0:T(8,128)(2,1)}...) custom-call(s32[1]{0:T(128)} %bitcast.12.meta, ...), custom_call_target="tpu_custom_call", output_to_operand_aliasing={{0}: (9, {}), {1}: (10, {}), {2}: (11, {}), {3}: (12, {}), ... | custom-call | flops 7600000000 | bytes 31457280 | tf_op jit(solution)/shard_map/expert_blocks/pallas_call | solution.py:555
  263.5 12.9 %expert_blocks.10 = (bf16[2048,2048]{1,0:T(8,128)(2,1)}, bf16[2048,2048]{1,0:T(8,128)(2,1)}, bf16[2048,512]{1,0:T(8,128)(2,1)}, bf16[2048,512]{1,0:T(8,128)(2,1)...) custom-call(s32[1]{0:T(128)} %bitcast.12.meta, ...), custom_call_target="tpu_custom_call", output_to_operand_aliasing={{0}: (9, {}), {1}: (10, {}), {2}: (11, {}), {3}: (12, {}), ... | custom-call | flops 7600000000 | bytes 31457280 | tf_op jit(solution)/shard_map/expert_blocks/pallas_call | solution.py:555
  276.4 5.9 collective-permute-done.47.refs_3_
  285.4 12.8 %expert_blocks.11 = (bf16[2048,2048]{1,0:T(8,128)(2,1)}, bf16[2048,2048]{1,0:T(8,128)(2,1)}, bf16[2048,512]{1,0:T(8,128)(2,1)}, bf16[2048,512]{1,0:T(8,128)(2,1)...) custom-call(s32[1]{0:T(128)} %bitcast.12.meta, ...), custom_call_target="tpu_custom_call", output_to_operand_aliasing={{0}: (9, {}), {1}: (10, {}), {2}: (11, {}), {3}: (12, {}), ... | custom-call | flops 7600000000 | bytes 31457280 | tf_op jit(solution)/shard_map/expert_blocks/pallas_call | solution.py:555
  298.2 5.2 collective-permute-done.50.refs_2_
  303.4 8.5 %collective-permute-done.51.refs_3_ = bf16[192,2048]{1,0:T(8,128)(2,1)} collective-permute-done((bf16[192,2048]{1,0:T(8,128)(2,1)S(1)}, bf16[192,2048]{1,0:T(8,128)(2,1)}, u32[]{:S(2)}, u32[]{:S(2)}) %collective-permute-start.51) | collective-permute-done | bytes 786464 | tf_op jit(solution)/shard_map/ppermute | solution.py:337
  315.2 12.8 %expert_blocks.12 = (bf16[2048,2048]{1,0:T(8,128)(2,1)}, bf16[2048,2048]{1,0:T(8,128)(2,1)}, bf16[2048,512]{1,0:T(8,128)(2,1)}, bf16[2048,512]{1,0:T(8,128)(2,1)...) custom-call(s32[1]{0:T(128)} %bitcast.12.meta, ...), custom_call_target="tpu_custom_call", output_to_operand_aliasing={{0}: (9, {}), {1}: (10, {}), {2}: (11, {}), {3}: (12, {}), ... | custom-call | flops 7600000000 | bytes 31457280 | tf_op jit(solution)/shard_map/expert_blocks/pallas_call | solution.py:555
  330.9 13.0 %expert_blocks.13 = (bf16[2048,2048]{1,0:T(8,128)(2,1)}, bf16[2048,2048]{1,0:T(8,128)(2,1)}, bf16[2048,512]{1,0:T(8,128)(2,1)}, bf16[2048,512]{1,0:T(8,128)(2,1)...) custom-call(s32[1]{0:T(128)} %bitcast.12.meta, ...), custom_call_target="tpu_custom_call", output_to_operand_aliasing={{0}: (9, {}), {1}: (10, {}), {2}: (11, {}), {3}: (12, {}), ... | custom-call | flops 7600000000 | bytes 31457280 | tf_op jit(solution)/shard_map/expert_blocks/pallas_call | solution.py:555
  345.4 6.2 collective-permute-done.55.refs_0_
  353.2 13.0 %expert_blocks.14 = (bf16[2048,2048]{1,0:T(8,128)(2,1)}, bf16[2048,2048]{1,0:T(8,128)(2,1)}, bf16[2048,512]{1,0:T(8,128)(2,1)}, bf16[2048,512]{1,0:T(8,128)(2,1)...) custom-call(s32[1]{0:T(128)} %bitcast.12.meta, ...), custom_call_target="tpu_custom_call", output_to_operand_aliasing={{0}: (9, {}), {1}: (10, {}), {2}: (11, {}), {3}: (12, {}), ... | custom-call | flops 7600000000 | bytes 31457280 | tf_op jit(solution)/shard_map/expert_blocks/pallas_call | solution.py:555
  369.6 9.0 %collective-permute-done.58.refs_1_ = bf16[192,2176]{1,0:T(8,128)(2,1)} collective-permute-done((bf16[192,2176]{1,0:T(8,128)(2,1)}, bf16[192,2176]{1,0:T(8,128)(2,1)}, u32[]{:S(2)}, u32[]{:S(2)}) %collective-permute-start.58) | collective-permute-done | bytes 835616 | tf_op jit(solution)/shard_map/ppermute | solution.py:337
  385.8 12.8 %expert_blocks.15 = (bf16[2048,2048]{1,0:T(8,128)(2,1)}, bf16[2048,2048]{1,0:T(8,128)(2,1)}, bf16[2048,512]{1,0:T(8,128)(2,1)}, bf16[2048,512]{1,0:T(8,128)(2,1)...) custom-call(s32[1]{0:T(128)} %bitcast.12.meta, ...), custom_call_target="tpu_custom_call", output_to_operand_aliasing={{0}: (9, {}), {1}: (10, {}), {2}: (11, {}), {3}: (12, {}), ... | custom-call | flops 7600000000 | bytes 31457280 | tf_op jit(solution)/shard_map/expert_blocks/pallas_call | solution.py:555
  403.3 9.3 %collective-permute-done.61 = bf16[192,2176]{1,0:T(8,128)(2,1)} collective-permute-done((bf16[192,2176]{1,0:T(8,128)(2,1)}, bf16[192,2176]{1,0:T(8,128)(2,1)}, u32[]{:S(2)}, u32[]{:S(2)}) %collective-permute-start.61) | collective-permute-done | bytes 835616 | tf_op jit(solution)/shard_map/ppermute | solution.py:337
  413.6 15.7 %fusion.19 = f32[2048,1024]{1,0:T(8,128)} fusion(bf16[2048,2048]{1,0:T(8,128)(2,1)} %get-tuple-element.861, bf16[2048,1024]{1,0:T(8,128)(2,1)} %get-tuple-element.719), kind=kOutput, calls=%fused_computation.107 | convolution fusion | flops 8589934592 | bytes 20971520 | tf_op jit(solution)/shard_map/dot_general | solution.py:71
  431.1 3.7 collective-permute-done.67
  439.0 6.0 fusion.20
  445.2 4.0 collective-permute-done.69
  456.2 15.0 %collective-permute-done.71.near = bf16[192,2176]{1,0:T(8,128)(2,1)S(1)} collective-permute-done((bf16[192,2176]{1,0:T(8,128)(2,1)S(1)}, bf16[192,2176]{1,0:T(8,128)(2,1)S(1)}, u32[]{:S(2)}, u32[]{:S(2)}) %collective-permute-start.71) | collective-permute-done | bytes 835616 | tf_op jit(solution)/shard_map/ppermute | solution.py:337
  474.8 5.9 route_back.1
  480.8 12.1 %collective-permute-done.72.refs_1_ = bf16[192,2048]{1,0:T(8,128)(2,1)S(1)} collective-permute-done((bf16[192,2048]{1,0:T(8,128)(2,1)}, bf16[192,2048]{1,0:T(8,128)(2,1)S(1)}, u32[]{:S(2)}, u32[]{:S(2)}) %collective-permute-start.72) | collective-permute-done | bytes 786464 | tf_op jit(solution)/shard_map/ppermute | solution.py:337
  501.0 10.3 %convolution_add_fusion.1 = f32[512,2048]{1,0:T(8,128)} fusion(f32[512,2048]{1,0:T(8,128)} %collective-permute-done.77, bf16[2048,512]{1,0:T(8,128)(2,1)S(1)} %copy-done.1, bf16[2048,2048]{1,0:T(8,128)(2,1)} %get-tuple-element.727), kind=kOutput, calls=%fused_computation.7 | convolution fusion | flops 4296015872 | bytes 18874368 | tf_op jit(solution)/shard_map/dot_general | solution.py:71
  511.3 8.1 %collective-permute-done.76.refs_3_ = bf16[192,2048]{1,0:T(8,128)(2,1)S(1)} collective-permute-done((bf16[192,2048]{1,0:T(8,128)(2,1)S(1)}, bf16[192,2048]{1,0:T(8,128)(2,1)S(1)}, u32[]{:S(2)}, u32[]{:S(2)}) %collective-permute-start.76) | collective-permute-done | bytes 786464 | tf_op jit(solution)/shard_map/ppermute | solution.py:337
  521.4 22.5 %attend_backward.1 = (f32[768,512]{1,0:T(8,128)}, f32[768,512]{1,0:T(8,128)}, bf16[768,512]{1,0:T(8,128)(2,1)}, f32[2,4,192]{2,1,0:T(4,128)}, bf16[4,64,2048]{2,...) custom-call(s32[6]{0:T(128)} %pad_add_fusion.meta, f32[2,4,192]{2,1,0:T(4,128)} %bitcast_select_fusion.2.totals, ...), custom_call_target="tpu_custom_call" | custom-call | flops 7000000000 | bytes 26214400 | tf_op jit(solution)/shard_map/attend_backward/pallas_call | solution.py:885
  559.4 20.2 %project_back.1 = (bf16[768,1536]{1,0:T(8,128)(2,1)}, bf16[4,64,1664]{2,1,0:T(8,128)(2,1)}, bf16[4,64,1664]{2,1,0:T(8,128)(2,1)}, bf16[4,64,1664]{2,1,0:T(8,128)...) custom-call(s32[6]{0:T(128)} %pad_add_fusion.meta, ...), custom_call_target="tpu_custom_call" | custom-call | flops 5000000000 | bytes 31457280 | tf_op jit(solution)/shard_map/project_back/pallas_call | solution.py:1031
  580.6 5.8 collective-permute-done.85
  598.9 13.9 %rows_back.1 = (bf16[192,2048]{1,0:T(8,128)(2,1)}, bf16[192,2048]{1,0:T(8,128)(2,1)}, bf16[192,2048]{1,0:T(8,128)(2,1)}, bf16[192,2048]{1,0:T(8,128)(2,1)}) custom-call(bf16[768,1536]{1,0:T(8,128)(2,1)} %get-tuple-element.842.dp_ref, bf16[2048,1664]{1,0:T(8,128)(2,1)} %get-tuple-element.843.in_w), custom_call_target="tpu_custom_call" | custom-call | flops 5000000000 | bytes 12582912 | tf_op jit(solution)/shard_map/rows_back/pallas_call | solution.py:1062
  614.6 3.7 collective-permute-start.93
  620.3 15.8 %convolution_add_fusion = f32[2048,1024]{1,0:T(8,128)} fusion(f32[2048,1024]{1,0:T(8,128)} %collective-permute-done.96, bf16[2048,2048]{1,0:T(8,128)(2,1)} %get-tuple-element.861, bf16[2048,1024]{1,0:T(8,128)(2,1)} %get-tuple-element.862), kind=kOutput, calls=%fused_computation.6 | convolution fusion | flops 8592031744 | bytes 29360128 | tf_op jit(solution)/shard_map/dot_general | solution.py:71
  646.0 13.4 %collective-permute-done.99 = bf16[192,2048]{1,0:T(8,128)(2,1)S(1)} collective-permute-done((bf16[192,2048]{1,0:T(8,128)(2,1)S(1)}, bf16[192,2048]{1,0:T(8,128)(2,1)S(1)}, u32[]{:S(2)}, u32[]{:S(2)}) %collective-permute-start.99) | collective-permute-done | bytes 786464 | tf_op jit(solution)/shard_map/ppermute | solution.py:337
  672.2 9.1 %collective-permute-done.106 = bf16[192,2048]{1,0:T(8,128)(2,1)S(1)} collective-permute-done((bf16[192,2048]{1,0:T(8,128)(2,1)S(1)}, bf16[192,2048]{1,0:T(8,128)(2,1)S(1)}, u32[]{:S(2)}, u32[]{:S(2)}) %collective-permute-start.106) | collective-permute-done | bytes 786464 | tf_op jit(solution)/shard_map/ppermute | solution.py:337
  (450 shorter events, 233.2 us)
Async XLA Ops:
  23.8 22.9 %collective-permute-start.4 = (bf16[4,64,1664]{2,1,0:T(8,128)(2,1)S(1)}, bf16[4,64,1664]{2,1,0:T(8,128)(2,1)}, u32[]{:S(2)}, u32[]{:S(2)}) collective-permute-start(bf16[4,64,1664]{2,1,0:T(8,128)(2,1)S(1)} %pad_maximum_fusion.refs_4_), channel_id=1, source_target_pairs={{0,16},{1,17},{2,18},{3,19},{4,20},{5,21},{6,22},{7,23},{8,0},{9,1... | collective-permute-start | bytes 2555912 | tf_op jit(solution)/shard_map/ppermute | solution.py:337
  28.7 32.1 %collective-permute-start.11 = (bf16[192,2048]{1,0:T(8,128)(2,1)S(1)}, bf16[192,2048]{1,0:T(8,128)(2,1)}, u32[]{:S(2)}, u32[]{:S(2)}) collective-permute-start(bf16[192,2048]{1,0:T(8,128)(2,1)S(1)} %copy-done.32), channel_id=1, source_target_pairs={{0,2},{1,5},{2,0},{3,7},{4,6},{5,1},{6,4},{7,3},{8,10},{9,13},{10,... | collective-permute-start | bytes 2359304 | tf_op jit(solution)/shard_map/ppermute | solution.py:337
  29.2 31.6 %collective-permute-start.9 = (bf16[192,2048]{1,0:T(8,128)(2,1)S(1)}, bf16[192,2048]{1,0:T(8,128)(2,1)}, u32[]{:S(2)}, u32[]{:S(2)}) collective-permute-start(bf16[192,2048]{1,0:T(8,128)(2,1)S(1)} %copy-done.4), channel_id=1, source_target_pairs={{0,4},{1,3},{2,6},{3,1},{4,0},{5,7},{6,2},{7,5},{8,12},{9,11},{10,... | collective-permute-start | bytes 2359304 | tf_op jit(solution)/shard_map/ppermute | solution.py:337
  60.8 104.6 %collective-permute-start.30 = (bf16[2048,1024]{1,0:T(8,128)(2,1)}, bf16[2048,1024]{1,0:T(8,128)(2,1)}, u32[]{:S(2)}, u32[]{:S(2)}) collective-permute-start(bf16[2048,1024]{1,0:T(8,128)(2,1)} %bitcast.65), channel_id=1, source_target_pairs={{0,1},{1,0},{2,3},{3,2},{4,5},{5,4},{6,7},{7,6},{8,9},{9,8},{10,11... | collective-permute-start | bytes 12582920 | tf_op jit(solution)/shard_map/ppermute | solution.py:337
  107.2 22.2 %collective-permute-start.23 = (bf16[192,2048]{1,0:T(8,128)(2,1)}, bf16[192,2048]{1,0:T(8,128)(2,1)}, u32[]{:S(2)}, u32[]{:S(2)}) collective-permute-start(bf16[192,2048]{1,0:T(8,128)(2,1)} %copy-done.50), channel_id=1, source_target_pairs={{0,4},{1,3},{2,6},{3,1},{4,0},{5,7},{6,2},{7,5},{8,12},{9,11},{10,... | collective-permute-start | bytes 2359304 | tf_op jit(solution)/shard_map/ppermute | solution.py:337
  133.7 31.6 %collective-permute-start.31 = (bf16[512,2048]{1,0:T(8,128)(2,1)S(1)}, bf16[512,2048]{1,0:T(8,128)(2,1)}, u32[]{:S(2)}, u32[]{:S(2)}) collective-permute-start(bf16[512,2048]{1,0:T(8,128)(2,1)S(1)} %bitcast.82), channel_id=1, source_target_pairs={{0,1},{1,0},{2,3},{3,2},{4,5},{5,4},{6,7},{7,6},{8,9},{9,8},{10,11... | collective-permute-start | bytes 6291464 | tf_op jit(solution)/shard_map/ppermute | solution.py:337
  149.0 33.8 %collective-permute-start.36 = (bf16[192,2048]{1,0:T(8,128)(2,1)}, bf16[192,2048]{1,0:T(8,128)(2,1)}, u32[]{:S(2)}, u32[]{:S(2)}) collective-permute-start(bf16[192,2048]{1,0:T(8,128)(2,1)} %collective-permute-done.15.refs_3_), channel_id=1, source_target_pairs={{0,16},{1,17},{2,18},{3,19},{4,20},{5,21},{6,22},{7,23},{8,0},{9,1... | collective-permute-start | bytes 2359304 | tf_op jit(solution)/shard_map/ppermute | solution.py:337
  209.2 30.3 %collective-permute-start.42 = (bf16[192,2176]{1,0:T(8,128)(2,1)}, bf16[192,2176]{1,0:T(8,128)(2,1)S(1)}, u32[]{:S(2)}, u32[]{:S(2)}) collective-permute-start(bf16[192,2176]{1,0:T(8,128)(2,1)} %get-tuple-element.556.refs_0_), channel_id=1, source_target_pairs={{0,16},{1,17},{2,18},{3,19},{4,20},{5,21},{6,22},{7,23},{8,0},{9,1... | collective-permute-start | bytes 2506760 | tf_op jit(solution)/shard_map/ppermute | solution.py:337
  222.8 38.4 %collective-permute-start.43 = (bf16[192,2176]{1,0:T(8,128)(2,1)}, bf16[192,2176]{1,0:T(8,128)(2,1)S(1)}, u32[]{:S(2)}, u32[]{:S(2)}) collective-permute-start(bf16[192,2176]{1,0:T(8,128)(2,1)} %collective-permute-done.39.refs_1_), channel_id=1, source_target_pairs={{0,16},{1,17},{2,18},{3,19},{4,20},{5,21},{6,22},{7,23},{8,0},{9,1... | collective-permute-start | bytes 2506760 | tf_op jit(solution)/shard_map/ppermute | solution.py:337
  244.7 37.7 %collective-permute-start.46 = (bf16[192,2176]{1,0:T(8,128)(2,1)S(1)}, bf16[192,2176]{1,0:T(8,128)(2,1)S(1)}, u32[]{:S(2)}, u32[]{:S(2)}) collective-permute-start(bf16[192,2176]{1,0:T(8,128)(2,1)S(1)} %collective-permute-done.42.refs_0_), channel_id=1, source_target_pairs={{0,16},{1,17},{2,18},{3,19},{4,20},{5,21},{6,22},{7,23},{8,0},{9,1... | collective-permute-start | bytes 2506760 | tf_op jit(solution)/shard_map/ppermute | solution.py:337
  263.3 40.0 %collective-permute-start.48 = (bf16[192,2176]{1,0:T(8,128)(2,1)S(1)}, bf16[192,2176]{1,0:T(8,128)(2,1)}, u32[]{:S(2)}, u32[]{:S(2)}) collective-permute-start(bf16[192,2176]{1,0:T(8,128)(2,1)S(1)} %collective-permute-done.43.refs_1_), channel_id=1, source_target_pairs={{0,16},{1,17},{2,18},{3,19},{4,20},{5,21},{6,22},{7,23},{8,0},{9,1... | collective-permute-start | bytes 2506760 | tf_op jit(solution)/shard_map/ppermute | solution.py:337
  282.4 29.5 %collective-permute-start.49 = (bf16[192,2176]{1,0:T(8,128)(2,1)S(1)}, bf16[192,2176]{1,0:T(8,128)(2,1)S(1)}, u32[]{:S(2)}, u32[]{:S(2)}) collective-permute-start(bf16[192,2176]{1,0:T(8,128)(2,1)S(1)} %collective-permute-done.46.refs_0_), channel_id=1, source_target_pairs={{0,4},{1,3},{2,6},{3,1},{4,0},{5,7},{6,2},{7,5},{8,12},{9,11},{10,... | collective-permute-start | bytes 2506760 | tf_op jit(solution)/shard_map/ppermute | solution.py:337
  284.5 27.4 %collective-permute-start.51 = (bf16[192,2048]{1,0:T(8,128)(2,1)S(1)}, bf16[192,2048]{1,0:T(8,128)(2,1)}, u32[]{:S(2)}, u32[]{:S(2)}) collective-permute-start(bf16[192,2048]{1,0:T(8,128)(2,1)S(1)} %collective-permute-done.38.refs_3_), channel_id=1, source_target_pairs={{0,4},{1,3},{2,6},{3,1},{4,0},{5,7},{6,2},{7,5},{8,12},{9,11},{10,... | collective-permute-start | bytes 2359304 | tf_op jit(solution)/shard_map/ppermute | solution.py:337
  285.2 42.8 %collective-permute-start.53 = (bf16[192,2176]{1,0:T(8,128)(2,1)S(1)}, bf16[192,2176]{1,0:T(8,128)(2,1)}, u32[]{:S(2)}, u32[]{:S(2)}) collective-permute-start(bf16[192,2176]{1,0:T(8,128)(2,1)S(1)} %collective-permute-done.46.refs_0_), channel_id=1, source_target_pairs={{0,16},{1,17},{2,18},{3,19},{4,20},{5,21},{6,22},{7,23},{8,0},{9,1... | collective-permute-start | bytes 2506760 | tf_op jit(solution)/shard_map/ppermute | solution.py:337
  312.7 31.3 %collective-permute-start.54 = (bf16[192,2176]{1,0:T(8,128)(2,1)}, bf16[192,2176]{1,0:T(8,128)(2,1)}, u32[]{:S(2)}, u32[]{:S(2)}) collective-permute-start(bf16[192,2176]{1,0:T(8,128)(2,1)} %collective-permute-done.48.refs_1_), channel_id=1, source_target_pairs={{0,16},{1,17},{2,18},{3,19},{4,20},{5,21},{6,22},{7,23},{8,0},{9,1... | collective-permute-start | bytes 2506760 | tf_op jit(solution)/shard_map/ppermute | solution.py:337
  313.1 32.2 %collective-permute-start.56 = (bf16[192,2176]{1,0:T(8,128)(2,1)}, bf16[192,2176]{1,0:T(8,128)(2,1)S(1)}, u32[]{:S(2)}, u32[]{:S(2)}) collective-permute-start(bf16[192,2176]{1,0:T(8,128)(2,1)} %get-tuple-element.666), channel_id=1, source_target_pairs={{0,4},{1,3},{2,6},{3,1},{4,0},{5,7},{6,2},{7,5},{8,12},{9,11},{10,... | collective-permute-start | bytes 2506760 | tf_op jit(solution)/shard_map/ppermute | solution.py:337
  314.5 30.9 %collective-permute-start.57 = (bf16[192,2176]{1,0:T(8,128)(2,1)}, bf16[192,2176]{1,0:T(8,128)(2,1)S(1)}, u32[]{:S(2)}, u32[]{:S(2)}) collective-permute-start(bf16[192,2176]{1,0:T(8,128)(2,1)} %get-tuple-element.667), channel_id=1, source_target_pairs={{0,4},{1,3},{2,6},{3,1},{4,0},{5,7},{6,2},{7,5},{8,12},{9,11},{10,... | collective-permute-start | bytes 2506760 | tf_op jit(solution)/shard_map/ppermute | solution.py:337
  328.9 22.7 %collective-permute-start.55 = (bf16[192,2176]{1,0:T(8,128)(2,1)}, bf16[192,2176]{1,0:T(8,128)(2,1)S(1)}, u32[]{:S(2)}, u32[]{:S(2)}) collective-permute-start(bf16[192,2176]{1,0:T(8,128)(2,1)} %collective-permute-done.53.refs_0_), channel_id=1, source_target_pairs={{0,4},{1,3},{2,6},{3,1},{4,0},{5,7},{6,2},{7,5},{8,12},{9,11},{10,... | collective-permute-start | bytes 2506760 | tf_op jit(solution)/shard_map/ppermute | solution.py:337
  330.2 36.0 %collective-permute-start.59 = (bf16[192,2176]{1,0:T(8,128)(2,1)}, bf16[192,2176]{1,0:T(8,128)(2,1)S(1)}, u32[]{:S(2)}, u32[]{:S(2)}) collective-permute-start(bf16[192,2176]{1,0:T(8,128)(2,1)} %get-tuple-element.682), channel_id=1, source_target_pairs={{0,4},{1,3},{2,6},{3,1},{4,0},{5,7},{6,2},{7,5},{8,12},{9,11},{10,... | collective-permute-start | bytes 2506760 | tf_op jit(solution)/shard_map/ppermute | solution.py:337
  344.0 25.6 %collective-permute-start.60 = (bf16[192,2176]{1,0:T(8,128)(2,1)}, bf16[192,2176]{1,0:T(8,128)(2,1)}, u32[]{:S(2)}, u32[]{:S(2)}) collective-permute-start(bf16[192,2176]{1,0:T(8,128)(2,1)} %get-tuple-element.683), channel_id=1, source_target_pairs={{0,4},{1,3},{2,6},{3,1},{4,0},{5,7},{6,2},{7,5},{8,12},{9,11},{10,... | collective-permute-start | bytes 2506760 | tf_op jit(solution)/shard_map/ppermute | solution.py:337
  352.5 26.1 %collective-permute-start.58 = (bf16[192,2176]{1,0:T(8,128)(2,1)}, bf16[192,2176]{1,0:T(8,128)(2,1)}, u32[]{:S(2)}, u32[]{:S(2)}) collective-permute-start(bf16[192,2176]{1,0:T(8,128)(2,1)} %collective-permute-done.54.refs_1_), channel_id=1, source_target_pairs={{0,4},{1,3},{2,6},{3,1},{4,0},{5,7},{6,2},{7,5},{8,12},{9,11},{10,... | collective-permute-start | bytes 2506760 | tf_op jit(solution)/shard_map/ppermute | solution.py:337
  382.0 30.6 %collective-permute-start.61 = (bf16[192,2176]{1,0:T(8,128)(2,1)}, bf16[192,2176]{1,0:T(8,128)(2,1)}, u32[]{:S(2)}, u32[]{:S(2)}) collective-permute-start(bf16[192,2176]{1,0:T(8,128)(2,1)} %add_convert_fusion.7), channel_id=1, source_target_pairs={{0,16},{1,17},{2,18},{3,19},{4,20},{5,21},{6,22},{7,23},{8,0},{9,1... | collective-permute-start | bytes 2506760 | tf_op jit(solution)/shard_map/ppermute | solution.py:337
  383.8 28.9 %collective-permute-start.63 = (bf16[192,2176]{1,0:T(8,128)(2,1)}, bf16[192,2176]{1,0:T(8,128)(2,1)}, u32[]{:S(2)}, u32[]{:S(2)}) collective-permute-start(bf16[192,2176]{1,0:T(8,128)(2,1)} %get-tuple-element.708), channel_id=1, source_target_pairs={{0,4},{1,3},{2,6},{3,1},{4,0},{5,7},{6,2},{7,5},{8,12},{9,11},{10,... | collective-permute-start | bytes 2506760 | tf_op jit(solution)/shard_map/ppermute | solution.py:337
  384.5 28.2 %collective-permute-start.64 = (bf16[192,2176]{1,0:T(8,128)(2,1)}, bf16[192,2176]{1,0:T(8,128)(2,1)S(1)}, u32[]{:S(2)}, u32[]{:S(2)}) collective-permute-start(bf16[192,2176]{1,0:T(8,128)(2,1)} %get-tuple-element.709), channel_id=1, source_target_pairs={{0,4},{1,3},{2,6},{3,1},{4,0},{5,7},{6,2},{7,5},{8,12},{9,11},{10,... | collective-permute-start | bytes 2506760 | tf_op jit(solution)/shard_map/ppermute | solution.py:337
  398.6 32.5 %collective-permute-start.66 = (bf16[192,2176]{1,0:T(8,128)(2,1)}, bf16[192,2176]{1,0:T(8,128)(2,1)S(1)}, u32[]{:S(2)}, u32[]{:S(2)}) collective-permute-start(bf16[192,2176]{1,0:T(8,128)(2,1)} %get-tuple-element.716), channel_id=1, source_target_pairs={{0,4},{1,3},{2,6},{3,1},{4,0},{5,7},{6,2},{7,5},{8,12},{9,11},{10,... | collective-permute-start | bytes 2506760 | tf_op jit(solution)/shard_map/ppermute | solution.py:337
  402.6 32.2 %collective-permute-start.67 = (bf16[192,2176]{1,0:T(8,128)(2,1)}, bf16[192,2176]{1,0:T(8,128)(2,1)S(1)}, u32[]{:S(2)}, u32[]{:S(2)}) collective-permute-start(bf16[192,2176]{1,0:T(8,128)(2,1)} %get-tuple-element.717), channel_id=1, source_target_pairs={{0,4},{1,3},{2,6},{3,1},{4,0},{5,7},{6,2},{7,5},{8,12},{9,11},{10,... | collective-permute-start | bytes 2506760 | tf_op jit(solution)/shard_map/ppermute | solution.py:337
  451.4 47.5 %collective-permute-start.77 = (f32[512,2048]{1,0:T(8,128)}, f32[512,2048]{1,0:T(8,128)}, u32[]{:S(2)}, u32[]{:S(2)}) collective-permute-start(f32[512,2048]{1,0:T(8,128)} %fusion.20), channel_id=1, source_target_pairs={{0,1},{1,0},{2,3},{3,2},{4,5},{5,4},{6,7},{7,6},{8,9},{9,8},{10,11... | collective-permute-start | bytes 12582920 | tf_op jit(solution)/shard_map/ppermute | solution.py:337
  452.1 21.8 %collective-permute-start.70 = (bf16[192,2176]{1,0:T(8,128)(2,1)S(1)}, bf16[192,2176]{1,0:T(8,128)(2,1)S(1)}, u32[]{:S(2)}, u32[]{:S(2)}) collective-permute-start(bf16[192,2176]{1,0:T(8,128)(2,1)S(1)} %add_convert_fusion.2), channel_id=1, source_target_pairs={{0,16},{1,17},{2,18},{3,19},{4,20},{5,21},{6,22},{7,23},{8,0},{9,1... | collective-permute-start | bytes 2506760 | tf_op jit(solution)/shard_map/ppermute | solution.py:337
  454.2 26.6 %collective-permute-start.73 = (bf16[192,2048]{1,0:T(8,128)(2,1)}, bf16[192,2048]{1,0:T(8,128)(2,1)S(1)}, u32[]{:S(2)}, u32[]{:S(2)}) collective-permute-start(bf16[192,2048]{1,0:T(8,128)(2,1)} %get-tuple-element.739), channel_id=1, source_target_pairs={{0,4},{1,3},{2,6},{3,1},{4,0},{5,7},{6,2},{7,5},{8,12},{9,11},{10,... | collective-permute-start | bytes 2359304 | tf_op jit(solution)/shard_map/ppermute | solution.py:337
  454.2 26.6 %collective-permute-start.74 = (bf16[192,2048]{1,0:T(8,128)(2,1)}, bf16[192,2048]{1,0:T(8,128)(2,1)S(1)}, u32[]{:S(2)}, u32[]{:S(2)}) collective-permute-start(bf16[192,2048]{1,0:T(8,128)(2,1)} %get-tuple-element.740), channel_id=1, source_target_pairs={{0,4},{1,3},{2,6},{3,1},{4,0},{5,7},{6,2},{7,5},{8,12},{9,11},{10,... | collective-permute-start | bytes 2359304 | tf_op jit(solution)/shard_map/ppermute | solution.py:337
  480.7 139.7 %collective-permute-start.96 = (f32[2048,1024]{1,0:T(8,128)}, f32[2048,1024]{1,0:T(8,128)}, u32[]{:S(2)}, u32[]{:S(2)}) collective-permute-start(f32[2048,1024]{1,0:T(8,128)} %fusion.19), channel_id=1, source_target_pairs={{0,1},{1,0},{2,3},{3,2},{4,5},{5,4},{6,7},{7,6},{8,9},{9,8},{10,11... | collective-permute-start | bytes 25165832 | tf_op jit(solution)/shard_map/ppermute | solution.py:337
  494.1 49.9 %collective-permute-start.81 = (bf16[192,2048]{1,0:T(8,128)(2,1)}, bf16[192,2048]{1,0:T(8,128)(2,1)S(1)}, u32[]{:S(2)}, u32[]{:S(2)}) collective-permute-start(bf16[192,2048]{1,0:T(8,128)(2,1)} %add_convert_fusion.15), channel_id=1, source_target_pairs={{0,16},{1,17},{2,18},{3,19},{4,20},{5,21},{6,22},{7,23},{8,0},{9,1... | collective-permute-start | bytes 2359304 | tf_op jit(solution)/shard_map/ppermute | solution.py:337
  497.4 46.6 %collective-permute-start.80 = (bf16[192,2048]{1,0:T(8,128)(2,1)}, bf16[192,2048]{1,0:T(8,128)(2,1)S(1)}, u32[]{:S(2)}, u32[]{:S(2)}) collective-permute-start(bf16[192,2048]{1,0:T(8,128)(2,1)} %add_convert_fusion.16), channel_id=1, source_target_pairs={{0,16},{1,17},{2,18},{3,19},{4,20},{5,21},{6,22},{7,23},{8,0},{9,1... | collective-permute-start | bytes 2359304 | tf_op jit(solution)/shard_map/ppermute | solution.py:337
  519.4 24.6 %collective-permute-start.78 = (bf16[192,2048]{1,0:T(8,128)(2,1)}, bf16[192,2048]{1,0:T(8,128)(2,1)}, u32[]{:S(2)}, u32[]{:S(2)}) collective-permute-start(bf16[192,2048]{1,0:T(8,128)(2,1)} %get-tuple-element.780), channel_id=1, source_target_pairs={{0,4},{1,3},{2,6},{3,1},{4,0},{5,7},{6,2},{7,5},{8,12},{9,11},{10,... | collective-permute-start | bytes 2359304 | tf_op jit(solution)/shard_map/ppermute | solution.py:337
  519.4 24.6 %collective-permute-start.79 = (bf16[192,2048]{1,0:T(8,128)(2,1)}, bf16[192,2048]{1,0:T(8,128)(2,1)}, u32[]{:S(2)}, u32[]{:S(2)}) collective-permute-start(bf16[192,2048]{1,0:T(8,128)(2,1)} %get-tuple-element.781), channel_id=1, source_target_pairs={{0,4},{1,3},{2,6},{3,1},{4,0},{5,7},{6,2},{7,5},{8,12},{9,11},{10,... | collective-permute-start | bytes 2359304 | tf_op jit(solution)/shard_map/ppermute | solution.py:337
  549.9 30.6 %collective-permute-start.86 = (bf16[192,2048]{1,0:T(8,128)(2,1)}, bf16[192,2048]{1,0:T(8,128)(2,1)}, u32[]{:S(2)}, u32[]{:S(2)}) collective-permute-start(bf16[192,2048]{1,0:T(8,128)(2,1)} %add_convert_fusion.13), channel_id=1, source_target_pairs={{0,16},{1,17},{2,18},{3,19},{4,20},{5,21},{6,22},{7,23},{8,0},{9,1... | collective-permute-start | bytes 2359304 | tf_op jit(solution)/shard_map/ppermute | solution.py:337
  556.0 30.5 %collective-permute-start.85 = (bf16[192,2048]{1,0:T(8,128)(2,1)}, bf16[192,2048]{1,0:T(8,128)(2,1)}, u32[]{:S(2)}, u32[]{:S(2)}) collective-permute-start(bf16[192,2048]{1,0:T(8,128)(2,1)} %add_convert_fusion.14), channel_id=1, source_target_pairs={{0,16},{1,17},{2,18},{3,19},{4,20},{5,21},{6,22},{7,23},{8,0},{9,1... | collective-permute-start | bytes 2359304 | tf_op jit(solution)/shard_map/ppermute | solution.py:337
  557.3 29.1 %collective-permute-start.87 = (bf16[192,2048]{1,0:T(8,128)(2,1)}, bf16[192,2048]{1,0:T(8,128)(2,1)}, u32[]{:S(2)}, u32[]{:S(2)}) collective-permute-start(bf16[192,2048]{1,0:T(8,128)(2,1)} %get-tuple-element.825), channel_id=1, source_target_pairs={{0,4},{1,3},{2,6},{3,1},{4,0},{5,7},{6,2},{7,5},{8,12},{9,11},{10,... | collective-permute-start | bytes 2359304 | tf_op jit(solution)/shard_map/ppermute | solution.py:337
  558.6 27.8 %collective-permute-start.88 = (bf16[192,2048]{1,0:T(8,128)(2,1)}, bf16[192,2048]{1,0:T(8,128)(2,1)}, u32[]{:S(2)}, u32[]{:S(2)}) collective-permute-start(bf16[192,2048]{1,0:T(8,128)(2,1)} %get-tuple-element.826), channel_id=1, source_target_pairs={{0,4},{1,3},{2,6},{3,1},{4,0},{5,7},{6,2},{7,5},{8,12},{9,11},{10,... | collective-permute-start | bytes 2359304 | tf_op jit(solution)/shard_map/ppermute | solution.py:337
  586.5 26.2 %collective-permute-start.91 = (bf16[3,4,64,1664]{3,2,1,0:T(8,128)(2,1)}, bf16[3,4,64,1664]{3,2,1,0:T(8,128)(2,1)S(1)}, u32[]{:S(2)}, u32[]{:S(2)}) collective-permute-start(bf16[3,4,64,1664]{3,2,1,0:T(8,128)(2,1)} %get-tuple-element.841), channel_id=1, source_target_pairs={{0,1},{1,0},{2,3},{3,2},{4,5},{5,4},{6,7},{7,6},{8,9},{9,8},{10,11... | collective-permute-start | bytes 7667720 | tf_op jit(solution)/shard_map/ppermute | solution.py:337
  590.4 22.3 %collective-permute-start.90 = (bf16[4,64,1664]{2,1,0:T(8,128)(2,1)}, bf16[4,64,1664]{2,1,0:T(8,128)(2,1)}, u32[]{:S(2)}, u32[]{:S(2)}) collective-permute-start(bf16[4,64,1664]{2,1,0:T(8,128)(2,1)} %add_convert_fusion), channel_id=1, source_target_pairs={{0,16},{1,17},{2,18},{3,19},{4,20},{5,21},{6,22},{7,23},{8,0},{9,1... | collective-permute-start | bytes 2555912 | tf_op jit(solution)/shard_map/ppermute | solution.py:337
  598.9 39.5 %collective-permute-start.97 = (bf16[64,2048]{1,0:T(8,128)(2,1)}, bf16[64,2048]{1,0:T(8,128)(2,1)}, u32[]{:S(2)}, u32[]{:S(2)}) collective-permute-start(bf16[64,2048]{1,0:T(8,128)(2,1)} %add_bitcast_fusion.2), channel_id=1, source_target_pairs={{0,16},{1,17},{2,18},{3,19},{4,20},{5,21},{6,22},{7,23},{8,0},{9,1... | collective-permute-start | bytes 786440 | tf_op jit(solution)/shard_map/ppermute | solution.py:337
  614.6 24.1 %collective-permute-start.93 = (bf16[4,64,1664]{2,1,0:T(8,128)(2,1)S(1)}, bf16[4,64,1664]{2,1,0:T(8,128)(2,1)S(1)}, u32[]{:S(2)}, u32[]{:S(2)}) collective-permute-start(bf16[4,64,1664]{2,1,0:T(8,128)(2,1)S(1)} %fusion.5), channel_id=1, source_target_pairs={{0,16},{1,17},{2,18},{3,19},{4,20},{5,21},{6,22},{7,23},{8,0},{9,1... | collective-permute-start | bytes 2555912 | tf_op jit(solution)/shard_map/ppermute | solution.py:337
  641.1 21.9 %collective-permute-start.98 = (bf16[4,64,1664]{2,1,0:T(8,128)(2,1)S(1)}, bf16[4,64,1664]{2,1,0:T(8,128)(2,1)S(1)}, u32[]{:S(2)}, u32[]{:S(2)}) collective-permute-start(bf16[4,64,1664]{2,1,0:T(8,128)(2,1)S(1)} %fusion.3), channel_id=1, source_target_pairs={{0,16},{1,17},{2,18},{3,19},{4,20},{5,21},{6,22},{7,23},{8,0},{9,1... | collective-permute-start | bytes 2555912 | tf_op jit(solution)/shard_map/ppermute | solution.py:337
  642.5 26.1 %collective-permute-start.105 = (bf16[64,2048]{1,0:T(8,128)(2,1)S(1)}, bf16[64,2048]{1,0:T(8,128)(2,1)S(1)}, u32[]{:S(2)}, u32[]{:S(2)}) collective-permute-start(bf16[64,2048]{1,0:T(8,128)(2,1)S(1)} %add_convert_fusion.19), channel_id=1, source_target_pairs={{0,16},{1,17},{2,18},{3,19},{4,20},{5,21},{6,22},{7,23},{8,0},{9,1... | collective-permute-start | bytes 786440 | tf_op jit(solution)/shard_map/ppermute | solution.py:337
  643.8 25.0 %collective-permute-start.103 = (bf16[192,2048]{1,0:T(8,128)(2,1)S(1)}, bf16[192,2048]{1,0:T(8,128)(2,1)S(1)}, u32[]{:S(2)}, u32[]{:S(2)}) collective-permute-start(bf16[192,2048]{1,0:T(8,128)(2,1)S(1)} %copy-done.69), channel_id=1, source_target_pairs={{0,4},{1,3},{2,6},{3,1},{4,0},{5,7},{6,2},{7,5},{8,12},{9,11},{10,... | collective-permute-start | bytes 2359304 | tf_op jit(solution)/shard_map/ppermute | solution.py:337
  643.9 28.3 %collective-permute-start.104 = (bf16[192,2048]{1,0:T(8,128)(2,1)S(1)}, bf16[192,2048]{1,0:T(8,128)(2,1)S(1)}, u32[]{:S(2)}, u32[]{:S(2)}) collective-permute-start(bf16[192,2048]{1,0:T(8,128)(2,1)S(1)} %copy-done.68), channel_id=1, source_target_pairs={{0,4},{1,3},{2,6},{3,1},{4,0},{5,7},{6,2},{7,5},{8,12},{9,11},{10,... | collective-permute-start | bytes 2359304 | tf_op jit(solution)/shard_map/ppermute | solution.py:337
  659.4 21.8 %collective-permute-start.106 = (bf16[192,2048]{1,0:T(8,128)(2,1)S(1)}, bf16[192,2048]{1,0:T(8,128)(2,1)S(1)}, u32[]{:S(2)}, u32[]{:S(2)}) collective-permute-start(bf16[192,2048]{1,0:T(8,128)(2,1)S(1)} %add_convert_fusion.11), channel_id=1, source_target_pairs={{0,16},{1,17},{2,18},{3,19},{4,20},{5,21},{6,22},{7,23},{8,0},{9,1... | collective-permute-start | bytes 2359304 | tf_op jit(solution)/shard_map/ppermute | solution.py:337
  (146 other events, 2129.4 us)

commit v5 on v4

--- a/solution.py
+++ b/solution.py
@@ -414,14 +414,18 @@
 
 
 def join_body(lines, meta, *refs):
-    *pieces, whole_ref, small_ref = refs
+    *pieces, weights, gains, whole_ref, small_ref = refs
     for mask, piece in enumerate(pieces):
         for whole_at, piece_at in column_places(meta[0], mask, lines):
             whole_ref[:, whole_at] = widen(piece[:, piece_at])
-    small_ref[...] = sum(widen(piece[:, piece.shape[1] - WIDE :]) for piece in pieces)
-
-
-def join_columns(spot, pieces):
+    small = sum(widen(piece[:, piece.shape[1] - WIDE :]) for piece in pieces)
+    lane = lax.broadcasted_iota(jnp.int32, small.shape, 1)
+    gain = as_column(widen(gains[...])[0:1, :])
+    gain_grad = jnp.sum(whole_ref[...] * widen(weights[...]), axis=1, keepdims=True)
+    small_ref[...] = jnp.where(lane == FIRST_GAIN, gain_grad / gain, small)
+
+
+def join_columns(spot, pieces, weights, gains):
     rows, wide = pieces[0].shape
     columns = wide - WIDE
     return pl.pallas_call(
@@ -430,11 +434,12 @@
             jax.ShapeDtypeStruct((rows, columns * SPOTS), jnp.float32),
             jax.ShapeDtypeStruct((rows, WIDE), jnp.float32),
         ],
-        in_specs=[SCALARS] + [full_spec(rows, wide)] * SPOTS,
+        in_specs=[SCALARS] + [full_spec(rows, wide)] * SPOTS
+        + [full_spec(*weights.shape), full_spec(*gains.shape)],
         out_specs=[full_spec(rows, columns * SPOTS), full_spec(rows, WIDE)],
         compiler_params=params(60),
         name="join_columns",
-    )(spot.reshape(1), *pieces)
+    )(spot.reshape(1), *pieces, weights, gains)
 
 
 def expert_body(index, cap, experts, blocks, meta, *refs):
@@ -805,7 +810,7 @@
         + [ANYWHERE] * (2 * planes),
         out_specs=[block_spec(count, mine)] * 4 + [full_spec(mine, D)] + by_block(count, D),
         scratch_shapes=[pltpu.SemaphoreType.DMA((2 * planes,))],
-        compiler_params=params(60),
+        compiler_params=params(40),
         cost_estimate=cost(5 * 10**9, 20 << 20),
         name="attend_forward",
     )(meta.astype(jnp.int32), totals, starts, gains, projected, cos_all, sin_all, *own, *other)
@@ -916,7 +921,7 @@
             pltpu.VMEM((mine, D), bf),
             pltpu.SemaphoreType.DMA((SPOTS,)),
         ],
-        compiler_params=params(60),
+        compiler_params=params(48),
         cost_estimate=cost(7 * 10**9, 25 << 20),
         name="attend_backward",
     )(
@@ -949,20 +954,15 @@
     dk_ref,
     dv_ref,
     a_ref,
-    in_w,
     *refs,
 ):
     dp_ref, own, other, rest = refs[0], refs[1 : 1 + planes], refs[1 + planes], refs[2 + planes]
-    a_v, in_v, own_v, other_v, riding_v, small, sem, done = refs[3 + planes :]
+    a_v, own_v, other_v, riding_v, small, sem, done = refs[3 + planes :]
     bf = jnp.bfloat16
     rows, mine = dv_ref.shape
     count = rows // SPOTS
-    fetches = [
-        pltpu.make_async_copy(a_ref, a_v, sem.at[0]),
-        pltpu.make_async_copy(in_w, in_v, sem.at[1]),
-    ]
-    for copy in fetches:
-        copy.start()
+    fetch = pltpu.make_async_copy(a_ref, a_v, sem.at[0])
+    fetch.start()
     for n, ref in enumerate((dq_ref, dk_ref)):
         columns = slice(n * mine, (n + 1) * mine)
         for j in range(SPOTS):
@@ -982,9 +982,7 @@
         lax.broadcasted_iota(jnp.int32, (small.shape[0], WIDE), 1)
     )
     riding_v[...] = dot_first(small[...].astype(bf), jnp.where(turn_by, 1.0, 0.0).astype(bf))
-    lane = lax.broadcasted_iota(jnp.int32, (own_rows, WIDE), 1)
-    for copy in fetches:
-        copy.wait()
+    fetch.wait()
     leaving = []
     span = PLANE * own_rows
     for k in [*range(1, planes), 0]:
@@ -996,9 +994,7 @@
                 at = (spot * 2 + c) * own_rows
                 grad = grads[at : at + own_rows, :]
                 rows_at = pl.ds(pl.multiple_of(first_row + at, own_rows), own_rows)
-                gain_grad = jnp.sum(grad * widen(in_v[rows_at, : 3 * mine]), axis=1, keepdims=True)
-                riding = riding_v[rows_at, :]
-                riding = jnp.where(lane == FIRST_GAIN, gain_grad / riding, riding).astype(bf)
+                riding = riding_v[rows_at, :].astype(bf)
 
                 def put(place, grad=grad, riding=riding):
                     place[:, : 3 * mine] = grad.astype(bf)
@@ -1020,7 +1016,7 @@
         copy.wait()
 
 
-def project_back(moves, totals, dots, gains, small, in_full, projected, dq, dk, dv, normed_all):
+def project_back(moves, totals, dots, gains, small, projected, dq, dk, dv, normed_all):
     rows, mine = dv.shape
     planes = moves.planes
     own_rows = D // (planes * PLANE)
@@ -1033,11 +1029,10 @@
         out_shape=[jax.ShapeDtypeStruct((rows, 3 * mine), bf)]
         + [jax.ShapeDtypeStruct(pieces, bf)] * (planes + 1)
         + [jax.ShapeDtypeStruct((planes - 1, *pieces), bf)],
-        in_specs=[SCALARS] + [full_spec(*item.shape) for item in inputs] + [ANYWHERE] * 2,
+        in_specs=[SCALARS] + [full_spec(*item.shape) for item in inputs] + [ANYWHERE],
         out_specs=[full_spec(rows, 3 * mine)] + [ANYWHERE] * (planes + 2),
         scratch_shapes=[
             pltpu.VMEM((rows, D), bf),
-            pltpu.VMEM(in_full.shape, bf),
             pltpu.VMEM((planes, *pieces), bf),
             pltpu.VMEM((planes, *pieces), bf),
             pltpu.VMEM((D, WIDE), jnp.float32),
@@ -1048,7 +1043,7 @@
         compiler_params=params(60),
         cost_estimate=cost(5 * 10**9, 30 << 20),
         name="project_back",
-    )(meta.astype(jnp.int32), *inputs, normed_all, in_full)
+    )(meta.astype(jnp.int32), *inputs, normed_all)
 
 
 def rows_back_body(dp_ref, in_w, *parts):
@@ -1065,7 +1060,7 @@
         out_shape=[jax.ShapeDtypeStruct((count, D), jnp.bfloat16)] * SPOTS,
         in_specs=[block_spec(count, columns), full_spec(*in_full.shape)],
         out_specs=by_block(count, D),
-        compiler_params=params(60),
+        compiler_params=params(40),
         cost_estimate=cost(5 * 10**9, 12 << 20),
         name="rows_back",
     )(projected_grad, in_full)
@@ -1116,7 +1111,7 @@
             full_spec(count, width + WIDE),
             full_spec(3, count, experts),
         ],
-        compiler_params=params(60),
+        compiler_params=params(40),
         cost_estimate=cost(10**8, 8 << 20),
         name="route",
     )(*inputs)
@@ -1170,7 +1165,7 @@
             full_spec(experts, width),
             full_spec(1, width),
         ],
-        compiler_params=params(60),
+        compiler_params=params(40),
         cost_estimate=cost(10**8, 10 << 20),
         name="route_back",
     )(*inputs)
@@ -1226,7 +1221,6 @@
     out_own = [attention_out, send(attention_out, ring)]
     out_other = [send(attention_out, cores)]
     grads = {(0, 0): [cotangent, near_0], (1, 0): [own_1, send(own_1, first)]}
-    grads[0, 1] = [send(item, second) for item in grads[0, 0]]
     columns = 3 * mine
     lengths_all = jnp.stack([piece[: lengths.shape[1], columns + SMALL] for piece in traded])
     lengths_all = jnp.where(core == 0, lengths_all, lengths_all[jnp.asarray([0, 2, 1, 3])])
@@ -1246,31 +1240,30 @@
     )
 
     in_other.append(send(in_own[3], cores))
-    in_other, out_own, grads = tie(in_other, out_own, grads)
+    (in_other,) = tie(in_other)
+    grads[0, 1] = [send(item, second) for item in grads[0, 0]]
+    projected, normed_all, in_full, sums, small_rows, gains = project(
+        moves, blocks_x, in_own, in_other
+    )
+    sums, out_own, grads = tie(sums, out_own, grads)
     out_own.append(send(out_own[1], ring))
     out_other.append(send(out_own[1], cores))
-    own_2 = send(own_1, ring)
-    grads[1, 1] = [send(item, second) for item in grads[1, 0]]
-    projected, normed_all, in_full, sums, small_rows, gains = project(
-        moves, blocks_x, in_own, in_other
-    )
-    sums, out_own, out_other, own_2, grads = tie(sums, out_own, out_other, own_2, grads)
+    sums = plane_step(moves, by_spot(moves, sums), 1)
+    sums, out_own, own_1 = tie(sums, out_own, own_1)
     out_own.append(send(out_own[2], ring))
     out_other.append(send(out_own[2], cores))
-    sums = plane_step(moves, by_spot(moves, sums), 1)
-    sums, own_2 = tie(sums, own_2)
-    own_3 = send(own_2, ring)
     totals = by_spot(moves, plane_step(moves, sums, 2))
     totals, out_own, out_other = tie(totals, out_own, out_other)
     out_other.append(send(out_own[3], cores))
-    totals, out_other, own_2 = tie(totals, out_other, own_2)
-
-    across_2 = send(own_2, second)
+    totals, out_other, grads, own_1 = tie(totals, out_other, grads, own_1)
+
+    own_2 = send(own_1, ring)
+    grads[1, 1] = [send(item, second) for item in grads[1, 0]]
     weights = [expert_in[0], send(expert_in[0], cores), expert_out[0], send(expert_out[0], cores)]
     attention = (moves, totals, starts, gains, projected, cos_all, sin_all)
     results = attend_forward(*attention, out_own, out_other)
     heads, out_full, parts = results[:4], results[4], results[5:]
-    parts, weights, own_3, across_2 = tie(parts, weights, own_3, across_2)
+    parts, weights, own_2, grads = tie(parts, weights, own_2, grads)
 
     def cross(parts):
         return [send(parts[2], second), send(parts[3], second)]
@@ -1280,14 +1273,14 @@
         return widen(parts[0]) + widen(backs[0]), send(near, first)
 
     backs = cross(parts)
-    near_2 = send(grads[1, 0][1], ring)
-    backs, parts, near_2 = tie(backs, parts, near_2)
+    own_3 = send(own_2, ring)
+    backs, parts, near_1 = tie(backs, parts, grads[1, 0][1])
     near = send(low(widen(parts[1]) + widen(backs[1])), first)
-    near_3 = send(near_2, ring)
-    (near,) = tie(near)
+    near_2 = send(near_1, ring)
+    near, own_3 = tie(near, own_3)
     grads[2, 0] = [own_2, near_2]
     residual, rows, probs = route(tokens, parts[0], backs[0], near, match, rank, small_rows)
-    rows, near_3 = tie(rows, near_3)
+    rows, near_2 = tie(rows, near_2)
 
     meta = (moves.device // 2).reshape(1).astype(jnp.int32)
     saved, done = None, 0
@@ -1321,41 +1314,38 @@
 
     row_2 = send(row_1, ring)
     across_row_1 = send(row_1, second)
-    grads[2, 1] = [across_2, send(near_2, second)]
-    grads[3, 0] = [own_3, near_3]
+    across_2 = send(own_2, second)
+    near_3 = send(near_2, ring)
     run_expert(0, 1, across)
-    saved, near_row_1, across_row_1 = tie(saved, near_row_1, across_row_1)
+    saved, near_row_1, across_row_1, across_2 = tie(saved, near_row_1, across_row_1, across_2)
 
     near_row_2 = send(near_row_1, ring)
     across = [across_row_1, send(near_row_1, second)]
-    across_3 = send(own_3, second)
+    grads[2, 0], grads[2, 1] = [own_2, near_2], [across_2, send(near_2, second)]
     run_expert(1, 0, [row_1, near_row_1])
-    saved, across, row_2, row_parts[0], grads[2, 1], near_3 = tie(
-        saved, across, row_2, row_parts[0], grads[2, 1], near_3
-    )
+    saved, across, row_2, grads[2, 1] = tie(saved, across, row_2, grads[2, 1])
 
     row_3 = send(row_2, ring)
     across_row_2 = send(row_2, second)
-    grads[3, 1] = [across_3, send(near_3, second)]
+    across_3 = send(own_3, second)
     run_expert(1, 1, across)
-    saved, near_row_2, across_row_2, row_parts[0], grads[3, 1] = tie(
-        saved, near_row_2, across_row_2, row_parts[0], grads[3, 1]
-    )
+    saved, near_row_2, across_row_2, across_3 = tie(saved, near_row_2, across_row_2, across_3)
 
     near_row_3 = send(near_row_2, ring)
     across = [across_row_2, send(near_row_2, second)]
-    backs_0 = cross(row_parts[0])
+    backs_1 = cross(row_parts[1])
     run_expert(2, 0, [row_2, near_row_2])
-    saved, across, row_3, row_parts[1] = tie(saved, across, row_3, row_parts[1])
-
+    saved, across, row_3, near_3 = tie(saved, across, row_3, near_3)
+
+    grads[3, 0] = [own_3, near_3]
     across_row_3 = send(row_3, second)
-    backs_1 = cross(row_parts[1])
+    grads[3, 1] = [across_3, send(near_3, second)]
     run_expert(2, 1, across)
-    saved, near_row_3, across_row_3, backs_0 = tie(saved, near_row_3, across_row_3, backs_0)
+    saved, near_row_3, across_row_3, backs_1 = tie(saved, near_row_3, across_row_3, backs_1)
 
     across = [across_row_3, send(near_row_3, second)]
     run_expert(3, 0, [row_3, near_row_3])
-    saved, across, backs_1, row_parts[2] = tie(saved, across, backs_1, row_parts[2])
+    saved, across, grads[3, 1], row_parts = tie(saved, across, grads[3, 1], row_parts)
 
     pair = [send(low(widen(row_parts[1][n]) + widen(backs_1[n])), ring) for n in range(2)]
     backs_2 = cross(row_parts[2])
@@ -1367,11 +1357,14 @@
     backs_3 = cross(row_parts[3])
     x_rows, dy_rows, m_own, m_other, du_own, du_other = saved
     in_theirs = dot_first(x_rows, du_other)
-    home, near, backs_3, in_theirs = tie(home, near, backs_3, in_theirs)
+    home, near, backs_3, in_theirs, row_parts[0] = tie(
+        home, near, backs_3, in_theirs, row_parts[0]
+    )
 
     total = send(low(home + widen(near)), ring)
     home, near = gather_near(row_parts[3], backs_3)
     in_theirs = send(in_theirs, cores)
+    backs_0 = cross(row_parts[0])
     out_theirs = dot_first(m_other, dy_rows)
     total, home, near, out_theirs = tie(total, home, near, out_theirs)
 
@@ -1384,9 +1377,7 @@
         total, row_parts[0][0], backs_0[0], near_0, match, probs, small_rows, residual, cotangent
     )
     branch_near = send(branch_grad, first)
-    branch_grad, branch_near, out_backs, out_parts = tie(
-        branch_grad, branch_near, out_backs, out_parts
-    )
+    branch_grad, branch_near, out_parts = tie(branch_grad, branch_near, out_parts)
 
     branch_blocks = [
         branch_grad,
@@ -1409,71 +1400,76 @@
     )
 
     other_grad = send(other_grad, cores)
-    out_pair = [
-        send(low(widen(out_pair[n]) + widen(out_parts[2][n]) + widen(out_backs[2][n])), ring)
-        for n in range(2)
-    ]
+    out_near = send(
+        low(widen(out_pair[1]) + widen(out_parts[2][1]) + widen(out_backs[2][1])), first
+    )
     dots = plane_step(moves, by_spot(moves, dots), 1)
+    dots, other_grad = tie(dots, other_grad)
+
+    def out_sum(step):
+        return widen(own_grad[step]) + widen(other_grad[step])
+
+    out_share = send(low(out_sum(1)), ring)
     dots = by_spot(moves, plane_step(moves, dots, 2))
-    dots, other_grad, out_parts = tie(dots, other_grad, out_parts)
-    out_sums = [widen(own_grad[k]) + widen(other_grad[k]) for k in range(planes)]
+    dots, out_share, out_near, out_parts, out_pair = tie(
+        dots, out_share, out_near, out_parts, out_pair
+    )
+    out_total = low(
+        widen(out_pair[0])
+        + (widen(out_parts[2][0]) + widen(out_backs[2][0]))
+        + widen(out_near)
+    )
+    out_total = send(out_total, ring)
     out_backs[3] = cross(out_parts[3])
     small = (router_grad, small_rows, gain_grads, second_gain_grad)
     projected_grad, *in_grads = project_back(
-        moves, totals, dots, gains, small, in_full, projected, dq, dk, dv, normed_all
-    )
-    in_grads, projected_grad, out_pair, out_backs, out_parts, out_sums = tie(
-        in_grads, projected_grad, out_pair, out_backs, out_parts, out_sums
+        moves, totals, dots, gains, small, projected, dq, dk, dv, normed_all
+    )
+    in_grads, projected_grad, out_share, out_parts, out_total, out_backs[3] = tie(
+        in_grads, projected_grad, out_share, out_parts, out_total, out_backs[3]
     )
 
     *in_grads, others, others_rest = in_grads
     others = send(others, cores)
-    projected_grad, in_full, others, out_backs = tie(projected_grad, in_full, others, out_backs)
+    projected_grad, in_full, others = tie(projected_grad, in_full, others)
     in_total = send(low(widen(in_grads[1]) + widen(others)), ring)
     others_rest = send(others_rest, cores)
-    out_near = send(
-        low(widen(out_pair[1]) + widen(out_parts[3][1]) + widen(out_backs[3][1])), first
-    )
-    out_share = send(low(out_sums[1]), ring)
+    out_share = send(low(widen(out_share) + out_sum(2)), ring)
+    out_backs[0] = cross(out_parts[0])
     parts = rows_back(projected_grad, in_full)
-    in_total, others_rest, parts, out_near, x_rows, out_parts = tie(
-        in_total, others_rest, parts, out_near, x_rows, out_parts
+    in_total, others_rest, parts, x_rows, out_share, out_parts, out_backs = tie(
+        in_total, others_rest, parts, x_rows, out_share, out_parts, out_backs
     )
 
     in_total = send(low(widen(in_total) + (widen(in_grads[2]) + widen(others_rest[0]))), ring)
     backs = cross(parts)
-    out_total = low(
-        widen(out_pair[0])
-        + (widen(out_parts[3][0]) + widen(out_backs[3][0]))
-        + widen(out_near)
-    )
     expert_in_grad = dot_first(x_rows, du_own) + in_theirs
-    in_total, backs, expert_in_grad, out_parts, out_total, out_share = tie(
-        in_total, backs, expert_in_grad, out_parts, out_total, out_share
-    )
-
+    out_home, out_near = gather_near(out_parts[3], out_backs[3])
+    in_total, backs, expert_in_grad, out_parts, out_home, out_near, out_share = tie(
+        in_total, backs, expert_in_grad, out_parts, out_home, out_near, out_share
+    )
+
+    in_total = send(low(widen(in_total) + (widen(in_grads[3]) + widen(others_rest[1]))), ring)
     home, near = gather_near(parts, backs)
-    in_total = send(low(widen(in_total) + (widen(in_grads[3]) + widen(others_rest[1]))), ring)
-    out_backs[0] = cross(out_parts[0])
-    out_share = send(low(widen(out_share) + out_sums[2]), ring)
-    out_total = send(out_total, ring)
-    in_total, home, near = tie(in_total, home, near)
+    out_total = low(widen(out_total) + (out_home + widen(out_near)))
+    out_share = send(low(widen(out_share) + out_sum(3)), ring)
+    out_home, out_near = gather_near(out_parts[0], out_backs[0])
+    in_total, home, near, out_total, out_share = tie(in_total, home, near, out_total, out_share)
 
     in_total = low(widen(in_total) + (widen(in_grads[0]) + widen(others_rest[2])))
     traded = [in_total[0]] + [send(in_total[m], moves.spots[m]) for m in range(1, SPOTS)]
+    out_total = send(out_total, ring)
+    out_share = widen(out_share) + out_sum(0)
     _, first_back = jax.vjp(
         lambda value: root_norm(value, small_rows[FIRST_GAIN]), widen(tokens)
     )
     (input_norm_grad,) = first_back(home + widen(near))
     input_grad = residual_grad + input_norm_grad
-    traded, input_grad, out_backs, out_share, out_total = tie(
-        traded, input_grad, out_backs, out_share, out_total
-    )
-    out_share = send(low(widen(out_share) + out_sums[3]), ring)
-
-    out_home, out_near = gather_near(out_parts[0], out_backs[0])
-    in_share, small_share = join_columns(spot, traded)
-    out_share = widen(out_share) + out_sums[0]
+    traded, input_grad, out_share, out_home, out_near = tie(
+        traded, input_grad, out_share, out_home, out_near
+    )
+    in_share, small_share = join_columns(spot, traded, attention_in, norm_gains)
+    out_total, in_share, out_near = tie(out_total, in_share, out_near)
     output = low(residual + (widen(out_total) + (out_home + widen(out_near))))
     return (
         output,

time: 708 us -> 687 us (0.970)
  Pallas kernels: 202 us -> 180 us
  local copies, waits for them, and re-layouts: 25 us -> 38.3 us
  starting transfers between devices: 126 us -> 113 us
    ppermute x109, starting transfers between devices: 126 us -> 113 us  [send(): return lax.ppermute(value, 'fsdp', pairs)]
    unnamed x173 -> x217, local copies, waits for them, and re-layouts: 12.5 us -> 25.1 us
    convert_element_type x23 -> x24, other arithmetic: 27.4 us -> 27.5 us  [low(): return value.astype(bf)]
  transfers between devices with their start and end apart: 109 -> 109, of which waited for: 44 -> 48; matrix products, arithmetic and copies ran while one was open for 14% -> 15% of each run, Pallas kernels for 29% -> 27%
where the time goes in v5:
time: 687 us; the launch traced here: 678 us
  waiting for transfers between devices  256 us (37%)
  Pallas kernels  180 us (26%)
  starting transfers between devices  113 us (16%)
  other arithmetic  46.8 us (7%)
  matrix products  42.2 us (6%)
  local copies, waits for them, and re-layouts  38.3 us (6%)
    ppermute x109, waiting for transfers between devices, send(): return lax.ppermute(value, 'fsdp', pairs)  256 us
    ppermute x109, starting transfers between devices, send(): return lax.ppermute(value, 'fsdp', pairs)  113 us
    pallas_call x8, Pallas kernels, expert_blocks(): pl.pallas_call(functools.partial(expert_body, index, cap, experts, blocks...  103 us
    dot_general x4, matrix products, dot_first(): lax.dot_general(left, right, (((0,), (0,)), ((), ())), preferred_element_...  42 us
    convert_element_type x24, other arithmetic, low(): return value.astype(bf)  27.5 us
    unnamed x217, local copies, waits for them, and re-layouts  25.1 us
    pallas_call x1, Pallas kernels, attend_backward(): pl.pallas_call(backward_body, grid=(SPOTS,), out_shape=[shape((rows, mine...  20.7 us
    pallas_call x1, Pallas kernels, project_back(): pl.pallas_call(functools.partial(project_back_body, planes, own_rows), ou...  15.4 us
  transfers between devices with their start and end apart: 109, of which 48 were waited for; matrix products, arithmetic and copies ran while one was open for 15% of the time, Pallas kernels for 27%

profile of v5, /device:TPU:0, one launch (start us, length us, event | category | flops | bytes accessed | tf_op | source)
XLA Modules:
  0.0 678.4 jit_solution(2454447483588383937)
XLA Ops:
  0.7 4.1 collective-permute-start.3
  11.8 4.9 collective-permute-done
  16.7 4.3 collective-permute-done.1
  30.4 15.9 %collective-permute-done.6.refs_1_ = bf16[192,2048]{1,0:T(8,128)(2,1)} collective-permute-done((bf16[192,2048]{1,0:T(8,128)(2,1)S(1)}, bf16[192,2048]{1,0:T(8,128)(2,1)}, u32[]{:S(2)}, u32[]{:S(2)}) %collective-permute-start.6) | collective-permute-done | bytes 786464 | tf_op jit(solution)/shard_map/ppermute | solution.py:337
  60.1 3.4 collective-permute-done.10.refs_3_
  71.7 3.8 collective-permute-done.15.refs_3_
  75.5 10.7 %collective-permute-done.12.refs_7_ = bf16[4,64,1664]{2,1,0:T(8,128)(2,1)} collective-permute-done((bf16[4,64,1664]{2,1,0:T(8,128)(2,1)}, bf16[4,64,1664]{2,1,0:T(8,128)(2,1)}, u32[]{:S(2)}, u32[]{:S(2)}) %collective-permute-start.12) | collective-permute-done | bytes 852000 | tf_op jit(solution)/shard_map/ppermute | solution.py:337
  93.0 12.6 %project.1 = (f32[768,1536]{1,0:T(8,128)}, bf16[768,2048]{1,0:T(8,128)(2,1)}, bf16[2048,1664]{1,0:T(8,128)(2,1)}, f32[2,4,192]{2,1,0:T(4,128)}, f32[32,2048]{1,0:T(8,128)}, /*index=5*/f32[2,512]{1,0:T(2,128)}) custom-call(s32[6]{0:T(128)} %pad_add_fusion.meta, bf16[192,2048]{1,0:T(8,128)(2,1)} %tokens.1, bf16[192,2048]{1,0:T(8,128)(2,1)} %collective-permute-done.6.refs_1_, ...), custom_call_target="tpu_custom_call" | custom-call | flops 5000000000 | bytes 20971520 | tf_op jit(solution)/shard_map/project/pallas_call | solution.py:698
  114.4 7.1 %collective-permute-done.21.refs_2_ = bf16[64,2048]{1,0:T(8,128)(2,1)S(1)} collective-permute-done((bf16[64,2048]{1,0:T(8,128)(2,1)S(1)}, bf16[64,2048]{1,0:T(8,128)(2,1)S(1)}, u32[]{:S(2)}, u32[]{:S(2)}) %collective-permute-start.21) | collective-permute-done | bytes 262176 | tf_op jit(solution)/shard_map/ppermute | solution.py:337
  126.5 5.1 collective-permute-done.23.refs_3_
  141.7 11.0 %attend_forward.1 = (bf16[768,512]{1,0:T(8,128)(2,1)S(1)}, bf16[768,512]{1,0:T(8,128)(2,1)S(1)}, bf16[768,512]{1,0:T(8,128)(2,1)S(1)}, bf16[768,512]{1,0:T(8,128...) custom-call(s32[6]{0:T(128)S(1)} %copy-done.22, ...), custom_call_target="tpu_custom_call" | custom-call | flops 5000000000 | bytes 20971520 | tf_op jit(solution)/shard_map/attend_forward/pallas_call | solution.py:795
  159.0 9.7 %collective-permute-done.32.back = bf16[192,2048]{1,0:T(8,128)(2,1)S(1)} collective-permute-done((bf16[192,2048]{1,0:T(8,128)(2,1)S(1)}, bf16[192,2048]{1,0:T(8,128)(2,1)S(1)}, u32[]{:S(2)}, u32[]{:S(2)}) %collective-permute-start.32) | collective-permute-done | bytes 786464 | tf_op jit(solution)/shard_map/ppermute | solution.py:337
  168.7 8.4 %collective-permute-done.33 = bf16[192,2048]{1,0:T(8,128)(2,1)S(1)} collective-permute-done((bf16[192,2048]{1,0:T(8,128)(2,1)S(1)}, bf16[192,2048]{1,0:T(8,128)(2,1)S(1)}, u32[]{:S(2)}, u32[]{:S(2)}) %collective-permute-start.33) | collective-permute-done | bytes 786464 | tf_op jit(solution)/shard_map/ppermute | solution.py:337
  179.5 11.0 %collective-permute-done.34.near = bf16[192,2048]{1,0:T(8,128)(2,1)S(1)} collective-permute-done((bf16[192,2048]{1,0:T(8,128)(2,1)}, bf16[192,2048]{1,0:T(8,128)(2,1)S(1)}, u32[]{:S(2)}, u32[]{:S(2)}) %collective-permute-start.34) | collective-permute-done | bytes 786464 | tf_op jit(solution)/shard_map/ppermute | solution.py:337
  198.5 11.1 %collective-permute-done.37.refs_1_ = bf16[192,2176]{1,0:T(8,128)(2,1)} collective-permute-done((bf16[192,2176]{1,0:T(8,128)(2,1)}, bf16[192,2176]{1,0:T(8,128)(2,1)}, u32[]{:S(2)}, u32[]{:S(2)}) %collective-permute-start.37) | collective-permute-done | bytes 835616 | tf_op jit(solution)/shard_map/ppermute | solution.py:337
  213.7 12.8 %expert_blocks.8 = (bf16[2048,2048]{1,0:T(8,128)(2,1)}, bf16[2048,2048]{1,0:T(8,128)(2,1)}, bf16[2048,512]{1,0:T(8,128)(2,1)}, bf16[2048,512]{1,0:T(8,128)(2,1)}...) custom-call(s32[1]{0:T(128)} %bitcast.12.meta, ...), custom_call_target="tpu_custom_call" | custom-call | flops 7600000000 | bytes 31457280 | tf_op jit(solution)/shard_map/expert_blocks/pallas_call | solution.py:560
  226.5 4.9 collective-permute-done.39.refs_1_
  235.4 12.8 %expert_blocks.9 = (bf16[2048,2048]{1,0:T(8,128)(2,1)}, bf16[2048,2048]{1,0:T(8,128)(2,1)}, bf16[2048,512]{1,0:T(8,128)(2,1)}, bf16[2048,512]{1,0:T(8,128)(2,1)}...) custom-call(s32[1]{0:T(128)} %bitcast.12.meta, ...), custom_call_target="tpu_custom_call", output_to_operand_aliasing={{0}: (9, {}), {1}: (10, {}), {2}: (11, {}), {3}: (12, {}), ... | custom-call | flops 7600000000 | bytes 31457280 | tf_op jit(solution)/shard_map/expert_blocks/pallas_call | solution.py:560
  248.2 4.5 collective-permute-done.43.refs_2_
  256.4 12.8 %expert_blocks.10 = (bf16[2048,2048]{1,0:T(8,128)(2,1)}, bf16[2048,2048]{1,0:T(8,128)(2,1)}, bf16[2048,512]{1,0:T(8,128)(2,1)}, bf16[2048,512]{1,0:T(8,128)(2,1)...) custom-call(s32[1]{0:T(128)} %bitcast.12.meta, ...), custom_call_target="tpu_custom_call", output_to_operand_aliasing={{0}: (9, {}), {1}: (10, {}), {2}: (11, {}), {3}: (12, {}), ... | custom-call | flops 7600000000 | bytes 31457280 | tf_op jit(solution)/shard_map/expert_blocks/pallas_call | solution.py:560
  269.2 4.6 collective-permute-done.46.refs_3_
  277.5 12.8 %expert_blocks.11 = (bf16[2048,2048]{1,0:T(8,128)(2,1)}, bf16[2048,2048]{1,0:T(8,128)(2,1)}, bf16[2048,512]{1,0:T(8,128)(2,1)}, bf16[2048,512]{1,0:T(8,128)(2,1)...) custom-call(s32[1]{0:T(128)} %bitcast.12.meta, ...), custom_call_target="tpu_custom_call", output_to_operand_aliasing={{0}: (9, {}), {1}: (10, {}), {2}: (11, {}), {3}: (12, {}), ... | custom-call | flops 7600000000 | bytes 31457280 | tf_op jit(solution)/shard_map/expert_blocks/pallas_call | solution.py:560
  290.3 4.8 collective-permute-done.49.refs_2_
  300.3 12.8 %expert_blocks.12 = (bf16[2048,2048]{1,0:T(8,128)(2,1)}, bf16[2048,2048]{1,0:T(8,128)(2,1)}, bf16[2048,512]{1,0:T(8,128)(2,1)}, bf16[2048,512]{1,0:T(8,128)(2,1)...) custom-call(s32[1]{0:T(128)} %bitcast.12.meta, ...), custom_call_target="tpu_custom_call", output_to_operand_aliasing={{0}: (9, {}), {1}: (10, {}), {2}: (11, {}), {3}: (12, {}), ... | custom-call | flops 7600000000 | bytes 31457280 | tf_op jit(solution)/shard_map/expert_blocks/pallas_call | solution.py:560
  315.8 12.8 %expert_blocks.13 = (bf16[2048,2048]{1,0:T(8,128)(2,1)}, bf16[2048,2048]{1,0:T(8,128)(2,1)}, bf16[2048,512]{1,0:T(8,128)(2,1)}, bf16[2048,512]{1,0:T(8,128)(2,1)...) custom-call(s32[1]{0:T(128)} %bitcast.12.meta, ...), custom_call_target="tpu_custom_call", output_to_operand_aliasing={{0}: (9, {}), {1}: (10, {}), {2}: (11, {}), {3}: (12, {}), ... | custom-call | flops 7600000000 | bytes 31457280 | tf_op jit(solution)/shard_map/expert_blocks/pallas_call | solution.py:560
  328.7 6.1 collective-permute-done.54.refs_0_
  336.8 13.2 %expert_blocks.14 = (bf16[2048,2048]{1,0:T(8,128)(2,1)}, bf16[2048,2048]{1,0:T(8,128)(2,1)}, bf16[2048,512]{1,0:T(8,128)(2,1)}, bf16[2048,512]{1,0:T(8,128)(2,1)...) custom-call(s32[1]{0:T(128)} %bitcast.12.meta, ...), custom_call_target="tpu_custom_call", output_to_operand_aliasing={{0}: (9, {}), {1}: (10, {}), {2}: (11, {}), {3}: (12, {}), ... | custom-call | flops 7600000000 | bytes 31457280 | tf_op jit(solution)/shard_map/expert_blocks/pallas_call | solution.py:560
  350.0 6.0 collective-permute-done.58.refs_3_
  364.0 12.8 %expert_blocks.15 = (bf16[2048,2048]{1,0:T(8,128)(2,1)}, bf16[2048,2048]{1,0:T(8,128)(2,1)}, bf16[2048,512]{1,0:T(8,128)(2,1)}, bf16[2048,512]{1,0:T(8,128)(2,1)...) custom-call(s32[1]{0:T(128)} %bitcast.12.meta, ...), custom_call_target="tpu_custom_call", output_to_operand_aliasing={{0}: (9, {}), {1}: (10, {}), {2}: (11, {}), {3}: (12, {}), ... | custom-call | flops 7600000000 | bytes 31457280 | tf_op jit(solution)/shard_map/expert_blocks/pallas_call | solution.py:560
  381.5 7.5 %collective-permute-done.60 = bf16[192,2176]{1,0:T(8,128)(2,1)} collective-permute-done((bf16[192,2176]{1,0:T(8,128)(2,1)}, bf16[192,2176]{1,0:T(8,128)(2,1)}, u32[]{:S(2)}, u32[]{:S(2)}) %collective-permute-start.60) | collective-permute-done | bytes 835616 | tf_op jit(solution)/shard_map/ppermute | solution.py:337
  391.3 15.0 %fusion.22 = f32[2048,1024]{1,0:T(8,128)} fusion(bf16[2048,2048]{1,0:T(8,128)(2,1)} %get-tuple-element.874, bf16[2048,1024]{1,0:T(8,128)(2,1)} %get-tuple-element.726), kind=kOutput, calls=%fused_computation.109 | convolution fusion | flops 8589934592 | bytes 20971520 | tf_op jit(solution)/shard_map/dot_general | solution.py:71
  408.0 4.0 collective-permute-done.65
  415.4 6.0 fusion.23
  425.3 9.1 %collective-permute-done.67 = bf16[192,2176]{1,0:T(8,128)(2,1)S(1)} collective-permute-done((bf16[192,2176]{1,0:T(8,128)(2,1)S(1)}, bf16[192,2176]{1,0:T(8,128)(2,1)S(1)}, u32[]{:S(2)}, u32[]{:S(2)}) %collective-permute-start.67) | collective-permute-done | bytes 835616 | tf_op jit(solution)/shard_map/ppermute | solution.py:337
  437.2 18.7 %collective-permute-done.68.total = bf16[192,2176]{1,0:T(8,128)(2,1)S(1)} collective-permute-done((bf16[192,2176]{1,0:T(8,128)(2,1)S(1)}, bf16[192,2176]{1,0:T(8,128)(2,1)S(1)}, u32[]{:S(2)}, u32[]{:S(2)}) %collective-permute-start.68) | collective-permute-done | bytes 835616 | tf_op jit(solution)/shard_map/ppermute | solution.py:337
  461.1 17.6 %collective-permute-done.72.refs_1_ = bf16[192,2048]{1,0:T(8,128)(2,1)S(1)} collective-permute-done((bf16[192,2048]{1,0:T(8,128)(2,1)S(1)}, bf16[192,2048]{1,0:T(8,128)(2,1)S(1)}, u32[]{:S(2)}, u32[]{:S(2)}) %collective-permute-start.72) | collective-permute-done | bytes 786464 | tf_op jit(solution)/shard_map/ppermute | solution.py:337
  481.9 4.5 collective-permute-done.77
  489.6 6.4 convolution_add_fusion.1
  496.0 7.2 %collective-permute-done.74.refs_3_ = bf16[192,2048]{1,0:T(8,128)(2,1)S(1)} collective-permute-done((bf16[192,2048]{1,0:T(8,128)(2,1)S(1)}, bf16[192,2048]{1,0:T(8,128)(2,1)S(1)}, u32[]{:S(2)}, u32[]{:S(2)}) %collective-permute-start.74) | collective-permute-done | bytes 786464 | tf_op jit(solution)/shard_map/ppermute | solution.py:337
  505.3 20.7 %attend_backward.1 = (f32[768,512]{1,0:T(8,128)}, f32[768,512]{1,0:T(8,128)}, bf16[768,512]{1,0:T(8,128)(2,1)S(1)}, f32[2,4,192]{2,1,0:T(4,128)S(1)}, bf16[4,64,...) custom-call(s32[6]{0:T(128)S(1)} %copy-done.23, f32[2,4,192]{2,1,0:T(4,128)S(1)} %copy-done.19, ...), custom_call_target="tpu_custom_call" | custom-call | flops 7000000000 | bytes 26214400 | tf_op jit(solution)/shard_map/attend_backward/pallas_call | solution.py:890
  539.1 5.4 collective-permute-done.86
  550.8 15.4 %project_back.1 = (bf16[768,1536]{1,0:T(8,128)(2,1)}, bf16[4,64,1664]{2,1,0:T(8,128)(2,1)}, bf16[4,64,1664]{2,1,0:T(8,128)(2,1)}, bf16[4,64,1664]{2,1,0:T(8,128)...) custom-call(s32[6]{0:T(128)} %pad_add_fusion.meta, ...), custom_call_target="tpu_custom_call" | custom-call | flops 5000000000 | bytes 31457280 | tf_op jit(solution)/shard_map/project_back/pallas_call | solution.py:1027
  572.3 3.4 collective-permute-done.90
  584.0 9.0 %rows_back.1 = (bf16[192,2048]{1,0:T(8,128)(2,1)S(1)}, bf16[192,2048]{1,0:T(8,128)(2,1)S(1)}, bf16[192,2048]{1,0:T(8,128)(2,1)S(1)}, bf16[192,2048]{1,0:T(8,128)(2,1)S(1)}) custom-call(bf16[768,1536]{1,0:T(8,128)(2,1)S(1)} %copy-done.34, bf16[2048,1664]{1,0:T(8,128)(2,1)S(1)} %copy-done.33), custom_call_target="tpu_custom_call" | custom-call | flops 5000000000 | bytes 12582912 | tf_op jit(solution)/shard_map/rows_back/pallas_call | solution.py:1057
  593.0 5.6 collective-permute-done.95
  606.5 14.6 %convolution_add_fusion = f32[2048,1024]{1,0:T(8,128)} fusion(f32[2048,1024]{1,0:T(8,128)} %collective-permute-done.99, bf16[2048,2048]{1,0:T(8,128)(2,1)} %get-tuple-element.874, bf16[2048,1024]{1,0:T(8,128)(2,1)S(1)} %copy-done.49), kind=kOutput, calls=%fused_computation.6 | convolution fusion | flops 8592031744 | bytes 29360128 | tf_op jit(solution)/shard_map/dot_general | solution.py:71
  622.6 7.5 %collective-permute-done.98 = bf16[192,2048]{1,0:T(8,128)(2,1)S(1)} collective-permute-done((bf16[192,2048]{1,0:T(8,128)(2,1)S(1)}, bf16[192,2048]{1,0:T(8,128)(2,1)S(1)}, u32[]{:S(2)}, u32[]{:S(2)}) %collective-permute-start.98) | collective-permute-done | bytes 786464 | tf_op jit(solution)/shard_map/ppermute | solution.py:337
  640.6 14.2 %collective-permute-done.103 = bf16[64,2048]{1,0:T(8,128)(2,1)S(1)} collective-permute-done((bf16[64,2048]{1,0:T(8,128)(2,1)S(1)}, bf16[64,2048]{1,0:T(8,128)(2,1)S(1)}, u32[]{:S(2)}, u32[]{:S(2)}) %collective-permute-start.103) | collective-permute-done | bytes 262176 | tf_op jit(solution)/shard_map/ppermute | solution.py:337
  (495 shorter events, 227.8 us)
Async XLA Ops:
  0.7 21.2 %collective-permute-start.3 = (bf16[192,2048]{1,0:T(8,128)(2,1)}, bf16[192,2048]{1,0:T(8,128)(2,1)S(1)}, u32[]{:S(2)}, u32[]{:S(2)}) collective-permute-start(bf16[192,2048]{1,0:T(8,128)(2,1)} %upstream.1), channel_id=1, source_target_pairs={{0,16},{1,17},{2,18},{3,19},{4,20},{5,21},{6,22},{7,23},{8,0},{9,1... | collective-permute-start | bytes 2359304 | tf_op jit(solution)/shard_map/ppermute | solution.py:337
  23.2 23.1 %collective-permute-start.4 = (bf16[4,64,1664]{2,1,0:T(8,128)(2,1)S(1)}, bf16[4,64,1664]{2,1,0:T(8,128)(2,1)}, u32[]{:S(2)}, u32[]{:S(2)}) collective-permute-start(bf16[4,64,1664]{2,1,0:T(8,128)(2,1)S(1)} %pad_maximum_fusion.refs_4_), channel_id=1, source_target_pairs={{0,16},{1,17},{2,18},{3,19},{4,20},{5,21},{6,22},{7,23},{8,0},{9,1... | collective-permute-start | bytes 2555912 | tf_op jit(solution)/shard_map/ppermute | solution.py:337
  28.0 28.8 %collective-permute-start.9 = (bf16[192,2048]{1,0:T(8,128)(2,1)S(1)}, bf16[192,2048]{1,0:T(8,128)(2,1)}, u32[]{:S(2)}, u32[]{:S(2)}) collective-permute-start(bf16[192,2048]{1,0:T(8,128)(2,1)S(1)} %copy-done), channel_id=1, source_target_pairs={{0,4},{1,3},{2,6},{3,1},{4,0},{5,7},{6,2},{7,5},{8,12},{9,11},{10,... | collective-permute-start | bytes 2359304 | tf_op jit(solution)/shard_map/ppermute | solution.py:337
  29.5 30.5 %collective-permute-start.11 = (bf16[192,2048]{1,0:T(8,128)(2,1)S(1)}, bf16[192,2048]{1,0:T(8,128)(2,1)}, u32[]{:S(2)}, u32[]{:S(2)}) collective-permute-start(bf16[192,2048]{1,0:T(8,128)(2,1)S(1)} %copy-done.6), channel_id=1, source_target_pairs={{0,2},{1,5},{2,0},{3,7},{4,6},{5,1},{6,4},{7,3},{8,10},{9,13},{10,... | collective-permute-start | bytes 2359304 | tf_op jit(solution)/shard_map/ppermute | solution.py:337
  60.0 95.7 %collective-permute-start.27 = (bf16[2048,1024]{1,0:T(8,128)(2,1)}, bf16[2048,1024]{1,0:T(8,128)(2,1)}, u32[]{:S(2)}, u32[]{:S(2)}) collective-permute-start(bf16[2048,1024]{1,0:T(8,128)(2,1)} %bitcast.69), channel_id=1, source_target_pairs={{0,1},{1,0},{2,3},{3,2},{4,5},{5,4},{6,7},{7,6},{8,9},{9,8},{10,11... | collective-permute-start | bytes 12582920 | tf_op jit(solution)/shard_map/ppermute | solution.py:337
  112.7 43.0 %collective-permute-start.28 = (bf16[512,2048]{1,0:T(8,128)(2,1)}, bf16[512,2048]{1,0:T(8,128)(2,1)}, u32[]{:S(2)}, u32[]{:S(2)}) collective-permute-start(bf16[512,2048]{1,0:T(8,128)(2,1)} %bitcast.78), channel_id=1, source_target_pairs={{0,1},{1,0},{2,3},{3,2},{4,5},{5,4},{6,7},{7,6},{8,9},{9,8},{10,11... | collective-permute-start | bytes 6291464 | tf_op jit(solution)/shard_map/ppermute | solution.py:337
  133.8 22.0 %collective-permute-start.29 = (bf16[192,2048]{1,0:T(8,128)(2,1)}, bf16[192,2048]{1,0:T(8,128)(2,1)}, u32[]{:S(2)}, u32[]{:S(2)}) collective-permute-start(bf16[192,2048]{1,0:T(8,128)(2,1)} %copy-done.77), channel_id=1, source_target_pairs={{0,16},{1,17},{2,18},{3,19},{4,20},{5,21},{6,22},{7,23},{8,0},{9,1... | collective-permute-start | bytes 2359304 | tf_op jit(solution)/shard_map/ppermute | solution.py:337
  158.8 20.7 %collective-permute-start.35 = (bf16[192,2048]{1,0:T(8,128)(2,1)}, bf16[192,2048]{1,0:T(8,128)(2,1)}, u32[]{:S(2)}, u32[]{:S(2)}) collective-permute-start(bf16[192,2048]{1,0:T(8,128)(2,1)} %collective-permute-done.29.refs_2_), channel_id=1, source_target_pairs={{0,16},{1,17},{2,18},{3,19},{4,20},{5,21},{6,22},{7,23},{8,0},{9,1... | collective-permute-start | bytes 2359304 | tf_op jit(solution)/shard_map/ppermute | solution.py:337
  197.1 29.4 %collective-permute-start.40 = (bf16[192,2176]{1,0:T(8,128)(2,1)}, bf16[192,2176]{1,0:T(8,128)(2,1)}, u32[]{:S(2)}, u32[]{:S(2)}) collective-permute-start(bf16[192,2176]{1,0:T(8,128)(2,1)} %get-tuple-element.568.refs_0_), channel_id=1, source_target_pairs={{0,16},{1,17},{2,18},{3,19},{4,20},{5,21},{6,22},{7,23},{8,0},{9,1... | collective-permute-start | bytes 2506760 | tf_op jit(solution)/shard_map/ppermute | solution.py:337
  211.6 41.0 %collective-permute-start.41 = (bf16[192,2176]{1,0:T(8,128)(2,1)}, bf16[192,2176]{1,0:T(8,128)(2,1)S(1)}, u32[]{:S(2)}, u32[]{:S(2)}) collective-permute-start(bf16[192,2176]{1,0:T(8,128)(2,1)} %collective-permute-done.37.refs_1_), channel_id=1, source_target_pairs={{0,16},{1,17},{2,18},{3,19},{4,20},{5,21},{6,22},{7,23},{8,0},{9,1... | collective-permute-start | bytes 2506760 | tf_op jit(solution)/shard_map/ppermute | solution.py:337
  231.4 21.3 %collective-permute-start.42 = (bf16[192,2176]{1,0:T(8,128)(2,1)}, bf16[192,2176]{1,0:T(8,128)(2,1)}, u32[]{:S(2)}, u32[]{:S(2)}) collective-permute-start(bf16[192,2176]{1,0:T(8,128)(2,1)} %collective-permute-done.40.refs_0_), channel_id=1, source_target_pairs={{0,4},{1,3},{2,6},{3,1},{4,0},{5,7},{6,2},{7,5},{8,12},{9,11},{10,... | collective-permute-start | bytes 2506760 | tf_op jit(solution)/shard_map/ppermute | solution.py:337
  233.4 40.4 %collective-permute-start.45 = (bf16[192,2176]{1,0:T(8,128)(2,1)}, bf16[192,2176]{1,0:T(8,128)(2,1)}, u32[]{:S(2)}, u32[]{:S(2)}) collective-permute-start(bf16[192,2176]{1,0:T(8,128)(2,1)} %collective-permute-done.40.refs_0_), channel_id=1, source_target_pairs={{0,16},{1,17},{2,18},{3,19},{4,20},{5,21},{6,22},{7,23},{8,0},{9,1... | collective-permute-start | bytes 2506760 | tf_op jit(solution)/shard_map/ppermute | solution.py:337
  252.7 21.1 %collective-permute-start.44 = (bf16[192,2176]{1,0:T(8,128)(2,1)S(1)}, bf16[192,2176]{1,0:T(8,128)(2,1)}, u32[]{:S(2)}, u32[]{:S(2)}) collective-permute-start(bf16[192,2176]{1,0:T(8,128)(2,1)S(1)} %collective-permute-done.41.refs_1_), channel_id=1, source_target_pairs={{0,4},{1,3},{2,6},{3,1},{4,0},{5,7},{6,2},{7,5},{8,12},{9,11},{10,... | collective-permute-start | bytes 2506760 | tf_op jit(solution)/shard_map/ppermute | solution.py:337
  254.8 40.3 %collective-permute-start.47 = (bf16[192,2176]{1,0:T(8,128)(2,1)S(1)}, bf16[192,2176]{1,0:T(8,128)(2,1)}, u32[]{:S(2)}, u32[]{:S(2)}) collective-permute-start(bf16[192,2176]{1,0:T(8,128)(2,1)S(1)} %collective-permute-done.41.refs_1_), channel_id=1, source_target_pairs={{0,16},{1,17},{2,18},{3,19},{4,20},{5,21},{6,22},{7,23},{8,0},{9,1... | collective-permute-start | bytes 2506760 | tf_op jit(solution)/shard_map/ppermute | solution.py:337
  273.8 21.3 %collective-permute-start.48 = (bf16[192,2176]{1,0:T(8,128)(2,1)}, bf16[192,2176]{1,0:T(8,128)(2,1)}, u32[]{:S(2)}, u32[]{:S(2)}) collective-permute-start(bf16[192,2176]{1,0:T(8,128)(2,1)} %collective-permute-done.45.refs_0_), channel_id=1, source_target_pairs={{0,4},{1,3},{2,6},{3,1},{4,0},{5,7},{6,2},{7,5},{8,12},{9,11},{10,... | collective-permute-start | bytes 2506760 | tf_op jit(solution)/shard_map/ppermute | solution.py:337
  275.8 38.2 %collective-permute-start.51 = (bf16[192,2176]{1,0:T(8,128)(2,1)}, bf16[192,2176]{1,0:T(8,128)(2,1)}, u32[]{:S(2)}, u32[]{:S(2)}) collective-permute-start(bf16[192,2176]{1,0:T(8,128)(2,1)} %collective-permute-done.45.refs_0_), channel_id=1, source_target_pairs={{0,16},{1,17},{2,18},{3,19},{4,20},{5,21},{6,22},{7,23},{8,0},{9,1... | collective-permute-start | bytes 2506760 | tf_op jit(solution)/shard_map/ppermute | solution.py:337
  298.3 30.4 %collective-permute-start.55 = (bf16[192,2176]{1,0:T(8,128)(2,1)}, bf16[192,2176]{1,0:T(8,128)(2,1)}, u32[]{:S(2)}, u32[]{:S(2)}) collective-permute-start(bf16[192,2176]{1,0:T(8,128)(2,1)} %get-tuple-element.665), channel_id=1, source_target_pairs={{0,4},{1,3},{2,6},{3,1},{4,0},{5,7},{6,2},{7,5},{8,12},{9,11},{10,... | collective-permute-start | bytes 2506760 | tf_op jit(solution)/shard_map/ppermute | solution.py:337
  298.9 29.7 %collective-permute-start.56 = (bf16[192,2176]{1,0:T(8,128)(2,1)}, bf16[192,2176]{1,0:T(8,128)(2,1)S(1)}, u32[]{:S(2)}, u32[]{:S(2)}) collective-permute-start(bf16[192,2176]{1,0:T(8,128)(2,1)} %get-tuple-element.666), channel_id=1, source_target_pairs={{0,4},{1,3},{2,6},{3,1},{4,0},{5,7},{6,2},{7,5},{8,12},{9,11},{10,... | collective-permute-start | bytes 2506760 | tf_op jit(solution)/shard_map/ppermute | solution.py:337
  314.1 20.7 %collective-permute-start.54 = (bf16[192,2176]{1,0:T(8,128)(2,1)}, bf16[192,2176]{1,0:T(8,128)(2,1)}, u32[]{:S(2)}, u32[]{:S(2)}) collective-permute-start(bf16[192,2176]{1,0:T(8,128)(2,1)} %collective-permute-done.51.refs_0_), channel_id=1, source_target_pairs={{0,4},{1,3},{2,6},{3,1},{4,0},{5,7},{6,2},{7,5},{8,12},{9,11},{10,... | collective-permute-start | bytes 2506760 | tf_op jit(solution)/shard_map/ppermute | solution.py:337
  334.8 21.3 %collective-permute-start.57 = (bf16[192,2176]{1,0:T(8,128)(2,1)}, bf16[192,2176]{1,0:T(8,128)(2,1)}, u32[]{:S(2)}, u32[]{:S(2)}) collective-permute-start(bf16[192,2176]{1,0:T(8,128)(2,1)} %collective-permute-done.53.refs_1_), channel_id=1, source_target_pairs={{0,4},{1,3},{2,6},{3,1},{4,0},{5,7},{6,2},{7,5},{8,12},{9,11},{10,... | collective-permute-start | bytes 2506760 | tf_op jit(solution)/shard_map/ppermute | solution.py:337
  358.3 21.8 %collective-permute-start.59 = (bf16[192,2176]{1,0:T(8,128)(2,1)}, bf16[192,2176]{1,0:T(8,128)(2,1)}, u32[]{:S(2)}, u32[]{:S(2)}) collective-permute-start(bf16[192,2176]{1,0:T(8,128)(2,1)} %add_convert_fusion.7), channel_id=1, source_target_pairs={{0,16},{1,17},{2,18},{3,19},{4,20},{5,21},{6,22},{7,23},{8,0},{9,1... | collective-permute-start | bytes 2506760 | tf_op jit(solution)/shard_map/ppermute | solution.py:337
  360.9 28.1 %collective-permute-start.60 = (bf16[192,2176]{1,0:T(8,128)(2,1)}, bf16[192,2176]{1,0:T(8,128)(2,1)}, u32[]{:S(2)}, u32[]{:S(2)}) collective-permute-start(bf16[192,2176]{1,0:T(8,128)(2,1)} %add_convert_fusion.6), channel_id=1, source_target_pairs={{0,16},{1,17},{2,18},{3,19},{4,20},{5,21},{6,22},{7,23},{8,0},{9,1... | collective-permute-start | bytes 2506760 | tf_op jit(solution)/shard_map/ppermute | solution.py:337
  362.0 27.1 %collective-permute-start.61 = (bf16[192,2176]{1,0:T(8,128)(2,1)}, bf16[192,2176]{1,0:T(8,128)(2,1)}, u32[]{:S(2)}, u32[]{:S(2)}) collective-permute-start(bf16[192,2176]{1,0:T(8,128)(2,1)} %get-tuple-element.715), channel_id=1, source_target_pairs={{0,4},{1,3},{2,6},{3,1},{4,0},{5,7},{6,2},{7,5},{8,12},{9,11},{10,... | collective-permute-start | bytes 2506760 | tf_op jit(solution)/shard_map/ppermute | solution.py:337
  363.0 26.1 %collective-permute-start.62 = (bf16[192,2176]{1,0:T(8,128)(2,1)}, bf16[192,2176]{1,0:T(8,128)(2,1)}, u32[]{:S(2)}, u32[]{:S(2)}) collective-permute-start(bf16[192,2176]{1,0:T(8,128)(2,1)} %get-tuple-element.716), channel_id=1, source_target_pairs={{0,4},{1,3},{2,6},{3,1},{4,0},{5,7},{6,2},{7,5},{8,12},{9,11},{10,... | collective-permute-start | bytes 2506760 | tf_op jit(solution)/shard_map/ppermute | solution.py:337
  376.8 31.1 %collective-permute-start.64 = (bf16[192,2176]{1,0:T(8,128)(2,1)}, bf16[192,2176]{1,0:T(8,128)(2,1)S(1)}, u32[]{:S(2)}, u32[]{:S(2)}) collective-permute-start(bf16[192,2176]{1,0:T(8,128)(2,1)} %get-tuple-element.723), channel_id=1, source_target_pairs={{0,4},{1,3},{2,6},{3,1},{4,0},{5,7},{6,2},{7,5},{8,12},{9,11},{10,... | collective-permute-start | bytes 2506760 | tf_op jit(solution)/shard_map/ppermute | solution.py:337
  380.1 31.8 %collective-permute-start.65 = (bf16[192,2176]{1,0:T(8,128)(2,1)}, bf16[192,2176]{1,0:T(8,128)(2,1)S(1)}, u32[]{:S(2)}, u32[]{:S(2)}) collective-permute-start(bf16[192,2176]{1,0:T(8,128)(2,1)} %get-tuple-element.724), channel_id=1, source_target_pairs={{0,4},{1,3},{2,6},{3,1},{4,0},{5,7},{6,2},{7,5},{8,12},{9,11},{10,... | collective-permute-start | bytes 2506760 | tf_op jit(solution)/shard_map/ppermute | solution.py:337
  390.9 21.0 %collective-permute-start.63 = (bf16[192,2176]{1,0:T(8,128)(2,1)S(1)}, bf16[192,2176]{1,0:T(8,128)(2,1)S(1)}, u32[]{:S(2)}, u32[]{:S(2)}) collective-permute-start(bf16[192,2176]{1,0:T(8,128)(2,1)S(1)} %add_convert_fusion.5), channel_id=1, source_target_pairs={{0,2},{1,5},{2,0},{3,7},{4,6},{5,1},{6,4},{7,3},{8,10},{9,13},{10,... | collective-permute-start | bytes 2506760 | tf_op jit(solution)/shard_map/ppermute | solution.py:337
  434.4 53.8 %collective-permute-start.75 = (f32[512,2048]{1,0:T(8,128)}, f32[512,2048]{1,0:T(8,128)S(1)}, u32[]{:S(2)}, u32[]{:S(2)}) collective-permute-start(f32[512,2048]{1,0:T(8,128)} %fusion.23), channel_id=1, source_target_pairs={{0,1},{1,0},{2,3},{3,2},{4,5},{5,4},{6,7},{7,6},{8,9},{9,8},{10,11... | collective-permute-start | bytes 12582920 | tf_op jit(solution)/shard_map/ppermute | solution.py:337
  434.8 21.1 %collective-permute-start.68 = (bf16[192,2176]{1,0:T(8,128)(2,1)S(1)}, bf16[192,2176]{1,0:T(8,128)(2,1)S(1)}, u32[]{:S(2)}, u32[]{:S(2)}) collective-permute-start(bf16[192,2176]{1,0:T(8,128)(2,1)S(1)} %add_convert_fusion.2), channel_id=1, source_target_pairs={{0,16},{1,17},{2,18},{3,19},{4,20},{5,21},{6,22},{7,23},{8,0},{9,1... | collective-permute-start | bytes 2506760 | tf_op jit(solution)/shard_map/ppermute | solution.py:337
  435.3 21.2 %collective-permute-start.70 = (bf16[192,2176]{1,0:T(8,128)(2,1)S(1)}, bf16[192,2176]{1,0:T(8,128)(2,1)S(1)}, u32[]{:S(2)}, u32[]{:S(2)}) collective-permute-start(bf16[192,2176]{1,0:T(8,128)(2,1)S(1)} %add_convert_fusion.1), channel_id=1, source_target_pairs={{0,2},{1,5},{2,0},{3,7},{4,6},{5,1},{6,4},{7,3},{8,10},{9,13},{10,... | collective-permute-start | bytes 2506760 | tf_op jit(solution)/shard_map/ppermute | solution.py:337
  459.1 21.0 %collective-permute-start.76 = (bf16[192,2048]{1,0:T(8,128)(2,1)}, bf16[192,2048]{1,0:T(8,128)(2,1)S(1)}, u32[]{:S(2)}, u32[]{:S(2)}) collective-permute-start(bf16[192,2048]{1,0:T(8,128)(2,1)} %get-tuple-element.756), channel_id=1, source_target_pairs={{0,4},{1,3},{2,6},{3,1},{4,0},{5,7},{6,2},{7,5},{8,12},{9,11},{10,... | collective-permute-start | bytes 2359304 | tf_op jit(solution)/shard_map/ppermute | solution.py:337
  460.0 26.4 %collective-permute-start.77 = (bf16[192,2048]{1,0:T(8,128)(2,1)S(1)}, bf16[192,2048]{1,0:T(8,128)(2,1)S(1)}, u32[]{:S(2)}, u32[]{:S(2)}) collective-permute-start(bf16[192,2048]{1,0:T(8,128)(2,1)S(1)} %copy-done.101), channel_id=1, source_target_pairs={{0,4},{1,3},{2,6},{3,1},{4,0},{5,7},{6,2},{7,5},{8,12},{9,11},{10,... | collective-permute-start | bytes 2359304 | tf_op jit(solution)/shard_map/ppermute | solution.py:337
  461.1 145.4 %collective-permute-start.99 = (f32[2048,1024]{1,0:T(8,128)}, f32[2048,1024]{1,0:T(8,128)}, u32[]{:S(2)}, u32[]{:S(2)}) collective-permute-start(f32[2048,1024]{1,0:T(8,128)} %fusion.22), channel_id=1, source_target_pairs={{0,1},{1,0},{2,3},{3,2},{4,5},{5,4},{6,7},{7,6},{8,9},{9,8},{10,11... | collective-permute-start | bytes 25165832 | tf_op jit(solution)/shard_map/ppermute | solution.py:337
  480.1 23.1 %collective-permute-start.74 = (bf16[192,2048]{1,0:T(8,128)(2,1)S(1)}, bf16[192,2048]{1,0:T(8,128)(2,1)S(1)}, u32[]{:S(2)}, u32[]{:S(2)}) collective-permute-start(bf16[192,2048]{1,0:T(8,128)(2,1)S(1)} %collective-permute-done.72.refs_1_), channel_id=1, source_target_pairs={{0,4},{1,3},{2,6},{3,1},{4,0},{5,7},{6,2},{7,5},{8,12},{9,11},{10,... | collective-permute-start | bytes 2359304 | tf_op jit(solution)/shard_map/ppermute | solution.py:337
  486.4 41.2 %collective-permute-start.80 = (bf16[192,2048]{1,0:T(8,128)(2,1)}, bf16[192,2048]{1,0:T(8,128)(2,1)}, u32[]{:S(2)}, u32[]{:S(2)}) collective-permute-start(bf16[192,2048]{1,0:T(8,128)(2,1)} %add_convert_fusion.16), channel_id=1, source_target_pairs={{0,16},{1,17},{2,18},{3,19},{4,20},{5,21},{6,22},{7,23},{8,0},{9,1... | collective-permute-start | bytes 2359304 | tf_op jit(solution)/shard_map/ppermute | solution.py:337
  488.3 39.3 %collective-permute-start.81 = (bf16[192,2048]{1,0:T(8,128)(2,1)}, bf16[192,2048]{1,0:T(8,128)(2,1)}, u32[]{:S(2)}, u32[]{:S(2)}) collective-permute-start(bf16[192,2048]{1,0:T(8,128)(2,1)} %add_convert_fusion.15), channel_id=1, source_target_pairs={{0,16},{1,17},{2,18},{3,19},{4,20},{5,21},{6,22},{7,23},{8,0},{9,1... | collective-permute-start | bytes 2359304 | tf_op jit(solution)/shard_map/ppermute | solution.py:337
  503.2 24.3 %collective-permute-start.78 = (bf16[192,2048]{1,0:T(8,128)(2,1)}, bf16[192,2048]{1,0:T(8,128)(2,1)}, u32[]{:S(2)}, u32[]{:S(2)}) collective-permute-start(bf16[192,2048]{1,0:T(8,128)(2,1)} %get-tuple-element.789), channel_id=1, source_target_pairs={{0,4},{1,3},{2,6},{3,1},{4,0},{5,7},{6,2},{7,5},{8,12},{9,11},{10,... | collective-permute-start | bytes 2359304 | tf_op jit(solution)/shard_map/ppermute | solution.py:337
  504.2 23.4 %collective-permute-start.79 = (bf16[192,2048]{1,0:T(8,128)(2,1)}, bf16[192,2048]{1,0:T(8,128)(2,1)}, u32[]{:S(2)}, u32[]{:S(2)}) collective-permute-start(bf16[192,2048]{1,0:T(8,128)(2,1)} %get-tuple-element.790), channel_id=1, source_target_pairs={{0,4},{1,3},{2,6},{3,1},{4,0},{5,7},{6,2},{7,5},{8,12},{9,11},{10,... | collective-permute-start | bytes 2359304 | tf_op jit(solution)/shard_map/ppermute | solution.py:337
  569.5 29.2 %collective-permute-start.92 = (bf16[3,4,64,1664]{3,2,1,0:T(8,128)(2,1)}, bf16[3,4,64,1664]{3,2,1,0:T(8,128)(2,1)S(1)}, u32[]{:S(2)}, u32[]{:S(2)}) collective-permute-start(bf16[3,4,64,1664]{3,2,1,0:T(8,128)(2,1)} %get-tuple-element.853), channel_id=1, source_target_pairs={{0,1},{1,0},{2,3},{3,2},{4,5},{5,4},{6,7},{7,6},{8,9},{9,8},{10,11... | collective-permute-start | bytes 7667720 | tf_op jit(solution)/shard_map/ppermute | solution.py:337
  577.1 21.5 %collective-permute-start.91 = (bf16[4,64,1664]{2,1,0:T(8,128)(2,1)S(1)}, bf16[4,64,1664]{2,1,0:T(8,128)(2,1)S(1)}, u32[]{:S(2)}, u32[]{:S(2)}) collective-permute-start(bf16[4,64,1664]{2,1,0:T(8,128)(2,1)S(1)} %add_convert_fusion), channel_id=1, source_target_pairs={{0,16},{1,17},{2,18},{3,19},{4,20},{5,21},{6,22},{7,23},{8,0},{9,1... | collective-permute-start | bytes 2555912 | tf_op jit(solution)/shard_map/ppermute | solution.py:337
  599.0 31.1 %collective-permute-start.96 = (bf16[4,64,1664]{2,1,0:T(8,128)(2,1)S(1)}, bf16[4,64,1664]{2,1,0:T(8,128)(2,1)S(1)}, u32[]{:S(2)}, u32[]{:S(2)}) collective-permute-start(bf16[4,64,1664]{2,1,0:T(8,128)(2,1)S(1)} %fusion.5), channel_id=1, source_target_pairs={{0,16},{1,17},{2,18},{3,19},{4,20},{5,21},{6,22},{7,23},{8,0},{9,1... | collective-permute-start | bytes 2555912 | tf_op jit(solution)/shard_map/ppermute | solution.py:337
  601.3 21.3 %collective-permute-start.97 = (bf16[192,2048]{1,0:T(8,128)(2,1)S(1)}, bf16[192,2048]{1,0:T(8,128)(2,1)S(1)}, u32[]{:S(2)}, u32[]{:S(2)}) collective-permute-start(bf16[192,2048]{1,0:T(8,128)(2,1)S(1)} %get-tuple-element.872), channel_id=1, source_target_pairs={{0,4},{1,3},{2,6},{3,1},{4,0},{5,7},{6,2},{7,5},{8,12},{9,11},{10,... | collective-permute-start | bytes 2359304 | tf_op jit(solution)/shard_map/ppermute | solution.py:337
  601.8 28.3 %collective-permute-start.98 = (bf16[192,2048]{1,0:T(8,128)(2,1)S(1)}, bf16[192,2048]{1,0:T(8,128)(2,1)S(1)}, u32[]{:S(2)}, u32[]{:S(2)}) collective-permute-start(bf16[192,2048]{1,0:T(8,128)(2,1)S(1)} %get-tuple-element.873), channel_id=1, source_target_pairs={{0,4},{1,3},{2,6},{3,1},{4,0},{5,7},{6,2},{7,5},{8,12},{9,11},{10,... | collective-permute-start | bytes 2359304 | tf_op jit(solution)/shard_map/ppermute | solution.py:337
  604.7 25.4 %collective-permute-start.100 = (bf16[192,2048]{1,0:T(8,128)(2,1)S(1)}, bf16[192,2048]{1,0:T(8,128)(2,1)S(1)}, u32[]{:S(2)}, u32[]{:S(2)}) collective-permute-start(bf16[192,2048]{1,0:T(8,128)(2,1)S(1)} %add_convert_fusion.12), channel_id=1, source_target_pairs={{0,2},{1,5},{2,0},{3,7},{4,6},{5,1},{6,4},{7,3},{8,10},{9,13},{10,... | collective-permute-start | bytes 2359304 | tf_op jit(solution)/shard_map/ppermute | solution.py:337
  630.5 24.4 %collective-permute-start.101 = (bf16[4,64,1664]{2,1,0:T(8,128)(2,1)S(1)}, bf16[4,64,1664]{2,1,0:T(8,128)(2,1)S(1)}, u32[]{:S(2)}, u32[]{:S(2)}) collective-permute-start(bf16[4,64,1664]{2,1,0:T(8,128)(2,1)S(1)} %fusion.3), channel_id=1, source_target_pairs={{0,16},{1,17},{2,18},{3,19},{4,20},{5,21},{6,22},{7,23},{8,0},{9,1... | collective-permute-start | bytes 2555912 | tf_op jit(solution)/shard_map/ppermute | solution.py:337
  631.7 23.2 %collective-permute-start.102 = (bf16[192,2048]{1,0:T(8,128)(2,1)S(1)}, bf16[192,2048]{1,0:T(8,128)(2,1)S(1)}, u32[]{:S(2)}, u32[]{:S(2)}) collective-permute-start(bf16[192,2048]{1,0:T(8,128)(2,1)S(1)} %add_convert_fusion.11), channel_id=1, source_target_pairs={{0,2},{1,5},{2,0},{3,7},{4,6},{5,1},{6,4},{7,3},{8,10},{9,13},{10,... | collective-permute-start | bytes 2359304 | tf_op jit(solution)/shard_map/ppermute | solution.py:337
  633.5 21.3 %collective-permute-start.103 = (bf16[64,2048]{1,0:T(8,128)(2,1)S(1)}, bf16[64,2048]{1,0:T(8,128)(2,1)S(1)}, u32[]{:S(2)}, u32[]{:S(2)}) collective-permute-start(bf16[64,2048]{1,0:T(8,128)(2,1)S(1)} %fusion.10), channel_id=1, source_target_pairs={{0,16},{1,17},{2,18},{3,19},{4,20},{5,21},{6,22},{7,23},{8,0},{9,1... | collective-permute-start | bytes 786440 | tf_op jit(solution)/shard_map/ppermute | solution.py:337
  635.3 29.1 %collective-permute-start.108 = (bf16[192,2048]{1,0:T(8,128)(2,1)S(1)}, bf16[192,2048]{1,0:T(8,128)(2,1)S(1)}, u32[]{:S(2)}, u32[]{:S(2)}) collective-permute-start(bf16[192,2048]{1,0:T(8,128)(2,1)S(1)} %add_convert_fusion.9), channel_id=1, source_target_pairs={{0,2},{1,5},{2,0},{3,7},{4,6},{5,1},{6,4},{7,3},{8,10},{9,13},{10,... | collective-permute-start | bytes 2359304 | tf_op jit(solution)/shard_map/ppermute | solution.py:337
  (168 other events, 2640.7 us)

commit v6 on v5

--- a/solution.py
+++ b/solution.py
@@ -1240,18 +1240,18 @@
     )
 
     in_other.append(send(in_own[3], cores))
-    (in_other,) = tie(in_other)
+    in_other, out_own = tie(in_other, out_own)
+    out_own.append(send(out_own[1], ring))
+    out_other.append(send(out_own[1], cores))
     grads[0, 1] = [send(item, second) for item in grads[0, 0]]
     projected, normed_all, in_full, sums, small_rows, gains = project(
         moves, blocks_x, in_own, in_other
     )
-    sums, out_own, grads = tie(sums, out_own, grads)
-    out_own.append(send(out_own[1], ring))
-    out_other.append(send(out_own[1], cores))
-    sums = plane_step(moves, by_spot(moves, sums), 1)
-    sums, out_own, own_1 = tie(sums, out_own, own_1)
+    sums, out_own, out_other, grads = tie(sums, out_own, out_other, grads)
     out_own.append(send(out_own[2], ring))
     out_other.append(send(out_own[2], cores))
+    sums = plane_step(moves, by_spot(moves, sums), 1)
+    sums, own_1 = tie(sums, own_1)
     totals = by_spot(moves, plane_step(moves, sums, 2))
     totals, out_own, out_other = tie(totals, out_own, out_other)
     out_other.append(send(out_own[3], cores))
@@ -1444,21 +1444,22 @@
     in_total = send(low(widen(in_total) + (widen(in_grads[2]) + widen(others_rest[0]))), ring)
     backs = cross(parts)
     expert_in_grad = dot_first(x_rows, du_own) + in_theirs
-    out_home, out_near = gather_near(out_parts[3], out_backs[3])
-    in_total, backs, expert_in_grad, out_parts, out_home, out_near, out_share = tie(
-        in_total, backs, expert_in_grad, out_parts, out_home, out_near, out_share
+    in_total, backs, expert_in_grad, out_parts, out_share = tie(
+        in_total, backs, expert_in_grad, out_parts, out_share
     )
 
     in_total = send(low(widen(in_total) + (widen(in_grads[3]) + widen(others_rest[1]))), ring)
     home, near = gather_near(parts, backs)
-    out_total = low(widen(out_total) + (out_home + widen(out_near)))
+    out_home_3, out_near_3 = gather_near(out_parts[3], out_backs[3])
     out_share = send(low(widen(out_share) + out_sum(3)), ring)
     out_home, out_near = gather_near(out_parts[0], out_backs[0])
-    in_total, home, near, out_total, out_share = tie(in_total, home, near, out_total, out_share)
+    in_total, home, near, out_home_3, out_near_3, out_share = tie(
+        in_total, home, near, out_home_3, out_near_3, out_share
+    )
 
     in_total = low(widen(in_total) + (widen(in_grads[0]) + widen(others_rest[2])))
     traded = [in_total[0]] + [send(in_total[m], moves.spots[m]) for m in range(1, SPOTS)]
-    out_total = send(out_total, ring)
+    out_total = send(low(widen(out_total) + (out_home_3 + widen(out_near_3))), ring)
     out_share = widen(out_share) + out_sum(0)
     _, first_back = jax.vjp(
         lambda value: root_norm(value, small_rows[FIRST_GAIN]), widen(tokens)

time: 687 us -> 676 us (0.984)
  waiting for transfers between devices: 256 us -> 238 us
  starting transfers between devices: 113 us -> 124 us
    ppermute x109, waiting for transfers between devices: 256 us -> 238 us  [send(): return lax.ppermute(value, 'fsdp', pairs)]
    ppermute x109, starting transfers between devices: 113 us -> 124 us  [send(): return lax.ppermute(value, 'fsdp', pairs)]
    unnamed x217 -> x201, local copies, waits for them, and re-layouts: 25.1 us -> 22.8 us
  transfers between devices with their start and end apart: 109 -> 109, of which waited for: 48 -> 47; matrix products, arithmetic and copies ran while one was open for 15% -> 14% of each run, Pallas kernels for 27% -> 27%
where the time goes in v6:
time: 676 us; the launch traced here: 667 us
  waiting for transfers between devices  238 us (35%)
  Pallas kernels  180 us (27%)
  starting transfers between devices  124 us (18%)
  other arithmetic  45 us (7%)
  matrix products  43.8 us (6%)
  local copies, waits for them, and re-layouts  33.3 us (5%)
    ppermute x109, waiting for transfers between devices, send(): return lax.ppermute(value, 'fsdp', pairs)  238 us
    ppermute x109, starting transfers between devices, send(): return lax.ppermute(value, 'fsdp', pairs)  124 us
    pallas_call x8, Pallas kernels, expert_blocks(): pl.pallas_call(functools.partial(expert_body, index, cap, experts, blocks...  103 us
    dot_general x4, matrix products, dot_first(): lax.dot_general(left, right, (((0,), (0,)), ((), ())), preferred_element_...  43.7 us
    convert_element_type x24, other arithmetic, low(): return value.astype(bf)  29.9 us
    unnamed x201, local copies, waits for them, and re-layouts  22.8 us
    pallas_call x1, Pallas kernels, attend_backward(): pl.pallas_call(backward_body, grid=(SPOTS,), out_shape=[shape((rows, mine...  20.5 us
    pallas_call x1, Pallas kernels, project_back(): pl.pallas_call(functools.partial(project_back_body, planes, own_rows), ou...  15.4 us
  transfers between devices with their start and end apart: 109, of which 47 were waited for; matrix products, arithmetic and copies ran while one was open for 14% of the time, Pallas kernels for 27%

profile of v6, /device:TPU:0, one launch (start us, length us, event | category | flops | bytes accessed | tf_op | source)
XLA Modules:
  0.0 667.2 jit_solution(7226450738846988029)
XLA Ops:
  0.7 4.1 collective-permute-start.3
  11.8 4.9 collective-permute-done
  16.7 4.3 collective-permute-done.1
  23.0 3.4 collective-permute-start.4
  30.3 15.9 %collective-permute-done.6.refs_1_ = bf16[192,2048]{1,0:T(8,128)(2,1)} collective-permute-done((bf16[192,2048]{1,0:T(8,128)(2,1)S(1)}, bf16[192,2048]{1,0:T(8,128)(2,1)}, u32[]{:S(2)}, u32[]{:S(2)}) %collective-permute-start.6) | collective-permute-done | bytes 786464 | tf_op jit(solution)/shard_map/ppermute | solution.py:337
  51.2 8.7 %collective-permute-done.11.refs_3_ = bf16[192,2048]{1,0:T(8,128)(2,1)S(1)} collective-permute-done((bf16[192,2048]{1,0:T(8,128)(2,1)S(1)}, bf16[192,2048]{1,0:T(8,128)(2,1)S(1)}, u32[]{:S(2)}, u32[]{:S(2)}) %collective-permute-start.11) | collective-permute-done | bytes 786464 | tf_op jit(solution)/shard_map/ppermute | solution.py:337
  69.6 6.0 collective-permute-done.15.refs_3_
  75.6 10.5 %collective-permute-done.12.refs_7_ = bf16[4,64,1664]{2,1,0:T(8,128)(2,1)} collective-permute-done((bf16[4,64,1664]{2,1,0:T(8,128)(2,1)}, bf16[4,64,1664]{2,1,0:T(8,128)(2,1)}, u32[]{:S(2)}, u32[]{:S(2)}) %collective-permute-start.12) | collective-permute-done | bytes 852000 | tf_op jit(solution)/shard_map/ppermute | solution.py:337
  97.3 12.6 %project.1 = (f32[768,1536]{1,0:T(8,128)}, bf16[768,2048]{1,0:T(8,128)(2,1)}, bf16[2048,1664]{1,0:T(8,128)(2,1)}, f32[2,4,192]{2,1,0:T(4,128)}, f32[32,2048]{1,0:T(8,128)}, /*index=5*/f32[2,512]{1,0:T(2,128)}) custom-call(s32[6]{0:T(128)} %pad_add_fusion.meta, bf16[192,2048]{1,0:T(8,128)(2,1)} %tokens.1, bf16[192,2048]{1,0:T(8,128)(2,1)} %collective-permute-done.6.refs_1_, ...), custom_call_target="tpu_custom_call" | custom-call | flops 5000000000 | bytes 20971520 | tf_op jit(solution)/shard_map/project/pallas_call | solution.py:698
  121.2 4.0 collective-permute-done.24.refs_3_
  134.4 11.0 %attend_forward.1 = (bf16[768,512]{1,0:T(8,128)(2,1)S(1)}, bf16[768,512]{1,0:T(8,128)(2,1)S(1)}, bf16[768,512]{1,0:T(8,128)(2,1)S(1)}, bf16[768,512]{1,0:T(8,128...) custom-call(s32[6]{0:T(128)S(1)} %copy-done.22, ...), custom_call_target="tpu_custom_call" | custom-call | flops 5000000000 | bytes 20971520 | tf_op jit(solution)/shard_map/attend_forward/pallas_call | solution.py:795
  151.8 9.7 %collective-permute-done.32.back = bf16[192,2048]{1,0:T(8,128)(2,1)S(1)} collective-permute-done((bf16[192,2048]{1,0:T(8,128)(2,1)S(1)}, bf16[192,2048]{1,0:T(8,128)(2,1)S(1)}, u32[]{:S(2)}, u32[]{:S(2)}) %collective-permute-start.32) | collective-permute-done | bytes 786464 | tf_op jit(solution)/shard_map/ppermute | solution.py:337
  161.5 8.4 %collective-permute-done.33 = bf16[192,2048]{1,0:T(8,128)(2,1)S(1)} collective-permute-done((bf16[192,2048]{1,0:T(8,128)(2,1)S(1)}, bf16[192,2048]{1,0:T(8,128)(2,1)S(1)}, u32[]{:S(2)}, u32[]{:S(2)}) %collective-permute-start.33) | collective-permute-done | bytes 786464 | tf_op jit(solution)/shard_map/ppermute | solution.py:337
  173.9 9.3 %collective-permute-done.34.near = bf16[192,2048]{1,0:T(8,128)(2,1)S(1)} collective-permute-done((bf16[192,2048]{1,0:T(8,128)(2,1)}, bf16[192,2048]{1,0:T(8,128)(2,1)S(1)}, u32[]{:S(2)}, u32[]{:S(2)}) %collective-permute-start.34) | collective-permute-done | bytes 786464 | tf_op jit(solution)/shard_map/ppermute | solution.py:337
  192.8 10.0 %collective-permute-done.37.refs_1_ = bf16[192,2176]{1,0:T(8,128)(2,1)} collective-permute-done((bf16[192,2176]{1,0:T(8,128)(2,1)}, bf16[192,2176]{1,0:T(8,128)(2,1)}, u32[]{:S(2)}, u32[]{:S(2)}) %collective-permute-start.37) | collective-permute-done | bytes 835616 | tf_op jit(solution)/shard_map/ppermute | solution.py:337
  206.5 12.8 %expert_blocks.8 = (bf16[2048,2048]{1,0:T(8,128)(2,1)}, bf16[2048,2048]{1,0:T(8,128)(2,1)}, bf16[2048,512]{1,0:T(8,128)(2,1)}, bf16[2048,512]{1,0:T(8,128)(2,1)}...) custom-call(s32[1]{0:T(128)} %bitcast.12.meta, ...), custom_call_target="tpu_custom_call" | custom-call | flops 7600000000 | bytes 31457280 | tf_op jit(solution)/shard_map/expert_blocks/pallas_call | solution.py:560
  219.3 5.2 collective-permute-done.39.refs_1_
  228.2 12.8 %expert_blocks.9 = (bf16[2048,2048]{1,0:T(8,128)(2,1)}, bf16[2048,2048]{1,0:T(8,128)(2,1)}, bf16[2048,512]{1,0:T(8,128)(2,1)}, bf16[2048,512]{1,0:T(8,128)(2,1)}...) custom-call(s32[1]{0:T(128)} %bitcast.12.meta, ...), custom_call_target="tpu_custom_call", output_to_operand_aliasing={{0}: (9, {}), {1}: (10, {}), {2}: (11, {}), {3}: (12, {}), ... | custom-call | flops 7600000000 | bytes 31457280 | tf_op jit(solution)/shard_map/expert_blocks/pallas_call | solution.py:560
  241.0 4.7 collective-permute-done.43.refs_2_
  249.2 12.8 %expert_blocks.10 = (bf16[2048,2048]{1,0:T(8,128)(2,1)}, bf16[2048,2048]{1,0:T(8,128)(2,1)}, bf16[2048,512]{1,0:T(8,128)(2,1)}, bf16[2048,512]{1,0:T(8,128)(2,1)...) custom-call(s32[1]{0:T(128)} %bitcast.12.meta, ...), custom_call_target="tpu_custom_call", output_to_operand_aliasing={{0}: (9, {}), {1}: (10, {}), {2}: (11, {}), {3}: (12, {}), ... | custom-call | flops 7600000000 | bytes 31457280 | tf_op jit(solution)/shard_map/expert_blocks/pallas_call | solution.py:560
  262.0 4.9 collective-permute-done.46.refs_3_
  270.3 12.8 %expert_blocks.11 = (bf16[2048,2048]{1,0:T(8,128)(2,1)}, bf16[2048,2048]{1,0:T(8,128)(2,1)}, bf16[2048,512]{1,0:T(8,128)(2,1)}, bf16[2048,512]{1,0:T(8,128)(2,1)...) custom-call(s32[1]{0:T(128)} %bitcast.12.meta, ...), custom_call_target="tpu_custom_call", output_to_operand_aliasing={{0}: (9, {}), {1}: (10, {}), {2}: (11, {}), {3}: (12, {}), ... | custom-call | flops 7600000000 | bytes 31457280 | tf_op jit(solution)/shard_map/expert_blocks/pallas_call | solution.py:560
  283.1 5.1 collective-permute-done.49.refs_2_
  293.0 12.8 %expert_blocks.12 = (bf16[2048,2048]{1,0:T(8,128)(2,1)}, bf16[2048,2048]{1,0:T(8,128)(2,1)}, bf16[2048,512]{1,0:T(8,128)(2,1)}, bf16[2048,512]{1,0:T(8,128)(2,1)...) custom-call(s32[1]{0:T(128)} %bitcast.12.meta, ...), custom_call_target="tpu_custom_call", output_to_operand_aliasing={{0}: (9, {}), {1}: (10, {}), {2}: (11, {}), {3}: (12, {}), ... | custom-call | flops 7600000000 | bytes 31457280 | tf_op jit(solution)/shard_map/expert_blocks/pallas_call | solution.py:560
  309.4 12.8 %expert_blocks.13 = (bf16[2048,2048]{1,0:T(8,128)(2,1)}, bf16[2048,2048]{1,0:T(8,128)(2,1)}, bf16[2048,512]{1,0:T(8,128)(2,1)}, bf16[2048,512]{1,0:T(8,128)(2,1)...) custom-call(s32[1]{0:T(128)} %bitcast.12.meta, ...), custom_call_target="tpu_custom_call", output_to_operand_aliasing={{0}: (9, {}), {1}: (10, {}), {2}: (11, {}), {3}: (12, {}), ... | custom-call | flops 7600000000 | bytes 31457280 | tf_op jit(solution)/shard_map/expert_blocks/pallas_call | solution.py:560
  322.3 5.6 collective-permute-done.54.refs_0_
  329.9 13.2 %expert_blocks.14 = (bf16[2048,2048]{1,0:T(8,128)(2,1)}, bf16[2048,2048]{1,0:T(8,128)(2,1)}, bf16[2048,512]{1,0:T(8,128)(2,1)}, bf16[2048,512]{1,0:T(8,128)(2,1)...) custom-call(s32[1]{0:T(128)} %bitcast.12.meta, ...), custom_call_target="tpu_custom_call", output_to_operand_aliasing={{0}: (9, {}), {1}: (10, {}), {2}: (11, {}), {3}: (12, {}), ... | custom-call | flops 7600000000 | bytes 31457280 | tf_op jit(solution)/shard_map/expert_blocks/pallas_call | solution.py:560
  343.2 6.0 collective-permute-done.58.refs_3_
  356.1 12.8 %expert_blocks.15 = (bf16[2048,2048]{1,0:T(8,128)(2,1)}, bf16[2048,2048]{1,0:T(8,128)(2,1)}, bf16[2048,512]{1,0:T(8,128)(2,1)}, bf16[2048,512]{1,0:T(8,128)(2,1)...) custom-call(s32[1]{0:T(128)} %bitcast.12.meta, ...), custom_call_target="tpu_custom_call", output_to_operand_aliasing={{0}: (9, {}), {1}: (10, {}), {2}: (11, {}), {3}: (12, {}), ... | custom-call | flops 7600000000 | bytes 31457280 | tf_op jit(solution)/shard_map/expert_blocks/pallas_call | solution.py:560
  374.3 7.6 %collective-permute-done.60 = bf16[192,2176]{1,0:T(8,128)(2,1)} collective-permute-done((bf16[192,2176]{1,0:T(8,128)(2,1)}, bf16[192,2176]{1,0:T(8,128)(2,1)}, u32[]{:S(2)}, u32[]{:S(2)}) %collective-permute-start.60) | collective-permute-done | bytes 835616 | tf_op jit(solution)/shard_map/ppermute | solution.py:337
  385.5 14.9 %fusion.22 = f32[2048,1024]{1,0:T(8,128)} fusion(bf16[2048,2048]{1,0:T(8,128)(2,1)} %get-tuple-element.880, bf16[2048,1024]{1,0:T(8,128)(2,1)} %get-tuple-element.731), kind=kOutput, calls=%fused_computation.109 | convolution fusion | flops 8589934592 | bytes 20971520 | tf_op jit(solution)/shard_map/dot_general | solution.py:71
  404.2 6.1 collective-permute-start.66
  412.2 6.2 fusion.23
  420.3 6.4 collective-permute-done.67
  427.4 3.9 collective-permute-done.69
  431.9 16.2 %collective-permute-done.68.total = bf16[192,2176]{1,0:T(8,128)(2,1)S(1)} collective-permute-done((bf16[192,2176]{1,0:T(8,128)(2,1)S(1)}, bf16[192,2176]{1,0:T(8,128)(2,1)S(1)}, u32[]{:S(2)}, u32[]{:S(2)}) %collective-permute-start.68) | collective-permute-done | bytes 835616 | tf_op jit(solution)/shard_map/ppermute | solution.py:337
  455.2 16.7 %collective-permute-done.72.refs_1_ = bf16[192,2048]{1,0:T(8,128)(2,1)S(1)} collective-permute-done((bf16[192,2048]{1,0:T(8,128)(2,1)S(1)}, bf16[192,2048]{1,0:T(8,128)(2,1)S(1)}, u32[]{:S(2)}, u32[]{:S(2)}) %collective-permute-start.72) | collective-permute-done | bytes 786464 | tf_op jit(solution)/shard_map/ppermute | solution.py:337
  482.5 8.0 %convolution_add_fusion.1 = f32[512,2048]{1,0:T(8,128)} fusion(f32[512,2048]{1,0:T(8,128)} %collective-permute-done.75, bf16[2048,512]{1,0:T(8,128)(2,1)S(1)} %copy-done.50, bf16[2048,2048]{1,0:T(8,128)(2,1)S(1)} %bitcast.68), kind=kOutput, calls=%fused_computation.7 | convolution fusion | flops 4296015872 | bytes 18874368 | tf_op jit(solution)/shard_map/dot_general | solution.py:71
  490.4 4.0 collective-permute-done.74.refs_3_
  496.5 20.5 %attend_backward.1 = (f32[768,512]{1,0:T(8,128)}, f32[768,512]{1,0:T(8,128)}, bf16[768,512]{1,0:T(8,128)(2,1)S(1)}, f32[2,4,192]{2,1,0:T(4,128)S(1)}, bf16[4,64,...) custom-call(s32[6]{0:T(128)S(1)} %copy-done.23, f32[2,4,192]{2,1,0:T(4,128)S(1)} %copy-done.19, ...), custom_call_target="tpu_custom_call" | custom-call | flops 7000000000 | bytes 26214400 | tf_op jit(solution)/shard_map/attend_backward/pallas_call | solution.py:890
  531.1 5.6 collective-permute-done.86
  545.3 15.4 %project_back.1 = (bf16[768,1536]{1,0:T(8,128)(2,1)}, bf16[4,64,1664]{2,1,0:T(8,128)(2,1)}, bf16[4,64,1664]{2,1,0:T(8,128)(2,1)}, bf16[4,64,1664]{2,1,0:T(8,128)...) custom-call(s32[6]{0:T(128)} %pad_add_fusion.meta, ...), custom_call_target="tpu_custom_call" | custom-call | flops 5000000000 | bytes 31457280 | tf_op jit(solution)/shard_map/project_back/pallas_call | solution.py:1027
  566.4 3.9 collective-permute-done.90
  578.9 9.0 %rows_back.1 = (bf16[192,2048]{1,0:T(8,128)(2,1)S(1)}, bf16[192,2048]{1,0:T(8,128)(2,1)S(1)}, bf16[192,2048]{1,0:T(8,128)(2,1)S(1)}, bf16[192,2048]{1,0:T(8,128)(2,1)S(1)}) custom-call(bf16[768,1536]{1,0:T(8,128)(2,1)S(1)} %copy-done.34, bf16[2048,1664]{1,0:T(8,128)(2,1)S(1)} %copy-done.33), custom_call_target="tpu_custom_call" | custom-call | flops 5000000000 | bytes 12582912 | tf_op jit(solution)/shard_map/rows_back/pallas_call | solution.py:1057
  587.9 4.9 collective-permute-done.95
  597.9 14.6 %convolution_add_fusion = f32[2048,1024]{1,0:T(8,128)} fusion(f32[2048,1024]{1,0:T(8,128)} %collective-permute-done.99, bf16[2048,2048]{1,0:T(8,128)(2,1)} %get-tuple-element.880, bf16[2048,1024]{1,0:T(8,128)(2,1)S(1)} %copy-done.49), kind=kOutput, calls=%fused_computation.6 | convolution fusion | flops 8592031744 | bytes 29360128 | tf_op jit(solution)/shard_map/dot_general | solution.py:71
  612.5 3.7 collective-permute-done.98
  630.5 10.6 %collective-permute-done.103 = bf16[64,2048]{1,0:T(8,128)(2,1)S(1)} collective-permute-done((bf16[64,2048]{1,0:T(8,128)(2,1)S(1)}, bf16[64,2048]{1,0:T(8,128)(2,1)S(1)}, u32[]{:S(2)}, u32[]{:S(2)}) %collective-permute-start.103) | collective-permute-done | bytes 262176 | tf_op jit(solution)/shard_map/ppermute | solution.py:337
  (479 shorter events, 229.8 us)
Async XLA Ops:
  0.7 21.2 %collective-permute-start.3 = (bf16[192,2048]{1,0:T(8,128)(2,1)}, bf16[192,2048]{1,0:T(8,128)(2,1)}, u32[]{:S(2)}, u32[]{:S(2)}) collective-permute-start(bf16[192,2048]{1,0:T(8,128)(2,1)} %upstream.1), channel_id=1, source_target_pairs={{0,16},{1,17},{2,18},{3,19},{4,20},{5,21},{6,22},{7,23},{8,0},{9,1... | collective-permute-start | bytes 2359304 | tf_op jit(solution)/shard_map/ppermute | solution.py:337
  23.0 23.2 %collective-permute-start.4 = (bf16[4,64,1664]{2,1,0:T(8,128)(2,1)S(1)}, bf16[4,64,1664]{2,1,0:T(8,128)(2,1)}, u32[]{:S(2)}, u32[]{:S(2)}) collective-permute-start(bf16[4,64,1664]{2,1,0:T(8,128)(2,1)S(1)} %pad_maximum_fusion.refs_4_), channel_id=1, source_target_pairs={{0,16},{1,17},{2,18},{3,19},{4,20},{5,21},{6,22},{7,23},{8,0},{9,1... | collective-permute-start | bytes 2555912 | tf_op jit(solution)/shard_map/ppermute | solution.py:337
  27.9 23.2 %collective-permute-start.9 = (bf16[192,2048]{1,0:T(8,128)(2,1)S(1)}, bf16[192,2048]{1,0:T(8,128)(2,1)}, u32[]{:S(2)}, u32[]{:S(2)}) collective-permute-start(bf16[192,2048]{1,0:T(8,128)(2,1)S(1)} %copy-done), channel_id=1, source_target_pairs={{0,4},{1,3},{2,6},{3,1},{4,0},{5,7},{6,2},{7,5},{8,12},{9,11},{10,... | collective-permute-start | bytes 2359304 | tf_op jit(solution)/shard_map/ppermute | solution.py:337
  29.4 30.5 %collective-permute-start.11 = (bf16[192,2048]{1,0:T(8,128)(2,1)S(1)}, bf16[192,2048]{1,0:T(8,128)(2,1)S(1)}, u32[]{:S(2)}, u32[]{:S(2)}) collective-permute-start(bf16[192,2048]{1,0:T(8,128)(2,1)S(1)} %copy-done.6), channel_id=1, source_target_pairs={{0,2},{1,5},{2,0},{3,7},{4,6},{5,1},{6,4},{7,3},{8,10},{9,13},{10,... | collective-permute-start | bytes 2359304 | tf_op jit(solution)/shard_map/ppermute | solution.py:337
  59.9 88.6 %collective-permute-start.27 = (bf16[2048,1024]{1,0:T(8,128)(2,1)}, bf16[2048,1024]{1,0:T(8,128)(2,1)}, u32[]{:S(2)}, u32[]{:S(2)}) collective-permute-start(bf16[2048,1024]{1,0:T(8,128)(2,1)} %bitcast.69), channel_id=1, source_target_pairs={{0,1},{1,0},{2,3},{3,2},{4,5},{5,4},{6,7},{7,6},{8,9},{9,8},{10,11... | collective-permute-start | bytes 12582920 | tf_op jit(solution)/shard_map/ppermute | solution.py:337
  65.8 20.3 %collective-permute-start.12 = (bf16[4,64,1664]{2,1,0:T(8,128)(2,1)}, bf16[4,64,1664]{2,1,0:T(8,128)(2,1)}, u32[]{:S(2)}, u32[]{:S(2)}) collective-permute-start(bf16[4,64,1664]{2,1,0:T(8,128)(2,1)} %collective-permute-done.7.refs_6_), channel_id=1, source_target_pairs={{0,16},{1,17},{2,18},{3,19},{4,20},{5,21},{6,22},{7,23},{8,0},{9,1... | collective-permute-start | bytes 2555912 | tf_op jit(solution)/shard_map/ppermute | solution.py:337
  87.7 22.2 %collective-permute-start.20 = (bf16[192,2048]{1,0:T(8,128)(2,1)S(1)}, bf16[192,2048]{1,0:T(8,128)(2,1)S(1)}, u32[]{:S(2)}, u32[]{:S(2)}) collective-permute-start(bf16[192,2048]{1,0:T(8,128)(2,1)S(1)} %copy-done.6), channel_id=1, source_target_pairs={{0,4},{1,3},{2,6},{3,1},{4,0},{5,7},{6,2},{7,5},{8,12},{9,11},{10,... | collective-permute-start | bytes 2359304 | tf_op jit(solution)/shard_map/ppermute | solution.py:337
  89.1 20.9 %collective-permute-start.21 = (bf16[192,2048]{1,0:T(8,128)(2,1)}, bf16[192,2048]{1,0:T(8,128)(2,1)}, u32[]{:S(2)}, u32[]{:S(2)}) collective-permute-start(bf16[192,2048]{1,0:T(8,128)(2,1)} %copy-done.90), channel_id=1, source_target_pairs={{0,4},{1,3},{2,6},{3,1},{4,0},{5,7},{6,2},{7,5},{8,12},{9,11},{10,... | collective-permute-start | bytes 2359304 | tf_op jit(solution)/shard_map/ppermute | solution.py:337
  115.2 33.3 %collective-permute-start.28 = (bf16[512,2048]{1,0:T(8,128)(2,1)}, bf16[512,2048]{1,0:T(8,128)(2,1)}, u32[]{:S(2)}, u32[]{:S(2)}) collective-permute-start(bf16[512,2048]{1,0:T(8,128)(2,1)} %bitcast.78), channel_id=1, source_target_pairs={{0,1},{1,0},{2,3},{3,2},{4,5},{5,4},{6,7},{7,6},{8,9},{9,8},{10,11... | collective-permute-start | bytes 6291464 | tf_op jit(solution)/shard_map/ppermute | solution.py:337
  127.4 21.1 %collective-permute-start.29 = (bf16[192,2048]{1,0:T(8,128)(2,1)}, bf16[192,2048]{1,0:T(8,128)(2,1)}, u32[]{:S(2)}, u32[]{:S(2)}) collective-permute-start(bf16[192,2048]{1,0:T(8,128)(2,1)} %collective-permute-done.3.refs_2_), channel_id=1, source_target_pairs={{0,16},{1,17},{2,18},{3,19},{4,20},{5,21},{6,22},{7,23},{8,0},{9,1... | collective-permute-start | bytes 2359304 | tf_op jit(solution)/shard_map/ppermute | solution.py:337
  151.5 22.4 %collective-permute-start.35 = (bf16[192,2048]{1,0:T(8,128)(2,1)}, bf16[192,2048]{1,0:T(8,128)(2,1)}, u32[]{:S(2)}, u32[]{:S(2)}) collective-permute-start(bf16[192,2048]{1,0:T(8,128)(2,1)} %collective-permute-done.29.refs_2_), channel_id=1, source_target_pairs={{0,16},{1,17},{2,18},{3,19},{4,20},{5,21},{6,22},{7,23},{8,0},{9,1... | collective-permute-start | bytes 2359304 | tf_op jit(solution)/shard_map/ppermute | solution.py:337
  191.3 28.0 %collective-permute-start.40 = (bf16[192,2176]{1,0:T(8,128)(2,1)}, bf16[192,2176]{1,0:T(8,128)(2,1)}, u32[]{:S(2)}, u32[]{:S(2)}) collective-permute-start(bf16[192,2176]{1,0:T(8,128)(2,1)} %get-tuple-element.573.refs_0_), channel_id=1, source_target_pairs={{0,16},{1,17},{2,18},{3,19},{4,20},{5,21},{6,22},{7,23},{8,0},{9,1... | collective-permute-start | bytes 2506760 | tf_op jit(solution)/shard_map/ppermute | solution.py:337
  203.7 20.8 %collective-permute-start.39 = (bf16[192,2176]{1,0:T(8,128)(2,1)}, bf16[192,2176]{1,0:T(8,128)(2,1)}, u32[]{:S(2)}, u32[]{:S(2)}) collective-permute-start(bf16[192,2176]{1,0:T(8,128)(2,1)} %collective-permute-done.37.refs_1_), channel_id=1, source_target_pairs={{0,4},{1,3},{2,6},{3,1},{4,0},{5,7},{6,2},{7,5},{8,12},{9,11},{10,... | collective-permute-start | bytes 2506760 | tf_op jit(solution)/shard_map/ppermute | solution.py:337
  204.8 41.0 %collective-permute-start.41 = (bf16[192,2176]{1,0:T(8,128)(2,1)}, bf16[192,2176]{1,0:T(8,128)(2,1)S(1)}, u32[]{:S(2)}, u32[]{:S(2)}) collective-permute-start(bf16[192,2176]{1,0:T(8,128)(2,1)} %collective-permute-done.37.refs_1_), channel_id=1, source_target_pairs={{0,16},{1,17},{2,18},{3,19},{4,20},{5,21},{6,22},{7,23},{8,0},{9,1... | collective-permute-start | bytes 2506760 | tf_op jit(solution)/shard_map/ppermute | solution.py:337
  224.5 21.3 %collective-permute-start.42 = (bf16[192,2176]{1,0:T(8,128)(2,1)}, bf16[192,2176]{1,0:T(8,128)(2,1)}, u32[]{:S(2)}, u32[]{:S(2)}) collective-permute-start(bf16[192,2176]{1,0:T(8,128)(2,1)} %collective-permute-done.40.refs_0_), channel_id=1, source_target_pairs={{0,4},{1,3},{2,6},{3,1},{4,0},{5,7},{6,2},{7,5},{8,12},{9,11},{10,... | collective-permute-start | bytes 2506760 | tf_op jit(solution)/shard_map/ppermute | solution.py:337
  225.5 20.3 %collective-permute-start.43 = (bf16[192,2048]{1,0:T(8,128)(2,1)}, bf16[192,2048]{1,0:T(8,128)(2,1)}, u32[]{:S(2)}, u32[]{:S(2)}) collective-permute-start(bf16[192,2048]{1,0:T(8,128)(2,1)} %collective-permute-done.29.refs_2_), channel_id=1, source_target_pairs={{0,4},{1,3},{2,6},{3,1},{4,0},{5,7},{6,2},{7,5},{8,12},{9,11},{10,... | collective-permute-start | bytes 2359304 | tf_op jit(solution)/shard_map/ppermute | solution.py:337
  226.6 40.4 %collective-permute-start.45 = (bf16[192,2176]{1,0:T(8,128)(2,1)}, bf16[192,2176]{1,0:T(8,128)(2,1)}, u32[]{:S(2)}, u32[]{:S(2)}) collective-permute-start(bf16[192,2176]{1,0:T(8,128)(2,1)} %collective-permute-done.40.refs_0_), channel_id=1, source_target_pairs={{0,16},{1,17},{2,18},{3,19},{4,20},{5,21},{6,22},{7,23},{8,0},{9,1... | collective-permute-start | bytes 2506760 | tf_op jit(solution)/shard_map/ppermute | solution.py:337
  245.8 21.1 %collective-permute-start.44 = (bf16[192,2176]{1,0:T(8,128)(2,1)S(1)}, bf16[192,2176]{1,0:T(8,128)(2,1)}, u32[]{:S(2)}, u32[]{:S(2)}) collective-permute-start(bf16[192,2176]{1,0:T(8,128)(2,1)S(1)} %collective-permute-done.41.refs_1_), channel_id=1, source_target_pairs={{0,4},{1,3},{2,6},{3,1},{4,0},{5,7},{6,2},{7,5},{8,12},{9,11},{10,... | collective-permute-start | bytes 2506760 | tf_op jit(solution)/shard_map/ppermute | solution.py:337
  247.9 40.3 %collective-permute-start.47 = (bf16[192,2176]{1,0:T(8,128)(2,1)S(1)}, bf16[192,2176]{1,0:T(8,128)(2,1)}, u32[]{:S(2)}, u32[]{:S(2)}) collective-permute-start(bf16[192,2176]{1,0:T(8,128)(2,1)S(1)} %collective-permute-done.41.refs_1_), channel_id=1, source_target_pairs={{0,16},{1,17},{2,18},{3,19},{4,20},{5,21},{6,22},{7,23},{8,0},{9,1... | collective-permute-start | bytes 2506760 | tf_op jit(solution)/shard_map/ppermute | solution.py:337
  266.9 21.3 %collective-permute-start.48 = (bf16[192,2176]{1,0:T(8,128)(2,1)}, bf16[192,2176]{1,0:T(8,128)(2,1)}, u32[]{:S(2)}, u32[]{:S(2)}) collective-permute-start(bf16[192,2176]{1,0:T(8,128)(2,1)} %collective-permute-done.45.refs_0_), channel_id=1, source_target_pairs={{0,4},{1,3},{2,6},{3,1},{4,0},{5,7},{6,2},{7,5},{8,12},{9,11},{10,... | collective-permute-start | bytes 2506760 | tf_op jit(solution)/shard_map/ppermute | solution.py:337
  268.9 38.9 %collective-permute-start.51 = (bf16[192,2176]{1,0:T(8,128)(2,1)}, bf16[192,2176]{1,0:T(8,128)(2,1)}, u32[]{:S(2)}, u32[]{:S(2)}) collective-permute-start(bf16[192,2176]{1,0:T(8,128)(2,1)} %collective-permute-done.45.refs_0_), channel_id=1, source_target_pairs={{0,16},{1,17},{2,18},{3,19},{4,20},{5,21},{6,22},{7,23},{8,0},{9,1... | collective-permute-start | bytes 2506760 | tf_op jit(solution)/shard_map/ppermute | solution.py:337
  291.0 31.2 %collective-permute-start.55 = (bf16[192,2176]{1,0:T(8,128)(2,1)}, bf16[192,2176]{1,0:T(8,128)(2,1)}, u32[]{:S(2)}, u32[]{:S(2)}) collective-permute-start(bf16[192,2176]{1,0:T(8,128)(2,1)} %get-tuple-element.670), channel_id=1, source_target_pairs={{0,4},{1,3},{2,6},{3,1},{4,0},{5,7},{6,2},{7,5},{8,12},{9,11},{10,... | collective-permute-start | bytes 2506760 | tf_op jit(solution)/shard_map/ppermute | solution.py:337
  291.7 30.5 %collective-permute-start.56 = (bf16[192,2176]{1,0:T(8,128)(2,1)}, bf16[192,2176]{1,0:T(8,128)(2,1)S(1)}, u32[]{:S(2)}, u32[]{:S(2)}) collective-permute-start(bf16[192,2176]{1,0:T(8,128)(2,1)} %get-tuple-element.671), channel_id=1, source_target_pairs={{0,4},{1,3},{2,6},{3,1},{4,0},{5,7},{6,2},{7,5},{8,12},{9,11},{10,... | collective-permute-start | bytes 2506760 | tf_op jit(solution)/shard_map/ppermute | solution.py:337
  327.9 21.3 %collective-permute-start.57 = (bf16[192,2176]{1,0:T(8,128)(2,1)}, bf16[192,2176]{1,0:T(8,128)(2,1)}, u32[]{:S(2)}, u32[]{:S(2)}) collective-permute-start(bf16[192,2176]{1,0:T(8,128)(2,1)} %collective-permute-done.53.refs_1_), channel_id=1, source_target_pairs={{0,4},{1,3},{2,6},{3,1},{4,0},{5,7},{6,2},{7,5},{8,12},{9,11},{10,... | collective-permute-start | bytes 2506760 | tf_op jit(solution)/shard_map/ppermute | solution.py:337
  351.5 21.4 %collective-permute-start.59 = (bf16[192,2176]{1,0:T(8,128)(2,1)}, bf16[192,2176]{1,0:T(8,128)(2,1)}, u32[]{:S(2)}, u32[]{:S(2)}) collective-permute-start(bf16[192,2176]{1,0:T(8,128)(2,1)} %add_convert_fusion.7), channel_id=1, source_target_pairs={{0,16},{1,17},{2,18},{3,19},{4,20},{5,21},{6,22},{7,23},{8,0},{9,1... | collective-permute-start | bytes 2506760 | tf_op jit(solution)/shard_map/ppermute | solution.py:337
  353.7 28.2 %collective-permute-start.60 = (bf16[192,2176]{1,0:T(8,128)(2,1)}, bf16[192,2176]{1,0:T(8,128)(2,1)}, u32[]{:S(2)}, u32[]{:S(2)}) collective-permute-start(bf16[192,2176]{1,0:T(8,128)(2,1)} %add_convert_fusion.6), channel_id=1, source_target_pairs={{0,16},{1,17},{2,18},{3,19},{4,20},{5,21},{6,22},{7,23},{8,0},{9,1... | collective-permute-start | bytes 2506760 | tf_op jit(solution)/shard_map/ppermute | solution.py:337
  354.0 27.8 %collective-permute-start.61 = (bf16[192,2176]{1,0:T(8,128)(2,1)}, bf16[192,2176]{1,0:T(8,128)(2,1)}, u32[]{:S(2)}, u32[]{:S(2)}) collective-permute-start(bf16[192,2176]{1,0:T(8,128)(2,1)} %get-tuple-element.720), channel_id=1, source_target_pairs={{0,4},{1,3},{2,6},{3,1},{4,0},{5,7},{6,2},{7,5},{8,12},{9,11},{10,... | collective-permute-start | bytes 2506760 | tf_op jit(solution)/shard_map/ppermute | solution.py:337
  355.0 26.9 %collective-permute-start.62 = (bf16[192,2176]{1,0:T(8,128)(2,1)}, bf16[192,2176]{1,0:T(8,128)(2,1)}, u32[]{:S(2)}, u32[]{:S(2)}) collective-permute-start(bf16[192,2176]{1,0:T(8,128)(2,1)} %get-tuple-element.721), channel_id=1, source_target_pairs={{0,4},{1,3},{2,6},{3,1},{4,0},{5,7},{6,2},{7,5},{8,12},{9,11},{10,... | collective-permute-start | bytes 2506760 | tf_op jit(solution)/shard_map/ppermute | solution.py:337
  368.8 33.3 %collective-permute-start.64 = (bf16[192,2176]{1,0:T(8,128)(2,1)}, bf16[192,2176]{1,0:T(8,128)(2,1)S(1)}, u32[]{:S(2)}, u32[]{:S(2)}) collective-permute-start(bf16[192,2176]{1,0:T(8,128)(2,1)} %get-tuple-element.728), channel_id=1, source_target_pairs={{0,4},{1,3},{2,6},{3,1},{4,0},{5,7},{6,2},{7,5},{8,12},{9,11},{10,... | collective-permute-start | bytes 2506760 | tf_op jit(solution)/shard_map/ppermute | solution.py:337
  372.9 31.1 %collective-permute-start.65 = (bf16[192,2176]{1,0:T(8,128)(2,1)}, bf16[192,2176]{1,0:T(8,128)(2,1)S(1)}, u32[]{:S(2)}, u32[]{:S(2)}) collective-permute-start(bf16[192,2176]{1,0:T(8,128)(2,1)} %get-tuple-element.729), channel_id=1, source_target_pairs={{0,4},{1,3},{2,6},{3,1},{4,0},{5,7},{6,2},{7,5},{8,12},{9,11},{10,... | collective-permute-start | bytes 2506760 | tf_op jit(solution)/shard_map/ppermute | solution.py:337
  426.7 54.5 %collective-permute-start.75 = (f32[512,2048]{1,0:T(8,128)}, f32[512,2048]{1,0:T(8,128)}, u32[]{:S(2)}, u32[]{:S(2)}) collective-permute-start(f32[512,2048]{1,0:T(8,128)} %fusion.23), channel_id=1, source_target_pairs={{0,1},{1,0},{2,3},{3,2},{4,5},{5,4},{6,7},{7,6},{8,9},{9,8},{10,11... | collective-permute-start | bytes 12582920 | tf_op jit(solution)/shard_map/ppermute | solution.py:337
  427.0 21.1 %collective-permute-start.68 = (bf16[192,2176]{1,0:T(8,128)(2,1)S(1)}, bf16[192,2176]{1,0:T(8,128)(2,1)S(1)}, u32[]{:S(2)}, u32[]{:S(2)}) collective-permute-start(bf16[192,2176]{1,0:T(8,128)(2,1)S(1)} %add_convert_fusion.2), channel_id=1, source_target_pairs={{0,16},{1,17},{2,18},{3,19},{4,20},{5,21},{6,22},{7,23},{8,0},{9,1... | collective-permute-start | bytes 2506760 | tf_op jit(solution)/shard_map/ppermute | solution.py:337
  451.4 20.5 %collective-permute-start.72 = (bf16[192,2048]{1,0:T(8,128)(2,1)S(1)}, bf16[192,2048]{1,0:T(8,128)(2,1)S(1)}, u32[]{:S(2)}, u32[]{:S(2)}) collective-permute-start(bf16[192,2048]{1,0:T(8,128)(2,1)S(1)} %get-tuple-element.789.refs_0_), channel_id=1, source_target_pairs={{0,2},{1,5},{2,0},{3,7},{4,6},{5,1},{6,4},{7,3},{8,10},{9,13},{10,... | collective-permute-start | bytes 2359304 | tf_op jit(solution)/shard_map/ppermute | solution.py:337
  453.7 23.8 %collective-permute-start.77 = (bf16[192,2048]{1,0:T(8,128)(2,1)S(1)}, bf16[192,2048]{1,0:T(8,128)(2,1)S(1)}, u32[]{:S(2)}, u32[]{:S(2)}) collective-permute-start(bf16[192,2048]{1,0:T(8,128)(2,1)S(1)} %copy-done.91), channel_id=1, source_target_pairs={{0,4},{1,3},{2,6},{3,1},{4,0},{5,7},{6,2},{7,5},{8,12},{9,11},{10,... | collective-permute-start | bytes 2359304 | tf_op jit(solution)/shard_map/ppermute | solution.py:337
  455.2 142.7 %collective-permute-start.99 = (f32[2048,1024]{1,0:T(8,128)}, f32[2048,1024]{1,0:T(8,128)}, u32[]{:S(2)}, u32[]{:S(2)}) collective-permute-start(f32[2048,1024]{1,0:T(8,128)} %fusion.22), channel_id=1, source_target_pairs={{0,1},{1,0},{2,3},{3,2},{4,5},{5,4},{6,7},{7,6},{8,9},{9,8},{10,11... | collective-permute-start | bytes 25165832 | tf_op jit(solution)/shard_map/ppermute | solution.py:337
  472.5 21.9 %collective-permute-start.74 = (bf16[192,2048]{1,0:T(8,128)(2,1)S(1)}, bf16[192,2048]{1,0:T(8,128)(2,1)S(1)}, u32[]{:S(2)}, u32[]{:S(2)}) collective-permute-start(bf16[192,2048]{1,0:T(8,128)(2,1)S(1)} %collective-permute-done.72.refs_1_), channel_id=1, source_target_pairs={{0,4},{1,3},{2,6},{3,1},{4,0},{5,7},{6,2},{7,5},{8,12},{9,11},{10,... | collective-permute-start | bytes 2359304 | tf_op jit(solution)/shard_map/ppermute | solution.py:337
  477.5 41.0 %collective-permute-start.80 = (bf16[192,2048]{1,0:T(8,128)(2,1)}, bf16[192,2048]{1,0:T(8,128)(2,1)}, u32[]{:S(2)}, u32[]{:S(2)}) collective-permute-start(bf16[192,2048]{1,0:T(8,128)(2,1)} %add_convert_fusion.16), channel_id=1, source_target_pairs={{0,16},{1,17},{2,18},{3,19},{4,20},{5,21},{6,22},{7,23},{8,0},{9,1... | collective-permute-start | bytes 2359304 | tf_op jit(solution)/shard_map/ppermute | solution.py:337
  481.2 37.3 %collective-permute-start.81 = (bf16[192,2048]{1,0:T(8,128)(2,1)}, bf16[192,2048]{1,0:T(8,128)(2,1)}, u32[]{:S(2)}, u32[]{:S(2)}) collective-permute-start(bf16[192,2048]{1,0:T(8,128)(2,1)} %add_convert_fusion.15), channel_id=1, source_target_pairs={{0,16},{1,17},{2,18},{3,19},{4,20},{5,21},{6,22},{7,23},{8,0},{9,1... | collective-permute-start | bytes 2359304 | tf_op jit(solution)/shard_map/ppermute | solution.py:337
  494.4 24.2 %collective-permute-start.78 = (bf16[192,2048]{1,0:T(8,128)(2,1)}, bf16[192,2048]{1,0:T(8,128)(2,1)}, u32[]{:S(2)}, u32[]{:S(2)}) collective-permute-start(bf16[192,2048]{1,0:T(8,128)(2,1)} %get-tuple-element.794), channel_id=1, source_target_pairs={{0,4},{1,3},{2,6},{3,1},{4,0},{5,7},{6,2},{7,5},{8,12},{9,11},{10,... | collective-permute-start | bytes 2359304 | tf_op jit(solution)/shard_map/ppermute | solution.py:337
  494.7 23.9 %collective-permute-start.79 = (bf16[192,2048]{1,0:T(8,128)(2,1)}, bf16[192,2048]{1,0:T(8,128)(2,1)}, u32[]{:S(2)}, u32[]{:S(2)}) collective-permute-start(bf16[192,2048]{1,0:T(8,128)(2,1)} %get-tuple-element.795), channel_id=1, source_target_pairs={{0,4},{1,3},{2,6},{3,1},{4,0},{5,7},{6,2},{7,5},{8,12},{9,11},{10,... | collective-permute-start | bytes 2359304 | tf_op jit(solution)/shard_map/ppermute | solution.py:337
  540.0 21.0 %collective-permute-start.87 = (bf16[192,2048]{1,0:T(8,128)(2,1)}, bf16[192,2048]{1,0:T(8,128)(2,1)}, u32[]{:S(2)}, u32[]{:S(2)}) collective-permute-start(bf16[192,2048]{1,0:T(8,128)(2,1)} %add_convert_fusion.13), channel_id=1, source_target_pairs={{0,16},{1,17},{2,18},{3,19},{4,20},{5,21},{6,22},{7,23},{8,0},{9,1... | collective-permute-start | bytes 2359304 | tf_op jit(solution)/shard_map/ppermute | solution.py:337
  564.0 28.9 %collective-permute-start.92 = (bf16[3,4,64,1664]{3,2,1,0:T(8,128)(2,1)}, bf16[3,4,64,1664]{3,2,1,0:T(8,128)(2,1)S(1)}, u32[]{:S(2)}, u32[]{:S(2)}) collective-permute-start(bf16[3,4,64,1664]{3,2,1,0:T(8,128)(2,1)} %get-tuple-element.859), channel_id=1, source_target_pairs={{0,1},{1,0},{2,3},{3,2},{4,5},{5,4},{6,7},{7,6},{8,9},{9,8},{10,11... | collective-permute-start | bytes 7667720 | tf_op jit(solution)/shard_map/ppermute | solution.py:337
  571.6 21.2 %collective-permute-start.91 = (bf16[4,64,1664]{2,1,0:T(8,128)(2,1)S(1)}, bf16[4,64,1664]{2,1,0:T(8,128)(2,1)}, u32[]{:S(2)}, u32[]{:S(2)}) collective-permute-start(bf16[4,64,1664]{2,1,0:T(8,128)(2,1)S(1)} %add_convert_fusion), channel_id=1, source_target_pairs={{0,16},{1,17},{2,18},{3,19},{4,20},{5,21},{6,22},{7,23},{8,0},{9,1... | collective-permute-start | bytes 2555912 | tf_op jit(solution)/shard_map/ppermute | solution.py:337
  594.4 21.9 %collective-permute-start.96 = (bf16[4,64,1664]{2,1,0:T(8,128)(2,1)S(1)}, bf16[4,64,1664]{2,1,0:T(8,128)(2,1)S(1)}, u32[]{:S(2)}, u32[]{:S(2)}) collective-permute-start(bf16[4,64,1664]{2,1,0:T(8,128)(2,1)S(1)} %fusion.5), channel_id=1, source_target_pairs={{0,16},{1,17},{2,18},{3,19},{4,20},{5,21},{6,22},{7,23},{8,0},{9,1... | collective-permute-start | bytes 2555912 | tf_op jit(solution)/shard_map/ppermute | solution.py:337
  616.6 24.5 %collective-permute-start.100 = (bf16[4,64,1664]{2,1,0:T(8,128)(2,1)S(1)}, bf16[4,64,1664]{2,1,0:T(8,128)(2,1)S(1)}, u32[]{:S(2)}, u32[]{:S(2)}) collective-permute-start(bf16[4,64,1664]{2,1,0:T(8,128)(2,1)S(1)} %fusion.3), channel_id=1, source_target_pairs={{0,16},{1,17},{2,18},{3,19},{4,20},{5,21},{6,22},{7,23},{8,0},{9,1... | collective-permute-start | bytes 2555912 | tf_op jit(solution)/shard_map/ppermute | solution.py:337
  617.4 23.7 %collective-permute-start.101 = (bf16[192,2048]{1,0:T(8,128)(2,1)S(1)}, bf16[192,2048]{1,0:T(8,128)(2,1)S(1)}, u32[]{:S(2)}, u32[]{:S(2)}) collective-permute-start(bf16[192,2048]{1,0:T(8,128)(2,1)S(1)} %add_convert_fusion.12), channel_id=1, source_target_pairs={{0,2},{1,5},{2,0},{3,7},{4,6},{5,1},{6,4},{7,3},{8,10},{9,13},{10,... | collective-permute-start | bytes 2359304 | tf_op jit(solution)/shard_map/ppermute | solution.py:337
  619.3 21.8 %collective-permute-start.102 = (bf16[192,2048]{1,0:T(8,128)(2,1)S(1)}, bf16[192,2048]{1,0:T(8,128)(2,1)S(1)}, u32[]{:S(2)}, u32[]{:S(2)}) collective-permute-start(bf16[192,2048]{1,0:T(8,128)(2,1)S(1)} %add_convert_fusion.11), channel_id=1, source_target_pairs={{0,2},{1,5},{2,0},{3,7},{4,6},{5,1},{6,4},{7,3},{8,10},{9,13},{10,... | collective-permute-start | bytes 2359304 | tf_op jit(solution)/shard_map/ppermute | solution.py:337
  625.3 27.5 %collective-permute-start.108 = (bf16[192,2048]{1,0:T(8,128)(2,1)S(1)}, bf16[192,2048]{1,0:T(8,128)(2,1)S(1)}, u32[]{:S(2)}, u32[]{:S(2)}) collective-permute-start(bf16[192,2048]{1,0:T(8,128)(2,1)S(1)} %add_convert_fusion.9), channel_id=1, source_target_pairs={{0,2},{1,5},{2,0},{3,7},{4,6},{5,1},{6,4},{7,3},{8,10},{9,13},{10,... | collective-permute-start | bytes 2359304 | tf_op jit(solution)/shard_map/ppermute | solution.py:337
  (160 other events, 2534.6 us)

commit v7 on v6

--- a/solution.py
+++ b/solution.py
@@ -363,7 +363,9 @@
 
 
 def cost(flops, moved, special=0):
-    return pl.CostEstimate(flops=flops, bytes_accessed=moved, transcendentals=special)
+    return pl.CostEstimate(
+        flops=flops // 2, bytes_accessed=moved // 2, transcendentals=special // 2
+    )
 
 
 def column_places(spot, mask, lines):

time: 676 us -> 678 us (level)
    unnamed x201 -> x195, local copies, waits for them, and re-layouts: 22.8 us -> 22.2 us
  transfers between devices with their start and end apart: 109 -> 109, of which waited for: 47 -> 48; matrix products, arithmetic and copies ran while one was open for 14% -> 15% of each run, Pallas kernels for 27% -> 27%
where the time goes in v7:
time: 678 us; the launch traced here: 669 us
  waiting for transfers between devices  240 us (35%)
  Pallas kernels  181 us (27%)
  starting transfers between devices  118 us (17%)
  other arithmetic  51.6 us (8%)
  matrix products  42.7 us (6%)
  local copies, waits for them, and re-layouts  34.5 us (5%)
    ppermute x109, waiting for transfers between devices, send(): return lax.ppermute(value, 'fsdp', pairs)  240 us
    ppermute x109, starting transfers between devices, send(): return lax.ppermute(value, 'fsdp', pairs)  118 us
    pallas_call x8, Pallas kernels, expert_blocks(): pl.pallas_call(functools.partial(expert_body, index, cap, experts, blocks...  103 us
    dot_general x4, matrix products, dot_first(): lax.dot_general(left, right, (((0,), (0,)), ((), ())), preferred_element_...  41.9 us
    convert_element_type x24, other arithmetic, low(): return value.astype(bf)  31.4 us
    unnamed x195, local copies, waits for them, and re-layouts  22.2 us
    pallas_call x1, Pallas kernels, attend_backward(): pl.pallas_call(backward_body, grid=(SPOTS,), out_shape=[shape((rows, mine...  20.6 us
    pallas_call x1, Pallas kernels, project_back(): pl.pallas_call(functools.partial(project_back_body, planes, own_rows), ou...  15.5 us
  transfers between devices with their start and end apart: 109, of which 48 were waited for; matrix products, arithmetic and copies ran while one was open for 15% of the time, Pallas kernels for 27%

profile of v7, /device:TPU:0, one launch (start us, length us, event | category | flops | bytes accessed | tf_op | source)
XLA Modules:
  0.0 669.1 jit_solution(2137055512955120287)
XLA Ops:
  0.7 4.1 collective-permute-start.3
  11.8 4.9 collective-permute-done
  16.7 4.3 collective-permute-done.1
  30.9 15.2 %collective-permute-done.6.refs_1_ = bf16[192,2048]{1,0:T(8,128)(2,1)} collective-permute-done((bf16[192,2048]{1,0:T(8,128)(2,1)S(1)}, bf16[192,2048]{1,0:T(8,128)(2,1)}, u32[]{:S(2)}, u32[]{:S(2)}) %collective-permute-start.6) | collective-permute-done | bytes 786464 | tf_op jit(solution)/shard_map/ppermute | solution.py:337
  59.2 4.1 collective-permute-done.10.refs_3_
  75.6 10.5 %collective-permute-done.12.refs_7_ = bf16[4,64,1664]{2,1,0:T(8,128)(2,1)} collective-permute-done((bf16[4,64,1664]{2,1,0:T(8,128)(2,1)}, bf16[4,64,1664]{2,1,0:T(8,128)(2,1)}, u32[]{:S(2)}, u32[]{:S(2)}) %collective-permute-start.12) | collective-permute-done | bytes 852000 | tf_op jit(solution)/shard_map/ppermute | solution.py:337
  92.3 4.8 collective-permute-done.17.refs_1_
  100.1 12.7 %project.1 = (f32[768,1536]{1,0:T(8,128)}, bf16[768,2048]{1,0:T(8,128)(2,1)}, bf16[2048,1664]{1,0:T(8,128)(2,1)}, f32[2,4,192]{2,1,0:T(4,128)}, f32[32,2048]{1,0:T(8,128)}, /*index=5*/f32[2,512]{1,0:T(2,128)}) custom-call(s32[6]{0:T(128)} %pad_add_fusion.meta, bf16[192,2048]{1,0:T(8,128)(2,1)} %tokens.1, bf16[192,2048]{1,0:T(8,128)(2,1)} %collective-permute-done.6.refs_1_, ...), custom_call_target="tpu_custom_call" | custom-call | flops 2500000000 | bytes 10485760 | tf_op jit(solution)/shard_map/project/pallas_call | solution.py:700
  124.1 3.9 collective-permute-done.24.refs_3_
  134.6 10.9 %attend_forward.1 = (bf16[768,512]{1,0:T(8,128)(2,1)S(1)}, bf16[768,512]{1,0:T(8,128)(2,1)S(1)}, bf16[768,512]{1,0:T(8,128)(2,1)S(1)}, bf16[768,512]{1,0:T(8,128...) custom-call(s32[6]{0:T(128)S(1)} %copy-done.35, ...), custom_call_target="tpu_custom_call" | custom-call | flops 2500000000 | bytes 10485760 | tf_op jit(solution)/shard_map/attend_forward/pallas_call | solution.py:797
  153.9 9.7 %collective-permute-done.32.back = bf16[192,2048]{1,0:T(8,128)(2,1)S(1)} collective-permute-done((bf16[192,2048]{1,0:T(8,128)(2,1)S(1)}, bf16[192,2048]{1,0:T(8,128)(2,1)S(1)}, u32[]{:S(2)}, u32[]{:S(2)}) %collective-permute-start.32) | collective-permute-done | bytes 786464 | tf_op jit(solution)/shard_map/ppermute | solution.py:337
  163.6 8.4 %collective-permute-done.33 = bf16[192,2048]{1,0:T(8,128)(2,1)S(1)} collective-permute-done((bf16[192,2048]{1,0:T(8,128)(2,1)S(1)}, bf16[192,2048]{1,0:T(8,128)(2,1)S(1)}, u32[]{:S(2)}, u32[]{:S(2)}) %collective-permute-start.33) | collective-permute-done | bytes 786464 | tf_op jit(solution)/shard_map/ppermute | solution.py:337
  175.3 10.0 %collective-permute-done.34.near = bf16[192,2048]{1,0:T(8,128)(2,1)S(1)} collective-permute-done((bf16[192,2048]{1,0:T(8,128)(2,1)}, bf16[192,2048]{1,0:T(8,128)(2,1)S(1)}, u32[]{:S(2)}, u32[]{:S(2)}) %collective-permute-start.34) | collective-permute-done | bytes 786464 | tf_op jit(solution)/shard_map/ppermute | solution.py:337
  195.0 10.1 %collective-permute-done.37.refs_1_ = bf16[192,2176]{1,0:T(8,128)(2,1)} collective-permute-done((bf16[192,2176]{1,0:T(8,128)(2,1)}, bf16[192,2176]{1,0:T(8,128)(2,1)}, u32[]{:S(2)}, u32[]{:S(2)}) %collective-permute-start.37) | collective-permute-done | bytes 835616 | tf_op jit(solution)/shard_map/ppermute | solution.py:337
  208.7 12.8 %expert_blocks.8 = (bf16[2048,2048]{1,0:T(8,128)(2,1)}, bf16[2048,2048]{1,0:T(8,128)(2,1)}, bf16[2048,512]{1,0:T(8,128)(2,1)}, bf16[2048,512]{1,0:T(8,128)(2,1)}...) custom-call(s32[1]{0:T(128)} %bitcast.12.meta, ...), custom_call_target="tpu_custom_call" | custom-call | flops 3800000000 | bytes 15728640 | tf_op jit(solution)/shard_map/expert_blocks/pallas_call | solution.py:562
  221.5 5.3 collective-permute-done.39.refs_1_
  230.4 12.8 %expert_blocks.9 = (bf16[2048,2048]{1,0:T(8,128)(2,1)}, bf16[2048,2048]{1,0:T(8,128)(2,1)}, bf16[2048,512]{1,0:T(8,128)(2,1)}, bf16[2048,512]{1,0:T(8,128)(2,1)}...) custom-call(s32[1]{0:T(128)} %bitcast.12.meta, ...), custom_call_target="tpu_custom_call", output_to_operand_aliasing={{0}: (9, {}), {1}: (10, {}), {2}: (11, {}), {3}: (12, {}), ... | custom-call | flops 3800000000 | bytes 15728640 | tf_op jit(solution)/shard_map/expert_blocks/pallas_call | solution.py:562
  243.2 4.9 collective-permute-done.43.refs_2_
  251.3 12.8 %expert_blocks.10 = (bf16[2048,2048]{1,0:T(8,128)(2,1)}, bf16[2048,2048]{1,0:T(8,128)(2,1)}, bf16[2048,512]{1,0:T(8,128)(2,1)}, bf16[2048,512]{1,0:T(8,128)(2,1)...) custom-call(s32[1]{0:T(128)} %bitcast.12.meta, ...), custom_call_target="tpu_custom_call", output_to_operand_aliasing={{0}: (9, {}), {1}: (10, {}), {2}: (11, {}), {3}: (12, {}), ... | custom-call | flops 3800000000 | bytes 15728640 | tf_op jit(solution)/shard_map/expert_blocks/pallas_call | solution.py:562
  264.1 5.2 collective-permute-done.46.refs_3_
  272.6 12.8 %expert_blocks.11 = (bf16[2048,2048]{1,0:T(8,128)(2,1)}, bf16[2048,2048]{1,0:T(8,128)(2,1)}, bf16[2048,512]{1,0:T(8,128)(2,1)}, bf16[2048,512]{1,0:T(8,128)(2,1)...) custom-call(s32[1]{0:T(128)} %bitcast.12.meta, ...), custom_call_target="tpu_custom_call", output_to_operand_aliasing={{0}: (9, {}), {1}: (10, {}), {2}: (11, {}), {3}: (12, {}), ... | custom-call | flops 3800000000 | bytes 15728640 | tf_op jit(solution)/shard_map/expert_blocks/pallas_call | solution.py:562
  285.4 5.2 collective-permute-done.49.refs_2_
  295.3 12.8 %expert_blocks.12 = (bf16[2048,2048]{1,0:T(8,128)(2,1)}, bf16[2048,2048]{1,0:T(8,128)(2,1)}, bf16[2048,512]{1,0:T(8,128)(2,1)}, bf16[2048,512]{1,0:T(8,128)(2,1)...) custom-call(s32[1]{0:T(128)} %bitcast.12.meta, ...), custom_call_target="tpu_custom_call", output_to_operand_aliasing={{0}: (9, {}), {1}: (10, {}), {2}: (11, {}), {3}: (12, {}), ... | custom-call | flops 3800000000 | bytes 15728640 | tf_op jit(solution)/shard_map/expert_blocks/pallas_call | solution.py:562
  311.8 12.8 %expert_blocks.13 = (bf16[2048,2048]{1,0:T(8,128)(2,1)}, bf16[2048,2048]{1,0:T(8,128)(2,1)}, bf16[2048,512]{1,0:T(8,128)(2,1)}, bf16[2048,512]{1,0:T(8,128)(2,1)...) custom-call(s32[1]{0:T(128)} %bitcast.12.meta, ...), custom_call_target="tpu_custom_call", output_to_operand_aliasing={{0}: (9, {}), {1}: (10, {}), {2}: (11, {}), {3}: (12, {}), ... | custom-call | flops 3800000000 | bytes 15728640 | tf_op jit(solution)/shard_map/expert_blocks/pallas_call | solution.py:562
  324.7 5.7 collective-permute-done.54.refs_0_
  332.4 13.2 %expert_blocks.14 = (bf16[2048,2048]{1,0:T(8,128)(2,1)}, bf16[2048,2048]{1,0:T(8,128)(2,1)}, bf16[2048,512]{1,0:T(8,128)(2,1)}, bf16[2048,512]{1,0:T(8,128)(2,1)...) custom-call(s32[1]{0:T(128)} %bitcast.12.meta, ...), custom_call_target="tpu_custom_call", output_to_operand_aliasing={{0}: (9, {}), {1}: (10, {}), {2}: (11, {}), {3}: (12, {}), ... | custom-call | flops 3800000000 | bytes 15728640 | tf_op jit(solution)/shard_map/expert_blocks/pallas_call | solution.py:562
  345.6 6.0 collective-permute-done.58.refs_3_
  359.8 12.8 %expert_blocks.15 = (bf16[2048,2048]{1,0:T(8,128)(2,1)}, bf16[2048,2048]{1,0:T(8,128)(2,1)}, bf16[2048,512]{1,0:T(8,128)(2,1)}, bf16[2048,512]{1,0:T(8,128)(2,1)...) custom-call(s32[1]{0:T(128)} %bitcast.12.meta, ...), custom_call_target="tpu_custom_call", output_to_operand_aliasing={{0}: (9, {}), {1}: (10, {}), {2}: (11, {}), {3}: (12, {}), ... | custom-call | flops 3800000000 | bytes 15728640 | tf_op jit(solution)/shard_map/expert_blocks/pallas_call | solution.py:562
  376.7 7.8 %collective-permute-done.60 = bf16[192,2176]{1,0:T(8,128)(2,1)} collective-permute-done((bf16[192,2176]{1,0:T(8,128)(2,1)}, bf16[192,2176]{1,0:T(8,128)(2,1)}, u32[]{:S(2)}, u32[]{:S(2)}) %collective-permute-start.60) | collective-permute-done | bytes 835616 | tf_op jit(solution)/shard_map/ppermute | solution.py:337
  388.4 14.8 %fusion.22 = f32[2048,1024]{1,0:T(8,128)} fusion(bf16[2048,2048]{1,0:T(8,128)(2,1)} %get-tuple-element.880, bf16[2048,1024]{1,0:T(8,128)(2,1)} %get-tuple-element.731), kind=kOutput, calls=%fused_computation.109 | convolution fusion | flops 8589934592 | bytes 20971520 | tf_op jit(solution)/shard_map/dot_general | solution.py:71
  404.9 3.9 collective-permute-done.65
  409.1 6.3 collective-permute-start.66
  417.3 6.0 fusion.23
  425.4 3.7 collective-permute-done.67
  429.8 8.8 %collective-permute-done.69 = bf16[192,2176]{1,0:T(8,128)(2,1)S(1)} collective-permute-done((bf16[192,2176]{1,0:T(8,128)(2,1)S(1)}, bf16[192,2176]{1,0:T(8,128)(2,1)S(1)}, u32[]{:S(2)}, u32[]{:S(2)}) %collective-permute-start.69) | collective-permute-done | bytes 835616 | tf_op jit(solution)/shard_map/ppermute | solution.py:337
  439.0 11.5 %collective-permute-done.68.total = bf16[192,2176]{1,0:T(8,128)(2,1)S(1)} collective-permute-done((bf16[192,2176]{1,0:T(8,128)(2,1)S(1)}, bf16[192,2176]{1,0:T(8,128)(2,1)S(1)}, u32[]{:S(2)}, u32[]{:S(2)}) %collective-permute-start.68) | collective-permute-done | bytes 835616 | tf_op jit(solution)/shard_map/ppermute | solution.py:337
  458.0 18.0 %collective-permute-done.72.refs_1_ = bf16[192,2048]{1,0:T(8,128)(2,1)S(1)} collective-permute-done((bf16[192,2048]{1,0:T(8,128)(2,1)S(1)}, bf16[192,2048]{1,0:T(8,128)(2,1)S(1)}, u32[]{:S(2)}, u32[]{:S(2)}) %collective-permute-start.72) | collective-permute-done | bytes 786464 | tf_op jit(solution)/shard_map/ppermute | solution.py:337
  483.8 6.4 convolution_add_fusion.1
  490.2 6.5 collective-permute-done.74.refs_3_
  498.9 20.6 %attend_backward.1 = (f32[768,512]{1,0:T(8,128)}, f32[768,512]{1,0:T(8,128)}, bf16[768,512]{1,0:T(8,128)(2,1)S(1)}, f32[2,4,192]{2,1,0:T(4,128)S(1)}, bf16[4,64,...) custom-call(s32[6]{0:T(128)S(1)} %copy-done.36, ...), custom_call_target="tpu_custom_call" | custom-call | flops 3500000000 | bytes 13107200 | tf_op jit(solution)/shard_map/attend_backward/pallas_call | solution.py:892
  532.3 6.2 collective-permute-done.86
  545.8 15.5 %project_back.1 = (bf16[768,1536]{1,0:T(8,128)(2,1)}, bf16[4,64,1664]{2,1,0:T(8,128)(2,1)}, bf16[4,64,1664]{2,1,0:T(8,128)(2,1)}, bf16[4,64,1664]{2,1,0:T(8,128)...) custom-call(s32[6]{0:T(128)} %pad_add_fusion.meta, ...), custom_call_target="tpu_custom_call" | custom-call | flops 2500000000 | bytes 15728640 | tf_op jit(solution)/shard_map/project_back/pallas_call | solution.py:1029
  566.9 3.8 collective-permute-done.90
  578.8 9.0 %rows_back.1 = (bf16[192,2048]{1,0:T(8,128)(2,1)S(1)}, bf16[192,2048]{1,0:T(8,128)(2,1)S(1)}, bf16[192,2048]{1,0:T(8,128)(2,1)S(1)}, bf16[192,2048]{1,0:T(8,128)(2,1)S(1)}) custom-call(bf16[768,1536]{1,0:T(8,128)(2,1)S(1)} %copy-done.38, bf16[2048,1664]{1,0:T(8,128)(2,1)S(1)} %copy-done.37), custom_call_target="tpu_custom_call" | custom-call | flops 2500000000 | bytes 6291456 | tf_op jit(solution)/shard_map/rows_back/pallas_call | solution.py:1059
  587.9 5.6 collective-permute-done.95
  600.1 14.6 %convolution_add_fusion = f32[2048,1024]{1,0:T(8,128)} fusion(f32[2048,1024]{1,0:T(8,128)} %collective-permute-done.99, bf16[2048,2048]{1,0:T(8,128)(2,1)} %get-tuple-element.880, bf16[2048,1024]{1,0:T(8,128)(2,1)S(1)} %copy-done.43), kind=kOutput, calls=%fused_computation.6 | convolution fusion | flops 8592031744 | bytes 29360128 | tf_op jit(solution)/shard_map/dot_general | solution.py:71
  614.7 3.7 collective-permute-done.98
  631.4 11.7 %collective-permute-done.103 = bf16[64,2048]{1,0:T(8,128)(2,1)S(1)} collective-permute-done((bf16[64,2048]{1,0:T(8,128)(2,1)S(1)}, bf16[64,2048]{1,0:T(8,128)(2,1)S(1)}, u32[]{:S(2)}, u32[]{:S(2)}) %collective-permute-start.103) | collective-permute-done | bytes 262176 | tf_op jit(solution)/shard_map/ppermute | solution.py:337
  (473 shorter events, 233.4 us)
Async XLA Ops:
  0.7 21.2 %collective-permute-start.3 = (bf16[192,2048]{1,0:T(8,128)(2,1)}, bf16[192,2048]{1,0:T(8,128)(2,1)}, u32[]{:S(2)}, u32[]{:S(2)}) collective-permute-start(bf16[192,2048]{1,0:T(8,128)(2,1)} %upstream.1), channel_id=1, source_target_pairs={{0,16},{1,17},{2,18},{3,19},{4,20},{5,21},{6,22},{7,23},{8,0},{9,1... | collective-permute-start | bytes 2359304 | tf_op jit(solution)/shard_map/ppermute | solution.py:337
  23.0 23.2 %collective-permute-start.4 = (bf16[4,64,1664]{2,1,0:T(8,128)(2,1)S(1)}, bf16[4,64,1664]{2,1,0:T(8,128)(2,1)S(1)}, u32[]{:S(2)}, u32[]{:S(2)}) collective-permute-start(bf16[4,64,1664]{2,1,0:T(8,128)(2,1)S(1)} %pad_maximum_fusion.refs_4_), channel_id=1, source_target_pairs={{0,16},{1,17},{2,18},{3,19},{4,20},{5,21},{6,22},{7,23},{8,0},{9,1... | collective-permute-start | bytes 2555912 | tf_op jit(solution)/shard_map/ppermute | solution.py:337
  27.9 29.7 %collective-permute-start.9 = (bf16[192,2048]{1,0:T(8,128)(2,1)S(1)}, bf16[192,2048]{1,0:T(8,128)(2,1)}, u32[]{:S(2)}, u32[]{:S(2)}) collective-permute-start(bf16[192,2048]{1,0:T(8,128)(2,1)S(1)} %copy-done), channel_id=1, source_target_pairs={{0,4},{1,3},{2,6},{3,1},{4,0},{5,7},{6,2},{7,5},{8,12},{9,11},{10,... | collective-permute-start | bytes 2359304 | tf_op jit(solution)/shard_map/ppermute | solution.py:337
  29.4 29.8 %collective-permute-start.11 = (bf16[192,2048]{1,0:T(8,128)(2,1)S(1)}, bf16[192,2048]{1,0:T(8,128)(2,1)}, u32[]{:S(2)}, u32[]{:S(2)}) collective-permute-start(bf16[192,2048]{1,0:T(8,128)(2,1)S(1)} %copy-done.2), channel_id=1, source_target_pairs={{0,2},{1,5},{2,0},{3,7},{4,6},{5,1},{6,4},{7,3},{8,10},{9,13},{10,... | collective-permute-start | bytes 2359304 | tf_op jit(solution)/shard_map/ppermute | solution.py:337
  59.2 90.4 %collective-permute-start.27 = (bf16[2048,1024]{1,0:T(8,128)(2,1)}, bf16[2048,1024]{1,0:T(8,128)(2,1)}, u32[]{:S(2)}, u32[]{:S(2)}) collective-permute-start(bf16[2048,1024]{1,0:T(8,128)(2,1)} %bitcast.69), channel_id=1, source_target_pairs={{0,1},{1,0},{2,3},{3,2},{4,5},{5,4},{6,7},{7,6},{8,9},{9,8},{10,11... | collective-permute-start | bytes 12582920 | tf_op jit(solution)/shard_map/ppermute | solution.py:337
  86.1 26.6 %collective-permute-start.20 = (bf16[192,2048]{1,0:T(8,128)(2,1)S(1)}, bf16[192,2048]{1,0:T(8,128)(2,1)S(1)}, u32[]{:S(2)}, u32[]{:S(2)}) collective-permute-start(bf16[192,2048]{1,0:T(8,128)(2,1)S(1)} %copy-done.2), channel_id=1, source_target_pairs={{0,4},{1,3},{2,6},{3,1},{4,0},{5,7},{6,2},{7,5},{8,12},{9,11},{10,... | collective-permute-start | bytes 2359304 | tf_op jit(solution)/shard_map/ppermute | solution.py:337
  86.9 25.9 %collective-permute-start.21 = (bf16[192,2048]{1,0:T(8,128)(2,1)}, bf16[192,2048]{1,0:T(8,128)(2,1)}, u32[]{:S(2)}, u32[]{:S(2)}) collective-permute-start(bf16[192,2048]{1,0:T(8,128)(2,1)} %collective-permute-done.11.refs_3_), channel_id=1, source_target_pairs={{0,4},{1,3},{2,6},{3,1},{4,0},{5,7},{6,2},{7,5},{8,12},{9,11},{10,... | collective-permute-start | bytes 2359304 | tf_op jit(solution)/shard_map/ppermute | solution.py:337
  118.1 31.5 %collective-permute-start.28 = (bf16[512,2048]{1,0:T(8,128)(2,1)}, bf16[512,2048]{1,0:T(8,128)(2,1)}, u32[]{:S(2)}, u32[]{:S(2)}) collective-permute-start(bf16[512,2048]{1,0:T(8,128)(2,1)} %bitcast.78), channel_id=1, source_target_pairs={{0,1},{1,0},{2,3},{3,2},{4,5},{5,4},{6,7},{7,6},{8,9},{9,8},{10,11... | collective-permute-start | bytes 6291464 | tf_op jit(solution)/shard_map/ppermute | solution.py:337
  153.6 21.7 %collective-permute-start.35 = (bf16[192,2048]{1,0:T(8,128)(2,1)}, bf16[192,2048]{1,0:T(8,128)(2,1)}, u32[]{:S(2)}, u32[]{:S(2)}) collective-permute-start(bf16[192,2048]{1,0:T(8,128)(2,1)} %collective-permute-done.29.refs_2_), channel_id=1, source_target_pairs={{0,16},{1,17},{2,18},{3,19},{4,20},{5,21},{6,22},{7,23},{8,0},{9,1... | collective-permute-start | bytes 2359304 | tf_op jit(solution)/shard_map/ppermute | solution.py:337
  193.6 27.9 %collective-permute-start.40 = (bf16[192,2176]{1,0:T(8,128)(2,1)}, bf16[192,2176]{1,0:T(8,128)(2,1)}, u32[]{:S(2)}, u32[]{:S(2)}) collective-permute-start(bf16[192,2176]{1,0:T(8,128)(2,1)} %get-tuple-element.573.refs_0_), channel_id=1, source_target_pairs={{0,16},{1,17},{2,18},{3,19},{4,20},{5,21},{6,22},{7,23},{8,0},{9,1... | collective-permute-start | bytes 2506760 | tf_op jit(solution)/shard_map/ppermute | solution.py:337
  205.9 21.0 %collective-permute-start.39 = (bf16[192,2176]{1,0:T(8,128)(2,1)}, bf16[192,2176]{1,0:T(8,128)(2,1)}, u32[]{:S(2)}, u32[]{:S(2)}) collective-permute-start(bf16[192,2176]{1,0:T(8,128)(2,1)} %collective-permute-done.37.refs_1_), channel_id=1, source_target_pairs={{0,4},{1,3},{2,6},{3,1},{4,0},{5,7},{6,2},{7,5},{8,12},{9,11},{10,... | collective-permute-start | bytes 2506760 | tf_op jit(solution)/shard_map/ppermute | solution.py:337
  207.1 41.0 %collective-permute-start.41 = (bf16[192,2176]{1,0:T(8,128)(2,1)}, bf16[192,2176]{1,0:T(8,128)(2,1)}, u32[]{:S(2)}, u32[]{:S(2)}) collective-permute-start(bf16[192,2176]{1,0:T(8,128)(2,1)} %collective-permute-done.37.refs_1_), channel_id=1, source_target_pairs={{0,16},{1,17},{2,18},{3,19},{4,20},{5,21},{6,22},{7,23},{8,0},{9,1... | collective-permute-start | bytes 2506760 | tf_op jit(solution)/shard_map/ppermute | solution.py:337
  226.8 21.3 %collective-permute-start.42 = (bf16[192,2176]{1,0:T(8,128)(2,1)}, bf16[192,2176]{1,0:T(8,128)(2,1)}, u32[]{:S(2)}, u32[]{:S(2)}) collective-permute-start(bf16[192,2176]{1,0:T(8,128)(2,1)} %collective-permute-done.40.refs_0_), channel_id=1, source_target_pairs={{0,4},{1,3},{2,6},{3,1},{4,0},{5,7},{6,2},{7,5},{8,12},{9,11},{10,... | collective-permute-start | bytes 2506760 | tf_op jit(solution)/shard_map/ppermute | solution.py:337
  228.9 40.5 %collective-permute-start.45 = (bf16[192,2176]{1,0:T(8,128)(2,1)}, bf16[192,2176]{1,0:T(8,128)(2,1)}, u32[]{:S(2)}, u32[]{:S(2)}) collective-permute-start(bf16[192,2176]{1,0:T(8,128)(2,1)} %collective-permute-done.40.refs_0_), channel_id=1, source_target_pairs={{0,16},{1,17},{2,18},{3,19},{4,20},{5,21},{6,22},{7,23},{8,0},{9,1... | collective-permute-start | bytes 2506760 | tf_op jit(solution)/shard_map/ppermute | solution.py:337
  248.1 21.3 %collective-permute-start.44 = (bf16[192,2176]{1,0:T(8,128)(2,1)}, bf16[192,2176]{1,0:T(8,128)(2,1)}, u32[]{:S(2)}, u32[]{:S(2)}) collective-permute-start(bf16[192,2176]{1,0:T(8,128)(2,1)} %collective-permute-done.41.refs_1_), channel_id=1, source_target_pairs={{0,4},{1,3},{2,6},{3,1},{4,0},{5,7},{6,2},{7,5},{8,12},{9,11},{10,... | collective-permute-start | bytes 2506760 | tf_op jit(solution)/shard_map/ppermute | solution.py:337
  248.9 20.4 %collective-permute-start.46 = (bf16[192,2048]{1,0:T(8,128)(2,1)}, bf16[192,2048]{1,0:T(8,128)(2,1)}, u32[]{:S(2)}, u32[]{:S(2)}) collective-permute-start(bf16[192,2048]{1,0:T(8,128)(2,1)} %collective-permute-done.36.refs_3_), channel_id=1, source_target_pairs={{0,4},{1,3},{2,6},{3,1},{4,0},{5,7},{6,2},{7,5},{8,12},{9,11},{10,... | collective-permute-start | bytes 2359304 | tf_op jit(solution)/shard_map/ppermute | solution.py:337
  250.1 40.5 %collective-permute-start.47 = (bf16[192,2176]{1,0:T(8,128)(2,1)}, bf16[192,2176]{1,0:T(8,128)(2,1)}, u32[]{:S(2)}, u32[]{:S(2)}) collective-permute-start(bf16[192,2176]{1,0:T(8,128)(2,1)} %collective-permute-done.41.refs_1_), channel_id=1, source_target_pairs={{0,16},{1,17},{2,18},{3,19},{4,20},{5,21},{6,22},{7,23},{8,0},{9,1... | collective-permute-start | bytes 2506760 | tf_op jit(solution)/shard_map/ppermute | solution.py:337
  269.4 21.3 %collective-permute-start.48 = (bf16[192,2176]{1,0:T(8,128)(2,1)}, bf16[192,2176]{1,0:T(8,128)(2,1)}, u32[]{:S(2)}, u32[]{:S(2)}) collective-permute-start(bf16[192,2176]{1,0:T(8,128)(2,1)} %collective-permute-done.45.refs_0_), channel_id=1, source_target_pairs={{0,4},{1,3},{2,6},{3,1},{4,0},{5,7},{6,2},{7,5},{8,12},{9,11},{10,... | collective-permute-start | bytes 2506760 | tf_op jit(solution)/shard_map/ppermute | solution.py:337
  270.2 20.4 %collective-permute-start.49 = (bf16[192,2048]{1,0:T(8,128)(2,1)}, bf16[192,2048]{1,0:T(8,128)(2,1)}, u32[]{:S(2)}, u32[]{:S(2)}) collective-permute-start(bf16[192,2048]{1,0:T(8,128)(2,1)} %collective-permute-done.35.refs_2_), channel_id=1, source_target_pairs={{0,4},{1,3},{2,6},{3,1},{4,0},{5,7},{6,2},{7,5},{8,12},{9,11},{10,... | collective-permute-start | bytes 2359304 | tf_op jit(solution)/shard_map/ppermute | solution.py:337
  271.4 38.8 %collective-permute-start.51 = (bf16[192,2176]{1,0:T(8,128)(2,1)}, bf16[192,2176]{1,0:T(8,128)(2,1)}, u32[]{:S(2)}, u32[]{:S(2)}) collective-permute-start(bf16[192,2176]{1,0:T(8,128)(2,1)} %collective-permute-done.45.refs_0_), channel_id=1, source_target_pairs={{0,16},{1,17},{2,18},{3,19},{4,20},{5,21},{6,22},{7,23},{8,0},{9,1... | collective-permute-start | bytes 2506760 | tf_op jit(solution)/shard_map/ppermute | solution.py:337
  293.3 31.4 %collective-permute-start.55 = (bf16[192,2176]{1,0:T(8,128)(2,1)}, bf16[192,2176]{1,0:T(8,128)(2,1)}, u32[]{:S(2)}, u32[]{:S(2)}) collective-permute-start(bf16[192,2176]{1,0:T(8,128)(2,1)} %get-tuple-element.670), channel_id=1, source_target_pairs={{0,4},{1,3},{2,6},{3,1},{4,0},{5,7},{6,2},{7,5},{8,12},{9,11},{10,... | collective-permute-start | bytes 2506760 | tf_op jit(solution)/shard_map/ppermute | solution.py:337
  294.1 30.6 %collective-permute-start.56 = (bf16[192,2176]{1,0:T(8,128)(2,1)}, bf16[192,2176]{1,0:T(8,128)(2,1)}, u32[]{:S(2)}, u32[]{:S(2)}) collective-permute-start(bf16[192,2176]{1,0:T(8,128)(2,1)} %get-tuple-element.671), channel_id=1, source_target_pairs={{0,4},{1,3},{2,6},{3,1},{4,0},{5,7},{6,2},{7,5},{8,12},{9,11},{10,... | collective-permute-start | bytes 2506760 | tf_op jit(solution)/shard_map/ppermute | solution.py:337
  330.3 21.3 %collective-permute-start.57 = (bf16[192,2176]{1,0:T(8,128)(2,1)}, bf16[192,2176]{1,0:T(8,128)(2,1)}, u32[]{:S(2)}, u32[]{:S(2)}) collective-permute-start(bf16[192,2176]{1,0:T(8,128)(2,1)} %collective-permute-done.53.refs_1_), channel_id=1, source_target_pairs={{0,4},{1,3},{2,6},{3,1},{4,0},{5,7},{6,2},{7,5},{8,12},{9,11},{10,... | collective-permute-start | bytes 2506760 | tf_op jit(solution)/shard_map/ppermute | solution.py:337
  354.1 21.4 %collective-permute-start.59 = (bf16[192,2176]{1,0:T(8,128)(2,1)}, bf16[192,2176]{1,0:T(8,128)(2,1)}, u32[]{:S(2)}, u32[]{:S(2)}) collective-permute-start(bf16[192,2176]{1,0:T(8,128)(2,1)} %add_convert_fusion.7), channel_id=1, source_target_pairs={{0,16},{1,17},{2,18},{3,19},{4,20},{5,21},{6,22},{7,23},{8,0},{9,1... | collective-permute-start | bytes 2506760 | tf_op jit(solution)/shard_map/ppermute | solution.py:337
  357.5 27.0 %collective-permute-start.60 = (bf16[192,2176]{1,0:T(8,128)(2,1)}, bf16[192,2176]{1,0:T(8,128)(2,1)}, u32[]{:S(2)}, u32[]{:S(2)}) collective-permute-start(bf16[192,2176]{1,0:T(8,128)(2,1)} %add_convert_fusion.6), channel_id=1, source_target_pairs={{0,16},{1,17},{2,18},{3,19},{4,20},{5,21},{6,22},{7,23},{8,0},{9,1... | collective-permute-start | bytes 2506760 | tf_op jit(solution)/shard_map/ppermute | solution.py:337
  357.8 26.7 %collective-permute-start.61 = (bf16[192,2176]{1,0:T(8,128)(2,1)}, bf16[192,2176]{1,0:T(8,128)(2,1)}, u32[]{:S(2)}, u32[]{:S(2)}) collective-permute-start(bf16[192,2176]{1,0:T(8,128)(2,1)} %get-tuple-element.720), channel_id=1, source_target_pairs={{0,4},{1,3},{2,6},{3,1},{4,0},{5,7},{6,2},{7,5},{8,12},{9,11},{10,... | collective-permute-start | bytes 2506760 | tf_op jit(solution)/shard_map/ppermute | solution.py:337
  358.7 25.7 %collective-permute-start.62 = (bf16[192,2176]{1,0:T(8,128)(2,1)}, bf16[192,2176]{1,0:T(8,128)(2,1)}, u32[]{:S(2)}, u32[]{:S(2)}) collective-permute-start(bf16[192,2176]{1,0:T(8,128)(2,1)} %get-tuple-element.721), channel_id=1, source_target_pairs={{0,4},{1,3},{2,6},{3,1},{4,0},{5,7},{6,2},{7,5},{8,12},{9,11},{10,... | collective-permute-start | bytes 2506760 | tf_op jit(solution)/shard_map/ppermute | solution.py:337
  372.6 32.3 %collective-permute-start.64 = (bf16[192,2176]{1,0:T(8,128)(2,1)}, bf16[192,2176]{1,0:T(8,128)(2,1)S(1)}, u32[]{:S(2)}, u32[]{:S(2)}) collective-permute-start(bf16[192,2176]{1,0:T(8,128)(2,1)} %get-tuple-element.728), channel_id=1, source_target_pairs={{0,4},{1,3},{2,6},{3,1},{4,0},{5,7},{6,2},{7,5},{8,12},{9,11},{10,... | collective-permute-start | bytes 2506760 | tf_op jit(solution)/shard_map/ppermute | solution.py:337
  375.5 33.4 %collective-permute-start.65 = (bf16[192,2176]{1,0:T(8,128)(2,1)}, bf16[192,2176]{1,0:T(8,128)(2,1)S(1)}, u32[]{:S(2)}, u32[]{:S(2)}) collective-permute-start(bf16[192,2176]{1,0:T(8,128)(2,1)} %get-tuple-element.729), channel_id=1, source_target_pairs={{0,4},{1,3},{2,6},{3,1},{4,0},{5,7},{6,2},{7,5},{8,12},{9,11},{10,... | collective-permute-start | bytes 2506760 | tf_op jit(solution)/shard_map/ppermute | solution.py:337
  386.6 22.3 %collective-permute-start.63 = (bf16[192,2176]{1,0:T(8,128)(2,1)S(1)}, bf16[192,2176]{1,0:T(8,128)(2,1)S(1)}, u32[]{:S(2)}, u32[]{:S(2)}) collective-permute-start(bf16[192,2176]{1,0:T(8,128)(2,1)S(1)} %add_convert_fusion.5), channel_id=1, source_target_pairs={{0,2},{1,5},{2,0},{3,7},{4,6},{5,1},{6,4},{7,3},{8,10},{9,13},{10,... | collective-permute-start | bytes 2506760 | tf_op jit(solution)/shard_map/ppermute | solution.py:337
  429.1 53.3 %collective-permute-start.75 = (f32[512,2048]{1,0:T(8,128)}, f32[512,2048]{1,0:T(8,128)S(1)}, u32[]{:S(2)}, u32[]{:S(2)}) collective-permute-start(f32[512,2048]{1,0:T(8,128)} %fusion.23), channel_id=1, source_target_pairs={{0,1},{1,0},{2,3},{3,2},{4,5},{5,4},{6,7},{7,6},{8,9},{9,8},{10,11... | collective-permute-start | bytes 12582920 | tf_op jit(solution)/shard_map/ppermute | solution.py:337
  429.5 21.1 %collective-permute-start.68 = (bf16[192,2176]{1,0:T(8,128)(2,1)S(1)}, bf16[192,2176]{1,0:T(8,128)(2,1)S(1)}, u32[]{:S(2)}, u32[]{:S(2)}) collective-permute-start(bf16[192,2176]{1,0:T(8,128)(2,1)S(1)} %add_convert_fusion.2), channel_id=1, source_target_pairs={{0,16},{1,17},{2,18},{3,19},{4,20},{5,21},{6,22},{7,23},{8,0},{9,1... | collective-permute-start | bytes 2506760 | tf_op jit(solution)/shard_map/ppermute | solution.py:337
  455.5 20.5 %collective-permute-start.72 = (bf16[192,2048]{1,0:T(8,128)(2,1)S(1)}, bf16[192,2048]{1,0:T(8,128)(2,1)S(1)}, u32[]{:S(2)}, u32[]{:S(2)}) collective-permute-start(bf16[192,2048]{1,0:T(8,128)(2,1)S(1)} %get-tuple-element.789.refs_0_), channel_id=1, source_target_pairs={{0,2},{1,5},{2,0},{3,7},{4,6},{5,1},{6,4},{7,3},{8,10},{9,13},{10,... | collective-permute-start | bytes 2359304 | tf_op jit(solution)/shard_map/ppermute | solution.py:337
  456.1 23.8 %collective-permute-start.77 = (bf16[192,2048]{1,0:T(8,128)(2,1)}, bf16[192,2048]{1,0:T(8,128)(2,1)S(1)}, u32[]{:S(2)}, u32[]{:S(2)}) collective-permute-start(bf16[192,2048]{1,0:T(8,128)(2,1)} %get-tuple-element.762), channel_id=1, source_target_pairs={{0,4},{1,3},{2,6},{3,1},{4,0},{5,7},{6,2},{7,5},{8,12},{9,11},{10,... | collective-permute-start | bytes 2359304 | tf_op jit(solution)/shard_map/ppermute | solution.py:337
  458.0 142.1 %collective-permute-start.99 = (f32[2048,1024]{1,0:T(8,128)}, f32[2048,1024]{1,0:T(8,128)}, u32[]{:S(2)}, u32[]{:S(2)}) collective-permute-start(f32[2048,1024]{1,0:T(8,128)} %fusion.22), channel_id=1, source_target_pairs={{0,1},{1,0},{2,3},{3,2},{4,5},{5,4},{6,7},{7,6},{8,9},{9,8},{10,11... | collective-permute-start | bytes 25165832 | tf_op jit(solution)/shard_map/ppermute | solution.py:337
  476.1 20.7 %collective-permute-start.74 = (bf16[192,2048]{1,0:T(8,128)(2,1)S(1)}, bf16[192,2048]{1,0:T(8,128)(2,1)S(1)}, u32[]{:S(2)}, u32[]{:S(2)}) collective-permute-start(bf16[192,2048]{1,0:T(8,128)(2,1)S(1)} %collective-permute-done.72.refs_1_), channel_id=1, source_target_pairs={{0,4},{1,3},{2,6},{3,1},{4,0},{5,7},{6,2},{7,5},{8,12},{9,11},{10,... | collective-permute-start | bytes 2359304 | tf_op jit(solution)/shard_map/ppermute | solution.py:337
  479.9 41.1 %collective-permute-start.80 = (bf16[192,2048]{1,0:T(8,128)(2,1)}, bf16[192,2048]{1,0:T(8,128)(2,1)}, u32[]{:S(2)}, u32[]{:S(2)}) collective-permute-start(bf16[192,2048]{1,0:T(8,128)(2,1)} %add_convert_fusion.16), channel_id=1, source_target_pairs={{0,16},{1,17},{2,18},{3,19},{4,20},{5,21},{6,22},{7,23},{8,0},{9,1... | collective-permute-start | bytes 2359304 | tf_op jit(solution)/shard_map/ppermute | solution.py:337
  482.4 38.7 %collective-permute-start.81 = (bf16[192,2048]{1,0:T(8,128)(2,1)}, bf16[192,2048]{1,0:T(8,128)(2,1)}, u32[]{:S(2)}, u32[]{:S(2)}) collective-permute-start(bf16[192,2048]{1,0:T(8,128)(2,1)} %add_convert_fusion.15), channel_id=1, source_target_pairs={{0,16},{1,17},{2,18},{3,19},{4,20},{5,21},{6,22},{7,23},{8,0},{9,1... | collective-permute-start | bytes 2359304 | tf_op jit(solution)/shard_map/ppermute | solution.py:337
  496.8 24.3 %collective-permute-start.78 = (bf16[192,2048]{1,0:T(8,128)(2,1)}, bf16[192,2048]{1,0:T(8,128)(2,1)}, u32[]{:S(2)}, u32[]{:S(2)}) collective-permute-start(bf16[192,2048]{1,0:T(8,128)(2,1)} %get-tuple-element.794), channel_id=1, source_target_pairs={{0,4},{1,3},{2,6},{3,1},{4,0},{5,7},{6,2},{7,5},{8,12},{9,11},{10,... | collective-permute-start | bytes 2359304 | tf_op jit(solution)/shard_map/ppermute | solution.py:337
  497.1 23.9 %collective-permute-start.79 = (bf16[192,2048]{1,0:T(8,128)(2,1)S(1)}, bf16[192,2048]{1,0:T(8,128)(2,1)}, u32[]{:S(2)}, u32[]{:S(2)}) collective-permute-start(bf16[192,2048]{1,0:T(8,128)(2,1)S(1)} %copy-done.93), channel_id=1, source_target_pairs={{0,4},{1,3},{2,6},{3,1},{4,0},{5,7},{6,2},{7,5},{8,12},{9,11},{10,... | collective-permute-start | bytes 2359304 | tf_op jit(solution)/shard_map/ppermute | solution.py:337
  541.5 21.5 %collective-permute-start.87 = (bf16[192,2048]{1,0:T(8,128)(2,1)}, bf16[192,2048]{1,0:T(8,128)(2,1)}, u32[]{:S(2)}, u32[]{:S(2)}) collective-permute-start(bf16[192,2048]{1,0:T(8,128)(2,1)} %add_convert_fusion.13), channel_id=1, source_target_pairs={{0,16},{1,17},{2,18},{3,19},{4,20},{5,21},{6,22},{7,23},{8,0},{9,1... | collective-permute-start | bytes 2359304 | tf_op jit(solution)/shard_map/ppermute | solution.py:337
  564.5 29.0 %collective-permute-start.92 = (bf16[3,4,64,1664]{3,2,1,0:T(8,128)(2,1)}, bf16[3,4,64,1664]{3,2,1,0:T(8,128)(2,1)S(1)}, u32[]{:S(2)}, u32[]{:S(2)}) collective-permute-start(bf16[3,4,64,1664]{3,2,1,0:T(8,128)(2,1)} %get-tuple-element.859), channel_id=1, source_target_pairs={{0,1},{1,0},{2,3},{3,2},{4,5},{5,4},{6,7},{7,6},{8,9},{9,8},{10,11... | collective-permute-start | bytes 7667720 | tf_op jit(solution)/shard_map/ppermute | solution.py:337
  572.1 21.4 %collective-permute-start.91 = (bf16[4,64,1664]{2,1,0:T(8,128)(2,1)S(1)}, bf16[4,64,1664]{2,1,0:T(8,128)(2,1)}, u32[]{:S(2)}, u32[]{:S(2)}) collective-permute-start(bf16[4,64,1664]{2,1,0:T(8,128)(2,1)S(1)} %add_convert_fusion), channel_id=1, source_target_pairs={{0,16},{1,17},{2,18},{3,19},{4,20},{5,21},{6,22},{7,23},{8,0},{9,1... | collective-permute-start | bytes 2555912 | tf_op jit(solution)/shard_map/ppermute | solution.py:337
  594.9 23.6 %collective-permute-start.96 = (bf16[4,64,1664]{2,1,0:T(8,128)(2,1)S(1)}, bf16[4,64,1664]{2,1,0:T(8,128)(2,1)S(1)}, u32[]{:S(2)}, u32[]{:S(2)}) collective-permute-start(bf16[4,64,1664]{2,1,0:T(8,128)(2,1)S(1)} %fusion.5), channel_id=1, source_target_pairs={{0,16},{1,17},{2,18},{3,19},{4,20},{5,21},{6,22},{7,23},{8,0},{9,1... | collective-permute-start | bytes 2555912 | tf_op jit(solution)/shard_map/ppermute | solution.py:337
  618.8 24.4 %collective-permute-start.100 = (bf16[4,64,1664]{2,1,0:T(8,128)(2,1)S(1)}, bf16[4,64,1664]{2,1,0:T(8,128)(2,1)S(1)}, u32[]{:S(2)}, u32[]{:S(2)}) collective-permute-start(bf16[4,64,1664]{2,1,0:T(8,128)(2,1)S(1)} %fusion.3), channel_id=1, source_target_pairs={{0,16},{1,17},{2,18},{3,19},{4,20},{5,21},{6,22},{7,23},{8,0},{9,1... | collective-permute-start | bytes 2555912 | tf_op jit(solution)/shard_map/ppermute | solution.py:337
  619.7 23.5 %collective-permute-start.101 = (bf16[192,2048]{1,0:T(8,128)(2,1)S(1)}, bf16[192,2048]{1,0:T(8,128)(2,1)S(1)}, u32[]{:S(2)}, u32[]{:S(2)}) collective-permute-start(bf16[192,2048]{1,0:T(8,128)(2,1)S(1)} %add_convert_fusion.12), channel_id=1, source_target_pairs={{0,2},{1,5},{2,0},{3,7},{4,6},{5,1},{6,4},{7,3},{8,10},{9,13},{10,... | collective-permute-start | bytes 2359304 | tf_op jit(solution)/shard_map/ppermute | solution.py:337
  621.7 21.5 %collective-permute-start.102 = (bf16[192,2048]{1,0:T(8,128)(2,1)S(1)}, bf16[192,2048]{1,0:T(8,128)(2,1)S(1)}, u32[]{:S(2)}, u32[]{:S(2)}) collective-permute-start(bf16[192,2048]{1,0:T(8,128)(2,1)S(1)} %add_convert_fusion.11), channel_id=1, source_target_pairs={{0,2},{1,5},{2,0},{3,7},{4,6},{5,1},{6,4},{7,3},{8,10},{9,13},{10,... | collective-permute-start | bytes 2359304 | tf_op jit(solution)/shard_map/ppermute | solution.py:337
  626.3 28.6 %collective-permute-start.108 = (bf16[192,2048]{1,0:T(8,128)(2,1)S(1)}, bf16[192,2048]{1,0:T(8,128)(2,1)S(1)}, u32[]{:S(2)}, u32[]{:S(2)}) collective-permute-start(bf16[192,2048]{1,0:T(8,128)(2,1)S(1)} %add_convert_fusion.9), channel_id=1, source_target_pairs={{0,2},{1,5},{2,0},{3,7},{4,6},{5,1},{6,4},{7,3},{8,10},{9,13},{10,... | collective-permute-start | bytes 2359304 | tf_op jit(solution)/shard_map/ppermute | solution.py:337
  (157 other events, 2820.3 us)
